TPU v7x, 32 devices: a whole 2x2x4 slice. The times are simulated.
32 devices in a mesh: gx: 8 (over y, x, core), gy: 4 (over z).
Axes of the slice: x: 2, y: 2, z: 4, core: 2. Of those that a mesh axis runs over, the one named last changes fastest.
Arguments:
- tiles: bfloat16 [3, 8, 384, 4352], P(None, None, 'gy', 'gx'), may hold values from 0.099609375 to 4
- offsets: int32 [4, 8, 2], P('gy', 'gx'), may hold values from 0 to 32, as said below
- psf: float32 [3, 3, 31], replicated, may hold values from 0.05 to 1
Outputs:
- restored: float32 [3, 8, 256, 4096], P(None, None, 'gy', 'gx')
- level_one: float32 [3, 4, 128, 2048], P(None, None, 'gy', 'gx')
- level_two: float32 [3, 2, 64, 1024], P(None, None, 'gy', 'gx')
Inputs may be any that keep to these rules, and one draw needn't show every extreme that they name: offsets[j, i, 0] is 0 for j = 0 and 32 for j = 3; offsets[j, i, 1] is 0 for i = 0 and 32 for i = 7.
All inputs are finite; a program needn't handle non-finite values.
Results may differ from a plain program's by a relative error of at most 0.0015.
Values may be sent and summed in bfloat16 or wider, within the bound.
No kernel may reach another device: no remote copies, remote signals or barrier semaphores. Data moves between devices by JAX's collectives and lax.ppermute only.
A program may use at most 128 MiB of HBM per device.

v0:
```python
import functools

import jax
import jax.numpy as jnp
import ml_dtypes
import numpy as np
from jax import lax
from jax.experimental import pallas as pl
from jax.experimental.pallas import tpu as pltpu
from jax.sharding import PartitionSpec as P

MARGIN = 32
REACH = 15
TAPS = 31
DEPTH = 8
LANE = 128
GAUSS = (1, 4, 6, 4, 1)
TINY = 1e-30
BF16 = jnp.bfloat16
F32 = jnp.float32
MIB = 1 << 20

BEFORE = 66
FRAME = 200
BIG = 34
SMALL = 26


def params(mib):
    return pltpu.CompilerParams(vmem_limit_bytes=mib * MIB)


def cost(flops, nbytes):
    return pl.CostEstimate(flops=int(flops), bytes_accessed=int(nbytes), transcendentals=0)


def dot(a, b):
    return jnp.dot(a, b, preferred_element_type=F32)


def split(value):
    high = value.astype(BF16)
    return high, (value - high.astype(F32)).astype(BF16)


def place_kernel(off_ref, tile_ref, own_ref, right_ref, low_ref, corner_ref, canvas):
    depth, tile_y, tile_x = tile_ref.shape[1:]
    parts = canvas.shape[0]
    wide = parts * LANE
    rows = own_ref.shape[1]
    cols = own_ref.shape[2]
    top = off_ref[0]
    left = off_ref[1]
    canvas[...] = jnp.zeros_like(canvas)
    shift = (
        lax.broadcasted_iota(jnp.int32, (tile_x, wide), 1)
        == lax.broadcasted_iota(jnp.int32, (tile_x, wide), 0) + left
    )
    shift = jnp.where(shift, 1.0, 0.0).astype(BF16)
    for z in range(depth):
        moved = dot(tile_ref[0, z], shift)
        for b in range(parts):
            to = pl.ds(top * depth + z, tile_y, stride=depth)
            canvas[b, to, :] = moved[:, b * LANE : (b + 1) * LANE]
    for b in range(parts - 1):
        to = slice(b * LANE, (b + 1) * LANE)
        own_ref[0, :, to] = canvas[b, :rows, :].astype(BF16)
        low_ref[0, :, to] = canvas[b, rows:, :].astype(BF16)
    right_ref[0] = canvas[parts - 1, :rows, :].astype(BF16)
    half = rows // 2
    upper = canvas[parts - 1, rows : rows + half, :]
    lower = canvas[parts - 1, rows + half :, :]
    corner_ref[0] = (upper + pltpu.roll(lower, LANE // 2, 1)).astype(BF16)


def place(tiles, offsets):
    n, depth, tile_y, tile_x = tiles.shape
    rows = (tile_y - MARGIN) * depth
    cols = tile_x - MARGIN
    block = lambda r, c: pl.BlockSpec((1, r, c), lambda i, off: (i, 0, 0))
    shape = lambda r, c: jax.ShapeDtypeStruct((n, r, c), BF16)
    sizes = ((rows, cols), (rows, LANE), (rows, cols), (rows // 2, LANE))
    return pl.pallas_call(
        place_kernel,
        grid_spec=pltpu.PrefetchScalarGridSpec(
            num_scalar_prefetch=1,
            grid=(n,),
            in_specs=[pl.BlockSpec((1, depth, tile_y, tile_x), lambda i, off: (i, 0, 0, 0))],
            out_specs=[block(*s) for s in sizes],
            scratch_shapes=[pltpu.VMEM((cols // LANE + 1, 2 * rows, LANE), F32)],
        ),
        out_shape=[shape(*s) for s in sizes],
        compiler_params=params(32),
        cost_estimate=cost(n * 2e9, n * 2.5e6),
        name="place",
    )(offsets, tiles)


def join_kernel(own_ref, low_ref, right_ref, corner_ref, exact_ref, short_ref):
    rows = own_ref.shape[1]
    half = rows // 2

    def seen(x):
        return jnp.where(x != 0, 1.0, 0.0)

    own = own_ref[0].astype(F32)
    low = low_ref[0].astype(F32)
    total = own + low
    count = seen(own) + seen(low)
    right = right_ref[0].astype(F32)
    corner = corner_ref[0].astype(F32)
    lane = lax.broadcasted_iota(jnp.int32, (half, LANE), 1)
    inside = lane < LANE // 2
    upper = jnp.where(inside, corner, 0.0)
    lower = jnp.where(inside, pltpu.roll(corner, LANE // 2, 1), 0.0)
    corner = jnp.concatenate([upper, lower], axis=0)
    edge_total = total[:, :LANE] + right + corner
    edge_count = count[:, :LANE] + seen(right) + seen(corner)
    edge = edge_total / edge_count
    rest = total[:, LANE:] / count[:, LANE:]
    exact_ref[0, :, :LANE] = edge
    exact_ref[0, :, LANE:] = rest
    short_ref[0, :, :LANE] = edge.astype(BF16)
    short_ref[0, :, LANE:] = rest.astype(BF16)


def join(own, low, right, corner):
    n, rows, cols = own.shape
    block = lambda a: pl.BlockSpec((1,) + a.shape[1:], lambda i: (i, 0, 0))
    return pl.pallas_call(
        join_kernel,
        grid=(n,),
        in_specs=[block(a) for a in (own, low, right, corner)],
        out_specs=[block(own), block(own)],
        out_shape=[jax.ShapeDtypeStruct(own.shape, F32), jax.ShapeDtypeStruct(own.shape, BF16)],
        compiler_params=params(32),
        cost_estimate=cost(n * 5e6, n * 3e6),
        name="join",
    )(own, low, right, corner)


def bands_kernel(kern_ref, across_ref, within_ref):
    which = pl.program_id(0)
    wide = 3 * 2 * LANE
    shape = (16, wide)
    row = lax.broadcasted_iota(jnp.int32, shape, 0)
    lane = lax.broadcasted_iota(jnp.int32, shape, 1)
    tap = row - (lane - 4 * LANE) - (LANE - REACH)
    base = jnp.zeros(shape, F32)
    for k in range(TAPS):
        base = jnp.where(tap == k, kern_ref[which, 2 * TAPS + k], base)

    @pl.loop(0, across_ref.shape[1] // 16)
    def _(q):
        turned = pltpu.roll(base, wide - 4 * LANE + 16 * q, 1)
        across_ref[0, pl.ds(pl.multiple_of(16 * q, 16), 16), :] = turned[:, : 2 * LANE].astype(BF16)

    shape = (16, within_ref.shape[2])
    row = lax.broadcasted_iota(jnp.int32, shape, 0)
    lane = lax.broadcasted_iota(jnp.int32, shape, 1)
    tap_y = lane // DEPTH - row // DEPTH
    tap_z = lane % DEPTH - row % DEPTH + REACH
    in_y = jnp.zeros(shape, F32)
    in_z = jnp.zeros(shape, F32)
    for k in range(TAPS):
        in_y = jnp.where(tap_y == k, kern_ref[which, TAPS + k], in_y)
    for k in range(REACH + 1 - DEPTH, REACH + DEPTH):
        in_z = jnp.where(tap_z == k, kern_ref[which, k], in_z)
    both = in_y * in_z

    @pl.loop(0, within_ref.shape[1] // 16)
    def _(q):
        turned = pltpu.roll(both, 16 * q, 1)
        within_ref[0, pl.ds(pl.multiple_of(16 * q, 16), 16), :] = turned.astype(BF16)


def bands(kern):
    count = kern.shape[0]
    shapes = ((4 * LANE, 2 * LANE), (BIG * DEPTH, (BIG + 2 * REACH) * DEPTH))
    return pl.pallas_call(
        bands_kernel,
        grid=(count,),
        in_specs=[pl.BlockSpec(memory_space=pltpu.SMEM)],
        out_specs=[pl.BlockSpec((1,) + s, lambda i: (i, 0, 0)) for s in shapes],
        out_shape=[jax.ShapeDtypeStruct((count,) + s, BF16) for s in shapes],
        compiler_params=params(32),
        cost_estimate=cost(count * 1e6, count * 4e6),
        name="bands",
    )(kern)


@functools.lru_cache(None)
def pyramid_matrices(rows, cols, depth):
    half_x, half_y, half_z = cols // 2, rows // 2, depth // 2
    taps = np.array(GAUSS, np.float32) / 16
    extra_x = (-2, -1, half_x)
    one_x = np.zeros((cols + 2 * LANE, half_x + LANE), np.float32)
    for lane in range(half_x + len(extra_x)):
        x = lane if lane < half_x else extra_x[lane - half_x]
        for k in range(5):
            one_x[LANE + 2 * x + k - 2, lane] = taps[k]
    extra_y = (-2, -1, half_y)
    order = [(z, y) for z in range(half_z) for y in range(half_y)]
    order += [(z, y) for y in extra_y for z in range(half_z)]
    height = -(-len(order) // 16) * 16
    reach_in = (rows + 10) * depth
    one_zy = np.zeros((height, reach_in), np.float32)
    for i, (z, y) in enumerate(order):
        for a in range(5):
            for b in range(5):
                zi = 2 * z + b - 2
                if 0 <= zi < depth:
                    one_zy[i, (2 * y + a - 2 + 6) * depth + zi] = taps[a] * taps[b]
    two_x = np.zeros((half_x + LANE, half_x // 2), np.float32)
    for x in range(half_x // 2):
        for k in range(5):
            source = 2 * x + k - 2
            lane = source if 0 <= source < half_x else half_x + extra_x.index(source)
            two_x[lane, x] = taps[k]
    place_of = {zy: i for i, zy in enumerate(order)}
    two_zy = np.zeros((half_z * half_y // 4, height), np.float32)
    for z in range(half_z // 2):
        for y in range(half_y // 2):
            for a in range(5):
                for b in range(5):
                    at = (2 * z + b - 2, 2 * y + a - 2)
                    if 0 <= at[0] < half_z:
                        two_zy[z * (half_y // 2) + y, place_of[at]] = taps[a] * taps[b]
    return tuple(m.astype(ml_dtypes.bfloat16) for m in (one_x, one_zy, two_x, two_zy))


def deconvolve_kernel(
    sides_ref,
    exact_ref,
    above_ref,
    below_ref,
    far_ref,
    left_ref,
    right_ref,
    across_ref,
    within_ref,
    one_x_ref,
    one_zy_ref,
    two_x_ref,
    two_zy_ref,
    restored_ref,
    level_one_ref,
    level_two_ref,
    joined,
    joined_short,
    ratio,
    estimate,
    estimate_short,
    result,
    high,
    low,
):
    rows8, cols = exact_ref.shape[1:]
    wide = cols + 2 * LANE
    far8 = far_ref.shape[1]
    own = slice(far8 + rows8, far8 + 2 * rows8)
    frame8 = far8 + 3 * rows8
    middle = slice(LANE, LANE + cols)

    joined_short[:far8, middle] = far_ref[0]
    joined_short[far8 : far8 + rows8, middle] = above_ref[0]
    joined_short[own, middle] = exact_ref[0].astype(BF16)
    joined_short[far8 + 2 * rows8 : frame8, middle] = below_ref[0]
    joined_short[:frame8, :LANE] = left_ref[0]
    joined_short[:frame8, LANE + cols :] = right_ref[0]
    joined_short[frame8:, :] = jnp.zeros_like(joined_short[frame8:, :])
    joined[...] = joined_short[...].astype(F32)
    joined[own, middle] = exact_ref[0]

    def run_x(source, which, chunks, size, exact):
        @pl.loop(0, chunks)
        def _(i):
            at = pl.ds(pl.multiple_of(i * size, 16), size)
            for n in range(wide // (2 * LANE)):
                begin = 2 * LANE * n - LANE
                lo, hi = max(begin, 0), min(begin + 4 * LANE, wide)
                out = dot(source[at, lo:hi], across_ref[0, which, lo - begin : hi - begin, :])
                to = slice(2 * LANE * n, 2 * LANE * (n + 1))
                if exact:
                    high[at, to], low[at, to] = split(out)
                else:
                    high[at, to] = out.astype(BF16)

    def run_zy(which, chunks, size, exact, finish):
        deep = (size + 2 * REACH) * DEPTH
        matrix = within_ref[0, which, : size * DEPTH, :deep]

        @pl.loop(0, chunks)
        def _(i):
            start = i * (size * DEPTH)
            at = pl.ds(pl.multiple_of(start, 16), deep)
            for n in range(wide // (2 * LANE)):
                to = slice(2 * LANE * n, 2 * LANE * (n + 1))
                out = dot(matrix, high[at, to])
                if exact:
                    out = out + dot(matrix, low[at, to])
                finish(start, size * DEPTH, to, out)

    def rows_at(start, shift, size):
        return pl.ds(pl.multiple_of(start + shift * DEPTH, 8), size)

    def ratio_from(shift):
        def finish(start, size, to, out):
            top = joined[rows_at(start, shift, size), to]
            at = pl.ds(pl.multiple_of(start, 16), size)
            ratio[at, to] = (top / jnp.maximum(out, TINY)).astype(BF16)

        return finish

    def first_estimate(start, size, to, out):
        at = pl.ds(pl.multiple_of(start, 16), size)
        value = joined[rows_at(start, 2 * REACH, size), to] * out
        estimate[at, to] = value
        estimate_short[at, to] = value.astype(BF16)

    def last_estimate(start, size, to, out):
        at = pl.ds(pl.multiple_of(start, 16), size)
        value = estimate[rows_at(start, 2 * REACH, size), to] * out
        for b in range(2):
            result[to.start // LANE + b, at, :] = value[:, b * LANE : (b + 1) * LANE]

    run_x(joined_short, 0, 5, 40 * DEPTH, False)
    run_zy(0, 5, BIG, False, ratio_from(REACH))
    run_x(ratio, 1, 5, BIG * DEPTH, True)
    run_zy(1, 4, BIG, True, first_estimate)
    run_x(estimate_short, 0, 4, BIG * DEPTH, False)
    run_zy(0, 4, SMALL, False, ratio_from(3 * REACH))
    ratio[4 * SMALL * DEPTH : (4 * SMALL + 4) * DEPTH, :] = jnp.zeros((4 * DEPTH, wide), BF16)
    run_x(ratio, 1, 3, 36 * DEPTH, True)
    run_zy(1, 3, SMALL, True, last_estimate)

    planes = restored_ref.shape[1]
    height = restored_ref.shape[2]
    for z in range(planes):
        at = pl.ds(6 * planes + z, height, stride=planes)
        for b in range(cols // LANE):
            restored_ref[0, z, :, b * LANE : (b + 1) * LANE] = result[1 + b, at, :]

    def twice(left, right):
        big, small = split(right)
        return dot(left, big) + dot(left, small)

    def twice_left(left, right):
        big, small = split(left)
        return dot(big, right) + dot(small, right)

    reach_in = one_zy_ref.shape[1]
    fine = jnp.concatenate([result[b, :reach_in, :] for b in range(wide // LANE)], axis=1)
    one = twice(one_zy_ref[...], twice_left(fine, one_x_ref[...]))
    half_z, half_y, half_x = level_one_ref.shape[1:]
    inner = half_z * half_y
    level_one_ref[0] = one[:inner, :half_x].reshape(half_z, half_y, half_x)
    row = lax.broadcasted_iota(jnp.int32, one.shape, 0) - inner
    lane = lax.broadcasted_iota(jnp.int32, one.shape, 1) - half_x
    up, down, left, right = (sides_ref[k] for k in range(4))
    keep_row = jnp.where(row < 0, 1, jnp.where(row < 2 * half_z, up, down))
    keep_lane = jnp.where(lane < 0, 1, jnp.where(lane < 2, left, right))
    one = jnp.where(keep_row * keep_lane > 0, one, 0.0)
    two = twice(two_zy_ref[...], twice_left(one, two_x_ref[...]))
    level_two_ref[0] = two.reshape(level_two_ref.shape[1:])


def deconvolve(sides, exact, above, below, far, left, right, across, within, matrices):
    n, rows8, cols = exact.shape
    rows = rows8 // DEPTH
    wide = cols + 2 * LANE
    per = lambda a: pl.BlockSpec((1,) + a.shape[1:], lambda i: (i,) + (0,) * (a.ndim - 1))
    same = lambda a: pl.BlockSpec(a.shape, lambda i: (0,) * a.ndim)
    operands = (exact, above, below, far, left, right, across, within)
    outs = (
        (n, DEPTH, rows, cols),
        (n, DEPTH // 2, rows // 2, cols // 2),
        (n, DEPTH // 4, rows // 4, cols // 4),
    )
    shapes = [jax.ShapeDtypeStruct(s, F32) for s in outs]
    first = 5 * BIG * DEPTH
    second = 4 * BIG * DEPTH
    third = 3 * SMALL * DEPTH
    return pl.pallas_call(
        deconvolve_kernel,
        grid=(n,),
        in_specs=[pl.BlockSpec(memory_space=pltpu.SMEM)]
        + [per(a) for a in operands]
        + [same(m) for m in matrices],
        out_specs=[per(s) for s in shapes],
        out_shape=shapes,
        scratch_shapes=[
            pltpu.VMEM((FRAME * DEPTH, wide), F32),
            pltpu.VMEM((FRAME * DEPTH, wide), BF16),
            pltpu.VMEM((first, wide), BF16),
            pltpu.VMEM((second, wide), F32),
            pltpu.VMEM((second, wide), BF16),
            pltpu.VMEM((wide // LANE, third, LANE), F32),
            pltpu.VMEM((FRAME * DEPTH, wide), BF16),
            pltpu.VMEM((first, wide), BF16),
        ],
        compiler_params=params(52),
        cost_estimate=cost(n * 9e9, n * 8e6),
        name="deconvolve",
    )(sides, *operands, *matrices)


def per_device(tiles, offsets, psf):
    chans, depth, tile_y, tile_x = tiles.shape
    cols = tile_x - MARGIN
    rows = tile_y - MARGIN
    size_x, size_y = lax.axis_size("gx"), lax.axis_size("gy")
    at_x, at_y = lax.axis_index("gx"), lax.axis_index("gy")

    def shift(block, axis, distance):
        devices = range(lax.axis_size(axis))
        route = [(i, i + distance) for i in devices if i + distance in devices]
        return lax.ppermute(block, axis, route)

    def shift_diagonal(block):
        route = [
            (x * size_y + y, (x + 1) * size_y + y + 1)
            for x in range(size_x - 1)
            for y in range(size_y - 1)
        ]
        return lax.ppermute(block, ("gx", "gy"), route)

    kern = psf / jnp.sum(psf, axis=-1, keepdims=True)
    both = jnp.stack([kern, kern[:, :, ::-1]], axis=1)
    across, within = bands(both.reshape(chans * 2, 3 * TAPS))
    across = across.reshape((chans, 2) + across.shape[1:])
    within = within.reshape((chans, 2) + within.shape[1:])
    matrices = [jnp.asarray(m) for m in pyramid_matrices(rows, cols, depth)]
    sides = jnp.stack([at_y > 0, at_y < size_y - 1, at_x > 0, at_x < size_x - 1])
    sides = sides.astype(jnp.int32)

    own, right, low, corner = place(tiles, offsets.reshape(2))
    low = shift(low, "gy", 1)
    right = shift(right, "gx", 1)
    corner = shift_diagonal(corner)
    exact, short = join(own, low, right, corner)
    above = shift(short, "gy", 1)
    below = shift(short, "gy", -1)
    far = shift(short[:, -2 * depth :, :], "gy", 2)
    column = (far, above, short, below)
    last = jnp.concatenate([a[:, :, -LANE:] for a in column], axis=1)
    first = jnp.concatenate([a[:, :, :LANE] for a in column], axis=1)
    left = shift(last, "gx", 1)
    right = shift(first, "gx", -1)
    return tuple(
        deconvolve(sides, exact, above, below, far, left, right, across, within, matrices)
    )


def solution(mesh):
    in_specs = (P(None, None, "gy", "gx"), P("gy", "gx", None), P())
    out_specs = (P(None, None, "gy", "gx"), P(None, None, "gy", "gx"), P(None, None, "gy", "gx"))
    return jax.shard_map(
        per_device, mesh=mesh, in_specs=in_specs, out_specs=out_specs, check_vma=False
    )
```

profile of v0, /device:TPU:11, one launch (start us, length us, event | category | flops | bytes accessed | tf_op | source)
XLA Modules:
  0.0 184.2 jit_solution(4281616712907903108)
XLA Ops:
  0.6 1.8 copy-done.1
  2.5 0.7 copy-done.2
  3.1 6.4 %place.1 = (bf16[3,512,512]{2,1,0:T(8,128)(2,1)S(1)}, bf16[3,512,128]{2,1,0:T(8,128)(2,1)S(1)}, bf16[3,512,512]{2,1,0:T(8,128)(2,1)S(1)}, bf16[3,256,128]{2,1,0:T(8,128)(2,1)S(1)}) custom-call(s32[2]{0:T(128)S(1)} %bitcast.10, bf16[3,8,96,544]{3,2,1,0:T(8,128)(2,1)S(1)} %copy-done.1), custom_call_target="tpu_custom_call" | custom-call | flops 6000000000 | bytes 7500000 | tf_op jit(solution)/shard_map/place/pallas_call | solution.py:83
  9.5 3.2 %collective-permute-start = (bf16[3,512,512]{2,1,0:T(8,128)(2,1)S(1)}, bf16[3,512,512]{2,1,0:T(8,128)(2,1)S(1)}, u32[]{:S(2)}, u32[]{:S(2)}) collective-permute-start(bf16[3,512,512]{2,1,0:T(8,128)(2,1)S(1)} %get-tuple-element.12), channel_id=1, source_target_pairs={{0,1},{1,2},{2,3},{4,5},{5,6},{6,7},{8,9},{9,10},{10,11},{12,13},{... | collective-permute-start | bytes 4718600 | tf_op jit(solution)/shard_map/ppermute | solution.py:418
  12.7 4.0 %collective-permute-start.1 = (bf16[3,512,128]{2,1,0:T(8,128)(2,1)S(1)}, bf16[3,512,128]{2,1,0:T(8,128)(2,1)S(1)}, u32[]{:S(2)}, u32[]{:S(2)}) collective-permute-start(bf16[3,512,128]{2,1,0:T(8,128)(2,1)S(1)} %get-tuple-element.13), channel_id=1, source_target_pairs={{0,4},{4,8},{8,12},{12,16},{16,20},{20,24},{24,28},{1,5},{5,9},{9,... | collective-permute-start | bytes 1179656 | tf_op jit(solution)/shard_map/ppermute | solution.py:418
  16.7 2.9 %collective-permute-start.2 = (bf16[3,256,128]{2,1,0:T(8,128)(2,1)S(1)}, bf16[3,256,128]{2,1,0:T(8,128)(2,1)S(1)}, u32[]{:S(2)}, u32[]{:S(2)}) collective-permute-start(bf16[3,256,128]{2,1,0:T(8,128)(2,1)S(1)} %get-tuple-element.14), channel_id=1, source_target_pairs={{0,5},{1,6},{2,7},{4,9},{5,10},{6,11},{8,13},{9,14},{10,15},{12,17... | collective-permute-start | bytes 589832 | tf_op jit(solution)/shard_map/ppermute | solution.py:426
  19.6 32.1 %collective-permute-done.2.corner_ref = bf16[3,256,128]{2,1,0:T(8,128)(2,1)S(1)} collective-permute-done((bf16[3,256,128]{2,1,0:T(8,128)(2,1)S(1)}, bf16[3,256,128]{2,1,0:T(8,128)(2,1)S(1)}, u32[]{:S(2)}, u32[]{:S(2)}) %collective-permute-start.2) | collective-permute-done | bytes 196640 | tf_op jit(solution)/shard_map/ppermute | solution.py:426
  51.7 2.7 %join.1 = (f32[3,512,512]{2,1,0:T(8,128)S(1)}, bf16[3,512,512]{2,1,0:T(8,128)(2,1)S(1)}) custom-call(bf16[3,512,512]{2,1,0:T(8,128)(2,1)S(1)} %get-tuple-element.11.own_ref, bf16[3,512,512]{2,1,0:T(8,128)(2,1)S(1)} %collective-permute-done.low_ref, bf16[3,512,128]{2,1,0:T(8,128)(2,1)S(1)} %collective-permute-done.1.right_ref, ...), custom_call_target="tpu_custom_call" | custom-call | flops 15000000 | bytes 9000000 | tf_op jit(solution)/shard_map/join/pallas_call | solution.py:130
  54.4 1.9 %collective-permute-start.4 = (bf16[3,512,512]{2,1,0:T(8,128)(2,1)S(1)}, bf16[3,512,512]{2,1,0:T(8,128)(2,1)S(1)}, u32[]{:S(2)}, u32[]{:S(2)}) collective-permute-start(bf16[3,512,512]{2,1,0:T(8,128)(2,1)S(1)} %get-tuple-element.16), channel_id=1, source_target_pairs={{1,0},{2,1},{3,2},{5,4},{6,5},{7,6},{9,8},{10,9},{11,10},{13,12},{... | collective-permute-start | bytes 4718600 | tf_op jit(solution)/shard_map/ppermute | solution.py:418
  56.3 3.4 %collective-permute-start.3 = (bf16[3,512,512]{2,1,0:T(8,128)(2,1)S(1)}, bf16[3,512,512]{2,1,0:T(8,128)(2,1)S(1)}, u32[]{:S(2)}, u32[]{:S(2)}) collective-permute-start(bf16[3,512,512]{2,1,0:T(8,128)(2,1)S(1)} %get-tuple-element.16), channel_id=1, source_target_pairs={{0,1},{1,2},{2,3},{4,5},{5,6},{6,7},{8,9},{9,10},{10,11},{12,13},{... | collective-permute-start | bytes 4718600 | tf_op jit(solution)/shard_map/ppermute | solution.py:418
  59.7 2.4 %collective-permute-start.5 = (bf16[3,16,512]{2,1,0:T(8,128)(2,1)S(1)}, bf16[3,16,512]{2,1,0:T(8,128)(2,1)S(1)}, u32[]{:S(2)}, u32[]{:S(2)}) collective-permute-start(bf16[3,16,512]{2,1,0:T(8,128)(2,1)S(1)} %slice.27), channel_id=1, source_target_pairs={{0,2},{1,3},{4,6},{5,7},{8,10},{9,11},{12,14},{13,15},{16,18},{17,... | collective-permute-start | bytes 147464 | tf_op jit(solution)/shard_map/ppermute | solution.py:418
  62.1 0.1 fusion.1
  62.2 33.3 %collective-permute-done.5.far_ref = bf16[3,16,512]{2,1,0:T(8,128)(2,1)S(1)} collective-permute-done((bf16[3,16,512]{2,1,0:T(8,128)(2,1)S(1)}, bf16[3,16,512]{2,1,0:T(8,128)(2,1)S(1)}, u32[]{:S(2)}, u32[]{:S(2)}) %collective-permute-start.5) | collective-permute-done | bytes 49184 | tf_op jit(solution)/shard_map/ppermute | solution.py:418
  95.6 0.1 fusion.2
  95.8 0.1 fusion
  95.9 0.8 copy-done.9
  96.7 0.6 copy-done.10
  97.3 0.1 pad_maximum_fusion
  97.4 0.0 copy-start.5
  97.4 4.0 %collective-permute-start.6 = (bf16[3,1552,128]{2,1,0:T(8,128)(2,1)S(1)}, bf16[3,1552,128]{2,1,0:T(8,128)(2,1)}, u32[]{:S(2)}, u32[]{:S(2)}) collective-permute-start(bf16[3,1552,128]{2,1,0:T(8,128)(2,1)S(1)} %pad_maximum_fusion), channel_id=1, source_target_pairs={{0,4},{4,8},{8,12},{12,16},{16,20},{20,24},{24,28},{1,5},{5,9},{9,... | collective-permute-start | bytes 3575816 | tf_op jit(solution)/shard_map/ppermute | solution.py:418
  101.4 0.1 pad_maximum_fusion.1
  101.5 1.9 %collective-permute-start.7 = (bf16[3,1552,128]{2,1,0:T(8,128)(2,1)S(1)}, bf16[3,1552,128]{2,1,0:T(8,128)(2,1)}, u32[]{:S(2)}, u32[]{:S(2)}) collective-permute-start(bf16[3,1552,128]{2,1,0:T(8,128)(2,1)S(1)} %pad_maximum_fusion.1), channel_id=1, source_target_pairs={{4,0},{8,4},{12,8},{16,12},{20,16},{24,20},{28,24},{5,1},{9,5},{13... | collective-permute-start | bytes 3575816 | tf_op jit(solution)/shard_map/ppermute | solution.py:418
  103.5 0.1 reduce_sum.9
  103.6 0.1 broadcast_divide_fusion
  103.6 0.1 rev.3
  103.7 0.1 fusion.4
  103.8 0.1 reshape.20.kern_ref
  103.9 24.7 %bands.1 = (bf16[6,512,256]{2,1,0:T(8,128)(2,1)S(1)}, bf16[6,272,512]{2,1,0:T(8,128)(2,1)S(1)}) custom-call(f32[6,93]{1,0:T(8,128)S(1)} %reshape.20.kern_ref), custom_call_target="tpu_custom_call" | custom-call | flops 6000000 | bytes 24000000 | tf_op jit(solution)/shard_map/bands/pallas_call | solution.py:180
  128.6 1.2 copy-done.3
  129.8 1.2 copy-done.4
  131.0 0.1 add_convert_fusion.sides_ref
  131.2 53.0 %deconvolve.1 = (f32[3,8,64,512]{3,2,1,0:T(8,128)}, f32[3,4,32,256]{3,2,1,0:T(8,128)}, f32[3,2,16,128]{3,2,1,0:T(8,128)}) custom-call(s32[4]{0:T(128)S(1)} %add_convert_fusion.sides_ref, f32[3,512,512]{2,1,0:T(8,128)} %copy-done, bf16[3,512,512]{2,1,0:T(8,128)(2,1)} %copy-done.10, bf16[3,512,512]{2,1,0:T(8,128)(2,1)} %copy-done.9, ...), custom_call_target="tpu_custom_call" | custom-call | flops 27000000512 | bytes 24000000 | tf_op jit(solution)/shard_map/deconvolve/pallas_call | solution.py:384
  (27 shorter events, 0.1 us)
Async XLA Ops:
  0.6 1.8 copy-start.1
  2.5 0.7 copy-start.2
  9.5 42.2 %collective-permute-start = (bf16[3,512,512]{2,1,0:T(8,128)(2,1)S(1)}, bf16[3,512,512]{2,1,0:T(8,128)(2,1)S(1)}, u32[]{:S(2)}, u32[]{:S(2)}) collective-permute-start(bf16[3,512,512]{2,1,0:T(8,128)(2,1)S(1)} %get-tuple-element.12), channel_id=1, source_target_pairs={{0,1},{1,2},{2,3},{4,5},{5,6},{6,7},{8,9},{9,10},{10,11},{12,13},{... | collective-permute-start | bytes 4718600 | tf_op jit(solution)/shard_map/ppermute | solution.py:418
  12.7 39.0 %collective-permute-start.1 = (bf16[3,512,128]{2,1,0:T(8,128)(2,1)S(1)}, bf16[3,512,128]{2,1,0:T(8,128)(2,1)S(1)}, u32[]{:S(2)}, u32[]{:S(2)}) collective-permute-start(bf16[3,512,128]{2,1,0:T(8,128)(2,1)S(1)} %get-tuple-element.13), channel_id=1, source_target_pairs={{0,4},{4,8},{8,12},{12,16},{16,20},{20,24},{24,28},{1,5},{5,9},{9,... | collective-permute-start | bytes 1179656 | tf_op jit(solution)/shard_map/ppermute | solution.py:418
  16.7 35.1 %collective-permute-start.2 = (bf16[3,256,128]{2,1,0:T(8,128)(2,1)S(1)}, bf16[3,256,128]{2,1,0:T(8,128)(2,1)S(1)}, u32[]{:S(2)}, u32[]{:S(2)}) collective-permute-start(bf16[3,256,128]{2,1,0:T(8,128)(2,1)S(1)} %get-tuple-element.14), channel_id=1, source_target_pairs={{0,5},{1,6},{2,7},{4,9},{5,10},{6,11},{8,13},{9,14},{10,15},{12,17... | collective-permute-start | bytes 589832 | tf_op jit(solution)/shard_map/ppermute | solution.py:426
  54.4 41.3 %copy-start = (f32[3,512,512]{2,1,0:T(8,128)}, f32[3,512,512]{2,1,0:T(8,128)S(1)}, u32[]{:S(2)}) copy-start(f32[3,512,512]{2,1,0:T(8,128)S(1)} %get-tuple-element.15.exact_ref) | copy-start | bytes 9437188
  54.4 41.2 %collective-permute-start.4 = (bf16[3,512,512]{2,1,0:T(8,128)(2,1)S(1)}, bf16[3,512,512]{2,1,0:T(8,128)(2,1)S(1)}, u32[]{:S(2)}, u32[]{:S(2)}) collective-permute-start(bf16[3,512,512]{2,1,0:T(8,128)(2,1)S(1)} %get-tuple-element.16), channel_id=1, source_target_pairs={{1,0},{2,1},{3,2},{5,4},{6,5},{7,6},{9,8},{10,9},{11,10},{13,12},{... | collective-permute-start | bytes 4718600 | tf_op jit(solution)/shard_map/ppermute | solution.py:418
  56.3 39.4 %collective-permute-start.3 = (bf16[3,512,512]{2,1,0:T(8,128)(2,1)S(1)}, bf16[3,512,512]{2,1,0:T(8,128)(2,1)S(1)}, u32[]{:S(2)}, u32[]{:S(2)}) collective-permute-start(bf16[3,512,512]{2,1,0:T(8,128)(2,1)S(1)} %get-tuple-element.16), channel_id=1, source_target_pairs={{0,1},{1,2},{2,3},{4,5},{5,6},{6,7},{8,9},{9,10},{10,11},{12,13},{... | collective-permute-start | bytes 4718600 | tf_op jit(solution)/shard_map/ppermute | solution.py:418
  59.7 35.9 %collective-permute-start.5 = (bf16[3,16,512]{2,1,0:T(8,128)(2,1)S(1)}, bf16[3,16,512]{2,1,0:T(8,128)(2,1)S(1)}, u32[]{:S(2)}, u32[]{:S(2)}) collective-permute-start(bf16[3,16,512]{2,1,0:T(8,128)(2,1)S(1)} %slice.27), channel_id=1, source_target_pairs={{0,2},{1,3},{4,6},{5,7},{8,10},{9,11},{12,14},{13,15},{16,18},{17,... | collective-permute-start | bytes 147464 | tf_op jit(solution)/shard_map/ppermute | solution.py:418
  95.6 1.1 copy-start.9
  95.8 1.5 copy-start.10
  97.4 6.1 %copy-start.11 = (f32[3,3,31]{2,1,0:T(4,128)S(1)}, f32[3,3,31]{2,1,0:T(4,128)}, u32[]{:S(2)}) copy-start(f32[3,3,31]{2,1,0:T(4,128)} %param.9) | copy-start | bytes 3352
  97.4 33.7 %copy-start.5 = (bf16[768,384]{1,0:T(8,128)(2,1)S(1)}, bf16[768,384]{1,0:T(8,128)(2,1)}, u32[]{:S(2)}) copy-start(bf16[768,384]{1,0:T(8,128)(2,1)} %constant.25.clone.one_x_ref) | copy-start | bytes 1769476
  97.4 33.7 %copy-start.6 = (bf16[144,592]{1,0:T(8,128)(2,1)S(1)}, bf16[144,592]{1,0:T(8,128)(2,1)}, u32[]{:S(2)}) copy-start(bf16[144,592]{1,0:T(8,128)(2,1)} %constant.26.clone.one_zy_ref) | copy-start | bytes 511492
  97.4 33.7 %copy-start.7 = (bf16[384,128]{1,0:T(8,128)(2,1)S(1)}, bf16[384,128]{1,0:T(8,128)(2,1)}, u32[]{:S(2)}) copy-start(bf16[384,128]{1,0:T(8,128)(2,1)} %constant.27.clone.two_x_ref) | copy-start | bytes 294916
  97.4 33.7 %copy-start.8 = (bf16[32,144]{1,0:T(8,128)(2,1)S(1)}, bf16[32,144]{1,0:T(8,128)(2,1)}, u32[]{:S(2)}) copy-start(bf16[32,144]{1,0:T(8,128)(2,1)} %constant.28.clone.two_zy_ref) | copy-start | bytes 27652
  97.4 33.7 %collective-permute-start.6 = (bf16[3,1552,128]{2,1,0:T(8,128)(2,1)S(1)}, bf16[3,1552,128]{2,1,0:T(8,128)(2,1)}, u32[]{:S(2)}, u32[]{:S(2)}) collective-permute-start(bf16[3,1552,128]{2,1,0:T(8,128)(2,1)S(1)} %pad_maximum_fusion), channel_id=1, source_target_pairs={{0,4},{4,8},{8,12},{12,16},{16,20},{20,24},{24,28},{1,5},{5,9},{9,... | collective-permute-start | bytes 3575816 | tf_op jit(solution)/shard_map/ppermute | solution.py:418
  101.5 29.6 %collective-permute-start.7 = (bf16[3,1552,128]{2,1,0:T(8,128)(2,1)S(1)}, bf16[3,1552,128]{2,1,0:T(8,128)(2,1)}, u32[]{:S(2)}, u32[]{:S(2)}) collective-permute-start(bf16[3,1552,128]{2,1,0:T(8,128)(2,1)S(1)} %pad_maximum_fusion.1), channel_id=1, source_target_pairs={{4,0},{8,4},{12,8},{16,12},{20,16},{24,20},{28,24},{5,1},{9,5},{13... | collective-permute-start | bytes 3575816 | tf_op jit(solution)/shard_map/ppermute | solution.py:418
  128.6 1.2 copy-start.3
  129.8 1.2 copy-start.4
where the time goes:
time: 186 us; the launch traced here: 184 us
  Pallas kernels  86.7 us (47%)
  waiting for transfers between devices  65.5 us (35%)
  starting transfers between devices  23.6 us (13%)
  local copies, waits for them, and re-layouts  6.96 us (4%)
    pallas_call x1, Pallas kernels, deconvolve(): pl.pallas_call(deconvolve_kernel, grid=(n,), in_specs=[pl.BlockSpec(memor...  53 us
    ppermute x7, waiting for transfers between devices, shift(): return lax.ppermute(block, axis, route)  33.4 us
    ppermute x1, waiting for transfers between devices, shift_diagonal(): return lax.ppermute(block, ('gx', 'gy'), route)  32.1 us
    pallas_call x1, Pallas kernels, bands(): pl.pallas_call(bands_kernel, grid=(count,), in_specs=[pl.BlockSpec(memory...  24.7 us
    ppermute x7, starting transfers between devices, shift(): return lax.ppermute(block, axis, route)  20.7 us
    pallas_call x1, Pallas kernels, place(): pl.pallas_call(place_kernel, grid_spec=pltpu.PrefetchScalarGridSpec(num_s...  6.37 us
    unnamed x24, local copies, waits for them, and re-layouts  6.36 us
  transfers between devices with their start and end apart: 8, of which 2 were waited for; matrix products, arithmetic and copies ran while one was open for 0% of the time, Pallas kernels for 13%

commit v1 on v0

--- a/solution.py
+++ b/solution.py
@@ -43,7 +43,7 @@
     return high, (value - high.astype(F32)).astype(BF16)
 
 
-def place_kernel(off_ref, tile_ref, own_ref, right_ref, low_ref, corner_ref, canvas):
+def place_kernel(off_ref, tile_ref, own_ref, right_ref, low_ref, canvas):
     depth, tile_y, tile_x = tile_ref.shape[1:]
     parts = canvas.shape[0]
     wide = parts * LANE
@@ -65,38 +65,43 @@
     for b in range(parts - 1):
         to = slice(b * LANE, (b + 1) * LANE)
         own_ref[0, :, to] = canvas[b, :rows, :].astype(BF16)
-        low_ref[0, :, to] = canvas[b, rows:, :].astype(BF16)
+        low_ref[0, :rows, to] = canvas[b, rows:, :].astype(BF16)
     right_ref[0] = canvas[parts - 1, :rows, :].astype(BF16)
     half = rows // 2
     upper = canvas[parts - 1, rows : rows + half, :]
     lower = canvas[parts - 1, rows + half :, :]
-    corner_ref[0] = (upper + pltpu.roll(lower, LANE // 2, 1)).astype(BF16)
-
-
-def place(tiles, offsets):
-    n, depth, tile_y, tile_x = tiles.shape
+    corner = (upper + pltpu.roll(lower, LANE // 2, 1)).astype(BF16)
+    eighth = half // (parts - 1)
+    for b in range(parts - 1):
+        low_ref[0, rows:, b * LANE : (b + 1) * LANE] = corner[b * eighth : (b + 1) * eighth]
+
+
+def place(tiles, offsets, begin, n):
+    _, depth, tile_y, tile_x = tiles.shape
     rows = (tile_y - MARGIN) * depth
     cols = tile_x - MARGIN
     block = lambda r, c: pl.BlockSpec((1, r, c), lambda i, off: (i, 0, 0))
     shape = lambda r, c: jax.ShapeDtypeStruct((n, r, c), BF16)
-    sizes = ((rows, cols), (rows, LANE), (rows, cols), (rows // 2, LANE))
+    extra = rows // 2 * LANE // cols
+    sizes = ((rows, cols), (rows, LANE), (rows + extra, cols))
+    tile = pl.BlockSpec((1, depth, tile_y, tile_x), lambda i, off: (begin + i, 0, 0, 0))
     return pl.pallas_call(
         place_kernel,
         grid_spec=pltpu.PrefetchScalarGridSpec(
             num_scalar_prefetch=1,
             grid=(n,),
-            in_specs=[pl.BlockSpec((1, depth, tile_y, tile_x), lambda i, off: (i, 0, 0, 0))],
+            in_specs=[tile],
             out_specs=[block(*s) for s in sizes],
             scratch_shapes=[pltpu.VMEM((cols // LANE + 1, 2 * rows, LANE), F32)],
         ),
         out_shape=[shape(*s) for s in sizes],
-        compiler_params=params(32),
+        compiler_params=params(16),
         cost_estimate=cost(n * 2e9, n * 2.5e6),
         name="place",
     )(offsets, tiles)
 
 
-def join_kernel(own_ref, low_ref, right_ref, corner_ref, exact_ref, short_ref):
+def join_kernel(own_ref, low_ref, side_ref, exact_ref, short_ref, tail_ref):
     rows = own_ref.shape[1]
     half = rows // 2
 
@@ -107,8 +112,8 @@
     low = low_ref[0].astype(F32)
     total = own + low
     count = seen(own) + seen(low)
-    right = right_ref[0].astype(F32)
-    corner = corner_ref[0].astype(F32)
+    right = side_ref[0, :rows].astype(F32)
+    corner = side_ref[0, rows:].astype(F32)
     lane = lax.broadcasted_iota(jnp.int32, (half, LANE), 1)
     inside = lane < LANE // 2
     upper = jnp.where(inside, corner, 0.0)
@@ -122,21 +127,26 @@
     exact_ref[0, :, LANE:] = rest
     short_ref[0, :, :LANE] = edge.astype(BF16)
     short_ref[0, :, LANE:] = rest.astype(BF16)
-
-
-def join(own, low, right, corner):
-    n, rows, cols = own.shape
-    block = lambda a: pl.BlockSpec((1,) + a.shape[1:], lambda i: (i, 0, 0))
+    tail = tail_ref.shape[1]
+    tail_ref[0, :, :LANE] = edge[rows - tail :].astype(BF16)
+    tail_ref[0, :, LANE:] = rest[rows - tail :].astype(BF16)
+
+
+def join(own, low, side, at):
+    _, rows, cols = own.shape
+    block = lambda r, c, k: pl.BlockSpec((1, r, c), lambda i: (k, 0, 0))
+    tail = 2 * DEPTH
+    sizes = ((rows, cols, F32), (rows, cols, BF16), (tail, cols, BF16))
     return pl.pallas_call(
         join_kernel,
-        grid=(n,),
-        in_specs=[block(a) for a in (own, low, right, corner)],
-        out_specs=[block(own), block(own)],
-        out_shape=[jax.ShapeDtypeStruct(own.shape, F32), jax.ShapeDtypeStruct(own.shape, BF16)],
-        compiler_params=params(32),
-        cost_estimate=cost(n * 5e6, n * 3e6),
+        grid=(1,),
+        in_specs=[block(rows, cols, at), block(rows, cols, at), block(*side.shape[1:], at)],
+        out_specs=[block(r, c, 0) for r, c, _ in sizes],
+        out_shape=[jax.ShapeDtypeStruct((1, r, c), t) for r, c, t in sizes],
+        compiler_params=params(16),
+        cost_estimate=cost(5e6, 3e6),
         name="join",
-    )(own, low, right, corner)
+    )(own, low, side)
 
 
 def bands_kernel(kern_ref, across_ref, within_ref):
@@ -150,10 +160,9 @@
     for k in range(TAPS):
         base = jnp.where(tap == k, kern_ref[which, 2 * TAPS + k], base)
 
-    @pl.loop(0, across_ref.shape[1] // 16)
-    def _(q):
-        turned = pltpu.roll(base, wide - 4 * LANE + 16 * q, 1)
-        across_ref[0, pl.ds(pl.multiple_of(16 * q, 16), 16), :] = turned[:, : 2 * LANE].astype(BF16)
+    for q in range(across_ref.shape[1] // 16):
+        turned = pltpu.roll(base, (wide - 4 * LANE + 16 * q) % wide, 1)
+        across_ref[0, 16 * q : 16 * (q + 1), :] = turned[:, : 2 * LANE].astype(BF16)
 
     shape = (16, within_ref.shape[2])
     row = lax.broadcasted_iota(jnp.int32, shape, 0)
@@ -168,10 +177,9 @@
         in_z = jnp.where(tap_z == k, kern_ref[which, k], in_z)
     both = in_y * in_z
 
-    @pl.loop(0, within_ref.shape[1] // 16)
-    def _(q):
+    for q in range(within_ref.shape[1] // 16):
         turned = pltpu.roll(both, 16 * q, 1)
-        within_ref[0, pl.ds(pl.multiple_of(16 * q, 16), 16), :] = turned.astype(BF16)
+        within_ref[0, 16 * q : 16 * (q + 1), :] = turned.astype(BF16)
 
 
 def bands(kern):
@@ -243,6 +251,42 @@
     one_zy_ref,
     two_x_ref,
     two_zy_ref,
+    *others,
+):
+    if len(others) > 11:
+        others = others[3:]
+    deconvolve_body(
+        sides_ref,
+        exact_ref,
+        above_ref,
+        below_ref,
+        far_ref,
+        left_ref,
+        right_ref,
+        across_ref,
+        within_ref,
+        one_x_ref,
+        one_zy_ref,
+        two_x_ref,
+        two_zy_ref,
+        *others,
+    )
+
+
+def deconvolve_body(
+    sides_ref,
+    exact_ref,
+    above_ref,
+    below_ref,
+    far_ref,
+    left_ref,
+    right_ref,
+    across_ref,
+    within_ref,
+    one_x_ref,
+    one_zy_ref,
+    two_x_ref,
+    two_zy_ref,
     restored_ref,
     level_one_ref,
     level_two_ref,
@@ -272,8 +316,8 @@
     joined[...] = joined_short[...].astype(F32)
     joined[own, middle] = exact_ref[0]
 
-    def run_x(source, which, chunks, size, exact):
-        @pl.loop(0, chunks)
+    def run_x(source, which, begin_at, end_at, size, exact):
+        @pl.loop(begin_at, end_at)
         def _(i):
             at = pl.ds(pl.multiple_of(i * size, 16), size)
             for n in range(wide // (2 * LANE)):
@@ -286,11 +330,11 @@
                 else:
                     high[at, to] = out.astype(BF16)
 
-    def run_zy(which, chunks, size, exact, finish):
+    def run_zy(which, begin_at, end_at, size, exact, finish):
         deep = (size + 2 * REACH) * DEPTH
         matrix = within_ref[0, which, : size * DEPTH, :deep]
 
-        @pl.loop(0, chunks)
+        @pl.loop(begin_at, end_at)
         def _(i):
             start = i * (size * DEPTH)
             at = pl.ds(pl.multiple_of(start, 16), deep)
@@ -324,15 +368,19 @@
         for b in range(2):
             result[to.start // LANE + b, at, :] = value[:, b * LANE : (b + 1) * LANE]
 
-    run_x(joined_short, 0, 5, 40 * DEPTH, False)
-    run_zy(0, 5, BIG, False, ratio_from(REACH))
-    run_x(ratio, 1, 5, BIG * DEPTH, True)
-    run_zy(1, 4, BIG, True, first_estimate)
-    run_x(estimate_short, 0, 4, BIG * DEPTH, False)
-    run_zy(0, 4, SMALL, False, ratio_from(3 * REACH))
+    run_x(joined_short, 0, 0, 5, 40 * DEPTH, False)
+    run_zy(0, 0, 5, BIG, False, ratio_from(REACH))
+    run_x(ratio, 1, 0, 1, BIG * DEPTH, False)
+    run_x(ratio, 1, 1, 4, BIG * DEPTH, True)
+    run_x(ratio, 1, 4, 5, BIG * DEPTH, False)
+    run_zy(1, 0, 1, BIG, False, first_estimate)
+    run_zy(1, 1, 3, BIG, True, first_estimate)
+    run_zy(1, 3, 4, BIG, False, first_estimate)
+    run_x(estimate_short, 0, 0, 4, BIG * DEPTH, False)
+    run_zy(0, 0, 4, SMALL, False, ratio_from(3 * REACH))
     ratio[4 * SMALL * DEPTH : (4 * SMALL + 4) * DEPTH, :] = jnp.zeros((4 * DEPTH, wide), BF16)
-    run_x(ratio, 1, 3, 36 * DEPTH, True)
-    run_zy(1, 3, SMALL, True, last_estimate)
+    run_x(ratio, 1, 0, 3, 36 * DEPTH, True)
+    run_zy(1, 0, 3, SMALL, True, last_estimate)
 
     planes = restored_ref.shape[1]
     height = restored_ref.shape[2]
@@ -351,7 +399,7 @@
 
     reach_in = one_zy_ref.shape[1]
     fine = jnp.concatenate([result[b, :reach_in, :] for b in range(wide // LANE)], axis=1)
-    one = twice(one_zy_ref[...], twice_left(fine, one_x_ref[...]))
+    one = twice(one_zy_ref[...], dot(fine.astype(BF16), one_x_ref[...]))
     half_z, half_y, half_x = level_one_ref.shape[1:]
     inner = half_z * half_y
     level_one_ref[0] = one[:inner, :half_x].reshape(half_z, half_y, half_x)
@@ -365,44 +413,48 @@
     level_two_ref[0] = two.reshape(level_two_ref.shape[1:])
 
 
-def deconvolve(sides, exact, above, below, far, left, right, across, within, matrices):
-    n, rows8, cols = exact.shape
+def deconvolve(at, chans, sides, group, across, within, matrices, earlier):
+    rows8, cols = group[0].shape[1:]
     rows = rows8 // DEPTH
     wide = cols + 2 * LANE
-    per = lambda a: pl.BlockSpec((1,) + a.shape[1:], lambda i: (i,) + (0,) * (a.ndim - 1))
+    first = lambda a: pl.BlockSpec((1,) + a.shape[1:], lambda i: (0,) * a.ndim)
+    mine = lambda s: pl.BlockSpec((1,) + s[1:], lambda i: (at,) + (0,) * (len(s) - 1))
     same = lambda a: pl.BlockSpec(a.shape, lambda i: (0,) * a.ndim)
-    operands = (exact, above, below, far, left, right, across, within)
     outs = (
-        (n, DEPTH, rows, cols),
-        (n, DEPTH // 2, rows // 2, cols // 2),
-        (n, DEPTH // 4, rows // 4, cols // 4),
+        (chans, DEPTH, rows, cols),
+        (chans, DEPTH // 2, rows // 2, cols // 2),
+        (chans, DEPTH // 4, rows // 4, cols // 4),
     )
     shapes = [jax.ShapeDtypeStruct(s, F32) for s in outs]
-    first = 5 * BIG * DEPTH
-    second = 4 * BIG * DEPTH
-    third = 3 * SMALL * DEPTH
+    ratio_rows = 5 * BIG * DEPTH
+    estimate_rows = 4 * BIG * DEPTH
+    result_rows = 3 * SMALL * DEPTH
+    operands = [sides, *group, across, within, *matrices]
     return pl.pallas_call(
         deconvolve_kernel,
-        grid=(n,),
+        grid=(1,),
         in_specs=[pl.BlockSpec(memory_space=pltpu.SMEM)]
-        + [per(a) for a in operands]
-        + [same(m) for m in matrices],
-        out_specs=[per(s) for s in shapes],
+        + [first(a) for a in group]
+        + [mine(across.shape), mine(within.shape)]
+        + [same(m) for m in matrices]
+        + [pl.BlockSpec(memory_space=pl.ANY) for _ in earlier],
+        out_specs=[mine(s) for s in outs],
         out_shape=shapes,
+        input_output_aliases={len(operands) + k: k for k in range(len(earlier))},
         scratch_shapes=[
             pltpu.VMEM((FRAME * DEPTH, wide), F32),
             pltpu.VMEM((FRAME * DEPTH, wide), BF16),
-            pltpu.VMEM((first, wide), BF16),
-            pltpu.VMEM((second, wide), F32),
-            pltpu.VMEM((second, wide), BF16),
-            pltpu.VMEM((wide // LANE, third, LANE), F32),
+            pltpu.VMEM((ratio_rows, wide), BF16),
+            pltpu.VMEM((estimate_rows, wide), F32),
+            pltpu.VMEM((estimate_rows, wide), BF16),
+            pltpu.VMEM((wide // LANE, result_rows, LANE), F32),
             pltpu.VMEM((FRAME * DEPTH, wide), BF16),
-            pltpu.VMEM((first, wide), BF16),
+            pltpu.VMEM((ratio_rows, wide), BF16),
         ],
-        compiler_params=params(52),
-        cost_estimate=cost(n * 9e9, n * 8e6),
+        compiler_params=params(40),
+        cost_estimate=cost(9e9, 8e6),
         name="deconvolve",
-    )(sides, *operands, *matrices)
+    )(*operands, *earlier)
 
 
 def per_device(tiles, offsets, psf):
@@ -417,39 +469,49 @@
         route = [(i, i + distance) for i in devices if i + distance in devices]
         return lax.ppermute(block, axis, route)
 
-    def shift_diagonal(block):
-        route = [
-            (x * size_y + y, (x + 1) * size_y + y + 1)
-            for x in range(size_x - 1)
-            for y in range(size_y - 1)
-        ]
-        return lax.ppermute(block, ("gx", "gy"), route)
-
+    sides = jnp.stack([at_y > 0, at_y < size_y - 1, at_x > 0, at_x < size_x - 1])
+    sides = sides.astype(jnp.int32)
+    matrices = [jnp.asarray(m) for m in pyramid_matrices(rows, cols, depth)]
+
+    parts = ((0, 1), (1, chans - 1))
+    placed = [place(tiles, offsets.reshape(2), begin, n) for begin, n in parts]
+    lows = [shift(low, "gy", 1) for _, _, low in placed]
+
+    psf, _ = lax.optimization_barrier((psf, placed[0][1]))
     kern = psf / jnp.sum(psf, axis=-1, keepdims=True)
     both = jnp.stack([kern, kern[:, :, ::-1]], axis=1)
     across, within = bands(both.reshape(chans * 2, 3 * TAPS))
     across = across.reshape((chans, 2) + across.shape[1:])
     within = within.reshape((chans, 2) + within.shape[1:])
-    matrices = [jnp.asarray(m) for m in pyramid_matrices(rows, cols, depth)]
-    sides = jnp.stack([at_y > 0, at_y < size_y - 1, at_x > 0, at_x < size_x - 1])
-    sides = sides.astype(jnp.int32)
-
-    own, right, low, corner = place(tiles, offsets.reshape(2))
-    low = shift(low, "gy", 1)
-    right = shift(right, "gx", 1)
-    corner = shift_diagonal(corner)
-    exact, short = join(own, low, right, corner)
-    above = shift(short, "gy", 1)
-    below = shift(short, "gy", -1)
-    far = shift(short[:, -2 * depth :, :], "gy", 2)
-    column = (far, above, short, below)
-    last = jnp.concatenate([a[:, :, -LANE:] for a in column], axis=1)
-    first = jnp.concatenate([a[:, :, :LANE] for a in column], axis=1)
-    left = shift(last, "gx", 1)
-    right = shift(first, "gx", -1)
-    return tuple(
-        deconvolve(sides, exact, above, below, far, left, right, across, within, matrices)
-    )
+    lows[0], across, within = lax.optimization_barrier((lows[0], across, within))
+
+    joined = []
+    for (begin, n), (own, right, _), low in zip(parts, placed, lows):
+        strips = [low[:, rows * depth :, k : k + LANE] for k in range(0, cols, LANE)]
+        side = shift(jnp.concatenate([right] + strips, axis=1), "gx", 1)
+        joined += [join(own, low, side, k) for k in range(n)]
+
+    arrived = []
+    for _, short, tail in joined:
+        above = shift(short, "gy", 1)
+        below = shift(short, "gy", -1)
+        far = shift(tail, "gy", 2)
+        arrived.append((above, below, far))
+
+    outs = ()
+    for at in range(chans):
+        exact, short, _ = joined[at]
+        above, below, far = arrived[at]
+        if at == chans - 1:
+            above, below, _ = lax.optimization_barrier((above, below, outs[2]))
+        column = (far, above, short, below)
+        last = jnp.concatenate([a[:, :, -LANE:] for a in column], axis=1)
+        first = jnp.concatenate([a[:, :, :LANE] for a in column], axis=1)
+        left = shift(last, "gx", 1)
+        right = shift(first, "gx", -1)
+        group = (exact, above, below, far, left, right)
+        outs = deconvolve(at, chans, sides, group, across, within, matrices, outs)
+    return tuple(outs)
 
 
 def solution(mesh):

time: 186 us -> 171 us (0.919)
  starting transfers between devices: 23.6 us -> 67.3 us
  waiting for transfers between devices: 65.5 us -> 31.3 us
  Pallas kernels: 86.7 us -> 64.1 us
  local copies, waits for them, and re-layouts: 6.96 us -> 4.71 us
    ppermute x7 -> x19, starting transfers between devices: 20.7 us -> 67.3 us  [shift(): return lax.ppermute(block, axis, route)]
    ppermute x1 -> x0, waiting for transfers between devices: 32.1 us -> none  [shift_diagonal(): return lax.ppermute(block, ('gx', 'gy'), route)]
    pallas_call x1, Pallas kernels: 24.7 us -> 2.3 us  [bands(): pl.pallas_call(bands_kernel, grid=(count,), in_specs=[pl.BlockSpec(memory...]
    ppermute x1 -> x0, starting transfers between devices: 2.92 us -> none  [shift_diagonal(): return lax.ppermute(block, ('gx', 'gy'), route)]
    unnamed x24 -> x26, local copies, waits for them, and re-layouts: 6.36 us -> 4.27 us
    pallas_call x2 -> x6, Pallas kernels: 55.7 us -> 53.6 us  [the longest x3 50.9 us: deconvolve(): pl.pallas_call(deconvolve_kernel, grid=(1,), in_specs=[pl.BlockSpec(memor...]
    ppermute x7 -> x19, waiting for transfers between devices: 33.4 us -> 31.3 us  [shift(): return lax.ppermute(block, axis, route)]
    pallas_call x1 -> x2, Pallas kernels: 6.37 us -> 8.16 us  [place(): pl.pallas_call(place_kernel, grid_spec=pltpu.PrefetchScalarGridSpec(num_s...]
  transfers between devices with their start and end apart: 8 -> 19, of which waited for: 2 -> 9; matrix products, arithmetic and copies ran while one was open for 0% -> 1% of each run, Pallas kernels for 13% -> 26%
where the time goes in v1:
time: 171 us; the launch traced here: 169 us
  starting transfers between devices  67.3 us (39%)
  Pallas kernels  64.1 us (37%)
  waiting for transfers between devices  31.3 us (18%)
  local copies, waits for them, and re-layouts  4.71 us (3%)
    ppermute x19, starting transfers between devices, shift(): return lax.ppermute(block, axis, route)  67.3 us
    pallas_call x3, Pallas kernels, deconvolve(): pl.pallas_call(deconvolve_kernel, grid=(1,), in_specs=[pl.BlockSpec(memor...  50.9 us
    ppermute x19, waiting for transfers between devices, shift(): return lax.ppermute(block, axis, route)  31.3 us
    pallas_call x2, Pallas kernels, place(): pl.pallas_call(place_kernel, grid_spec=pltpu.PrefetchScalarGridSpec(num_s...  8.16 us
    unnamed x26, local copies, waits for them, and re-layouts  4.27 us
  transfers between devices with their start and end apart: 19, of which 9 were waited for; matrix products, arithmetic and copies ran while one was open for 1% of the time, Pallas kernels for 26%

profile of v1, /device:TPU:11, one launch (start us, length us, event | category | flops | bytes accessed | tf_op | source)
XLA Modules:
  0.0 169.0 jit_solution(17534739159700527133)
XLA Ops:
  0.6 1.8 %copy-done.1 = bf16[3,8,96,544]{3,2,1,0:T(8,128)(2,1)S(1)} copy-done((bf16[3,8,96,544]{3,2,1,0:T(8,128)(2,1)S(1)}, bf16[3,8,96,544]{3,2,1,0:T(8,128)(2,1)}, u32[]{:S(2)}) %copy-start.1) | copy-done | bytes 2506776
  3.1 3.2 %place.3 = (bf16[1,512,512]{2,1,0:T(8,128)(2,1)S(1)}, bf16[1,512,128]{2,1,0:T(8,128)(2,1)S(1)}, bf16[1,576,512]{2,1,0:T(8,128)(2,1)}) custom-call(s32[2]{0:T(128)S(1)} %bitcast.10, bf16[3,8,96,544]{3,2,1,0:T(8,128)(2,1)S(1)} %copy-done.1), custom_call_target="tpu_custom_call" | custom-call | flops 2000000000 | bytes 2500000 | tf_op jit(solution)/shard_map/place/pallas_call | solution.py:88
  6.3 3.3 %collective-permute-start.9 = (bf16[1,576,512]{2,1,0:T(8,128)(2,1)}, bf16[1,576,512]{2,1,0:T(8,128)(2,1)S(1)}, u32[]{:S(2)}, u32[]{:S(2)}) collective-permute-start(bf16[1,576,512]{2,1,0:T(8,128)(2,1)} %get-tuple-element.40), channel_id=1, source_target_pairs={{0,1},{1,2},{2,3},{4,5},{5,6},{6,7},{8,9},{9,10},{10,11},{12,13},{... | collective-permute-start | bytes 1769480 | tf_op jit(solution)/shard_map/ppermute | solution.py:470
  9.6 5.0 %place.2 = (bf16[2,512,512]{2,1,0:T(8,128)(2,1)S(1)}, bf16[2,512,128]{2,1,0:T(8,128)(2,1)S(1)}, bf16[2,576,512]{2,1,0:T(8,128)(2,1)}) custom-call(s32[2]{0:T(128)S(1)} %bitcast.11, bf16[3,8,96,544]{3,2,1,0:T(8,128)(2,1)S(1)} %copy-done.1), custom_call_target="tpu_custom_call" | custom-call | flops 4000000000 | bytes 5000000 | tf_op jit(solution)/shard_map/place/pallas_call | solution.py:88
  15.3 3.2 %collective-permute-start = (bf16[2,576,512]{2,1,0:T(8,128)(2,1)}, bf16[2,576,512]{2,1,0:T(8,128)(2,1)S(1)}, u32[]{:S(2)}, u32[]{:S(2)}) collective-permute-start(bf16[2,576,512]{2,1,0:T(8,128)(2,1)} %get-tuple-element.33), channel_id=1, source_target_pairs={{0,1},{1,2},{2,3},{4,5},{5,6},{6,7},{8,9},{9,10},{10,11},{12,13},{... | collective-permute-start | bytes 3538952 | tf_op jit(solution)/shard_map/ppermute | solution.py:470
  19.0 2.3 %bands.1 = (bf16[6,512,256]{2,1,0:T(8,128)(2,1)S(1)}, bf16[6,272,512]{2,1,0:T(8,128)(2,1)S(1)}) custom-call(f32[6,93]{1,0:T(8,128)S(1)} %reshape.21.kern_ref), custom_call_target="tpu_custom_call" | custom-call | flops 6000000 | bytes 24000000 | tf_op jit(solution)/shard_map/bands/pallas_call | solution.py:188
  22.8 5.7 %collective-permute-start.10 = (bf16[1,768,128]{2,1,0:T(8,128)(2,1)S(1)}, bf16[1,768,128]{2,1,0:T(8,128)(2,1)S(1)}, u32[]{:S(2)}, u32[]{:S(2)}) collective-permute-start(bf16[1,768,128]{2,1,0:T(8,128)(2,1)S(1)} %constant_dynamic-update-slice_fusion.1), channel_id=1, source_target_pairs={{0,4},{4,8},{8,12},{12,16},{16,20},{20,24},{24,28},{1,5},{5,9},{9,... | collective-permute-start | bytes 589832 | tf_op jit(solution)/shard_map/ppermute | solution.py:470
  29.5 1.5 collective-permute-done.10.side_ref
  32.0 4.2 %collective-permute-start.13 = (bf16[1,16,512]{2,1,0:T(8,128)(2,1)S(1)}, bf16[1,16,512]{2,1,0:T(8,128)(2,1)S(1)}, u32[]{:S(2)}, u32[]{:S(2)}) collective-permute-start(bf16[1,16,512]{2,1,0:T(8,128)(2,1)S(1)} %get-tuple-element.51), channel_id=1, source_target_pairs={{0,2},{1,3},{4,6},{5,7},{8,10},{9,11},{12,14},{13,15},{16,18},{17,... | collective-permute-start | bytes 49160 | tf_op jit(solution)/shard_map/ppermute | solution.py:470
  36.2 2.1 %collective-permute-start.12 = (bf16[1,512,512]{2,1,0:T(8,128)(2,1)S(1)}, bf16[1,512,512]{2,1,0:T(8,128)(2,1)S(1)}, u32[]{:S(2)}, u32[]{:S(2)}) collective-permute-start(bf16[1,512,512]{2,1,0:T(8,128)(2,1)S(1)} %get-tuple-element.50), channel_id=1, source_target_pairs={{1,0},{2,1},{3,2},{5,4},{6,5},{7,6},{9,8},{10,9},{11,10},{13,12},{... | collective-permute-start | bytes 1572872 | tf_op jit(solution)/shard_map/ppermute | solution.py:470
  38.3 3.2 %collective-permute-start.11 = (bf16[1,512,512]{2,1,0:T(8,128)(2,1)S(1)}, bf16[1,512,512]{2,1,0:T(8,128)(2,1)S(1)}, u32[]{:S(2)}, u32[]{:S(2)}) collective-permute-start(bf16[1,512,512]{2,1,0:T(8,128)(2,1)S(1)} %get-tuple-element.50), channel_id=1, source_target_pairs={{0,1},{1,2},{2,3},{4,5},{5,6},{6,7},{8,9},{9,10},{10,11},{12,13},{... | collective-permute-start | bytes 1572872 | tf_op jit(solution)/shard_map/ppermute | solution.py:470
  41.5 5.9 %collective-permute-done.13.far_ref = bf16[1,16,512]{2,1,0:T(8,128)(2,1)S(1)} collective-permute-done((bf16[1,16,512]{2,1,0:T(8,128)(2,1)S(1)}, bf16[1,16,512]{2,1,0:T(8,128)(2,1)S(1)}, u32[]{:S(2)}, u32[]{:S(2)}) %collective-permute-start.13) | collective-permute-done | bytes 16416 | tf_op jit(solution)/shard_map/ppermute | solution.py:470
  48.1 5.7 %collective-permute-start.1 = (bf16[2,768,128]{2,1,0:T(8,128)(2,1)S(1)}, bf16[2,768,128]{2,1,0:T(8,128)(2,1)S(1)}, u32[]{:S(2)}, u32[]{:S(2)}) collective-permute-start(bf16[2,768,128]{2,1,0:T(8,128)(2,1)S(1)} %slice_dynamic-update-slice_fusion), channel_id=1, source_target_pairs={{0,4},{4,8},{8,12},{12,16},{16,20},{20,24},{24,28},{1,5},{5,9},{9,... | collective-permute-start | bytes 1179656 | tf_op jit(solution)/shard_map/ppermute | solution.py:470
  53.8 5.8 %collective-permute-done.11.above_ref = bf16[1,512,512]{2,1,0:T(8,128)(2,1)S(1)} collective-permute-done((bf16[1,512,512]{2,1,0:T(8,128)(2,1)S(1)}, bf16[1,512,512]{2,1,0:T(8,128)(2,1)S(1)}, u32[]{:S(2)}, u32[]{:S(2)}) %collective-permute-start.11) | collective-permute-done | bytes 524320 | tf_op jit(solution)/shard_map/ppermute | solution.py:470
  59.6 4.6 %collective-permute-start.14 = (bf16[1,1552,128]{2,1,0:T(8,128)(2,1)S(1)}, bf16[1,1552,128]{2,1,0:T(8,128)(2,1)S(1)}, u32[]{:S(2)}, u32[]{:S(2)}) collective-permute-start(bf16[1,1552,128]{2,1,0:T(8,128)(2,1)S(1)} %pad_maximum_fusion.2), channel_id=1, source_target_pairs={{0,4},{4,8},{8,12},{12,16},{16,20},{20,24},{24,28},{1,5},{5,9},{9,... | collective-permute-start | bytes 1191944 | tf_op jit(solution)/shard_map/ppermute | solution.py:470
  64.2 1.9 %collective-permute-start.15 = (bf16[1,1552,128]{2,1,0:T(8,128)(2,1)S(1)}, bf16[1,1552,128]{2,1,0:T(8,128)(2,1)S(1)}, u32[]{:S(2)}, u32[]{:S(2)}) collective-permute-start(bf16[1,1552,128]{2,1,0:T(8,128)(2,1)S(1)} %pad_maximum_fusion.3), channel_id=1, source_target_pairs={{4,0},{8,4},{12,8},{16,12},{20,16},{24,20},{28,24},{5,1},{9,5},{13... | collective-permute-start | bytes 1191944 | tf_op jit(solution)/shard_map/ppermute | solution.py:470
  67.1 1.9 %collective-permute-start.5 = (bf16[1,512,512]{2,1,0:T(8,128)(2,1)S(1)}, bf16[1,512,512]{2,1,0:T(8,128)(2,1)S(1)}, u32[]{:S(2)}, u32[]{:S(2)}) collective-permute-start(bf16[1,512,512]{2,1,0:T(8,128)(2,1)S(1)} %get-tuple-element.38), channel_id=1, source_target_pairs={{1,0},{2,1},{3,2},{5,4},{6,5},{7,6},{9,8},{10,9},{11,10},{13,12},{... | collective-permute-start | bytes 1572872 | tf_op jit(solution)/shard_map/ppermute | solution.py:470
  69.0 3.6 %collective-permute-start.4 = (bf16[1,512,512]{2,1,0:T(8,128)(2,1)S(1)}, bf16[1,512,512]{2,1,0:T(8,128)(2,1)S(1)}, u32[]{:S(2)}, u32[]{:S(2)}) collective-permute-start(bf16[1,512,512]{2,1,0:T(8,128)(2,1)S(1)} %get-tuple-element.38), channel_id=1, source_target_pairs={{0,1},{1,2},{2,3},{4,5},{5,6},{6,7},{8,9},{9,10},{10,11},{12,13},{... | collective-permute-start | bytes 1572872 | tf_op jit(solution)/shard_map/ppermute | solution.py:470
  72.6 2.5 %collective-permute-start.6 = (bf16[1,16,512]{2,1,0:T(8,128)(2,1)S(1)}, bf16[1,16,512]{2,1,0:T(8,128)(2,1)S(1)}, u32[]{:S(2)}, u32[]{:S(2)}) collective-permute-start(bf16[1,16,512]{2,1,0:T(8,128)(2,1)S(1)} %get-tuple-element.39), channel_id=1, source_target_pairs={{0,2},{1,3},{4,6},{5,7},{8,10},{9,11},{12,14},{13,15},{16,18},{17,... | collective-permute-start | bytes 49160 | tf_op jit(solution)/shard_map/ppermute | solution.py:470
  76.1 7.4 %collective-permute-done.6.far_ref = bf16[1,16,512]{2,1,0:T(8,128)(2,1)S(1)} collective-permute-done((bf16[1,16,512]{2,1,0:T(8,128)(2,1)S(1)}, bf16[1,16,512]{2,1,0:T(8,128)(2,1)S(1)}, u32[]{:S(2)}, u32[]{:S(2)}) %collective-permute-start.6) | collective-permute-done | bytes 16416 | tf_op jit(solution)/shard_map/ppermute | solution.py:470
  83.5 4.8 %collective-permute-start.16 = (bf16[1,16,512]{2,1,0:T(8,128)(2,1)S(1)}, bf16[1,16,512]{2,1,0:T(8,128)(2,1)S(1)}, u32[]{:S(2)}, u32[]{:S(2)}) collective-permute-start(bf16[1,16,512]{2,1,0:T(8,128)(2,1)S(1)} %get-tuple-element.58), channel_id=1, source_target_pairs={{0,2},{1,3},{4,6},{5,7},{8,10},{9,11},{12,14},{13,15},{16,18},{17,... | collective-permute-start | bytes 49160 | tf_op jit(solution)/shard_map/ppermute | solution.py:470
  89.2 1.9 %collective-permute-start.3 = (bf16[1,512,512]{2,1,0:T(8,128)(2,1)S(1)}, bf16[1,512,512]{2,1,0:T(8,128)(2,1)S(1)}, u32[]{:S(2)}, u32[]{:S(2)}) collective-permute-start(bf16[1,512,512]{2,1,0:T(8,128)(2,1)S(1)} %get-tuple-element.36), channel_id=1, source_target_pairs={{1,0},{2,1},{3,2},{5,4},{6,5},{7,6},{9,8},{10,9},{11,10},{13,12},{... | collective-permute-start | bytes 1572872 | tf_op jit(solution)/shard_map/ppermute | solution.py:470
  91.2 3.4 %collective-permute-start.2 = (bf16[1,512,512]{2,1,0:T(8,128)(2,1)S(1)}, bf16[1,512,512]{2,1,0:T(8,128)(2,1)S(1)}, u32[]{:S(2)}, u32[]{:S(2)}) collective-permute-start(bf16[1,512,512]{2,1,0:T(8,128)(2,1)S(1)} %get-tuple-element.36), channel_id=1, source_target_pairs={{0,1},{1,2},{2,3},{4,5},{5,6},{6,7},{8,9},{9,10},{10,11},{12,13},{... | collective-permute-start | bytes 1572872 | tf_op jit(solution)/shard_map/ppermute | solution.py:470
  94.6 6.5 %collective-permute-start.7 = (bf16[1,1552,128]{2,1,0:T(8,128)(2,1)S(1)}, bf16[1,1552,128]{2,1,0:T(8,128)(2,1)S(1)}, u32[]{:S(2)}, u32[]{:S(2)}) collective-permute-start(bf16[1,1552,128]{2,1,0:T(8,128)(2,1)S(1)} %pad_maximum_fusion), channel_id=1, source_target_pairs={{0,4},{4,8},{8,12},{12,16},{16,20},{20,24},{24,28},{1,5},{5,9},{9,... | collective-permute-start | bytes 1191944 | tf_op jit(solution)/shard_map/ppermute | solution.py:470
  101.2 2.1 %collective-permute-start.8 = (bf16[1,1552,128]{2,1,0:T(8,128)(2,1)S(1)}, bf16[1,1552,128]{2,1,0:T(8,128)(2,1)S(1)}, u32[]{:S(2)}, u32[]{:S(2)}) collective-permute-start(bf16[1,1552,128]{2,1,0:T(8,128)(2,1)S(1)} %pad_maximum_fusion.1), channel_id=1, source_target_pairs={{4,0},{8,4},{12,8},{16,12},{20,16},{24,20},{28,24},{5,1},{9,5},{13... | collective-permute-start | bytes 1191944 | tf_op jit(solution)/shard_map/ppermute | solution.py:470
  103.3 17.0 %deconvolve.3 = (f32[3,8,64,512]{3,2,1,0:T(8,128)}, f32[3,4,32,256]{3,2,1,0:T(8,128)}, f32[3,2,16,128]{3,2,1,0:T(8,128)}) custom-call(s32[4]{0:T(128)S(1)} %add_convert_fusion.sides_ref, f32[1,512,512]{2,1,0:T(8,128)S(1)} %get-tuple-element.49.exact_ref, bf16[1,512,512]{2,1,0:T(8,128)(2,1)S(1)} %collective-permute-done.11.above_ref, ...), custom_call_target="tpu_custom_call" | custom-call | flops 8999999488 | bytes 8000000 | tf_op jit(solution)/shard_map/deconvolve/pallas_call | solution.py:433
  120.3 17.0 %deconvolve.4 = (f32[3,8,64,512]{3,2,1,0:T(8,128)}, f32[3,4,32,256]{3,2,1,0:T(8,128)}, f32[3,2,16,128]{3,2,1,0:T(8,128)}) custom-call(s32[4]{0:T(128)S(1)} %add_convert_fusion.sides_ref, f32[1,512,512]{2,1,0:T(8,128)S(1)} %get-tuple-element.37.exact_ref, ...), custom_call_target="tpu_custom_call", output_to_operand_aliasing={{0}: (13, {}), {1}: (14, {}), {2}: (15, {})} | custom-call | flops 8999999488 | bytes 8000000 | tf_op jit(solution)/shard_map/deconvolve/pallas_call | solution.py:433
  137.4 4.5 %collective-permute-start.17 = (bf16[1,1552,128]{2,1,0:T(8,128)(2,1)S(1)}, bf16[1,1552,128]{2,1,0:T(8,128)(2,1)S(1)}, u32[]{:S(2)}, u32[]{:S(2)}) collective-permute-start(bf16[1,1552,128]{2,1,0:T(8,128)(2,1)S(1)} %pad_maximum_fusion.4), channel_id=1, source_target_pairs={{0,4},{4,8},{8,12},{12,16},{16,20},{20,24},{24,28},{1,5},{5,9},{9,... | collective-permute-start | bytes 1191944 | tf_op jit(solution)/shard_map/ppermute | solution.py:470
  142.0 2.1 %collective-permute-start.18 = (bf16[1,1552,128]{2,1,0:T(8,128)(2,1)S(1)}, bf16[1,1552,128]{2,1,0:T(8,128)(2,1)S(1)}, u32[]{:S(2)}, u32[]{:S(2)}) collective-permute-start(bf16[1,1552,128]{2,1,0:T(8,128)(2,1)S(1)} %pad_maximum_fusion.5), channel_id=1, source_target_pairs={{4,0},{8,4},{12,8},{16,12},{20,16},{24,20},{28,24},{5,1},{9,5},{13... | collective-permute-start | bytes 1191944 | tf_op jit(solution)/shard_map/ppermute | solution.py:470
  144.2 4.9 %collective-permute-done.17.left_ref = bf16[1,1552,128]{2,1,0:T(8,128)(2,1)S(1)} collective-permute-done((bf16[1,1552,128]{2,1,0:T(8,128)(2,1)S(1)}, bf16[1,1552,128]{2,1,0:T(8,128)(2,1)S(1)}, u32[]{:S(2)}, u32[]{:S(2)}) %collective-permute-start.17) | collective-permute-done | bytes 397344 | tf_op jit(solution)/shard_map/ppermute | solution.py:470
  149.0 3.0 %collective-permute-done.18.right_ref = bf16[1,1552,128]{2,1,0:T(8,128)(2,1)S(1)} collective-permute-done((bf16[1,1552,128]{2,1,0:T(8,128)(2,1)S(1)}, bf16[1,1552,128]{2,1,0:T(8,128)(2,1)S(1)}, u32[]{:S(2)}, u32[]{:S(2)}) %collective-permute-start.18) | collective-permute-done | bytes 397344 | tf_op jit(solution)/shard_map/ppermute | solution.py:470
  152.1 17.0 %deconvolve.5 = (f32[3,8,64,512]{3,2,1,0:T(8,128)}, f32[3,4,32,256]{3,2,1,0:T(8,128)}, f32[3,2,16,128]{3,2,1,0:T(8,128)}) custom-call(s32[4]{0:T(128)S(1)} %add_convert_fusion.sides_ref, f32[1,512,512]{2,1,0:T(8,128)S(1)} %get-tuple-element.35.exact_ref, ...), custom_call_target="tpu_custom_call", output_to_operand_aliasing={{0}: (13, {}), {1}: (14, {}), {2}: (15, {})} | custom-call | flops 8999999488 | bytes 8000000 | tf_op jit(solution)/shard_map/deconvolve/pallas_call | solution.py:433
  (68 shorter events, 8.8 us)
Async XLA Ops:
  0.6 1.8 %copy-start.1 = (bf16[3,8,96,544]{3,2,1,0:T(8,128)(2,1)S(1)}, bf16[3,8,96,544]{3,2,1,0:T(8,128)(2,1)}, u32[]{:S(2)}) copy-start(bf16[3,8,96,544]{3,2,1,0:T(8,128)(2,1)} %tile_ref.3) | copy-start | bytes 7520260
  2.5 0.7 copy-start.2
  3.1 6.5 %copy-start.3 = (s32[1,1,2]{2,1,0:T(1,128)S(1)}, s32[1,1,2]{2,1,0:T(1,128)}, u32[]{:S(2)}) copy-start(s32[1,1,2]{2,1,0:T(1,128)} %param.8) | copy-start | bytes 28
  6.3 12.3 %copy-start.8 = (f32[3,3,31]{2,1,0:T(4,128)S(1)}, f32[3,3,31]{2,1,0:T(4,128)}, u32[]{:S(2)}) copy-start(f32[3,3,31]{2,1,0:T(4,128)} %param.9) | copy-start | bytes 3352
  6.3 16.4 %collective-permute-start.9 = (bf16[1,576,512]{2,1,0:T(8,128)(2,1)}, bf16[1,576,512]{2,1,0:T(8,128)(2,1)S(1)}, u32[]{:S(2)}, u32[]{:S(2)}) collective-permute-start(bf16[1,576,512]{2,1,0:T(8,128)(2,1)} %get-tuple-element.40), channel_id=1, source_target_pairs={{0,1},{1,2},{2,3},{4,5},{5,6},{6,7},{8,9},{9,10},{10,11},{12,13},{... | collective-permute-start | bytes 1769480 | tf_op jit(solution)/shard_map/ppermute | solution.py:470
  14.6 0.7 copy-start
  15.3 32.6 %collective-permute-start = (bf16[2,576,512]{2,1,0:T(8,128)(2,1)}, bf16[2,576,512]{2,1,0:T(8,128)(2,1)S(1)}, u32[]{:S(2)}, u32[]{:S(2)}) collective-permute-start(bf16[2,576,512]{2,1,0:T(8,128)(2,1)} %get-tuple-element.33), channel_id=1, source_target_pairs={{0,1},{1,2},{2,3},{4,5},{5,6},{6,7},{8,9},{9,10},{10,11},{12,13},{... | collective-permute-start | bytes 3538952 | tf_op jit(solution)/shard_map/ppermute | solution.py:470
  22.8 8.3 %collective-permute-start.10 = (bf16[1,768,128]{2,1,0:T(8,128)(2,1)S(1)}, bf16[1,768,128]{2,1,0:T(8,128)(2,1)S(1)}, u32[]{:S(2)}, u32[]{:S(2)}) collective-permute-start(bf16[1,768,128]{2,1,0:T(8,128)(2,1)S(1)} %constant_dynamic-update-slice_fusion.1), channel_id=1, source_target_pairs={{0,4},{4,8},{8,12},{12,16},{16,20},{20,24},{24,28},{1,5},{5,9},{9,... | collective-permute-start | bytes 589832 | tf_op jit(solution)/shard_map/ppermute | solution.py:470
  32.0 15.5 %collective-permute-start.13 = (bf16[1,16,512]{2,1,0:T(8,128)(2,1)S(1)}, bf16[1,16,512]{2,1,0:T(8,128)(2,1)S(1)}, u32[]{:S(2)}, u32[]{:S(2)}) collective-permute-start(bf16[1,16,512]{2,1,0:T(8,128)(2,1)S(1)} %get-tuple-element.51), channel_id=1, source_target_pairs={{0,2},{1,3},{4,6},{5,7},{8,10},{9,11},{12,14},{13,15},{16,18},{17,... | collective-permute-start | bytes 49160 | tf_op jit(solution)/shard_map/ppermute | solution.py:470
  36.2 17.6 %collective-permute-start.12 = (bf16[1,512,512]{2,1,0:T(8,128)(2,1)S(1)}, bf16[1,512,512]{2,1,0:T(8,128)(2,1)S(1)}, u32[]{:S(2)}, u32[]{:S(2)}) collective-permute-start(bf16[1,512,512]{2,1,0:T(8,128)(2,1)S(1)} %get-tuple-element.50), channel_id=1, source_target_pairs={{1,0},{2,1},{3,2},{5,4},{6,5},{7,6},{9,8},{10,9},{11,10},{13,12},{... | collective-permute-start | bytes 1572872 | tf_op jit(solution)/shard_map/ppermute | solution.py:470
  38.3 21.3 %collective-permute-start.11 = (bf16[1,512,512]{2,1,0:T(8,128)(2,1)S(1)}, bf16[1,512,512]{2,1,0:T(8,128)(2,1)S(1)}, u32[]{:S(2)}, u32[]{:S(2)}) collective-permute-start(bf16[1,512,512]{2,1,0:T(8,128)(2,1)S(1)} %get-tuple-element.50), channel_id=1, source_target_pairs={{0,1},{1,2},{2,3},{4,5},{5,6},{6,7},{8,9},{9,10},{10,11},{12,13},{... | collective-permute-start | bytes 1572872 | tf_op jit(solution)/shard_map/ppermute | solution.py:470
  48.1 18.1 %collective-permute-start.1 = (bf16[2,768,128]{2,1,0:T(8,128)(2,1)S(1)}, bf16[2,768,128]{2,1,0:T(8,128)(2,1)S(1)}, u32[]{:S(2)}, u32[]{:S(2)}) collective-permute-start(bf16[2,768,128]{2,1,0:T(8,128)(2,1)S(1)} %slice_dynamic-update-slice_fusion), channel_id=1, source_target_pairs={{0,4},{4,8},{8,12},{12,16},{16,20},{20,24},{24,28},{1,5},{5,9},{9,... | collective-permute-start | bytes 1179656 | tf_op jit(solution)/shard_map/ppermute | solution.py:470
  59.6 41.5 %collective-permute-start.14 = (bf16[1,1552,128]{2,1,0:T(8,128)(2,1)S(1)}, bf16[1,1552,128]{2,1,0:T(8,128)(2,1)S(1)}, u32[]{:S(2)}, u32[]{:S(2)}) collective-permute-start(bf16[1,1552,128]{2,1,0:T(8,128)(2,1)S(1)} %pad_maximum_fusion.2), channel_id=1, source_target_pairs={{0,4},{4,8},{8,12},{12,16},{16,20},{20,24},{24,28},{1,5},{5,9},{9,... | collective-permute-start | bytes 1191944 | tf_op jit(solution)/shard_map/ppermute | solution.py:470
  64.2 39.0 %collective-permute-start.15 = (bf16[1,1552,128]{2,1,0:T(8,128)(2,1)S(1)}, bf16[1,1552,128]{2,1,0:T(8,128)(2,1)S(1)}, u32[]{:S(2)}, u32[]{:S(2)}) collective-permute-start(bf16[1,1552,128]{2,1,0:T(8,128)(2,1)S(1)} %pad_maximum_fusion.3), channel_id=1, source_target_pairs={{4,0},{8,4},{12,8},{16,12},{20,16},{24,20},{28,24},{5,1},{9,5},{13... | collective-permute-start | bytes 1191944 | tf_op jit(solution)/shard_map/ppermute | solution.py:470
  67.1 24.0 %collective-permute-start.5 = (bf16[1,512,512]{2,1,0:T(8,128)(2,1)S(1)}, bf16[1,512,512]{2,1,0:T(8,128)(2,1)S(1)}, u32[]{:S(2)}, u32[]{:S(2)}) collective-permute-start(bf16[1,512,512]{2,1,0:T(8,128)(2,1)S(1)} %get-tuple-element.38), channel_id=1, source_target_pairs={{1,0},{2,1},{3,2},{5,4},{6,5},{7,6},{9,8},{10,9},{11,10},{13,12},{... | collective-permute-start | bytes 1572872 | tf_op jit(solution)/shard_map/ppermute | solution.py:470
  69.0 25.5 %collective-permute-start.4 = (bf16[1,512,512]{2,1,0:T(8,128)(2,1)S(1)}, bf16[1,512,512]{2,1,0:T(8,128)(2,1)S(1)}, u32[]{:S(2)}, u32[]{:S(2)}) collective-permute-start(bf16[1,512,512]{2,1,0:T(8,128)(2,1)S(1)} %get-tuple-element.38), channel_id=1, source_target_pairs={{0,1},{1,2},{2,3},{4,5},{5,6},{6,7},{8,9},{9,10},{10,11},{12,13},{... | collective-permute-start | bytes 1572872 | tf_op jit(solution)/shard_map/ppermute | solution.py:470
  72.6 10.9 %collective-permute-start.6 = (bf16[1,16,512]{2,1,0:T(8,128)(2,1)S(1)}, bf16[1,16,512]{2,1,0:T(8,128)(2,1)S(1)}, u32[]{:S(2)}, u32[]{:S(2)}) collective-permute-start(bf16[1,16,512]{2,1,0:T(8,128)(2,1)S(1)} %get-tuple-element.39), channel_id=1, source_target_pairs={{0,2},{1,3},{4,6},{5,7},{8,10},{9,11},{12,14},{13,15},{16,18},{17,... | collective-permute-start | bytes 49160 | tf_op jit(solution)/shard_map/ppermute | solution.py:470
  76.0 27.3 %copy-start.4 = (bf16[768,384]{1,0:T(8,128)(2,1)S(1)}, bf16[768,384]{1,0:T(8,128)(2,1)}, u32[]{:S(2)}) copy-start(bf16[768,384]{1,0:T(8,128)(2,1)} %constant.25.clone.one_x_ref) | copy-start | bytes 1769476
  76.0 27.3 %copy-start.5 = (bf16[144,592]{1,0:T(8,128)(2,1)S(1)}, bf16[144,592]{1,0:T(8,128)(2,1)}, u32[]{:S(2)}) copy-start(bf16[144,592]{1,0:T(8,128)(2,1)} %constant.26.clone.one_zy_ref) | copy-start | bytes 511492
  76.0 27.3 %copy-start.6 = (bf16[384,128]{1,0:T(8,128)(2,1)S(1)}, bf16[384,128]{1,0:T(8,128)(2,1)}, u32[]{:S(2)}) copy-start(bf16[384,128]{1,0:T(8,128)(2,1)} %constant.27.clone.two_x_ref) | copy-start | bytes 294916
  76.0 27.3 %copy-start.7 = (bf16[32,144]{1,0:T(8,128)(2,1)S(1)}, bf16[32,144]{1,0:T(8,128)(2,1)}, u32[]{:S(2)}) copy-start(bf16[32,144]{1,0:T(8,128)(2,1)} %constant.28.clone.two_zy_ref) | copy-start | bytes 27652
  83.5 5.7 %collective-permute-start.16 = (bf16[1,16,512]{2,1,0:T(8,128)(2,1)S(1)}, bf16[1,16,512]{2,1,0:T(8,128)(2,1)S(1)}, u32[]{:S(2)}, u32[]{:S(2)}) collective-permute-start(bf16[1,16,512]{2,1,0:T(8,128)(2,1)S(1)} %get-tuple-element.58), channel_id=1, source_target_pairs={{0,2},{1,3},{4,6},{5,7},{8,10},{9,11},{12,14},{13,15},{16,18},{17,... | collective-permute-start | bytes 49160 | tf_op jit(solution)/shard_map/ppermute | solution.py:470
  89.2 48.1 %collective-permute-start.3 = (bf16[1,512,512]{2,1,0:T(8,128)(2,1)S(1)}, bf16[1,512,512]{2,1,0:T(8,128)(2,1)S(1)}, u32[]{:S(2)}, u32[]{:S(2)}) collective-permute-start(bf16[1,512,512]{2,1,0:T(8,128)(2,1)S(1)} %get-tuple-element.36), channel_id=1, source_target_pairs={{1,0},{2,1},{3,2},{5,4},{6,5},{7,6},{9,8},{10,9},{11,10},{13,12},{... | collective-permute-start | bytes 1572872 | tf_op jit(solution)/shard_map/ppermute | solution.py:470
  91.2 46.1 %collective-permute-start.2 = (bf16[1,512,512]{2,1,0:T(8,128)(2,1)S(1)}, bf16[1,512,512]{2,1,0:T(8,128)(2,1)S(1)}, u32[]{:S(2)}, u32[]{:S(2)}) collective-permute-start(bf16[1,512,512]{2,1,0:T(8,128)(2,1)S(1)} %get-tuple-element.36), channel_id=1, source_target_pairs={{0,1},{1,2},{2,3},{4,5},{5,6},{6,7},{8,9},{9,10},{10,11},{12,13},{... | collective-permute-start | bytes 1572872 | tf_op jit(solution)/shard_map/ppermute | solution.py:470
  94.6 25.7 %collective-permute-start.7 = (bf16[1,1552,128]{2,1,0:T(8,128)(2,1)S(1)}, bf16[1,1552,128]{2,1,0:T(8,128)(2,1)S(1)}, u32[]{:S(2)}, u32[]{:S(2)}) collective-permute-start(bf16[1,1552,128]{2,1,0:T(8,128)(2,1)S(1)} %pad_maximum_fusion), channel_id=1, source_target_pairs={{0,4},{4,8},{8,12},{12,16},{16,20},{20,24},{24,28},{1,5},{5,9},{9,... | collective-permute-start | bytes 1191944 | tf_op jit(solution)/shard_map/ppermute | solution.py:470
  101.2 19.1 %collective-permute-start.8 = (bf16[1,1552,128]{2,1,0:T(8,128)(2,1)S(1)}, bf16[1,1552,128]{2,1,0:T(8,128)(2,1)S(1)}, u32[]{:S(2)}, u32[]{:S(2)}) collective-permute-start(bf16[1,1552,128]{2,1,0:T(8,128)(2,1)S(1)} %pad_maximum_fusion.1), channel_id=1, source_target_pairs={{4,0},{8,4},{12,8},{16,12},{20,16},{24,20},{28,24},{5,1},{9,5},{13... | collective-permute-start | bytes 1191944 | tf_op jit(solution)/shard_map/ppermute | solution.py:470
  137.4 11.6 %collective-permute-start.17 = (bf16[1,1552,128]{2,1,0:T(8,128)(2,1)S(1)}, bf16[1,1552,128]{2,1,0:T(8,128)(2,1)S(1)}, u32[]{:S(2)}, u32[]{:S(2)}) collective-permute-start(bf16[1,1552,128]{2,1,0:T(8,128)(2,1)S(1)} %pad_maximum_fusion.4), channel_id=1, source_target_pairs={{0,4},{4,8},{8,12},{12,16},{16,20},{20,24},{24,28},{1,5},{5,9},{9,... | collective-permute-start | bytes 1191944 | tf_op jit(solution)/shard_map/ppermute | solution.py:470
  142.0 10.0 %collective-permute-start.18 = (bf16[1,1552,128]{2,1,0:T(8,128)(2,1)S(1)}, bf16[1,1552,128]{2,1,0:T(8,128)(2,1)S(1)}, u32[]{:S(2)}, u32[]{:S(2)}) collective-permute-start(bf16[1,1552,128]{2,1,0:T(8,128)(2,1)S(1)} %pad_maximum_fusion.5), channel_id=1, source_target_pairs={{4,0},{8,4},{12,8},{16,12},{20,16},{24,20},{28,24},{5,1},{9,5},{13... | collective-permute-start | bytes 1191944 | tf_op jit(solution)/shard_map/ppermute | solution.py:470

commit v2 on v1

--- a/solution.py
+++ b/solution.py
@@ -316,71 +316,61 @@
     joined[...] = joined_short[...].astype(F32)
     joined[own, middle] = exact_ref[0]
 
-    def run_x(source, which, begin_at, end_at, size, exact):
-        @pl.loop(begin_at, end_at)
-        def _(i):
-            at = pl.ds(pl.multiple_of(i * size, 16), size)
-            for n in range(wide // (2 * LANE)):
-                begin = 2 * LANE * n - LANE
-                lo, hi = max(begin, 0), min(begin + 4 * LANE, wide)
-                out = dot(source[at, lo:hi], across_ref[0, which, lo - begin : hi - begin, :])
-                to = slice(2 * LANE * n, 2 * LANE * (n + 1))
-                if exact:
-                    high[at, to], low[at, to] = split(out)
-                else:
-                    high[at, to] = out.astype(BF16)
-
-    def run_zy(which, begin_at, end_at, size, exact, finish):
+    blocks = range(wide // (2 * LANE))
+
+    def correlate(source, which, size, start, exact, finish):
         deep = (size + 2 * REACH) * DEPTH
-        matrix = within_ref[0, which, : size * DEPTH, :deep]
-
-        @pl.loop(begin_at, end_at)
-        def _(i):
-            start = i * (size * DEPTH)
-            at = pl.ds(pl.multiple_of(start, 16), deep)
-            for n in range(wide // (2 * LANE)):
-                to = slice(2 * LANE * n, 2 * LANE * (n + 1))
-                out = dot(matrix, high[at, to])
-                if exact:
-                    out = out + dot(matrix, low[at, to])
-                finish(start, size * DEPTH, to, out)
-
-    def rows_at(start, shift, size):
-        return pl.ds(pl.multiple_of(start + shift * DEPTH, 8), size)
+        size8 = size * DEPTH
+        matrix = within_ref[0, which, :size8, :deep]
+        here = slice(start, start + size8)
+        for n in blocks:
+            to = slice(2 * LANE * n, 2 * LANE * (n + 1))
+            out = dot(matrix, source[start : start + deep, to])
+            if exact:
+                high[here, to], low[here, to] = split(out)
+            else:
+                high[here, to] = out.astype(BF16)
+        for n in blocks:
+            begin = 2 * LANE * n - LANE
+            lo, hi = max(begin, 0), min(begin + 4 * LANE, wide)
+            band = across_ref[0, which, lo - begin : hi - begin, :]
+            out = dot(high[here, lo:hi], band)
+            if exact:
+                out = out + dot(low[here, lo:hi], band)
+            finish(start, size8, slice(2 * LANE * n, 2 * LANE * (n + 1)), out)
 
     def ratio_from(shift):
-        def finish(start, size, to, out):
-            top = joined[rows_at(start, shift, size), to]
-            at = pl.ds(pl.multiple_of(start, 16), size)
-            ratio[at, to] = (top / jnp.maximum(out, TINY)).astype(BF16)
+        def finish(start, size8, to, out):
+            top = joined[start + shift * DEPTH : start + shift * DEPTH + size8, to]
+            bottom = jnp.maximum(out, TINY)
+            inverse = pl.reciprocal(bottom, approx=True)
+            inverse = inverse * (2.0 - bottom * inverse)
+            ratio[start : start + size8, to] = (top * inverse).astype(BF16)
 
         return finish
 
-    def first_estimate(start, size, to, out):
-        at = pl.ds(pl.multiple_of(start, 16), size)
-        value = joined[rows_at(start, 2 * REACH, size), to] * out
+    def first_estimate(start, size8, to, out):
+        at = slice(start, start + size8)
+        begin = start + 2 * REACH * DEPTH
+        value = joined[begin : begin + size8, to] * out
         estimate[at, to] = value
         estimate_short[at, to] = value.astype(BF16)
 
-    def last_estimate(start, size, to, out):
-        at = pl.ds(pl.multiple_of(start, 16), size)
-        value = estimate[rows_at(start, 2 * REACH, size), to] * out
+    def last_estimate(start, size8, to, out):
+        begin = start + 2 * REACH * DEPTH
+        value = estimate[begin : begin + size8, to] * out
         for b in range(2):
-            result[to.start // LANE + b, at, :] = value[:, b * LANE : (b + 1) * LANE]
-
-    run_x(joined_short, 0, 0, 5, 40 * DEPTH, False)
-    run_zy(0, 0, 5, BIG, False, ratio_from(REACH))
-    run_x(ratio, 1, 0, 1, BIG * DEPTH, False)
-    run_x(ratio, 1, 1, 4, BIG * DEPTH, True)
-    run_x(ratio, 1, 4, 5, BIG * DEPTH, False)
-    run_zy(1, 0, 1, BIG, False, first_estimate)
-    run_zy(1, 1, 3, BIG, True, first_estimate)
-    run_zy(1, 3, 4, BIG, False, first_estimate)
-    run_x(estimate_short, 0, 0, 4, BIG * DEPTH, False)
-    run_zy(0, 0, 4, SMALL, False, ratio_from(3 * REACH))
+            result[to.start // LANE + b, start : start + size8, :] = value[:, b * LANE : (b + 1) * LANE]
+
+    for i in range(5):
+        correlate(joined_short, 0, BIG, i * BIG * DEPTH, False, ratio_from(REACH))
+    for i in range(4):
+        correlate(ratio, 1, BIG, i * BIG * DEPTH, i in (1, 2), first_estimate)
+    for i in range(4):
+        correlate(estimate_short, 0, SMALL, i * SMALL * DEPTH, False, ratio_from(3 * REACH))
     ratio[4 * SMALL * DEPTH : (4 * SMALL + 4) * DEPTH, :] = jnp.zeros((4 * DEPTH, wide), BF16)
-    run_x(ratio, 1, 0, 3, 36 * DEPTH, True)
-    run_zy(1, 0, 3, SMALL, True, last_estimate)
+    for i in range(3):
+        correlate(ratio, 1, SMALL, i * SMALL * DEPTH, True, last_estimate)
 
     planes = restored_ref.shape[1]
     height = restored_ref.shape[2]
@@ -448,7 +438,7 @@
             pltpu.VMEM((estimate_rows, wide), F32),
             pltpu.VMEM((estimate_rows, wide), BF16),
             pltpu.VMEM((wide // LANE, result_rows, LANE), F32),
-            pltpu.VMEM((FRAME * DEPTH, wide), BF16),
+            pltpu.VMEM((ratio_rows, wide), BF16),
             pltpu.VMEM((ratio_rows, wide), BF16),
         ],
         compiler_params=params(40),
@@ -491,18 +481,18 @@
         side = shift(jnp.concatenate([right] + strips, axis=1), "gx", 1)
         joined += [join(own, low, side, k) for k in range(n)]
 
+    fars = shift(jnp.concatenate([tail for _, _, tail in joined], axis=0), "gy", 2)
     arrived = []
-    for _, short, tail in joined:
+    for at, (_, short, _) in enumerate(joined):
         above = shift(short, "gy", 1)
         below = shift(short, "gy", -1)
-        far = shift(tail, "gy", 2)
-        arrived.append((above, below, far))
+        arrived.append((above, below, fars[at : at + 1]))
 
     outs = ()
     for at in range(chans):
         exact, short, _ = joined[at]
         above, below, far = arrived[at]
-        if at == chans - 1:
+        if at:
             above, below, _ = lax.optimization_barrier((above, below, outs[2]))
         column = (far, above, short, below)
         last = jnp.concatenate([a[:, :, -LANE:] for a in column], axis=1)

time: 171 us -> 145 us (0.85)
  the two profiles are of different devices: /device:TPU:11 before, /device:TPU:6 now
where the time goes in v2:
time: 145 us; the launch traced here: 144 us
  starting transfers between devices  46.5 us (32%)
  Pallas kernels  46.1 us (32%)
  waiting for transfers between devices  42.4 us (29%)
  local copies, waits for them, and re-layouts  7.72 us (5%)
    ppermute x17, starting transfers between devices, shift(): return lax.ppermute(block, axis, route)  46.5 us
    ppermute x17, waiting for transfers between devices, shift(): return lax.ppermute(block, axis, route)  42.4 us
    pallas_call x3, Pallas kernels, deconvolve(): pl.pallas_call(deconvolve_kernel, grid=(1,), in_specs=[pl.BlockSpec(memor...  33 us
    pallas_call x2, Pallas kernels, place(): pl.pallas_call(place_kernel, grid_spec=pltpu.PrefetchScalarGridSpec(num_s...  8.16 us
    unnamed x26, local copies, waits for them, and re-layouts  6.69 us
  transfers between devices with their start and end apart: 17, of which 9 were waited for; matrix products, arithmetic and copies ran while one was open for 3% of the time, Pallas kernels for 22%

profile of v2, /device:TPU:6, one launch (start us, length us, event | category | flops | bytes accessed | tf_op | source)
XLA Modules:
  0.0 144.3 jit_solution(13445034095656088602)
XLA Ops:
  0.6 1.8 %copy-done.1 = bf16[3,8,96,544]{3,2,1,0:T(8,128)(2,1)S(1)} copy-done((bf16[3,8,96,544]{3,2,1,0:T(8,128)(2,1)S(1)}, bf16[3,8,96,544]{3,2,1,0:T(8,128)(2,1)}, u32[]{:S(2)}) %copy-start.1) | copy-done | bytes 2506776
  3.1 3.2 %place.3 = (bf16[1,512,512]{2,1,0:T(8,128)(2,1)S(1)}, bf16[1,512,128]{2,1,0:T(8,128)(2,1)S(1)}, bf16[1,576,512]{2,1,0:T(8,128)(2,1)}) custom-call(s32[2]{0:T(128)S(1)} %bitcast.10, bf16[3,8,96,544]{3,2,1,0:T(8,128)(2,1)S(1)} %copy-done.1), custom_call_target="tpu_custom_call" | custom-call | flops 2000000000 | bytes 2500000 | tf_op jit(solution)/shard_map/place/pallas_call | solution.py:88
  6.3 3.6 %collective-permute-start.6 = (bf16[1,576,512]{2,1,0:T(8,128)(2,1)}, bf16[1,576,512]{2,1,0:T(8,128)(2,1)S(1)}, u32[]{:S(2)}, u32[]{:S(2)}) collective-permute-start(bf16[1,576,512]{2,1,0:T(8,128)(2,1)} %get-tuple-element.42), channel_id=1, source_target_pairs={{0,1},{1,2},{2,3},{4,5},{5,6},{6,7},{8,9},{9,10},{10,11},{12,13},{... | collective-permute-start | bytes 1769480 | tf_op jit(solution)/shard_map/ppermute | solution.py:460
  10.0 5.0 %place.2 = (bf16[2,512,512]{2,1,0:T(8,128)(2,1)S(1)}, bf16[2,512,128]{2,1,0:T(8,128)(2,1)S(1)}, bf16[2,576,512]{2,1,0:T(8,128)(2,1)}) custom-call(s32[2]{0:T(128)S(1)} %bitcast.11, bf16[3,8,96,544]{3,2,1,0:T(8,128)(2,1)S(1)} %copy-done.1), custom_call_target="tpu_custom_call" | custom-call | flops 4000000000 | bytes 5000000 | tf_op jit(solution)/shard_map/place/pallas_call | solution.py:88
  15.6 3.5 %collective-permute-start = (bf16[2,576,512]{2,1,0:T(8,128)(2,1)}, bf16[2,576,512]{2,1,0:T(8,128)(2,1)S(1)}, u32[]{:S(2)}, u32[]{:S(2)}) collective-permute-start(bf16[2,576,512]{2,1,0:T(8,128)(2,1)} %get-tuple-element.35), channel_id=1, source_target_pairs={{0,1},{1,2},{2,3},{4,5},{5,6},{6,7},{8,9},{9,10},{10,11},{12,13},{... | collective-permute-start | bytes 3538952 | tf_op jit(solution)/shard_map/ppermute | solution.py:460
  20.3 2.3 %bands.1 = (bf16[6,512,256]{2,1,0:T(8,128)(2,1)S(1)}, bf16[6,272,512]{2,1,0:T(8,128)(2,1)S(1)}) custom-call(f32[6,93]{1,0:T(8,128)S(1)} %reshape.21.kern_ref), custom_call_target="tpu_custom_call" | custom-call | flops 6000000 | bytes 24000000 | tf_op jit(solution)/shard_map/bands/pallas_call | solution.py:188
  22.6 1.3 collective-permute-done.6.low_ref
  26.3 1.9 %collective-permute-start.7 = (bf16[1,768,128]{2,1,0:T(8,128)(2,1)}, bf16[1,768,128]{2,1,0:T(8,128)(2,1)S(1)}, u32[]{:S(2)}, u32[]{:S(2)}) collective-permute-start(bf16[1,768,128]{2,1,0:T(8,128)(2,1)} %constant_dynamic-update-slice_fusion.1), channel_id=1, source_target_pairs={{0,4},{4,8},{8,12},{12,16},{16,20},{20,24},{24,28},{1,5},{5,9},{9,... | collective-permute-start | bytes 589832 | tf_op jit(solution)/shard_map/ppermute | solution.py:460
  29.3 4.2 %collective-permute-done.7.side_ref = bf16[1,768,128]{2,1,0:T(8,128)(2,1)S(1)} collective-permute-done((bf16[1,768,128]{2,1,0:T(8,128)(2,1)}, bf16[1,768,128]{2,1,0:T(8,128)(2,1)S(1)}, u32[]{:S(2)}, u32[]{:S(2)}) %collective-permute-start.7) | collective-permute-done | bytes 196640 | tf_op jit(solution)/shard_map/ppermute | solution.py:460
  34.4 4.3 %collective-permute-start.8 = (bf16[1,512,512]{2,1,0:T(8,128)(2,1)S(1)}, bf16[1,512,512]{2,1,0:T(8,128)(2,1)S(1)}, u32[]{:S(2)}, u32[]{:S(2)}) collective-permute-start(bf16[1,512,512]{2,1,0:T(8,128)(2,1)S(1)} %get-tuple-element.49), channel_id=1, source_target_pairs={{0,1},{1,2},{2,3},{4,5},{5,6},{6,7},{8,9},{9,10},{10,11},{12,13},{... | collective-permute-start | bytes 1572872 | tf_op jit(solution)/shard_map/ppermute | solution.py:460
  38.8 1.3 collective-permute-start.9
  40.1 9.2 %collective-permute-done.low_ref = bf16[2,576,512]{2,1,0:T(8,128)(2,1)S(1)} collective-permute-done((bf16[2,576,512]{2,1,0:T(8,128)(2,1)}, bf16[2,576,512]{2,1,0:T(8,128)(2,1)S(1)}, u32[]{:S(2)}, u32[]{:S(2)}) %collective-permute-start) | collective-permute-done | bytes 1179680 | tf_op jit(solution)/shard_map/ppermute | solution.py:460
  49.3 1.9 %collective-permute-start.1 = (bf16[2,768,128]{2,1,0:T(8,128)(2,1)S(1)}, bf16[2,768,128]{2,1,0:T(8,128)(2,1)S(1)}, u32[]{:S(2)}, u32[]{:S(2)}) collective-permute-start(bf16[2,768,128]{2,1,0:T(8,128)(2,1)S(1)} %slice_dynamic-update-slice_fusion), channel_id=1, source_target_pairs={{0,4},{4,8},{8,12},{12,16},{16,20},{20,24},{24,28},{1,5},{5,9},{9,... | collective-permute-start | bytes 1179656 | tf_op jit(solution)/shard_map/ppermute | solution.py:460
  51.2 8.0 %collective-permute-done.8.above_ref = bf16[1,512,512]{2,1,0:T(8,128)(2,1)S(1)} collective-permute-done((bf16[1,512,512]{2,1,0:T(8,128)(2,1)S(1)}, bf16[1,512,512]{2,1,0:T(8,128)(2,1)S(1)}, u32[]{:S(2)}, u32[]{:S(2)}) %collective-permute-start.8) | collective-permute-done | bytes 524320 | tf_op jit(solution)/shard_map/ppermute | solution.py:460
  61.1 5.5 %collective-permute-start.10 = (bf16[3,16,512]{2,1,0:T(8,128)(2,1)S(1)}, bf16[3,16,512]{2,1,0:T(8,128)(2,1)S(1)}, u32[]{:S(2)}, u32[]{:S(2)}) collective-permute-start(bf16[3,16,512]{2,1,0:T(8,128)(2,1)S(1)} %pad_maximum_fusion.6), channel_id=1, source_target_pairs={{0,2},{1,3},{4,6},{5,7},{8,10},{9,11},{12,14},{13,15},{16,18},{17,... | collective-permute-start | bytes 147464 | tf_op jit(solution)/shard_map/ppermute | solution.py:460
  66.7 3.5 %collective-permute-start.4 = (bf16[1,512,512]{2,1,0:T(8,128)(2,1)S(1)}, bf16[1,512,512]{2,1,0:T(8,128)(2,1)S(1)}, u32[]{:S(2)}, u32[]{:S(2)}) collective-permute-start(bf16[1,512,512]{2,1,0:T(8,128)(2,1)S(1)} %get-tuple-element.40), channel_id=1, source_target_pairs={{0,1},{1,2},{2,3},{4,5},{5,6},{6,7},{8,9},{9,10},{10,11},{12,13},{... | collective-permute-start | bytes 1572872 | tf_op jit(solution)/shard_map/ppermute | solution.py:460
  71.6 1.9 %collective-permute-start.12 = (bf16[1,1552,128]{2,1,0:T(8,128)(2,1)S(1)}, bf16[1,1552,128]{2,1,0:T(8,128)(2,1)S(1)}, u32[]{:S(2)}, u32[]{:S(2)}) collective-permute-start(bf16[1,1552,128]{2,1,0:T(8,128)(2,1)S(1)} %pad_maximum_fusion.1), channel_id=1, source_target_pairs={{4,0},{8,4},{12,8},{16,12},{20,16},{24,20},{28,24},{5,1},{9,5},{13... | collective-permute-start | bytes 1191944 | tf_op jit(solution)/shard_map/ppermute | solution.py:460
  73.5 2.6 %collective-permute-start.11 = (bf16[1,1552,128]{2,1,0:T(8,128)(2,1)S(1)}, bf16[1,1552,128]{2,1,0:T(8,128)(2,1)S(1)}, u32[]{:S(2)}, u32[]{:S(2)}) collective-permute-start(bf16[1,1552,128]{2,1,0:T(8,128)(2,1)S(1)} %pad_maximum_fusion), channel_id=1, source_target_pairs={{0,4},{4,8},{8,12},{12,16},{16,20},{20,24},{24,28},{1,5},{5,9},{9,... | collective-permute-start | bytes 1191944 | tf_op jit(solution)/shard_map/ppermute | solution.py:460
  76.2 2.6 %collective-permute-done.12.right_ref = bf16[1,1552,128]{2,1,0:T(8,128)(2,1)S(1)} collective-permute-done((bf16[1,1552,128]{2,1,0:T(8,128)(2,1)S(1)}, bf16[1,1552,128]{2,1,0:T(8,128)(2,1)S(1)}, u32[]{:S(2)}, u32[]{:S(2)}) %collective-permute-start.12) | collective-permute-done | bytes 397344 | tf_op jit(solution)/shard_map/ppermute | solution.py:460
  78.8 5.2 %collective-permute-done.11.left_ref = bf16[1,1552,128]{2,1,0:T(8,128)(2,1)S(1)} collective-permute-done((bf16[1,1552,128]{2,1,0:T(8,128)(2,1)S(1)}, bf16[1,1552,128]{2,1,0:T(8,128)(2,1)S(1)}, u32[]{:S(2)}, u32[]{:S(2)}) %collective-permute-start.11) | collective-permute-done | bytes 397344 | tf_op jit(solution)/shard_map/ppermute | solution.py:460
  84.1 11.0 %deconvolve.3 = (f32[3,8,64,512]{3,2,1,0:T(8,128)}, f32[3,4,32,256]{3,2,1,0:T(8,128)}, f32[3,2,16,128]{3,2,1,0:T(8,128)}) custom-call(s32[4]{0:T(128)S(1)} %add_convert_fusion.sides_ref, f32[1,512,512]{2,1,0:T(8,128)S(1)} %get-tuple-element.48.exact_ref, bf16[1,512,512]{2,1,0:T(8,128)(2,1)S(1)} %collective-permute-done.8.above_ref, ...), custom_call_target="tpu_custom_call" | custom-call | flops 8999999488 | bytes 8000000 | tf_op jit(solution)/shard_map/deconvolve/pallas_call | solution.py:423
  95.2 1.9 %collective-permute-start.14 = (bf16[1,1552,128]{2,1,0:T(8,128)(2,1)S(1)}, bf16[1,1552,128]{2,1,0:T(8,128)(2,1)S(1)}, u32[]{:S(2)}, u32[]{:S(2)}) collective-permute-start(bf16[1,1552,128]{2,1,0:T(8,128)(2,1)S(1)} %pad_maximum_fusion.3), channel_id=1, source_target_pairs={{4,0},{8,4},{12,8},{16,12},{20,16},{24,20},{28,24},{5,1},{9,5},{13... | collective-permute-start | bytes 1191944 | tf_op jit(solution)/shard_map/ppermute | solution.py:460
  97.2 2.4 %collective-permute-start.13 = (bf16[1,1552,128]{2,1,0:T(8,128)(2,1)S(1)}, bf16[1,1552,128]{2,1,0:T(8,128)(2,1)S(1)}, u32[]{:S(2)}, u32[]{:S(2)}) collective-permute-start(bf16[1,1552,128]{2,1,0:T(8,128)(2,1)S(1)} %pad_maximum_fusion.2), channel_id=1, source_target_pairs={{0,4},{4,8},{8,12},{12,16},{16,20},{20,24},{24,28},{1,5},{5,9},{9,... | collective-permute-start | bytes 1191944 | tf_op jit(solution)/shard_map/ppermute | solution.py:460
  99.6 4.6 %collective-permute-start.2 = (bf16[1,512,512]{2,1,0:T(8,128)(2,1)S(1)}, bf16[1,512,512]{2,1,0:T(8,128)(2,1)S(1)}, u32[]{:S(2)}, u32[]{:S(2)}) collective-permute-start(bf16[1,512,512]{2,1,0:T(8,128)(2,1)S(1)} %get-tuple-element.38), channel_id=1, source_target_pairs={{0,1},{1,2},{2,3},{4,5},{5,6},{6,7},{8,9},{9,10},{10,11},{12,13},{... | collective-permute-start | bytes 1572872 | tf_op jit(solution)/shard_map/ppermute | solution.py:460
  104.2 1.5 %collective-permute-start.3 = (bf16[1,512,512]{2,1,0:T(8,128)(2,1)S(1)}, bf16[1,512,512]{2,1,0:T(8,128)(2,1)S(1)}, u32[]{:S(2)}, u32[]{:S(2)}) collective-permute-start(bf16[1,512,512]{2,1,0:T(8,128)(2,1)S(1)} %get-tuple-element.38), channel_id=1, source_target_pairs={{1,0},{2,1},{3,2},{5,4},{6,5},{7,6},{9,8},{10,9},{11,10},{13,12},{... | collective-permute-start | bytes 1572872 | tf_op jit(solution)/shard_map/ppermute | solution.py:460
  105.8 2.8 %collective-permute-done.13.left_ref = bf16[1,1552,128]{2,1,0:T(8,128)(2,1)S(1)} collective-permute-done((bf16[1,1552,128]{2,1,0:T(8,128)(2,1)S(1)}, bf16[1,1552,128]{2,1,0:T(8,128)(2,1)S(1)}, u32[]{:S(2)}, u32[]{:S(2)}) %collective-permute-start.13) | collective-permute-done | bytes 397344 | tf_op jit(solution)/shard_map/ppermute | solution.py:460
  108.6 11.0 %deconvolve.4 = (f32[3,8,64,512]{3,2,1,0:T(8,128)}, f32[3,4,32,256]{3,2,1,0:T(8,128)}, f32[3,2,16,128]{3,2,1,0:T(8,128)}) custom-call(s32[4]{0:T(128)S(1)} %add_convert_fusion.sides_ref, f32[1,512,512]{2,1,0:T(8,128)S(1)} %get-tuple-element.39.exact_ref, ...), custom_call_target="tpu_custom_call", output_to_operand_aliasing={{0}: (13, {}), {1}: (14, {}), {2}: (15, {})} | custom-call | flops 8999999488 | bytes 8000000 | tf_op jit(solution)/shard_map/deconvolve/pallas_call | solution.py:423
  119.7 2.3 %collective-permute-start.16 = (bf16[1,1552,128]{2,1,0:T(8,128)(2,1)S(1)}, bf16[1,1552,128]{2,1,0:T(8,128)(2,1)S(1)}, u32[]{:S(2)}, u32[]{:S(2)}) collective-permute-start(bf16[1,1552,128]{2,1,0:T(8,128)(2,1)S(1)} %pad_maximum_fusion.5), channel_id=1, source_target_pairs={{4,0},{8,4},{12,8},{16,12},{20,16},{24,20},{28,24},{5,1},{9,5},{13... | collective-permute-start | bytes 1191944 | tf_op jit(solution)/shard_map/ppermute | solution.py:460
  122.0 2.3 %collective-permute-start.15 = (bf16[1,1552,128]{2,1,0:T(8,128)(2,1)S(1)}, bf16[1,1552,128]{2,1,0:T(8,128)(2,1)S(1)}, u32[]{:S(2)}, u32[]{:S(2)}) collective-permute-start(bf16[1,1552,128]{2,1,0:T(8,128)(2,1)S(1)} %pad_maximum_fusion.4), channel_id=1, source_target_pairs={{0,4},{4,8},{8,12},{12,16},{16,20},{20,24},{24,28},{1,5},{5,9},{9,... | collective-permute-start | bytes 1191944 | tf_op jit(solution)/shard_map/ppermute | solution.py:460
  124.3 2.9 %collective-permute-done.16.right_ref = bf16[1,1552,128]{2,1,0:T(8,128)(2,1)S(1)} collective-permute-done((bf16[1,1552,128]{2,1,0:T(8,128)(2,1)S(1)}, bf16[1,1552,128]{2,1,0:T(8,128)(2,1)S(1)}, u32[]{:S(2)}, u32[]{:S(2)}) %collective-permute-start.16) | collective-permute-done | bytes 397344 | tf_op jit(solution)/shard_map/ppermute | solution.py:460
  127.3 6.0 %collective-permute-done.15.left_ref = bf16[1,1552,128]{2,1,0:T(8,128)(2,1)S(1)} collective-permute-done((bf16[1,1552,128]{2,1,0:T(8,128)(2,1)S(1)}, bf16[1,1552,128]{2,1,0:T(8,128)(2,1)S(1)}, u32[]{:S(2)}, u32[]{:S(2)}) %collective-permute-start.15) | collective-permute-done | bytes 397344 | tf_op jit(solution)/shard_map/ppermute | solution.py:460
  133.3 11.0 %deconvolve.5 = (f32[3,8,64,512]{3,2,1,0:T(8,128)}, f32[3,4,32,256]{3,2,1,0:T(8,128)}, f32[3,2,16,128]{3,2,1,0:T(8,128)}) custom-call(s32[4]{0:T(128)S(1)} %add_convert_fusion.sides_ref, f32[1,512,512]{2,1,0:T(8,128)S(1)} %get-tuple-element.37.exact_ref, ...), custom_call_target="tpu_custom_call", output_to_operand_aliasing={{0}: (13, {}), {1}: (14, {}), {2}: (15, {})} | custom-call | flops 8999999488 | bytes 8000000 | tf_op jit(solution)/shard_map/deconvolve/pallas_call | solution.py:423
  (64 shorter events, 10.4 us)
Async XLA Ops:
  0.6 1.8 %copy-start.1 = (bf16[3,8,96,544]{3,2,1,0:T(8,128)(2,1)S(1)}, bf16[3,8,96,544]{3,2,1,0:T(8,128)(2,1)}, u32[]{:S(2)}) copy-start(bf16[3,8,96,544]{3,2,1,0:T(8,128)(2,1)} %tile_ref.3) | copy-start | bytes 7520260
  2.5 0.7 copy-start.2
  3.1 6.8 %copy-start.3 = (s32[1,1,2]{2,1,0:T(1,128)S(1)}, s32[1,1,2]{2,1,0:T(1,128)}, u32[]{:S(2)}) copy-start(s32[1,1,2]{2,1,0:T(1,128)} %param.8) | copy-start | bytes 28
  6.3 12.9 %copy-start.8 = (f32[3,3,31]{2,1,0:T(4,128)S(1)}, f32[3,3,31]{2,1,0:T(4,128)}, u32[]{:S(2)}) copy-start(f32[3,3,31]{2,1,0:T(4,128)} %param.9) | copy-start | bytes 3352
  6.3 17.6 %collective-permute-start.6 = (bf16[1,576,512]{2,1,0:T(8,128)(2,1)}, bf16[1,576,512]{2,1,0:T(8,128)(2,1)S(1)}, u32[]{:S(2)}, u32[]{:S(2)}) collective-permute-start(bf16[1,576,512]{2,1,0:T(8,128)(2,1)} %get-tuple-element.42), channel_id=1, source_target_pairs={{0,1},{1,2},{2,3},{4,5},{5,6},{6,7},{8,9},{9,10},{10,11},{12,13},{... | collective-permute-start | bytes 1769480 | tf_op jit(solution)/shard_map/ppermute | solution.py:460
  14.9 0.7 copy-start
  15.6 33.6 %collective-permute-start = (bf16[2,576,512]{2,1,0:T(8,128)(2,1)}, bf16[2,576,512]{2,1,0:T(8,128)(2,1)S(1)}, u32[]{:S(2)}, u32[]{:S(2)}) collective-permute-start(bf16[2,576,512]{2,1,0:T(8,128)(2,1)} %get-tuple-element.35), channel_id=1, source_target_pairs={{0,1},{1,2},{2,3},{4,5},{5,6},{6,7},{8,9},{9,10},{10,11},{12,13},{... | collective-permute-start | bytes 3538952 | tf_op jit(solution)/shard_map/ppermute | solution.py:460
  26.3 7.2 %collective-permute-start.7 = (bf16[1,768,128]{2,1,0:T(8,128)(2,1)}, bf16[1,768,128]{2,1,0:T(8,128)(2,1)S(1)}, u32[]{:S(2)}, u32[]{:S(2)}) collective-permute-start(bf16[1,768,128]{2,1,0:T(8,128)(2,1)} %constant_dynamic-update-slice_fusion.1), channel_id=1, source_target_pairs={{0,4},{4,8},{8,12},{12,16},{16,20},{20,24},{24,28},{1,5},{5,9},{9,... | collective-permute-start | bytes 589832 | tf_op jit(solution)/shard_map/ppermute | solution.py:460
  34.4 24.8 %collective-permute-start.8 = (bf16[1,512,512]{2,1,0:T(8,128)(2,1)S(1)}, bf16[1,512,512]{2,1,0:T(8,128)(2,1)S(1)}, u32[]{:S(2)}, u32[]{:S(2)}) collective-permute-start(bf16[1,512,512]{2,1,0:T(8,128)(2,1)S(1)} %get-tuple-element.49), channel_id=1, source_target_pairs={{0,1},{1,2},{2,3},{4,5},{5,6},{6,7},{8,9},{9,10},{10,11},{12,13},{... | collective-permute-start | bytes 1572872 | tf_op jit(solution)/shard_map/ppermute | solution.py:460
  38.8 27.9 %collective-permute-start.9 = (bf16[1,512,512]{2,1,0:T(8,128)(2,1)S(1)}, bf16[1,512,512]{2,1,0:T(8,128)(2,1)S(1)}, u32[]{:S(2)}, u32[]{:S(2)}) collective-permute-start(bf16[1,512,512]{2,1,0:T(8,128)(2,1)S(1)} %get-tuple-element.49), channel_id=1, source_target_pairs={{1,0},{2,1},{3,2},{5,4},{6,5},{7,6},{9,8},{10,9},{11,10},{13,12},{... | collective-permute-start | bytes 1572872 | tf_op jit(solution)/shard_map/ppermute | solution.py:460
  49.3 9.9 %collective-permute-start.1 = (bf16[2,768,128]{2,1,0:T(8,128)(2,1)S(1)}, bf16[2,768,128]{2,1,0:T(8,128)(2,1)S(1)}, u32[]{:S(2)}, u32[]{:S(2)}) collective-permute-start(bf16[2,768,128]{2,1,0:T(8,128)(2,1)S(1)} %slice_dynamic-update-slice_fusion), channel_id=1, source_target_pairs={{0,4},{4,8},{8,12},{12,16},{16,20},{20,24},{24,28},{1,5},{5,9},{9,... | collective-permute-start | bytes 1179656 | tf_op jit(solution)/shard_map/ppermute | solution.py:460
  61.0 23.0 %copy-start.4 = (bf16[768,384]{1,0:T(8,128)(2,1)S(1)}, bf16[768,384]{1,0:T(8,128)(2,1)}, u32[]{:S(2)}) copy-start(bf16[768,384]{1,0:T(8,128)(2,1)} %constant.25.clone.one_x_ref) | copy-start | bytes 1769476
  61.0 23.0 %copy-start.5 = (bf16[144,592]{1,0:T(8,128)(2,1)S(1)}, bf16[144,592]{1,0:T(8,128)(2,1)}, u32[]{:S(2)}) copy-start(bf16[144,592]{1,0:T(8,128)(2,1)} %constant.26.clone.one_zy_ref) | copy-start | bytes 511492
  61.1 23.0 %copy-start.6 = (bf16[384,128]{1,0:T(8,128)(2,1)S(1)}, bf16[384,128]{1,0:T(8,128)(2,1)}, u32[]{:S(2)}) copy-start(bf16[384,128]{1,0:T(8,128)(2,1)} %constant.27.clone.two_x_ref) | copy-start | bytes 294916
  61.1 23.0 %copy-start.7 = (bf16[32,144]{1,0:T(8,128)(2,1)S(1)}, bf16[32,144]{1,0:T(8,128)(2,1)}, u32[]{:S(2)}) copy-start(bf16[32,144]{1,0:T(8,128)(2,1)} %constant.28.clone.two_zy_ref) | copy-start | bytes 27652
  61.1 10.4 %collective-permute-start.10 = (bf16[3,16,512]{2,1,0:T(8,128)(2,1)S(1)}, bf16[3,16,512]{2,1,0:T(8,128)(2,1)S(1)}, u32[]{:S(2)}, u32[]{:S(2)}) collective-permute-start(bf16[3,16,512]{2,1,0:T(8,128)(2,1)S(1)} %pad_maximum_fusion.6), channel_id=1, source_target_pairs={{0,2},{1,3},{4,6},{5,7},{8,10},{9,11},{12,14},{13,15},{16,18},{17,... | collective-permute-start | bytes 147464 | tf_op jit(solution)/shard_map/ppermute | solution.py:460
  66.7 28.4 %collective-permute-start.4 = (bf16[1,512,512]{2,1,0:T(8,128)(2,1)S(1)}, bf16[1,512,512]{2,1,0:T(8,128)(2,1)S(1)}, u32[]{:S(2)}, u32[]{:S(2)}) collective-permute-start(bf16[1,512,512]{2,1,0:T(8,128)(2,1)S(1)} %get-tuple-element.40), channel_id=1, source_target_pairs={{0,1},{1,2},{2,3},{4,5},{5,6},{6,7},{8,9},{9,10},{10,11},{12,13},{... | collective-permute-start | bytes 1572872 | tf_op jit(solution)/shard_map/ppermute | solution.py:460
  70.2 24.9 %collective-permute-start.5 = (bf16[1,512,512]{2,1,0:T(8,128)(2,1)S(1)}, bf16[1,512,512]{2,1,0:T(8,128)(2,1)S(1)}, u32[]{:S(2)}, u32[]{:S(2)}) collective-permute-start(bf16[1,512,512]{2,1,0:T(8,128)(2,1)S(1)} %get-tuple-element.40), channel_id=1, source_target_pairs={{1,0},{2,1},{3,2},{5,4},{6,5},{7,6},{9,8},{10,9},{11,10},{13,12},{... | collective-permute-start | bytes 1572872 | tf_op jit(solution)/shard_map/ppermute | solution.py:460
  71.6 7.2 %collective-permute-start.12 = (bf16[1,1552,128]{2,1,0:T(8,128)(2,1)S(1)}, bf16[1,1552,128]{2,1,0:T(8,128)(2,1)S(1)}, u32[]{:S(2)}, u32[]{:S(2)}) collective-permute-start(bf16[1,1552,128]{2,1,0:T(8,128)(2,1)S(1)} %pad_maximum_fusion.1), channel_id=1, source_target_pairs={{4,0},{8,4},{12,8},{16,12},{20,16},{24,20},{28,24},{5,1},{9,5},{13... | collective-permute-start | bytes 1191944 | tf_op jit(solution)/shard_map/ppermute | solution.py:460
  73.5 10.5 %collective-permute-start.11 = (bf16[1,1552,128]{2,1,0:T(8,128)(2,1)S(1)}, bf16[1,1552,128]{2,1,0:T(8,128)(2,1)S(1)}, u32[]{:S(2)}, u32[]{:S(2)}) collective-permute-start(bf16[1,1552,128]{2,1,0:T(8,128)(2,1)S(1)} %pad_maximum_fusion), channel_id=1, source_target_pairs={{0,4},{4,8},{8,12},{12,16},{16,20},{20,24},{24,28},{1,5},{5,9},{9,... | collective-permute-start | bytes 1191944 | tf_op jit(solution)/shard_map/ppermute | solution.py:460
  95.2 10.5 %collective-permute-start.14 = (bf16[1,1552,128]{2,1,0:T(8,128)(2,1)S(1)}, bf16[1,1552,128]{2,1,0:T(8,128)(2,1)S(1)}, u32[]{:S(2)}, u32[]{:S(2)}) collective-permute-start(bf16[1,1552,128]{2,1,0:T(8,128)(2,1)S(1)} %pad_maximum_fusion.3), channel_id=1, source_target_pairs={{4,0},{8,4},{12,8},{16,12},{20,16},{24,20},{28,24},{5,1},{9,5},{13... | collective-permute-start | bytes 1191944 | tf_op jit(solution)/shard_map/ppermute | solution.py:460
  97.2 11.4 %collective-permute-start.13 = (bf16[1,1552,128]{2,1,0:T(8,128)(2,1)S(1)}, bf16[1,1552,128]{2,1,0:T(8,128)(2,1)S(1)}, u32[]{:S(2)}, u32[]{:S(2)}) collective-permute-start(bf16[1,1552,128]{2,1,0:T(8,128)(2,1)S(1)} %pad_maximum_fusion.2), channel_id=1, source_target_pairs={{0,4},{4,8},{8,12},{12,16},{16,20},{20,24},{24,28},{1,5},{5,9},{9,... | collective-permute-start | bytes 1191944 | tf_op jit(solution)/shard_map/ppermute | solution.py:460
  99.6 20.0 %collective-permute-start.2 = (bf16[1,512,512]{2,1,0:T(8,128)(2,1)S(1)}, bf16[1,512,512]{2,1,0:T(8,128)(2,1)S(1)}, u32[]{:S(2)}, u32[]{:S(2)}) collective-permute-start(bf16[1,512,512]{2,1,0:T(8,128)(2,1)S(1)} %get-tuple-element.38), channel_id=1, source_target_pairs={{0,1},{1,2},{2,3},{4,5},{5,6},{6,7},{8,9},{9,10},{10,11},{12,13},{... | collective-permute-start | bytes 1572872 | tf_op jit(solution)/shard_map/ppermute | solution.py:460
  104.2 15.4 %collective-permute-start.3 = (bf16[1,512,512]{2,1,0:T(8,128)(2,1)S(1)}, bf16[1,512,512]{2,1,0:T(8,128)(2,1)S(1)}, u32[]{:S(2)}, u32[]{:S(2)}) collective-permute-start(bf16[1,512,512]{2,1,0:T(8,128)(2,1)S(1)} %get-tuple-element.38), channel_id=1, source_target_pairs={{1,0},{2,1},{3,2},{5,4},{6,5},{7,6},{9,8},{10,9},{11,10},{13,12},{... | collective-permute-start | bytes 1572872 | tf_op jit(solution)/shard_map/ppermute | solution.py:460
  119.7 7.6 %collective-permute-start.16 = (bf16[1,1552,128]{2,1,0:T(8,128)(2,1)S(1)}, bf16[1,1552,128]{2,1,0:T(8,128)(2,1)S(1)}, u32[]{:S(2)}, u32[]{:S(2)}) collective-permute-start(bf16[1,1552,128]{2,1,0:T(8,128)(2,1)S(1)} %pad_maximum_fusion.5), channel_id=1, source_target_pairs={{4,0},{8,4},{12,8},{16,12},{20,16},{24,20},{28,24},{5,1},{9,5},{13... | collective-permute-start | bytes 1191944 | tf_op jit(solution)/shard_map/ppermute | solution.py:460
  122.0 11.3 %collective-permute-start.15 = (bf16[1,1552,128]{2,1,0:T(8,128)(2,1)S(1)}, bf16[1,1552,128]{2,1,0:T(8,128)(2,1)S(1)}, u32[]{:S(2)}, u32[]{:S(2)}) collective-permute-start(bf16[1,1552,128]{2,1,0:T(8,128)(2,1)S(1)} %pad_maximum_fusion.4), channel_id=1, source_target_pairs={{0,4},{4,8},{8,12},{12,16},{16,20},{20,24},{24,28},{1,5},{5,9},{9,... | collective-permute-start | bytes 1191944 | tf_op jit(solution)/shard_map/ppermute | solution.py:460

commit v3 on v2

--- a/solution.py
+++ b/solution.py
@@ -43,7 +43,7 @@
     return high, (value - high.astype(F32)).astype(BF16)
 
 
-def place_kernel(off_ref, tile_ref, own_ref, right_ref, low_ref, canvas):
+def place_kernel(off_ref, tile_ref, own_ref, right_ref, low_ref, corner_ref, canvas):
     depth, tile_y, tile_x = tile_ref.shape[1:]
     parts = canvas.shape[0]
     wide = parts * LANE
@@ -65,15 +65,12 @@
     for b in range(parts - 1):
         to = slice(b * LANE, (b + 1) * LANE)
         own_ref[0, :, to] = canvas[b, :rows, :].astype(BF16)
-        low_ref[0, :rows, to] = canvas[b, rows:, :].astype(BF16)
+        low_ref[0, :, to] = canvas[b, rows:, :].astype(BF16)
     right_ref[0] = canvas[parts - 1, :rows, :].astype(BF16)
     half = rows // 2
     upper = canvas[parts - 1, rows : rows + half, :]
     lower = canvas[parts - 1, rows + half :, :]
-    corner = (upper + pltpu.roll(lower, LANE // 2, 1)).astype(BF16)
-    eighth = half // (parts - 1)
-    for b in range(parts - 1):
-        low_ref[0, rows:, b * LANE : (b + 1) * LANE] = corner[b * eighth : (b + 1) * eighth]
+    corner_ref[0] = (upper + pltpu.roll(lower, LANE // 2, 1)).astype(BF16)
 
 
 def place(tiles, offsets, begin, n):
@@ -82,8 +79,7 @@
     cols = tile_x - MARGIN
     block = lambda r, c: pl.BlockSpec((1, r, c), lambda i, off: (i, 0, 0))
     shape = lambda r, c: jax.ShapeDtypeStruct((n, r, c), BF16)
-    extra = rows // 2 * LANE // cols
-    sizes = ((rows, cols), (rows, LANE), (rows + extra, cols))
+    sizes = ((rows, cols), (rows, LANE), (rows, cols), (rows // 2, LANE))
     tile = pl.BlockSpec((1, depth, tile_y, tile_x), lambda i, off: (begin + i, 0, 0, 0))
     return pl.pallas_call(
         place_kernel,
@@ -101,8 +97,8 @@
     )(offsets, tiles)
 
 
-def join_kernel(own_ref, low_ref, side_ref, exact_ref, short_ref, tail_ref):
-    rows = own_ref.shape[1]
+def join_kernel(own_ref, low_ref, right_ref, corner_ref, exact_ref, first_ref, last_ref):
+    rows, cols = own_ref.shape[1:]
     half = rows // 2
 
     def seen(x):
@@ -112,8 +108,8 @@
     low = low_ref[0].astype(F32)
     total = own + low
     count = seen(own) + seen(low)
-    right = side_ref[0, :rows].astype(F32)
-    corner = side_ref[0, rows:].astype(F32)
+    right = right_ref[0].astype(F32)
+    corner = corner_ref[0].astype(F32)
     lane = lax.broadcasted_iota(jnp.int32, (half, LANE), 1)
     inside = lane < LANE // 2
     upper = jnp.where(inside, corner, 0.0)
@@ -125,28 +121,63 @@
     rest = total[:, LANE:] / count[:, LANE:]
     exact_ref[0, :, :LANE] = edge
     exact_ref[0, :, LANE:] = rest
-    short_ref[0, :, :LANE] = edge.astype(BF16)
-    short_ref[0, :, LANE:] = rest.astype(BF16)
-    tail = tail_ref.shape[1]
-    tail_ref[0, :, :LANE] = edge[rows - tail :].astype(BF16)
-    tail_ref[0, :, LANE:] = rest[rows - tail :].astype(BF16)
-
-
-def join(own, low, side, at):
-    _, rows, cols = own.shape
-    block = lambda r, c, k: pl.BlockSpec((1, r, c), lambda i: (k, 0, 0))
-    tail = 2 * DEPTH
-    sizes = ((rows, cols, F32), (rows, cols, BF16), (tail, cols, BF16))
+    first_ref[0] = edge.astype(BF16)
+    last_ref[0] = rest[:, -LANE:].astype(BF16)
+
+
+def join(own, low, right, corner):
+    n, rows, cols = own.shape
+    block = lambda r, c: pl.BlockSpec((1, r, c), lambda i: (i, 0, 0))
+    sizes = ((rows, cols, F32), (rows, LANE, BF16), (rows, LANE, BF16))
     return pl.pallas_call(
         join_kernel,
-        grid=(1,),
-        in_specs=[block(rows, cols, at), block(rows, cols, at), block(*side.shape[1:], at)],
-        out_specs=[block(r, c, 0) for r, c, _ in sizes],
-        out_shape=[jax.ShapeDtypeStruct((1, r, c), t) for r, c, t in sizes],
+        grid=(n,),
+        in_specs=[block(*a.shape[1:]) for a in (own, low, right, corner)],
+        out_specs=[block(r, c) for r, c, _ in sizes],
+        out_shape=[jax.ShapeDtypeStruct((n, r, c), t) for r, c, t in sizes],
         compiler_params=params(16),
         cost_estimate=cost(5e6, 3e6),
         name="join",
-    )(own, low, side)
+    )(own, low, right, corner)
+
+
+SIDE = 63
+
+
+def pack_kernel(exact_ref, left_ref, right_ref, out_ref, tail_ref):
+    rows, cols = exact_ref.shape[1:]
+    lane = lax.broadcasted_iota(jnp.int32, (rows, LANE), 1)
+    out_ref[0, :rows, :cols] = exact_ref[0].astype(BF16)
+    left = left_ref[0].astype(F32)
+    right = right_ref[0].astype(F32)
+    out_ref[0, :rows, cols:] = jnp.where(lane < SIDE, right, left).astype(BF16)
+    extra = out_ref.shape[1] - rows
+    pick = lax.broadcasted_iota(jnp.int32, (extra, LANE), 1) == SIDE - 1
+    pick &= lax.broadcasted_iota(jnp.int32, (extra, LANE), 0) == 0
+    pick = jnp.where(pick, 1.0, 0.0).astype(BF16)
+    column = lax.dot_general(
+        pick, left_ref[0], (((1,), (1,)), ((), ())), preferred_element_type=F32
+    )
+    out_ref[0, rows:, :cols] = column.astype(BF16)
+    out_ref[0, rows:, cols:] = jnp.zeros((extra, LANE), BF16)
+    tail_ref[0] = out_ref[0, rows - 2 * DEPTH :, :]
+
+
+def pack(exact, left, right, at):
+    _, rows, cols = exact.shape
+    block = lambda r, c, k: pl.BlockSpec((1, r, c), lambda i: (k, 0, 0))
+    extra = 2 * DEPTH
+    sizes = ((rows + extra, cols + LANE), (2 * extra, cols + LANE))
+    return pl.pallas_call(
+        pack_kernel,
+        grid=(1,),
+        in_specs=[block(*a.shape[1:], at) for a in (exact, left, right)],
+        out_specs=[block(*s, 0) for s in sizes],
+        out_shape=[jax.ShapeDtypeStruct((1,) + s, BF16) for s in sizes],
+        compiler_params=params(16),
+        cost_estimate=cost(1e6, 1e6),
+        name="pack",
+    )(exact, left, right)
 
 
 def bands_kernel(kern_ref, across_ref, within_ref):
@@ -301,17 +332,33 @@
 ):
     rows8, cols = exact_ref.shape[1:]
     wide = cols + 2 * LANE
-    far8 = far_ref.shape[1]
+    far8 = far_ref.shape[1] // 2
     own = slice(far8 + rows8, far8 + 2 * rows8)
     frame8 = far8 + 3 * rows8
     middle = slice(LANE, LANE + cols)
-
-    joined_short[:far8, middle] = far_ref[0]
-    joined_short[far8 : far8 + rows8, middle] = above_ref[0]
+    after = slice(LANE + cols, wide)
+
+    extra = far8
+    lane = lax.broadcasted_iota(jnp.int32, (extra, LANE), 1)
+    pick = jnp.where(lane == SIDE - 1, 1.0, 0.0).astype(BF16)
+
+    def unpack(source, count, begin):
+        to = slice(begin, begin + count)
+        joined_short[to, middle] = source[0, :count, :cols]
+        sides = source[0, :count, cols:]
+        joined_short[to, after] = sides
+        column = lax.dot_general(
+            source[0, count:, :cols], pick, (((0,), (0,)), ((), ())), preferred_element_type=F32
+        )[rows8 - count :]
+        lane = lax.broadcasted_iota(jnp.int32, (count, LANE), 1)
+        joined_short[to, :LANE] = jnp.where(lane == SIDE - 1, column, sides.astype(F32)).astype(BF16)
+
+    unpack(far_ref, far8, 0)
+    unpack(above_ref, rows8, far8)
+    unpack(below_ref, rows8, far8 + 2 * rows8)
     joined_short[own, middle] = exact_ref[0].astype(BF16)
-    joined_short[far8 + 2 * rows8 : frame8, middle] = below_ref[0]
-    joined_short[:frame8, :LANE] = left_ref[0]
-    joined_short[:frame8, LANE + cols :] = right_ref[0]
+    joined_short[own, :LANE] = left_ref[0]
+    joined_short[own, after] = right_ref[0]
     joined_short[frame8:, :] = jnp.zeros_like(joined_short[frame8:, :])
     joined[...] = joined_short[...].astype(F32)
     joined[own, middle] = exact_ref[0]
@@ -403,11 +450,11 @@
     level_two_ref[0] = two.reshape(level_two_ref.shape[1:])
 
 
-def deconvolve(at, chans, sides, group, across, within, matrices, earlier):
+def deconvolve(at, chans, sides, group, places, across, within, matrices, earlier):
     rows8, cols = group[0].shape[1:]
     rows = rows8 // DEPTH
     wide = cols + 2 * LANE
-    first = lambda a: pl.BlockSpec((1,) + a.shape[1:], lambda i: (0,) * a.ndim)
+    one = lambda a, k: pl.BlockSpec((1,) + a.shape[1:], lambda i: (k, 0, 0))
     mine = lambda s: pl.BlockSpec((1,) + s[1:], lambda i: (at,) + (0,) * (len(s) - 1))
     same = lambda a: pl.BlockSpec(a.shape, lambda i: (0,) * a.ndim)
     outs = (
@@ -424,7 +471,7 @@
         deconvolve_kernel,
         grid=(1,),
         in_specs=[pl.BlockSpec(memory_space=pltpu.SMEM)]
-        + [first(a) for a in group]
+        + [one(a, k) for a, k in zip(group, places)]
         + [mine(across.shape), mine(within.shape)]
         + [same(m) for m in matrices]
         + [pl.BlockSpec(memory_space=pl.ANY) for _ in earlier],
@@ -442,7 +489,7 @@
             pltpu.VMEM((ratio_rows, wide), BF16),
         ],
         compiler_params=params(40),
-        cost_estimate=cost(9e9, 8e6),
+        cost_estimate=cost(1e6, 1e5),
         name="deconvolve",
     )(*operands, *earlier)
 
@@ -459,48 +506,51 @@
         route = [(i, i + distance) for i in devices if i + distance in devices]
         return lax.ppermute(block, axis, route)
 
+    def shift_diagonal(block):
+        route = [
+            (x * size_y + y, (x + 1) * size_y + y + 1)
+            for x in range(size_x - 1)
+            for y in range(size_y - 1)
+        ]
+        return lax.ppermute(block, ("gx", "gy"), route)
+
     sides = jnp.stack([at_y > 0, at_y < size_y - 1, at_x > 0, at_x < size_x - 1])
     sides = sides.astype(jnp.int32)
     matrices = [jnp.asarray(m) for m in pyramid_matrices(rows, cols, depth)]
 
     parts = ((0, 1), (1, chans - 1))
-    placed = [place(tiles, offsets.reshape(2), begin, n) for begin, n in parts]
-    lows = [shift(low, "gy", 1) for _, _, low in placed]
-
-    psf, _ = lax.optimization_barrier((psf, placed[0][1]))
+    sent = []
+    for begin, n in parts:
+        own, right, low, corner = place(tiles, offsets.reshape(2), begin, n)
+        sent.append(
+            [own, shift(low, "gy", 1), shift(right, "gx", 1), shift_diagonal(corner)]
+        )
+
+    psf, _ = lax.optimization_barrier((psf, sent[0][0]))
     kern = psf / jnp.sum(psf, axis=-1, keepdims=True)
     both = jnp.stack([kern, kern[:, :, ::-1]], axis=1)
     across, within = bands(both.reshape(chans * 2, 3 * TAPS))
     across = across.reshape((chans, 2) + across.shape[1:])
     within = within.reshape((chans, 2) + within.shape[1:])
-    lows[0], across, within = lax.optimization_barrier((lows[0], across, within))
-
-    joined = []
-    for (begin, n), (own, right, _), low in zip(parts, placed, lows):
-        strips = [low[:, rows * depth :, k : k + LANE] for k in range(0, cols, LANE)]
-        side = shift(jnp.concatenate([right] + strips, axis=1), "gx", 1)
-        joined += [join(own, low, side, k) for k in range(n)]
-
-    fars = shift(jnp.concatenate([tail for _, _, tail in joined], axis=0), "gy", 2)
-    arrived = []
-    for at, (_, short, _) in enumerate(joined):
-        above = shift(short, "gy", 1)
-        below = shift(short, "gy", -1)
-        arrived.append((above, below, fars[at : at + 1]))
-
-    outs = ()
-    for at in range(chans):
-        exact, short, _ = joined[at]
-        above, below, far = arrived[at]
-        if at:
-            above, below, _ = lax.optimization_barrier((above, below, outs[2]))
-        column = (far, above, short, below)
-        last = jnp.concatenate([a[:, :, -LANE:] for a in column], axis=1)
-        first = jnp.concatenate([a[:, :, :LANE] for a in column], axis=1)
+    sent[0][1], across, within = lax.optimization_barrier((sent[0][1], across, within))
+
+    groups = []
+    for (begin, n), pieces in zip(parts, sent):
+        exact, first, last = join(*pieces)
         left = shift(last, "gx", 1)
         right = shift(first, "gx", -1)
+        for at in range(n):
+            message, tail = pack(exact, left, right, at)
+            above = shift(message, "gy", 1)
+            below = shift(message, "gy", -1)
+            groups.append((exact, above, below, tail, left, right, at))
+    far = shift(jnp.concatenate([g[3] for g in groups], axis=0), "gy", 2)
+
+    outs = ()
+    for at, (exact, above, below, _, left, right, k) in enumerate(groups):
         group = (exact, above, below, far, left, right)
-        outs = deconvolve(at, chans, sides, group, across, within, matrices, outs)
+        places = (k, 0, 0, at, k, k)
+        outs = deconvolve(at, chans, sides, group, places, across, within, matrices, outs)
     return tuple(outs)
 
 

time: 145 us -> 166 us (1.14)
  the two profiles are of different devices: /device:TPU:6 before, /device:TPU:11 now
where the time goes in v3:
time: 166 us; the launch traced here: 165 us
  Pallas kernels  51.4 us (31%)
  starting transfers between devices  45.9 us (28%)
  waiting for transfers between devices  45.5 us (27%)
  local copies, waits for them, and re-layouts  18.2 us (11%)
  other arithmetic  2.87 us (2%)
    ppermute x15, starting transfers between devices, shift(): return lax.ppermute(block, axis, route)  41.1 us
    pallas_call x3, Pallas kernels, deconvolve(): pl.pallas_call(deconvolve_kernel, grid=(1,), in_specs=[pl.BlockSpec(memor...  36.3 us
    ppermute x15, waiting for transfers between devices, shift(): return lax.ppermute(block, axis, route)  27.5 us
    ppermute x2, waiting for transfers between devices, shift_diagonal(): return lax.ppermute(block, ('gx', 'gy'), route)  18.1 us
    unnamed x54, local copies, waits for them, and re-layouts  17.4 us
    pallas_call x2, Pallas kernels, place(): pl.pallas_call(place_kernel, grid_spec=pltpu.PrefetchScalarGridSpec(num_s...  8.12 us
    ppermute x2, starting transfers between devices, shift_diagonal(): return lax.ppermute(block, ('gx', 'gy'), route)  4.85 us
  transfers between devices with their start and end apart: 17, of which 5 were waited for; matrix products, arithmetic and copies ran while one was open for 2% of the time, Pallas kernels for 22%

profile of v3, /device:TPU:11, one launch (start us, length us, event | category | flops | bytes accessed | tf_op | source)
XLA Modules:
  0.0 164.9 jit_solution(4959422315030014628)
XLA Ops:
  0.6 1.8 %copy-done.22 = bf16[3,8,96,544]{3,2,1,0:T(8,128)(2,1)S(1)} copy-done((bf16[3,8,96,544]{3,2,1,0:T(8,128)(2,1)S(1)}, bf16[3,8,96,544]{3,2,1,0:T(8,128)(2,1)}, u32[]{:S(2)}) %copy-start.22) | copy-done | bytes 2506776
  3.1 3.1 %place.3 = (bf16[1,512,512]{2,1,0:T(8,128)(2,1)S(1)}, bf16[1,512,128]{2,1,0:T(8,128)(2,1)}, bf16[1,512,512]{2,1,0:T(8,128)(2,1)}, bf16[1,256,128]{2,1,0:T(8,128)(2,1)S(1)}) custom-call(s32[2]{0:T(128)S(1)} %bitcast.16, bf16[3,8,96,544]{3,2,1,0:T(8,128)(2,1)S(1)} %copy-done.22), custom_call_target="tpu_custom_call" | custom-call | flops 2000000000 | bytes 2500000 | tf_op jit(solution)/shard_map/place/pallas_call | solution.py:84
  6.3 3.2 %collective-permute-start.7 = (bf16[1,512,512]{2,1,0:T(8,128)(2,1)}, bf16[1,512,512]{2,1,0:T(8,128)(2,1)S(1)}, u32[]{:S(2)}, u32[]{:S(2)}) collective-permute-start(bf16[1,512,512]{2,1,0:T(8,128)(2,1)} %get-tuple-element.44), channel_id=1, source_target_pairs={{0,1},{1,2},{2,3},{4,5},{5,6},{6,7},{8,9},{9,10},{10,11},{12,13},{... | collective-permute-start | bytes 1572872 | tf_op jit(solution)/shard_map/ppermute | solution.py:507
  9.5 4.0 %collective-permute-start.8 = (bf16[1,512,128]{2,1,0:T(8,128)(2,1)}, bf16[1,512,128]{2,1,0:T(8,128)(2,1)S(1)}, u32[]{:S(2)}, u32[]{:S(2)}) collective-permute-start(bf16[1,512,128]{2,1,0:T(8,128)(2,1)} %get-tuple-element.49), channel_id=1, source_target_pairs={{0,4},{4,8},{8,12},{12,16},{16,20},{20,24},{24,28},{1,5},{5,9},{9,... | collective-permute-start | bytes 393224 | tf_op jit(solution)/shard_map/ppermute | solution.py:507
  13.5 2.9 %collective-permute-start.9 = (bf16[1,256,128]{2,1,0:T(8,128)(2,1)S(1)}, bf16[1,256,128]{2,1,0:T(8,128)(2,1)S(1)}, u32[]{:S(2)}, u32[]{:S(2)}) collective-permute-start(bf16[1,256,128]{2,1,0:T(8,128)(2,1)S(1)} %get-tuple-element.50), channel_id=1, source_target_pairs={{0,5},{1,6},{2,7},{4,9},{5,10},{6,11},{8,13},{9,14},{10,15},{12,17... | collective-permute-start | bytes 196616 | tf_op jit(solution)/shard_map/ppermute | solution.py:515
  16.4 5.0 %place.2 = (bf16[2,512,512]{2,1,0:T(8,128)(2,1)S(1)}, bf16[2,512,128]{2,1,0:T(8,128)(2,1)S(1)}, bf16[2,512,512]{2,1,0:T(8,128)(2,1)}, bf16[2,256,128]{2,1,0:T(8,128)(2,1)S(1)}) custom-call(s32[2]{0:T(128)S(1)} %bitcast.17, bf16[3,8,96,544]{3,2,1,0:T(8,128)(2,1)S(1)} %copy-done.22), custom_call_target="tpu_custom_call" | custom-call | flops 4000000000 | bytes 5000000 | tf_op jit(solution)/shard_map/place/pallas_call | solution.py:84
  22.1 2.2 %collective-permute-start = (bf16[2,512,512]{2,1,0:T(8,128)(2,1)}, bf16[2,512,512]{2,1,0:T(8,128)(2,1)S(1)}, u32[]{:S(2)}, u32[]{:S(2)}) collective-permute-start(bf16[2,512,512]{2,1,0:T(8,128)(2,1)} %get-tuple-element.36), channel_id=1, source_target_pairs={{0,1},{1,2},{2,3},{4,5},{5,6},{6,7},{8,9},{9,10},{10,11},{12,13},{... | collective-permute-start | bytes 3145736 | tf_op jit(solution)/shard_map/ppermute | solution.py:507
  27.3 2.3 %bands.1 = (bf16[6,512,256]{2,1,0:T(8,128)(2,1)S(1)}, bf16[6,272,512]{2,1,0:T(8,128)(2,1)S(1)}) custom-call(f32[6,93]{1,0:T(8,128)S(1)} %reshape.21.kern_ref), custom_call_target="tpu_custom_call" | custom-call | flops 6000000 | bytes 24000000 | tf_op jit(solution)/shard_map/bands/pallas_call | solution.py:219
  30.4 3.4 %collective-permute-start.10 = (bf16[1,512,128]{2,1,0:T(8,128)(2,1)S(1)}, bf16[1,512,128]{2,1,0:T(8,128)(2,1)S(1)}, u32[]{:S(2)}, u32[]{:S(2)}) collective-permute-start(bf16[1,512,128]{2,1,0:T(8,128)(2,1)S(1)} %get-tuple-element.52), channel_id=1, source_target_pairs={{0,4},{4,8},{8,12},{12,16},{16,20},{20,24},{24,28},{1,5},{5,9},{9,... | collective-permute-start | bytes 393224 | tf_op jit(solution)/shard_map/ppermute | solution.py:507
  33.9 1.9 %collective-permute-start.11 = (bf16[1,512,128]{2,1,0:T(8,128)(2,1)S(1)}, bf16[1,512,128]{2,1,0:T(8,128)(2,1)S(1)}, u32[]{:S(2)}, u32[]{:S(2)}) collective-permute-start(bf16[1,512,128]{2,1,0:T(8,128)(2,1)S(1)} %get-tuple-element.53), channel_id=1, source_target_pairs={{4,0},{8,4},{12,8},{16,12},{20,16},{24,20},{28,24},{5,1},{9,5},{13... | collective-permute-start | bytes 393224 | tf_op jit(solution)/shard_map/ppermute | solution.py:507
  35.8 5.2 %collective-permute-done.11.right_ref = bf16[1,512,128]{2,1,0:T(8,128)(2,1)S(1)} collective-permute-done((bf16[1,512,128]{2,1,0:T(8,128)(2,1)S(1)}, bf16[1,512,128]{2,1,0:T(8,128)(2,1)S(1)}, u32[]{:S(2)}, u32[]{:S(2)}) %collective-permute-start.11) | collective-permute-done | bytes 131104 | tf_op jit(solution)/shard_map/ppermute | solution.py:507
  42.5 1.9 %collective-permute-start.15 = (bf16[1,528,640]{2,1,0:T(8,128)(2,1)S(1)}, bf16[1,528,640]{2,1,0:T(8,128)(2,1)S(1)}, u32[]{:S(2)}, u32[]{:S(2)}) collective-permute-start(bf16[1,528,640]{2,1,0:T(8,128)(2,1)S(1)} %get-tuple-element.60), channel_id=1, source_target_pairs={{0,1},{1,2},{2,3},{4,5},{5,6},{6,7},{8,9},{9,10},{10,11},{12,13},{... | collective-permute-start | bytes 2027528 | tf_op jit(solution)/shard_map/ppermute | solution.py:507
  44.4 1.9 %collective-permute-start.1 = (bf16[2,512,128]{2,1,0:T(8,128)(2,1)}, bf16[2,512,128]{2,1,0:T(8,128)(2,1)S(1)}, u32[]{:S(2)}, u32[]{:S(2)}) collective-permute-start(bf16[2,512,128]{2,1,0:T(8,128)(2,1)} %copy-done.23), channel_id=1, source_target_pairs={{0,4},{4,8},{8,12},{12,16},{16,20},{20,24},{24,28},{1,5},{5,9},{9,... | collective-permute-start | bytes 786440 | tf_op jit(solution)/shard_map/ppermute | solution.py:507
  46.4 1.9 %collective-permute-start.2 = (bf16[2,256,128]{2,1,0:T(8,128)(2,1)S(1)}, bf16[2,256,128]{2,1,0:T(8,128)(2,1)S(1)}, u32[]{:S(2)}, u32[]{:S(2)}) collective-permute-start(bf16[2,256,128]{2,1,0:T(8,128)(2,1)S(1)} %get-tuple-element.38), channel_id=1, source_target_pairs={{0,5},{1,6},{2,7},{4,9},{5,10},{6,11},{8,13},{9,14},{10,15},{12,17... | collective-permute-start | bytes 393224 | tf_op jit(solution)/shard_map/ppermute | solution.py:515
  48.3 18.1 %collective-permute-done.2.corner_ref = bf16[2,256,128]{2,1,0:T(8,128)(2,1)S(1)} collective-permute-done((bf16[2,256,128]{2,1,0:T(8,128)(2,1)S(1)}, bf16[2,256,128]{2,1,0:T(8,128)(2,1)S(1)}, u32[]{:S(2)}, u32[]{:S(2)}) %collective-permute-start.2) | collective-permute-done | bytes 131104 | tf_op jit(solution)/shard_map/ppermute | solution.py:515
  67.3 1.2 copy-done.11
  68.6 1.6 join.2
  70.2 3.6 %collective-permute-start.3 = (bf16[2,512,128]{2,1,0:T(8,128)(2,1)S(1)}, bf16[2,512,128]{2,1,0:T(8,128)(2,1)S(1)}, u32[]{:S(2)}, u32[]{:S(2)}) collective-permute-start(bf16[2,512,128]{2,1,0:T(8,128)(2,1)S(1)} %get-tuple-element.40), channel_id=1, source_target_pairs={{0,4},{4,8},{8,12},{12,16},{16,20},{20,24},{24,28},{1,5},{5,9},{9,... | collective-permute-start | bytes 786440 | tf_op jit(solution)/shard_map/ppermute | solution.py:507
  73.8 1.9 %collective-permute-start.4 = (bf16[2,512,128]{2,1,0:T(8,128)(2,1)S(1)}, bf16[2,512,128]{2,1,0:T(8,128)(2,1)S(1)}, u32[]{:S(2)}, u32[]{:S(2)}) collective-permute-start(bf16[2,512,128]{2,1,0:T(8,128)(2,1)S(1)} %get-tuple-element.41), channel_id=1, source_target_pairs={{4,0},{8,4},{12,8},{16,12},{20,16},{24,20},{28,24},{5,1},{9,5},{13... | collective-permute-start | bytes 786440 | tf_op jit(solution)/shard_map/ppermute | solution.py:507
  75.7 1.9 %collective-permute-start.16 = (bf16[1,528,640]{2,1,0:T(8,128)(2,1)S(1)}, bf16[1,528,640]{2,1,0:T(8,128)(2,1)S(1)}, u32[]{:S(2)}, u32[]{:S(2)}) collective-permute-start(bf16[1,528,640]{2,1,0:T(8,128)(2,1)S(1)} %get-tuple-element.60), channel_id=1, source_target_pairs={{1,0},{2,1},{3,2},{5,4},{6,5},{7,6},{9,8},{10,9},{11,10},{13,12},{... | collective-permute-start | bytes 2027528 | tf_op jit(solution)/shard_map/ppermute | solution.py:507
  78.0 4.4 %collective-permute-done.4.right_ref = bf16[2,512,128]{2,1,0:T(8,128)(2,1)S(1)} collective-permute-done((bf16[2,512,128]{2,1,0:T(8,128)(2,1)S(1)}, bf16[2,512,128]{2,1,0:T(8,128)(2,1)S(1)}, u32[]{:S(2)}, u32[]{:S(2)}) %collective-permute-start.4) | collective-permute-done | bytes 262176 | tf_op jit(solution)/shard_map/ppermute | solution.py:507
  83.4 2.8 %collective-permute-start.13 = (bf16[1,528,640]{2,1,0:T(8,128)(2,1)}, bf16[1,528,640]{2,1,0:T(8,128)(2,1)}, u32[]{:S(2)}, u32[]{:S(2)}) collective-permute-start(bf16[1,528,640]{2,1,0:T(8,128)(2,1)} %get-tuple-element.59), channel_id=1, source_target_pairs={{0,1},{1,2},{2,3},{4,5},{5,6},{6,7},{8,9},{9,10},{10,11},{12,13},{... | collective-permute-start | bytes 2027528 | tf_op jit(solution)/shard_map/ppermute | solution.py:507
  86.2 3.3 %collective-permute-start.14 = (bf16[1,528,640]{2,1,0:T(8,128)(2,1)}, bf16[1,528,640]{2,1,0:T(8,128)(2,1)}, u32[]{:S(2)}, u32[]{:S(2)}) collective-permute-start(bf16[1,528,640]{2,1,0:T(8,128)(2,1)} %get-tuple-element.59), channel_id=1, source_target_pairs={{1,0},{2,1},{3,2},{5,4},{6,5},{7,6},{9,8},{10,9},{11,10},{13,12},{... | collective-permute-start | bytes 2027528 | tf_op jit(solution)/shard_map/ppermute | solution.py:507
  90.6 2.0 %collective-permute-start.5 = (bf16[1,528,640]{2,1,0:T(8,128)(2,1)}, bf16[1,528,640]{2,1,0:T(8,128)(2,1)}, u32[]{:S(2)}, u32[]{:S(2)}) collective-permute-start(bf16[1,528,640]{2,1,0:T(8,128)(2,1)} %get-tuple-element.42), channel_id=1, source_target_pairs={{0,1},{1,2},{2,3},{4,5},{5,6},{6,7},{8,9},{9,10},{10,11},{12,13},{... | collective-permute-start | bytes 2027528 | tf_op jit(solution)/shard_map/ppermute | solution.py:507
  93.4 4.1 %collective-permute-start.6 = (bf16[1,528,640]{2,1,0:T(8,128)(2,1)}, bf16[1,528,640]{2,1,0:T(8,128)(2,1)}, u32[]{:S(2)}, u32[]{:S(2)}) collective-permute-start(bf16[1,528,640]{2,1,0:T(8,128)(2,1)} %get-tuple-element.42), channel_id=1, source_target_pairs={{1,0},{2,1},{3,2},{5,4},{6,5},{7,6},{9,8},{10,9},{11,10},{13,12},{... | collective-permute-start | bytes 2027528 | tf_op jit(solution)/shard_map/ppermute | solution.py:507
  99.1 3.0 %collective-permute-start.12 = (bf16[3,32,640]{2,1,0:T(8,128)(2,1)}, bf16[3,32,640]{2,1,0:T(8,128)(2,1)S(1)}, u32[]{:S(2)}, u32[]{:S(2)}) collective-permute-start(bf16[3,32,640]{2,1,0:T(8,128)(2,1)} %pad_maximum_fusion), channel_id=1, source_target_pairs={{0,2},{1,3},{4,6},{5,7},{8,10},{9,11},{12,14},{13,15},{16,18},{17,... | collective-permute-start | bytes 368648 | tf_op jit(solution)/shard_map/ppermute | solution.py:507
  102.1 17.5 %collective-permute-done.12.far_ref = bf16[3,32,640]{2,1,0:T(8,128)(2,1)S(1)} collective-permute-done((bf16[3,32,640]{2,1,0:T(8,128)(2,1)}, bf16[3,32,640]{2,1,0:T(8,128)(2,1)S(1)}, u32[]{:S(2)}, u32[]{:S(2)}) %collective-permute-start.12) | collective-permute-done | bytes 122912 | tf_op jit(solution)/shard_map/ppermute | solution.py:507
  119.6 1.4 copy-done.1
  121.1 1.4 copy-done.4
  128.6 11.5 %deconvolve.3 = (f32[3,8,64,512]{3,2,1,0:T(8,128)}, f32[3,4,32,256]{3,2,1,0:T(8,128)}, f32[3,2,16,128]{3,2,1,0:T(8,128)}) custom-call(s32[4]{0:T(128)S(1)} %add_convert_fusion.sides_ref, f32[1,512,512]{2,1,0:T(8,128)S(1)} %copy-done.8, bf16[1,528,640]{2,1,0:T(8,128)(2,1)S(1)} %copy-done.14, bf16[1,528,640]{2,1,0:T(8,128)(2,1)S(1)} %copy-done.16, ...), custom_call_target="tpu_custom_call" | custom-call | flops 1000000 | bytes 100000 | tf_op jit(solution)/shard_map/deconvolve/pallas_call | solution.py:470
  140.1 12.5 %deconvolve.4 = (f32[3,8,64,512]{3,2,1,0:T(8,128)}, f32[3,4,32,256]{3,2,1,0:T(8,128)}, f32[3,2,16,128]{3,2,1,0:T(8,128)}) custom-call(s32[4]{0:T(128)S(1)} %add_convert_fusion.sides_ref, f32[2,512,512]{2,1,0:T(8,128)S(1)} %get-tuple-element.39.exact_ref, ...), custom_call_target="tpu_custom_call", output_to_operand_aliasing={{0}: (13, {}), {1}: (14, {}), {2}: (15, {})} | custom-call | flops 1000000 | bytes 100000 | tf_op jit(solution)/shard_map/deconvolve/pallas_call | solution.py:470
  152.7 12.3 %deconvolve.5 = (f32[3,8,64,512]{3,2,1,0:T(8,128)}, f32[3,4,32,256]{3,2,1,0:T(8,128)}, f32[3,2,16,128]{3,2,1,0:T(8,128)}) custom-call(s32[4]{0:T(128)S(1)} %add_convert_fusion.sides_ref, f32[2,512,512]{2,1,0:T(8,128)S(1)} %get-tuple-element.39.exact_ref, ...), custom_call_target="tpu_custom_call", output_to_operand_aliasing={{0}: (13, {}), {1}: (14, {}), {2}: (15, {})} | custom-call | flops 1000000 | bytes 100000 | tf_op jit(solution)/shard_map/deconvolve/pallas_call | solution.py:470
  (76 shorter events, 18.7 us)
Async XLA Ops:
  0.6 1.8 %copy-start.22 = (bf16[3,8,96,544]{3,2,1,0:T(8,128)(2,1)S(1)}, bf16[3,8,96,544]{3,2,1,0:T(8,128)(2,1)}, u32[]{:S(2)}) copy-start(bf16[3,8,96,544]{3,2,1,0:T(8,128)(2,1)} %tile_ref.3) | copy-start | bytes 7520260
  3.1 13.3 %copy-start.25 = (s32[1,1,2]{2,1,0:T(1,128)S(1)}, s32[1,1,2]{2,1,0:T(1,128)}, u32[]{:S(2)}) copy-start(s32[1,1,2]{2,1,0:T(1,128)} %param.8) | copy-start | bytes 28
  6.3 23.3 %collective-permute-start.7 = (bf16[1,512,512]{2,1,0:T(8,128)(2,1)}, bf16[1,512,512]{2,1,0:T(8,128)(2,1)S(1)}, u32[]{:S(2)}, u32[]{:S(2)}) collective-permute-start(bf16[1,512,512]{2,1,0:T(8,128)(2,1)} %get-tuple-element.44), channel_id=1, source_target_pairs={{0,1},{1,2},{2,3},{4,5},{5,6},{6,7},{8,9},{9,10},{10,11},{12,13},{... | collective-permute-start | bytes 1572872 | tf_op jit(solution)/shard_map/ppermute | solution.py:507
  9.5 20.1 %collective-permute-start.8 = (bf16[1,512,128]{2,1,0:T(8,128)(2,1)}, bf16[1,512,128]{2,1,0:T(8,128)(2,1)S(1)}, u32[]{:S(2)}, u32[]{:S(2)}) collective-permute-start(bf16[1,512,128]{2,1,0:T(8,128)(2,1)} %get-tuple-element.49), channel_id=1, source_target_pairs={{0,4},{4,8},{8,12},{12,16},{16,20},{20,24},{24,28},{1,5},{5,9},{9,... | collective-permute-start | bytes 393224 | tf_op jit(solution)/shard_map/ppermute | solution.py:507
  13.4 10.8 %copy-start.26 = (f32[3,3,31]{2,1,0:T(4,128)S(1)}, f32[3,3,31]{2,1,0:T(4,128)}, u32[]{:S(2)}) copy-start(f32[3,3,31]{2,1,0:T(4,128)} %param.9) | copy-start | bytes 3352
  13.5 16.2 %collective-permute-start.9 = (bf16[1,256,128]{2,1,0:T(8,128)(2,1)S(1)}, bf16[1,256,128]{2,1,0:T(8,128)(2,1)S(1)}, u32[]{:S(2)}, u32[]{:S(2)}) collective-permute-start(bf16[1,256,128]{2,1,0:T(8,128)(2,1)S(1)} %get-tuple-element.50), channel_id=1, source_target_pairs={{0,5},{1,6},{2,7},{4,9},{5,10},{6,11},{8,13},{9,14},{10,15},{12,17... | collective-permute-start | bytes 196616 | tf_op jit(solution)/shard_map/ppermute | solution.py:515
  22.1 44.3 %collective-permute-start = (bf16[2,512,512]{2,1,0:T(8,128)(2,1)}, bf16[2,512,512]{2,1,0:T(8,128)(2,1)S(1)}, u32[]{:S(2)}, u32[]{:S(2)}) collective-permute-start(bf16[2,512,512]{2,1,0:T(8,128)(2,1)} %get-tuple-element.36), channel_id=1, source_target_pairs={{0,1},{1,2},{2,3},{4,5},{5,6},{6,7},{8,9},{9,10},{10,11},{12,13},{... | collective-permute-start | bytes 3145736 | tf_op jit(solution)/shard_map/ppermute | solution.py:507
  29.6 53.8 %copy-start = (bf16[6,272,512]{2,1,0:T(8,128)(2,1)}, bf16[6,272,512]{2,1,0:T(8,128)(2,1)S(1)}, u32[]{:S(2)}) copy-start(bf16[6,272,512]{2,1,0:T(8,128)(2,1)S(1)} %get-tuple-element.47) | copy-start | bytes 5013508
  29.6 53.8 %copy-start.3 = (bf16[6,512,256]{2,1,0:T(8,128)(2,1)}, bf16[6,512,256]{2,1,0:T(8,128)(2,1)S(1)}, u32[]{:S(2)}) copy-start(bf16[6,512,256]{2,1,0:T(8,128)(2,1)S(1)} %get-tuple-element.46) | copy-start | bytes 4718596
  30.4 51.9 %copy-start.7 = (f32[1,512,512]{2,1,0:T(8,128)}, f32[1,512,512]{2,1,0:T(8,128)S(1)}, u32[]{:S(2)}) copy-start(f32[1,512,512]{2,1,0:T(8,128)S(1)} %get-tuple-element.51.exact_ref) | copy-start | bytes 3145732
  30.4 5.3 %collective-permute-start.10 = (bf16[1,512,128]{2,1,0:T(8,128)(2,1)S(1)}, bf16[1,512,128]{2,1,0:T(8,128)(2,1)S(1)}, u32[]{:S(2)}, u32[]{:S(2)}) collective-permute-start(bf16[1,512,128]{2,1,0:T(8,128)(2,1)S(1)} %get-tuple-element.52), channel_id=1, source_target_pairs={{0,4},{4,8},{8,12},{12,16},{16,20},{20,24},{24,28},{1,5},{5,9},{9,... | collective-permute-start | bytes 393224 | tf_op jit(solution)/shard_map/ppermute | solution.py:507
  33.9 7.2 %collective-permute-start.11 = (bf16[1,512,128]{2,1,0:T(8,128)(2,1)S(1)}, bf16[1,512,128]{2,1,0:T(8,128)(2,1)S(1)}, u32[]{:S(2)}, u32[]{:S(2)}) collective-permute-start(bf16[1,512,128]{2,1,0:T(8,128)(2,1)S(1)} %get-tuple-element.53), channel_id=1, source_target_pairs={{4,0},{8,4},{12,8},{16,12},{20,16},{24,20},{28,24},{5,1},{9,5},{13... | collective-permute-start | bytes 393224 | tf_op jit(solution)/shard_map/ppermute | solution.py:507
  42.5 50.0 %collective-permute-start.15 = (bf16[1,528,640]{2,1,0:T(8,128)(2,1)S(1)}, bf16[1,528,640]{2,1,0:T(8,128)(2,1)S(1)}, u32[]{:S(2)}, u32[]{:S(2)}) collective-permute-start(bf16[1,528,640]{2,1,0:T(8,128)(2,1)S(1)} %get-tuple-element.60), channel_id=1, source_target_pairs={{0,1},{1,2},{2,3},{4,5},{5,6},{6,7},{8,9},{9,10},{10,11},{12,13},{... | collective-permute-start | bytes 2027528 | tf_op jit(solution)/shard_map/ppermute | solution.py:507
  44.4 21.9 %collective-permute-start.1 = (bf16[2,512,128]{2,1,0:T(8,128)(2,1)}, bf16[2,512,128]{2,1,0:T(8,128)(2,1)S(1)}, u32[]{:S(2)}, u32[]{:S(2)}) collective-permute-start(bf16[2,512,128]{2,1,0:T(8,128)(2,1)} %copy-done.23), channel_id=1, source_target_pairs={{0,4},{4,8},{8,12},{12,16},{16,20},{20,24},{24,28},{1,5},{5,9},{9,... | collective-permute-start | bytes 786440 | tf_op jit(solution)/shard_map/ppermute | solution.py:507
  46.4 20.0 %collective-permute-start.2 = (bf16[2,256,128]{2,1,0:T(8,128)(2,1)S(1)}, bf16[2,256,128]{2,1,0:T(8,128)(2,1)S(1)}, u32[]{:S(2)}, u32[]{:S(2)}) collective-permute-start(bf16[2,256,128]{2,1,0:T(8,128)(2,1)S(1)} %get-tuple-element.38), channel_id=1, source_target_pairs={{0,5},{1,6},{2,7},{4,9},{5,10},{6,11},{8,13},{9,14},{10,15},{12,17... | collective-permute-start | bytes 393224 | tf_op jit(solution)/shard_map/ppermute | solution.py:515
  67.3 1.2 copy-start.11
  70.2 49.5 %copy-start.6 = (bf16[768,384]{1,0:T(8,128)(2,1)S(1)}, bf16[768,384]{1,0:T(8,128)(2,1)}, u32[]{:S(2)}) copy-start(bf16[768,384]{1,0:T(8,128)(2,1)} %constant.25.clone.one_x_ref) | copy-start | bytes 1769476
  70.2 49.5 %copy-start.9 = (bf16[144,592]{1,0:T(8,128)(2,1)S(1)}, bf16[144,592]{1,0:T(8,128)(2,1)}, u32[]{:S(2)}) copy-start(bf16[144,592]{1,0:T(8,128)(2,1)} %constant.26.clone.one_zy_ref) | copy-start | bytes 511492
  70.2 49.5 %copy-start.21 = (bf16[32,144]{1,0:T(8,128)(2,1)S(1)}, bf16[32,144]{1,0:T(8,128)(2,1)}, u32[]{:S(2)}) copy-start(bf16[32,144]{1,0:T(8,128)(2,1)} %constant.28.clone.two_zy_ref) | copy-start | bytes 27652
  70.2 7.8 %collective-permute-start.3 = (bf16[2,512,128]{2,1,0:T(8,128)(2,1)S(1)}, bf16[2,512,128]{2,1,0:T(8,128)(2,1)S(1)}, u32[]{:S(2)}, u32[]{:S(2)}) collective-permute-start(bf16[2,512,128]{2,1,0:T(8,128)(2,1)S(1)} %get-tuple-element.40), channel_id=1, source_target_pairs={{0,4},{4,8},{8,12},{12,16},{16,20},{20,24},{24,28},{1,5},{5,9},{9,... | collective-permute-start | bytes 786440 | tf_op jit(solution)/shard_map/ppermute | solution.py:507
  73.8 8.6 %collective-permute-start.4 = (bf16[2,512,128]{2,1,0:T(8,128)(2,1)S(1)}, bf16[2,512,128]{2,1,0:T(8,128)(2,1)S(1)}, u32[]{:S(2)}, u32[]{:S(2)}) collective-permute-start(bf16[2,512,128]{2,1,0:T(8,128)(2,1)S(1)} %get-tuple-element.41), channel_id=1, source_target_pairs={{4,0},{8,4},{12,8},{16,12},{20,16},{24,20},{28,24},{5,1},{9,5},{13... | collective-permute-start | bytes 786440 | tf_op jit(solution)/shard_map/ppermute | solution.py:507
  75.7 22.5 %collective-permute-start.16 = (bf16[1,528,640]{2,1,0:T(8,128)(2,1)S(1)}, bf16[1,528,640]{2,1,0:T(8,128)(2,1)S(1)}, u32[]{:S(2)}, u32[]{:S(2)}) collective-permute-start(bf16[1,528,640]{2,1,0:T(8,128)(2,1)S(1)} %get-tuple-element.60), channel_id=1, source_target_pairs={{1,0},{2,1},{3,2},{5,4},{6,5},{7,6},{9,8},{10,9},{11,10},{13,12},{... | collective-permute-start | bytes 2027528 | tf_op jit(solution)/shard_map/ppermute | solution.py:507
  83.4 56.7 %collective-permute-start.13 = (bf16[1,528,640]{2,1,0:T(8,128)(2,1)}, bf16[1,528,640]{2,1,0:T(8,128)(2,1)}, u32[]{:S(2)}, u32[]{:S(2)}) collective-permute-start(bf16[1,528,640]{2,1,0:T(8,128)(2,1)} %get-tuple-element.59), channel_id=1, source_target_pairs={{0,1},{1,2},{2,3},{4,5},{5,6},{6,7},{8,9},{9,10},{10,11},{12,13},{... | collective-permute-start | bytes 2027528 | tf_op jit(solution)/shard_map/ppermute | solution.py:507
  86.2 53.9 %collective-permute-start.14 = (bf16[1,528,640]{2,1,0:T(8,128)(2,1)}, bf16[1,528,640]{2,1,0:T(8,128)(2,1)}, u32[]{:S(2)}, u32[]{:S(2)}) collective-permute-start(bf16[1,528,640]{2,1,0:T(8,128)(2,1)} %get-tuple-element.59), channel_id=1, source_target_pairs={{1,0},{2,1},{3,2},{5,4},{6,5},{7,6},{9,8},{10,9},{11,10},{13,12},{... | collective-permute-start | bytes 2027528 | tf_op jit(solution)/shard_map/ppermute | solution.py:507
  90.6 62.1 %collective-permute-start.5 = (bf16[1,528,640]{2,1,0:T(8,128)(2,1)}, bf16[1,528,640]{2,1,0:T(8,128)(2,1)}, u32[]{:S(2)}, u32[]{:S(2)}) collective-permute-start(bf16[1,528,640]{2,1,0:T(8,128)(2,1)} %get-tuple-element.42), channel_id=1, source_target_pairs={{0,1},{1,2},{2,3},{4,5},{5,6},{6,7},{8,9},{9,10},{10,11},{12,13},{... | collective-permute-start | bytes 2027528 | tf_op jit(solution)/shard_map/ppermute | solution.py:507
  93.4 59.2 %collective-permute-start.6 = (bf16[1,528,640]{2,1,0:T(8,128)(2,1)}, bf16[1,528,640]{2,1,0:T(8,128)(2,1)}, u32[]{:S(2)}, u32[]{:S(2)}) collective-permute-start(bf16[1,528,640]{2,1,0:T(8,128)(2,1)} %get-tuple-element.42), channel_id=1, source_target_pairs={{1,0},{2,1},{3,2},{5,4},{6,5},{7,6},{9,8},{10,9},{11,10},{13,12},{... | collective-permute-start | bytes 2027528 | tf_op jit(solution)/shard_map/ppermute | solution.py:507
  99.1 20.6 %collective-permute-start.12 = (bf16[3,32,640]{2,1,0:T(8,128)(2,1)}, bf16[3,32,640]{2,1,0:T(8,128)(2,1)S(1)}, u32[]{:S(2)}, u32[]{:S(2)}) collective-permute-start(bf16[3,32,640]{2,1,0:T(8,128)(2,1)} %pad_maximum_fusion), channel_id=1, source_target_pairs={{0,2},{1,3},{4,6},{5,7},{8,10},{9,11},{12,14},{13,15},{16,18},{17,... | collective-permute-start | bytes 368648 | tf_op jit(solution)/shard_map/ppermute | solution.py:507
  119.6 1.4 copy-start.1
  121.1 1.4 copy-start.4
  122.5 1.2 copy-start.8
  128.6 11.5 %copy-start.2 = (bf16[6,272,512]{2,1,0:T(8,128)(2,1)S(1)}, bf16[6,272,512]{2,1,0:T(8,128)(2,1)}, u32[]{:S(2)}) copy-start(bf16[6,272,512]{2,1,0:T(8,128)(2,1)} %copy-done) | copy-start | bytes 5013508
  128.6 11.5 %copy-start.5 = (bf16[6,512,256]{2,1,0:T(8,128)(2,1)S(1)}, bf16[6,512,256]{2,1,0:T(8,128)(2,1)}, u32[]{:S(2)}) copy-start(bf16[6,512,256]{2,1,0:T(8,128)(2,1)} %copy-done.3) | copy-start | bytes 4718596
  (12 other events, 10.2 us)

commit v4 on v3

--- a/solution.py
+++ b/solution.py
@@ -34,6 +34,16 @@
     return pl.CostEstimate(flops=int(flops), bytes_accessed=int(nbytes), transcendentals=0)
 
 
+ANY = pl.BlockSpec(memory_space=pl.ANY)
+
+
+def skipping(kernel, at, count):
+    def run(*refs):
+        kernel(*refs[:at], *refs[at + count :])
+
+    return run
+
+
 def dot(a, b):
     return jnp.dot(a, b, preferred_element_type=F32)
 
@@ -43,7 +53,7 @@
     return high, (value - high.astype(F32)).astype(BF16)
 
 
-def place_kernel(off_ref, tile_ref, own_ref, right_ref, low_ref, corner_ref, canvas):
+def place_kernel(off_ref, tile_ref, own_ref, right_ref, low_ref, canvas):
     depth, tile_y, tile_x = tile_ref.shape[1:]
     parts = canvas.shape[0]
     wide = parts * LANE
@@ -65,119 +75,160 @@
     for b in range(parts - 1):
         to = slice(b * LANE, (b + 1) * LANE)
         own_ref[0, :, to] = canvas[b, :rows, :].astype(BF16)
-        low_ref[0, :, to] = canvas[b, rows:, :].astype(BF16)
+        low_ref[0, :rows, to] = canvas[b, rows:, :].astype(BF16)
     right_ref[0] = canvas[parts - 1, :rows, :].astype(BF16)
     half = rows // 2
     upper = canvas[parts - 1, rows : rows + half, :]
     lower = canvas[parts - 1, rows + half :, :]
-    corner_ref[0] = (upper + pltpu.roll(lower, LANE // 2, 1)).astype(BF16)
-
-
-def place(tiles, offsets, begin, n):
+    corner = (upper + pltpu.roll(lower, LANE // 2, 1)).astype(BF16)
+    part = half // (parts - 1)
+    for b in range(parts - 1):
+        low_ref[0, rows:, b * LANE : (b + 1) * LANE] = corner[b * part : (b + 1) * part]
+
+
+def place(tiles, offsets, begin, n, after):
     _, depth, tile_y, tile_x = tiles.shape
     rows = (tile_y - MARGIN) * depth
     cols = tile_x - MARGIN
     block = lambda r, c: pl.BlockSpec((1, r, c), lambda i, off: (i, 0, 0))
     shape = lambda r, c: jax.ShapeDtypeStruct((n, r, c), BF16)
-    sizes = ((rows, cols), (rows, LANE), (rows, cols), (rows // 2, LANE))
+    extra = rows // 2 * LANE // cols
+    sizes = ((rows, cols), (rows, LANE), (rows + extra, cols))
     tile = pl.BlockSpec((1, depth, tile_y, tile_x), lambda i, off: (begin + i, 0, 0, 0))
     return pl.pallas_call(
-        place_kernel,
+        skipping(place_kernel, 2, len(after)),
         grid_spec=pltpu.PrefetchScalarGridSpec(
             num_scalar_prefetch=1,
             grid=(n,),
-            in_specs=[tile],
+            in_specs=[tile] + [ANY] * len(after),
             out_specs=[block(*s) for s in sizes],
             scratch_shapes=[pltpu.VMEM((cols // LANE + 1, 2 * rows, LANE), F32)],
         ),
         out_shape=[shape(*s) for s in sizes],
         compiler_params=params(16),
-        cost_estimate=cost(n * 2e9, n * 2.5e6),
+        cost_estimate=cost(n * 2e9, 1),
         name="place",
-    )(offsets, tiles)
-
-
-def join_kernel(own_ref, low_ref, right_ref, corner_ref, exact_ref, first_ref, last_ref):
+    )(offsets, tiles, *after)
+
+
+def seen(x):
+    return jnp.where(x != 0, 1.0, 0.0)
+
+
+def lanes(rows):
+    return lax.broadcasted_iota(jnp.int32, (rows, LANE), 1)
+
+
+def edges_kernel(own_ref, right_ref, low_ref, to_right_ref, to_left_ref):
     rows, cols = own_ref.shape[1:]
     half = rows // 2
-
-    def seen(x):
-        return jnp.where(x != 0, 1.0, 0.0)
+    packed = low_ref[0, rows:, :].astype(F32)
+    corner = jnp.concatenate([packed[:, k : k + LANE] for k in range(0, cols, LANE)], axis=0)
+    corner = jnp.concatenate([pltpu.roll(corner, LANE // 2, 1), corner], axis=0)
+    right = right_ref[0].astype(F32)
+    to_right_ref[0, :rows] = jnp.where(lanes(rows) < LANE // 2, right, corner).astype(BF16)
+    own = own_ref[0, :, cols - LANE :].astype(F32)
+    low = low_ref[0, :rows, cols - LANE :].astype(F32)
+    to_right_ref[0, rows:] = ((own + low) / (seen(own) + seen(low))).astype(BF16)
+    to_left_ref[0, :rows] = own_ref[0, :, :LANE]
+    to_left_ref[0, rows:] = low_ref[0, :rows, :LANE]
+
+
+def edges(own, right, low, after):
+    n, rows, _ = own.shape
+    block = lambda r, c: pl.BlockSpec((1, r, c), lambda i: (i, 0, 0))
+    out = (2 * rows, LANE)
+    return pl.pallas_call(
+        skipping(edges_kernel, 3, len(after)),
+        grid=(n,),
+        in_specs=[block(*a.shape[1:]) for a in (own, right, low)] + [ANY] * len(after),
+        out_specs=[block(*out)] * 2,
+        out_shape=[jax.ShapeDtypeStruct((n,) + out, BF16)] * 2,
+        compiler_params=params(16),
+        cost_estimate=cost(4e10 if own.shape[0] == 1 else 1, 1),
+        name="edges",
+    )(own, right, low, *after)
+
+
+SIDE = 63
+
+
+def join_kernel(
+    sides_ref, own_ref, low_ref, mine_ref, left_ref, right_ref, exact_ref, strip_ref, out_ref, tail_ref
+):
+    rows, cols = own_ref.shape[1:]
+    inside = lanes(rows) < LANE // 2
+
+    def parts(ref):
+        pair = ref[0, :rows].astype(F32)
+        return jnp.where(inside, pair, 0.0), jnp.where(inside, pltpu.roll(pair, LANE // 2, 1), 0.0)
 
     own = own_ref[0].astype(F32)
     low = low_ref[0].astype(F32)
     total = own + low
     count = seen(own) + seen(low)
-    right = right_ref[0].astype(F32)
-    corner = corner_ref[0].astype(F32)
-    lane = lax.broadcasted_iota(jnp.int32, (half, LANE), 1)
-    inside = lane < LANE // 2
-    upper = jnp.where(inside, corner, 0.0)
-    lower = jnp.where(inside, pltpu.roll(corner, LANE // 2, 1), 0.0)
-    corner = jnp.concatenate([upper, lower], axis=0)
-    edge_total = total[:, :LANE] + right + corner
-    edge_count = count[:, :LANE] + seen(right) + seen(corner)
-    edge = edge_total / edge_count
+    a, b = parts(left_ref)
+    edge = (total[:, :LANE] + a + b) / (count[:, :LANE] + seen(a) + seen(b))
     rest = total[:, LANE:] / count[:, LANE:]
     exact_ref[0, :, :LANE] = edge
     exact_ref[0, :, LANE:] = rest
-    first_ref[0] = edge.astype(BF16)
-    last_ref[0] = rest[:, -LANE:].astype(BF16)
-
-
-def join(own, low, right, corner):
-    n, rows, cols = own.shape
-    block = lambda r, c: pl.BlockSpec((1, r, c), lambda i: (i, 0, 0))
-    sizes = ((rows, cols, F32), (rows, LANE, BF16), (rows, LANE, BF16))
-    return pl.pallas_call(
-        join_kernel,
-        grid=(n,),
-        in_specs=[block(*a.shape[1:]) for a in (own, low, right, corner)],
-        out_specs=[block(r, c) for r, c, _ in sizes],
-        out_shape=[jax.ShapeDtypeStruct((n, r, c), t) for r, c, t in sizes],
-        compiler_params=params(16),
-        cost_estimate=cost(5e6, 3e6),
-        name="join",
-    )(own, low, right, corner)
-
-
-SIDE = 63
-
-
-def pack_kernel(exact_ref, left_ref, right_ref, out_ref, tail_ref):
-    rows, cols = exact_ref.shape[1:]
-    lane = lax.broadcasted_iota(jnp.int32, (rows, LANE), 1)
-    out_ref[0, :rows, :cols] = exact_ref[0].astype(BF16)
-    left = left_ref[0].astype(F32)
-    right = right_ref[0].astype(F32)
-    out_ref[0, :rows, cols:] = jnp.where(lane < SIDE, right, left).astype(BF16)
+    out_ref[0, :rows, :LANE] = edge.astype(BF16)
+    out_ref[0, :rows, LANE:cols] = rest.astype(BF16)
+
+    a, b = parts(mine_ref)
+    own = right_ref[0, :rows].astype(F32)
+    low = right_ref[0, rows:].astype(F32)
+    count = seen(own) + seen(low) + seen(a) + seen(b)
+    strip = (own + low + a + b) / jnp.maximum(count, 1.0)
+    strip = jnp.where(sides_ref[3] > 0, strip, 0.0)
+    strip_ref[0] = strip.astype(BF16)
+
+    left = left_ref[0, rows:]
+    out_ref[0, :rows, cols:] = jnp.where(lanes(rows) < SIDE, strip, left.astype(F32)).astype(BF16)
     extra = out_ref.shape[1] - rows
-    pick = lax.broadcasted_iota(jnp.int32, (extra, LANE), 1) == SIDE - 1
+    pick = lanes(extra) == SIDE - 1
     pick &= lax.broadcasted_iota(jnp.int32, (extra, LANE), 0) == 0
     pick = jnp.where(pick, 1.0, 0.0).astype(BF16)
-    column = lax.dot_general(
-        pick, left_ref[0], (((1,), (1,)), ((), ())), preferred_element_type=F32
-    )
+    column = lax.dot_general(pick, left, (((1,), (1,)), ((), ())), preferred_element_type=F32)
     out_ref[0, rows:, :cols] = column.astype(BF16)
     out_ref[0, rows:, cols:] = jnp.zeros((extra, LANE), BF16)
     tail_ref[0] = out_ref[0, rows - 2 * DEPTH :, :]
 
 
-def pack(exact, left, right, at):
-    _, rows, cols = exact.shape
+def join(sides, own, low, mine, left, right, at):
+    _, rows, cols = own.shape
     block = lambda r, c, k: pl.BlockSpec((1, r, c), lambda i: (k, 0, 0))
+    pair = block(2 * rows, LANE, at)
     extra = 2 * DEPTH
-    sizes = ((rows + extra, cols + LANE), (2 * extra, cols + LANE))
+    sizes = (
+        (rows, cols, F32),
+        (rows, LANE, BF16),
+        (rows + extra, cols + LANE, BF16),
+        (2 * extra, cols + LANE, BF16),
+    )
     return pl.pallas_call(
-        pack_kernel,
+        join_kernel,
         grid=(1,),
-        in_specs=[block(*a.shape[1:], at) for a in (exact, left, right)],
-        out_specs=[block(*s, 0) for s in sizes],
-        out_shape=[jax.ShapeDtypeStruct((1,) + s, BF16) for s in sizes],
+        in_specs=[pl.BlockSpec(memory_space=pltpu.SMEM)]
+        + [block(rows, cols, at), block(rows, cols, at), pair, pair, pair],
+        out_specs=[block(r, c, 0) for r, c, _ in sizes],
+        out_shape=[jax.ShapeDtypeStruct((1, r, c), t) for r, c, t in sizes],
         compiler_params=params(16),
-        cost_estimate=cost(1e6, 1e6),
-        name="pack",
-    )(exact, left, right)
+        cost_estimate=cost(1, 1),
+        name="join",
+    )(sides, own, low, mine, left, right)
+
+
+def gate(message, after):
+    return pl.pallas_call(
+        lambda *refs: None,
+        in_specs=[ANY] * (1 + len(after)),
+        out_specs=ANY,
+        out_shape=jax.ShapeDtypeStruct(message.shape, message.dtype),
+        input_output_aliases={0: 0},
+        cost_estimate=cost(1, 1),
+        name="gate",
+    )(message, *after)
 
 
 def bands_kernel(kern_ref, across_ref, within_ref):
@@ -213,19 +264,19 @@
         within_ref[0, 16 * q : 16 * (q + 1), :] = turned.astype(BF16)
 
 
-def bands(kern):
+def bands(kern, after):
     count = kern.shape[0]
     shapes = ((4 * LANE, 2 * LANE), (BIG * DEPTH, (BIG + 2 * REACH) * DEPTH))
     return pl.pallas_call(
-        bands_kernel,
+        skipping(bands_kernel, 1, len(after)),
         grid=(count,),
-        in_specs=[pl.BlockSpec(memory_space=pltpu.SMEM)],
+        in_specs=[pl.BlockSpec(memory_space=pltpu.SMEM)] + [ANY] * len(after),
         out_specs=[pl.BlockSpec((1,) + s, lambda i: (i, 0, 0)) for s in shapes],
         out_shape=[jax.ShapeDtypeStruct((count,) + s, BF16) for s in shapes],
         compiler_params=params(32),
-        cost_estimate=cost(count * 1e6, count * 4e6),
+        cost_estimate=cost(2e9, 1),
         name="bands",
-    )(kern)
+    )(kern, *after)
 
 
 @functools.lru_cache(None)
@@ -357,7 +408,7 @@
     unpack(above_ref, rows8, far8)
     unpack(below_ref, rows8, far8 + 2 * rows8)
     joined_short[own, middle] = exact_ref[0].astype(BF16)
-    joined_short[own, :LANE] = left_ref[0]
+    joined_short[own, :LANE] = left_ref[0, rows8:]
     joined_short[own, after] = right_ref[0]
     joined_short[frame8:, :] = jnp.zeros_like(joined_short[frame8:, :])
     joined[...] = joined_short[...].astype(F32)
@@ -489,7 +540,7 @@
             pltpu.VMEM((ratio_rows, wide), BF16),
         ],
         compiler_params=params(40),
-        cost_estimate=cost(1e6, 1e5),
+        cost_estimate=cost(1, 1),
         name="deconvolve",
     )(*operands, *earlier)
 
@@ -506,50 +557,42 @@
         route = [(i, i + distance) for i in devices if i + distance in devices]
         return lax.ppermute(block, axis, route)
 
-    def shift_diagonal(block):
-        route = [
-            (x * size_y + y, (x + 1) * size_y + y + 1)
-            for x in range(size_x - 1)
-            for y in range(size_y - 1)
-        ]
-        return lax.ppermute(block, ("gx", "gy"), route)
-
     sides = jnp.stack([at_y > 0, at_y < size_y - 1, at_x > 0, at_x < size_x - 1])
     sides = sides.astype(jnp.int32)
     matrices = [jnp.asarray(m) for m in pyramid_matrices(rows, cols, depth)]
 
-    parts = ((0, 1), (1, chans - 1))
-    sent = []
-    for begin, n in parts:
-        own, right, low, corner = place(tiles, offsets.reshape(2), begin, n)
-        sent.append(
-            [own, shift(low, "gy", 1), shift(right, "gx", 1), shift_diagonal(corner)]
-        )
-
-    psf, _ = lax.optimization_barrier((psf, sent[0][0]))
+    at_tile = offsets.reshape(2)
+    own, right, low = place(tiles, at_tile, 0, 1, ())
     kern = psf / jnp.sum(psf, axis=-1, keepdims=True)
     both = jnp.stack([kern, kern[:, :, ::-1]], axis=1)
-    across, within = bands(both.reshape(chans * 2, 3 * TAPS))
+    across, within = bands(both.reshape(chans * 2, 3 * TAPS), (right,))
+    pieces = [(own, right, shift(low, "gy", 1))]
+    own, right, low = place(tiles, at_tile, 1, chans - 1, (within,))
+    pieces.append((own, right, shift(low, "gy", 1)))
     across = across.reshape((chans, 2) + across.shape[1:])
     within = within.reshape((chans, 2) + within.shape[1:])
-    sent[0][1], across, within = lax.optimization_barrier((sent[0][1], across, within))
 
     groups = []
-    for (begin, n), pieces in zip(parts, sent):
-        exact, first, last = join(*pieces)
-        left = shift(last, "gx", 1)
-        right = shift(first, "gx", -1)
-        for at in range(n):
-            message, tail = pack(exact, left, right, at)
+    before = (pieces[1][1],)
+    for own, right, low in pieces:
+        mine, to_left = edges(own, right, low, before)
+        left = shift(mine, "gx", 1)
+        right = shift(to_left, "gx", -1)
+        joined = [
+            join(sides, own, low, mine, left, right, k) for k in range(own.shape[0])
+        ]
+        before = (joined[0][2],)
+        far = jnp.concatenate([tail for *_, tail in joined], axis=0)
+        far = shift(far, "gy", 2)
+        for k, (exact, strip, message, _) in enumerate(joined):
+            if k:
+                message = gate(message, (far,))
             above = shift(message, "gy", 1)
             below = shift(message, "gy", -1)
-            groups.append((exact, above, below, tail, left, right, at))
-    far = shift(jnp.concatenate([g[3] for g in groups], axis=0), "gy", 2)
+            groups.append(((exact, above, below, far, left, strip), (0, 0, 0, k, k, 0)))
 
     outs = ()
-    for at, (exact, above, below, _, left, right, k) in enumerate(groups):
-        group = (exact, above, below, far, left, right)
-        places = (k, 0, 0, at, k, k)
+    for at, (group, places) in enumerate(groups):
         outs = deconvolve(at, chans, sides, group, places, across, within, matrices, outs)
     return tuple(outs)
 

time: 166 us -> 147 us (0.89)
  waiting for transfers between devices: 45.5 us -> 26.2 us
  Pallas kernels: 51.4 us -> 56.9 us
  other arithmetic: 2.87 us -> 0.34 us
  starting transfers between devices: 45.9 us -> 43.9 us
    ppermute x2 -> x0, waiting for transfers between devices: 18.1 us -> none  [shift_diagonal(): return lax.ppermute(block, ('gx', 'gy'), route)]
    pallas_call x8 -> x9, Pallas kernels: 15.1 us -> 21.5 us  [the longest x2 8.16 us: place(): pl.pallas_call(skipping(place_kernel, 2, len(after)), grid_spec=pltpu.Pre...]
    ppermute x2 -> x0, starting transfers between devices: 4.85 us -> none  [shift_diagonal(): return lax.ppermute(block, ('gx', 'gy'), route)]
    ppermute x15 -> x14, starting transfers between devices: 41.1 us -> 43.9 us  [shift(): return lax.ppermute(block, axis, route)]
    ppermute x15 -> x14, waiting for transfers between devices: 27.5 us -> 26.2 us  [shift(): return lax.ppermute(block, axis, route)]
    unnamed x54 -> x68, local copies, waits for them, and re-layouts: 17.4 us -> 16.5 us
  transfers between devices with their start and end apart: 17 -> 14, of which waited for: 5 -> 7; matrix products, arithmetic and copies ran while one was open for 2% -> 0% of each run, Pallas kernels for 22% -> 28%
where the time goes in v4:
time: 147 us; the launch traced here: 145 us
  Pallas kernels  56.9 us (39%)
  starting transfers between devices  43.9 us (30%)
  waiting for transfers between devices  26.2 us (18%)
  local copies, waits for them, and re-layouts  16.7 us (11%)
    ppermute x14, starting transfers between devices, shift(): return lax.ppermute(block, axis, route)  43.9 us
    pallas_call x3, Pallas kernels, deconvolve(): pl.pallas_call(deconvolve_kernel, grid=(1,), in_specs=[pl.BlockSpec(memor...  35.4 us
    ppermute x14, waiting for transfers between devices, shift(): return lax.ppermute(block, axis, route)  26.2 us
    unnamed x68, local copies, waits for them, and re-layouts  16.5 us
    pallas_call x2, Pallas kernels, place(): pl.pallas_call(skipping(place_kernel, 2, len(after)), grid_spec=pltpu.Pre...  8.16 us
    pallas_call x3, Pallas kernels, join(): pl.pallas_call(join_kernel, grid=(1,), in_specs=[pl.BlockSpec(memory_spac...  7.34 us
    pallas_call x2, Pallas kernels, edges(): pl.pallas_call(skipping(edges_kernel, 3, len(after)), grid=(n,), in_specs...  3.66 us
  transfers between devices with their start and end apart: 14, of which 7 were waited for; matrix products, arithmetic and copies ran while one was open for 0% of the time, Pallas kernels for 28%

profile of v4, /device:TPU:11, one launch (start us, length us, event | category | flops | bytes accessed | tf_op | source)
XLA Modules:
  0.0 145.0 jit_solution(2855851979598715537)
XLA Ops:
  0.6 1.8 %copy-done.29 = bf16[3,8,96,544]{3,2,1,0:T(8,128)(2,1)S(1)} copy-done((bf16[3,8,96,544]{3,2,1,0:T(8,128)(2,1)S(1)}, bf16[3,8,96,544]{3,2,1,0:T(8,128)(2,1)}, u32[]{:S(2)}) %copy-start.29) | copy-done | bytes 2506776
  3.1 3.2 %place.2 = (bf16[1,512,512]{2,1,0:T(8,128)(2,1)S(1)}, bf16[1,512,128]{2,1,0:T(8,128)(2,1)S(1)}, bf16[1,576,512]{2,1,0:T(8,128)(2,1)}) custom-call(s32[2]{0:T(128)S(1)} %bitcast.16, bf16[3,8,96,544]{3,2,1,0:T(8,128)(2,1)S(1)} %copy-done.29), custom_call_target="tpu_custom_call" | custom-call | flops 2000000000 | bytes 1 | tf_op jit(solution)/shard_map/place/pallas_call | solution.py:98
  7.1 3.2 %collective-permute-start.1 = (bf16[1,576,512]{2,1,0:T(8,128)(2,1)}, bf16[1,576,512]{2,1,0:T(8,128)(2,1)}, u32[]{:S(2)}, u32[]{:S(2)}) collective-permute-start(bf16[1,576,512]{2,1,0:T(8,128)(2,1)} %get-tuple-element.39), channel_id=1, source_target_pairs={{0,1},{1,2},{2,3},{4,5},{5,6},{6,7},{8,9},{9,10},{10,11},{12,13},{... | collective-permute-start | bytes 1769480 | tf_op jit(solution)/shard_map/ppermute | solution.py:558
  10.8 2.3 %bands.1 = (bf16[6,512,256]{2,1,0:T(8,128)(2,1)S(1)}, bf16[6,272,512]{2,1,0:T(8,128)(2,1)S(1)}) custom-call(f32[6,93]{1,0:T(8,128)S(1)} %reshape.20.refs_0_, bf16[1,512,128]{2,1,0:T(8,128)(2,1)S(1)} %get-tuple-element.33.refs_1_), custom_call_target="tpu_custom_call" | custom-call | flops 2000000000 | bytes 1 | tf_op jit(solution)/shard_map/bands/pallas_call | solution.py:270
  13.1 5.0 %place.3 = (bf16[2,512,512]{2,1,0:T(8,128)(2,1)S(1)}, bf16[2,512,128]{2,1,0:T(8,128)(2,1)S(1)}, bf16[2,576,512]{2,1,0:T(8,128)(2,1)}) custom-call(s32[2]{0:T(128)S(1)} %bitcast.17, bf16[3,8,96,544]{3,2,1,0:T(8,128)(2,1)S(1)} %copy-done.30, bf16[6,272,512]{2,1,0:T(8,128)(2,1)S(1)} %get-tuple-element.34.refs_2_), custom_call_target="tpu_custom_call" | custom-call | flops 4000000000 | bytes 1 | tf_op jit(solution)/shard_map/place/pallas_call | solution.py:98
  18.1 3.2 %collective-permute-start = (bf16[2,576,512]{2,1,0:T(8,128)(2,1)}, bf16[2,576,512]{2,1,0:T(8,128)(2,1)}, u32[]{:S(2)}, u32[]{:S(2)}) collective-permute-start(bf16[2,576,512]{2,1,0:T(8,128)(2,1)} %get-tuple-element.36), channel_id=1, source_target_pairs={{0,1},{1,2},{2,3},{4,5},{5,6},{6,7},{8,9},{9,10},{10,11},{12,13},{... | collective-permute-start | bytes 3538952 | tf_op jit(solution)/shard_map/ppermute | solution.py:558
  21.3 2.2 %collective-permute-done.1.refs_2_.low_ref = bf16[1,576,512]{2,1,0:T(8,128)(2,1)} collective-permute-done((bf16[1,576,512]{2,1,0:T(8,128)(2,1)}, bf16[1,576,512]{2,1,0:T(8,128)(2,1)}, u32[]{:S(2)}, u32[]{:S(2)}) %collective-permute-start.1) | collective-permute-done | bytes 589856 | tf_op jit(solution)/shard_map/ppermute | solution.py:558
  23.5 2.0 %edges.2 = (bf16[1,1024,128]{2,1,0:T(8,128)(2,1)}, bf16[1,1024,128]{2,1,0:T(8,128)(2,1)}) custom-call(bf16[1,512,512]{2,1,0:T(8,128)(2,1)S(1)} %copy-done.18, bf16[1,512,128]{2,1,0:T(8,128)(2,1)S(1)} %get-tuple-element.33.refs_1_, bf16[1,576,512]{2,1,0:T(8,128)(2,1)} %collective-permute-done.1.refs_2_.low_ref, ...), custom_call_target="tpu_custom_call" | custom-call | flops 40000000000 | bytes 1 | tf_op jit(solution)/shard_map/edges/pallas_call | solution.py:141
  25.5 5.7 %collective-permute-start.2 = (bf16[1,1024,128]{2,1,0:T(8,128)(2,1)}, bf16[1,1024,128]{2,1,0:T(8,128)(2,1)S(1)}, u32[]{:S(2)}, u32[]{:S(2)}) collective-permute-start(bf16[1,1024,128]{2,1,0:T(8,128)(2,1)} %get-tuple-element.40.mine_ref), channel_id=1, source_target_pairs={{0,4},{4,8},{8,12},{12,16},{16,20},{20,24},{24,28},{1,5},{5,9},{9,... | collective-permute-start | bytes 786440 | tf_op jit(solution)/shard_map/ppermute | solution.py:558
  31.2 1.9 %collective-permute-start.3 = (bf16[1,1024,128]{2,1,0:T(8,128)(2,1)}, bf16[1,1024,128]{2,1,0:T(8,128)(2,1)}, u32[]{:S(2)}, u32[]{:S(2)}) collective-permute-start(bf16[1,1024,128]{2,1,0:T(8,128)(2,1)} %get-tuple-element.41), channel_id=1, source_target_pairs={{4,0},{8,4},{12,8},{16,12},{20,16},{24,20},{28,24},{5,1},{9,5},{13... | collective-permute-start | bytes 786440 | tf_op jit(solution)/shard_map/ppermute | solution.py:558
  34.8 5.3 %collective-permute-done.3.right_ref = bf16[1,1024,128]{2,1,0:T(8,128)(2,1)} collective-permute-done((bf16[1,1024,128]{2,1,0:T(8,128)(2,1)}, bf16[1,1024,128]{2,1,0:T(8,128)(2,1)}, u32[]{:S(2)}, u32[]{:S(2)}) %collective-permute-start.3) | collective-permute-done | bytes 262176 | tf_op jit(solution)/shard_map/ppermute | solution.py:558
  41.2 2.8 %join.3 = (f32[1,512,512]{2,1,0:T(8,128)S(1)}, bf16[1,512,128]{2,1,0:T(8,128)(2,1)S(1)}, bf16[1,528,640]{2,1,0:T(8,128)(2,1)}, bf16[1,32,640]{2,1,0:T(8,128)(2,1)}) custom-call(s32[4]{0:T(128)S(1)} %add_convert_fusion.sides_ref, bf16[1,512,512]{2,1,0:T(8,128)(2,1)S(1)} %copy-done.19, bf16[1,576,512]{2,1,0:T(8,128)(2,1)} %collective-permute-done.1.refs_2_.low_ref, ...), custom_call_target="tpu_custom_call" | custom-call | flops 1 | bytes 1 | tf_op jit(solution)/shard_map/join/pallas_call | solution.py:209
  45.6 3.1 %collective-permute-done.refs_2_.low_ref = bf16[2,576,512]{2,1,0:T(8,128)(2,1)} collective-permute-done((bf16[2,576,512]{2,1,0:T(8,128)(2,1)}, bf16[2,576,512]{2,1,0:T(8,128)(2,1)}, u32[]{:S(2)}, u32[]{:S(2)}) %collective-permute-start) | collective-permute-done | bytes 1179680 | tf_op jit(solution)/shard_map/ppermute | solution.py:558
  50.9 1.6 %edges.3 = (bf16[2,1024,128]{2,1,0:T(8,128)(2,1)S(1)}, bf16[2,1024,128]{2,1,0:T(8,128)(2,1)S(1)}) custom-call(bf16[2,512,512]{2,1,0:T(8,128)(2,1)S(1)} %copy-done.1, bf16[2,512,128]{2,1,0:T(8,128)(2,1)S(1)} %copy-done.21, bf16[2,576,512]{2,1,0:T(8,128)(2,1)} %collective-permute-done.refs_2_.low_ref, bf16[1,528,640]{2,1,0:T(8,128)(2,1)} %get-tuple-element.42.refs_3_), custom_call_target="tpu_custom_call" | custom-call | flops 1 | bytes 1 | tf_op jit(solution)/shard_map/edges/pallas_call | solution.py:141
  52.6 4.5 %collective-permute-start.4 = (bf16[2,1024,128]{2,1,0:T(8,128)(2,1)S(1)}, bf16[2,1024,128]{2,1,0:T(8,128)(2,1)S(1)}, u32[]{:S(2)}, u32[]{:S(2)}) collective-permute-start(bf16[2,1024,128]{2,1,0:T(8,128)(2,1)S(1)} %get-tuple-element.43.mine_ref), channel_id=1, source_target_pairs={{0,4},{4,8},{8,12},{12,16},{16,20},{20,24},{24,28},{1,5},{5,9},{9,... | collective-permute-start | bytes 1572872 | tf_op jit(solution)/shard_map/ppermute | solution.py:558
  57.1 1.9 %collective-permute-start.5 = (bf16[2,1024,128]{2,1,0:T(8,128)(2,1)S(1)}, bf16[2,1024,128]{2,1,0:T(8,128)(2,1)S(1)}, u32[]{:S(2)}, u32[]{:S(2)}) collective-permute-start(bf16[2,1024,128]{2,1,0:T(8,128)(2,1)S(1)} %get-tuple-element.44), channel_id=1, source_target_pairs={{4,0},{8,4},{12,8},{16,12},{20,16},{24,20},{28,24},{5,1},{9,5},{13... | collective-permute-start | bytes 1572872 | tf_op jit(solution)/shard_map/ppermute | solution.py:558
  59.1 3.2 %collective-permute-start.11 = (bf16[1,528,640]{2,1,0:T(8,128)(2,1)}, bf16[1,528,640]{2,1,0:T(8,128)(2,1)}, u32[]{:S(2)}, u32[]{:S(2)}) collective-permute-start(bf16[1,528,640]{2,1,0:T(8,128)(2,1)} %get-tuple-element.42.refs_3_), channel_id=1, source_target_pairs={{0,1},{1,2},{2,3},{4,5},{5,6},{6,7},{8,9},{9,10},{10,11},{12,13},{... | collective-permute-start | bytes 2027528 | tf_op jit(solution)/shard_map/ppermute | solution.py:558
  62.3 3.8 %collective-permute-done.4.left_ref = bf16[2,1024,128]{2,1,0:T(8,128)(2,1)S(1)} collective-permute-done((bf16[2,1024,128]{2,1,0:T(8,128)(2,1)S(1)}, bf16[2,1024,128]{2,1,0:T(8,128)(2,1)S(1)}, u32[]{:S(2)}, u32[]{:S(2)}) %collective-permute-start.4) | collective-permute-done | bytes 524320 | tf_op jit(solution)/shard_map/ppermute | solution.py:558
  66.0 4.5 %collective-permute-done.5.right_ref = bf16[2,1024,128]{2,1,0:T(8,128)(2,1)S(1)} collective-permute-done((bf16[2,1024,128]{2,1,0:T(8,128)(2,1)S(1)}, bf16[2,1024,128]{2,1,0:T(8,128)(2,1)S(1)}, u32[]{:S(2)}, u32[]{:S(2)}) %collective-permute-start.5) | collective-permute-done | bytes 524320 | tf_op jit(solution)/shard_map/ppermute | solution.py:558
  70.5 2.7 %join.5 = (f32[1,512,512]{2,1,0:T(8,128)S(1)}, bf16[1,512,128]{2,1,0:T(8,128)(2,1)S(1)}, bf16[1,528,640]{2,1,0:T(8,128)(2,1)}, bf16[1,32,640]{2,1,0:T(8,128)(2,1)S(1)}) custom-call(s32[4]{0:T(128)S(1)} %add_convert_fusion.sides_ref, bf16[2,512,512]{2,1,0:T(8,128)(2,1)S(1)} %copy-done.1, bf16[2,576,512]{2,1,0:T(8,128)(2,1)} %collective-permute-done.refs_2_.low_ref, ...), custom_call_target="tpu_custom_call" | custom-call | flops 1 | bytes 1 | tf_op jit(solution)/shard_map/join/pallas_call | solution.py:209
  74.8 1.8 %join.4 = (f32[1,512,512]{2,1,0:T(8,128)S(1)}, bf16[1,512,128]{2,1,0:T(8,128)(2,1)S(1)}, bf16[1,528,640]{2,1,0:T(8,128)(2,1)S(1)}, bf16[1,32,640]{2,1,0:T(8,128)(2,1)S(1)}) custom-call(s32[4]{0:T(128)S(1)} %add_convert_fusion.sides_ref, bf16[2,512,512]{2,1,0:T(8,128)(2,1)S(1)} %copy-done.1, bf16[2,576,512]{2,1,0:T(8,128)(2,1)} %collective-permute-done.refs_2_.low_ref, ...), custom_call_target="tpu_custom_call" | custom-call | flops 1 | bytes 1 | tf_op jit(solution)/shard_map/join/pallas_call | solution.py:209
  79.2 4.8 %collective-permute-start.6 = (bf16[2,32,640]{2,1,0:T(8,128)(2,1)S(1)}, bf16[2,32,640]{2,1,0:T(8,128)(2,1)}, u32[]{:S(2)}, u32[]{:S(2)}) collective-permute-start(bf16[2,32,640]{2,1,0:T(8,128)(2,1)S(1)} %pad_maximum_fusion), channel_id=1, source_target_pairs={{0,2},{1,3},{4,6},{5,7},{8,10},{9,11},{12,14},{13,15},{16,18},{17,... | collective-permute-start | bytes 245768 | tf_op jit(solution)/shard_map/ppermute | solution.py:558
  84.1 1.9 %collective-permute-start.13 = (bf16[1,32,640]{2,1,0:T(8,128)(2,1)}, bf16[1,32,640]{2,1,0:T(8,128)(2,1)}, u32[]{:S(2)}, u32[]{:S(2)}) collective-permute-start(bf16[1,32,640]{2,1,0:T(8,128)(2,1)} %get-tuple-element.55), channel_id=1, source_target_pairs={{0,2},{1,3},{4,6},{5,7},{8,10},{9,11},{12,14},{13,15},{16,18},{17,... | collective-permute-start | bytes 122888 | tf_op jit(solution)/shard_map/ppermute | solution.py:558
  86.0 2.1 %collective-permute-start.12 = (bf16[1,528,640]{2,1,0:T(8,128)(2,1)}, bf16[1,528,640]{2,1,0:T(8,128)(2,1)}, u32[]{:S(2)}, u32[]{:S(2)}) collective-permute-start(bf16[1,528,640]{2,1,0:T(8,128)(2,1)} %get-tuple-element.42.refs_3_), channel_id=1, source_target_pairs={{1,0},{2,1},{3,2},{5,4},{6,5},{7,6},{9,8},{10,9},{11,10},{13,12},{... | collective-permute-start | bytes 2027528 | tf_op jit(solution)/shard_map/ppermute | solution.py:558
  88.1 1.9 %collective-permute-start.10 = (bf16[1,528,640]{2,1,0:T(8,128)(2,1)}, bf16[1,528,640]{2,1,0:T(8,128)(2,1)}, u32[]{:S(2)}, u32[]{:S(2)}) collective-permute-start(bf16[1,528,640]{2,1,0:T(8,128)(2,1)} %get-tuple-element.52), channel_id=1, source_target_pairs={{1,0},{2,1},{3,2},{5,4},{6,5},{7,6},{9,8},{10,9},{11,10},{13,12},{... | collective-permute-start | bytes 2027528 | tf_op jit(solution)/shard_map/ppermute | solution.py:558
  90.0 3.4 %collective-permute-start.9 = (bf16[1,528,640]{2,1,0:T(8,128)(2,1)}, bf16[1,528,640]{2,1,0:T(8,128)(2,1)}, u32[]{:S(2)}, u32[]{:S(2)}) collective-permute-start(bf16[1,528,640]{2,1,0:T(8,128)(2,1)} %get-tuple-element.52), channel_id=1, source_target_pairs={{0,1},{1,2},{2,3},{4,5},{5,6},{6,7},{8,9},{9,10},{10,11},{12,13},{... | collective-permute-start | bytes 2027528 | tf_op jit(solution)/shard_map/ppermute | solution.py:558
  93.4 4.0 %collective-permute-start.7 = (bf16[1,528,640]{2,1,0:T(8,128)(2,1)}, bf16[1,528,640]{2,1,0:T(8,128)(2,1)S(1)}, u32[]{:S(2)}, u32[]{:S(2)}) collective-permute-start(bf16[1,528,640]{2,1,0:T(8,128)(2,1)} %gate.1), channel_id=1, source_target_pairs={{0,1},{1,2},{2,3},{4,5},{5,6},{6,7},{8,9},{9,10},{10,11},{12,13},{... | collective-permute-start | bytes 2027528 | tf_op jit(solution)/shard_map/ppermute | solution.py:558
  97.4 2.1 %collective-permute-start.8 = (bf16[1,528,640]{2,1,0:T(8,128)(2,1)}, bf16[1,528,640]{2,1,0:T(8,128)(2,1)S(1)}, u32[]{:S(2)}, u32[]{:S(2)}) collective-permute-start(bf16[1,528,640]{2,1,0:T(8,128)(2,1)} %gate.1), channel_id=1, source_target_pairs={{1,0},{2,1},{3,2},{5,4},{6,5},{7,6},{9,8},{10,9},{11,10},{13,12},{... | collective-permute-start | bytes 2027528 | tf_op jit(solution)/shard_map/ppermute | solution.py:558
  99.5 5.7 %collective-permute-done.12.below_ref = bf16[1,528,640]{2,1,0:T(8,128)(2,1)} collective-permute-done((bf16[1,528,640]{2,1,0:T(8,128)(2,1)}, bf16[1,528,640]{2,1,0:T(8,128)(2,1)}, u32[]{:S(2)}, u32[]{:S(2)}) %collective-permute-start.12) | collective-permute-done | bytes 675872 | tf_op jit(solution)/shard_map/ppermute | solution.py:558
  109.5 12.0 %deconvolve.3 = (f32[3,8,64,512]{3,2,1,0:T(8,128)}, f32[3,4,32,256]{3,2,1,0:T(8,128)}, f32[3,2,16,128]{3,2,1,0:T(8,128)}) custom-call(s32[4]{0:T(128)S(1)} %add_convert_fusion.sides_ref, f32[1,512,512]{2,1,0:T(8,128)S(1)} %copy-done.10, bf16[1,528,640]{2,1,0:T(8,128)(2,1)} %collective-permute-done.11.above_ref, ...), custom_call_target="tpu_custom_call" | custom-call | flops 1 | bytes 1 | tf_op jit(solution)/shard_map/deconvolve/pallas_call | solution.py:521
  121.5 12.1 %deconvolve.4 = (f32[3,8,64,512]{3,2,1,0:T(8,128)}, f32[3,4,32,256]{3,2,1,0:T(8,128)}, f32[3,2,16,128]{3,2,1,0:T(8,128)}) custom-call(s32[4]{0:T(128)S(1)} %add_convert_fusion.sides_ref, f32[1,512,512]{2,1,0:T(8,128)S(1)} %copy-done.12, ...), custom_call_target="tpu_custom_call", output_to_operand_aliasing={{0}: (13, {}), {1}: (14, {}), {2}: (15, {})} | custom-call | flops 1 | bytes 1 | tf_op jit(solution)/shard_map/deconvolve/pallas_call | solution.py:521
  133.7 11.3 %deconvolve.5 = (f32[3,8,64,512]{3,2,1,0:T(8,128)}, f32[3,4,32,256]{3,2,1,0:T(8,128)}, f32[3,2,16,128]{3,2,1,0:T(8,128)}) custom-call(s32[4]{0:T(128)S(1)} %add_convert_fusion.sides_ref, f32[1,512,512]{2,1,0:T(8,128)S(1)} %copy-done.8, ...), custom_call_target="tpu_custom_call", output_to_operand_aliasing={{0}: (13, {}), {1}: (14, {}), {2}: (15, {})} | custom-call | flops 1 | bytes 1 | tf_op jit(solution)/shard_map/deconvolve/pallas_call | solution.py:521
  (85 shorter events, 16.8 us)
Async XLA Ops:
  0.6 1.8 %copy-start.29 = (bf16[3,8,96,544]{3,2,1,0:T(8,128)(2,1)S(1)}, bf16[3,8,96,544]{3,2,1,0:T(8,128)(2,1)}, u32[]{:S(2)}) copy-start(bf16[3,8,96,544]{3,2,1,0:T(8,128)(2,1)} %refs_1_.3) | copy-start | bytes 7520260
  3.1 7.2 %copy-start.33 = (f32[3,3,31]{2,1,0:T(4,128)S(1)}, f32[3,3,31]{2,1,0:T(4,128)}, u32[]{:S(2)}) copy-start(f32[3,3,31]{2,1,0:T(4,128)} %param.9) | copy-start | bytes 3352
  7.1 16.4 %collective-permute-start.1 = (bf16[1,576,512]{2,1,0:T(8,128)(2,1)}, bf16[1,576,512]{2,1,0:T(8,128)(2,1)}, u32[]{:S(2)}, u32[]{:S(2)}) collective-permute-start(bf16[1,576,512]{2,1,0:T(8,128)(2,1)} %get-tuple-element.39), channel_id=1, source_target_pairs={{0,1},{1,2},{2,3},{4,5},{5,6},{6,7},{8,9},{9,10},{10,11},{12,13},{... | collective-permute-start | bytes 1769480 | tf_op jit(solution)/shard_map/ppermute | solution.py:558
  10.7 2.3 %copy-start.30 = (bf16[3,8,96,544]{3,2,1,0:T(8,128)(2,1)S(1)}, bf16[3,8,96,544]{3,2,1,0:T(8,128)(2,1)}, u32[]{:S(2)}) copy-start(bf16[3,8,96,544]{3,2,1,0:T(8,128)(2,1)} %refs_1_.3) | copy-start | bytes 7520260
  10.7 2.3 %copy-start.32 = (s32[1,1,2]{2,1,0:T(1,128)S(1)}, s32[1,1,2]{2,1,0:T(1,128)}, u32[]{:S(2)}) copy-start(s32[1,1,2]{2,1,0:T(1,128)} %param.8) | copy-start | bytes 28
  13.1 10.4 %copy-start.18 = (bf16[1,512,512]{2,1,0:T(8,128)(2,1)S(1)}, bf16[1,512,512]{2,1,0:T(8,128)(2,1)}, u32[]{:S(2)}) copy-start(bf16[1,512,512]{2,1,0:T(8,128)(2,1)} %copy-done.17) | copy-start | bytes 1572868
  18.1 7.4 %copy-start = (bf16[2,512,512]{2,1,0:T(8,128)(2,1)}, bf16[2,512,512]{2,1,0:T(8,128)(2,1)S(1)}, u32[]{:S(2)}) copy-start(bf16[2,512,512]{2,1,0:T(8,128)(2,1)S(1)} %get-tuple-element.35.refs_0_.own_ref) | copy-start | bytes 3145732
  18.1 7.4 %copy-start.20 = (bf16[2,512,128]{2,1,0:T(8,128)(2,1)}, bf16[2,512,128]{2,1,0:T(8,128)(2,1)S(1)}, u32[]{:S(2)}) copy-start(bf16[2,512,128]{2,1,0:T(8,128)(2,1)S(1)} %get-tuple-element.37.refs_3_.refs_1_) | copy-start | bytes 786436
  18.1 30.7 %collective-permute-start = (bf16[2,576,512]{2,1,0:T(8,128)(2,1)}, bf16[2,576,512]{2,1,0:T(8,128)(2,1)}, u32[]{:S(2)}, u32[]{:S(2)}) collective-permute-start(bf16[2,576,512]{2,1,0:T(8,128)(2,1)} %get-tuple-element.36), channel_id=1, source_target_pairs={{0,1},{1,2},{2,3},{4,5},{5,6},{6,7},{8,9},{9,10},{10,11},{12,13},{... | collective-permute-start | bytes 3538952 | tf_op jit(solution)/shard_map/ppermute | solution.py:558
  25.5 9.3 %collective-permute-start.2 = (bf16[1,1024,128]{2,1,0:T(8,128)(2,1)}, bf16[1,1024,128]{2,1,0:T(8,128)(2,1)S(1)}, u32[]{:S(2)}, u32[]{:S(2)}) collective-permute-start(bf16[1,1024,128]{2,1,0:T(8,128)(2,1)} %get-tuple-element.40.mine_ref), channel_id=1, source_target_pairs={{0,4},{4,8},{8,12},{12,16},{16,20},{20,24},{24,28},{1,5},{5,9},{9,... | collective-permute-start | bytes 786440 | tf_op jit(solution)/shard_map/ppermute | solution.py:558
  31.2 8.9 %collective-permute-start.3 = (bf16[1,1024,128]{2,1,0:T(8,128)(2,1)}, bf16[1,1024,128]{2,1,0:T(8,128)(2,1)}, u32[]{:S(2)}, u32[]{:S(2)}) collective-permute-start(bf16[1,1024,128]{2,1,0:T(8,128)(2,1)} %get-tuple-element.41), channel_id=1, source_target_pairs={{4,0},{8,4},{12,8},{16,12},{20,16},{24,20},{28,24},{5,1},{9,5},{13... | collective-permute-start | bytes 786440 | tf_op jit(solution)/shard_map/ppermute | solution.py:558
  34.8 35.7 %copy-start.13 = (bf16[1,1024,128]{2,1,0:T(8,128)(2,1)}, bf16[1,1024,128]{2,1,0:T(8,128)(2,1)S(1)}, u32[]{:S(2)}) copy-start(bf16[1,1024,128]{2,1,0:T(8,128)(2,1)S(1)} %collective-permute-done.2.left_ref) | copy-start | bytes 786436
  52.6 13.5 %collective-permute-start.4 = (bf16[2,1024,128]{2,1,0:T(8,128)(2,1)S(1)}, bf16[2,1024,128]{2,1,0:T(8,128)(2,1)S(1)}, u32[]{:S(2)}, u32[]{:S(2)}) collective-permute-start(bf16[2,1024,128]{2,1,0:T(8,128)(2,1)S(1)} %get-tuple-element.43.mine_ref), channel_id=1, source_target_pairs={{0,4},{4,8},{8,12},{12,16},{16,20},{20,24},{24,28},{1,5},{5,9},{9,... | collective-permute-start | bytes 1572872 | tf_op jit(solution)/shard_map/ppermute | solution.py:558
  57.1 13.4 %collective-permute-start.5 = (bf16[2,1024,128]{2,1,0:T(8,128)(2,1)S(1)}, bf16[2,1024,128]{2,1,0:T(8,128)(2,1)S(1)}, u32[]{:S(2)}, u32[]{:S(2)}) collective-permute-start(bf16[2,1024,128]{2,1,0:T(8,128)(2,1)S(1)} %get-tuple-element.44), channel_id=1, source_target_pairs={{4,0},{8,4},{12,8},{16,12},{20,16},{24,20},{28,24},{5,1},{9,5},{13... | collective-permute-start | bytes 1572872 | tf_op jit(solution)/shard_map/ppermute | solution.py:558
  59.1 38.4 %collective-permute-start.11 = (bf16[1,528,640]{2,1,0:T(8,128)(2,1)}, bf16[1,528,640]{2,1,0:T(8,128)(2,1)}, u32[]{:S(2)}, u32[]{:S(2)}) collective-permute-start(bf16[1,528,640]{2,1,0:T(8,128)(2,1)} %get-tuple-element.42.refs_3_), channel_id=1, source_target_pairs={{0,1},{1,2},{2,3},{4,5},{5,6},{6,7},{8,9},{9,10},{10,11},{12,13},{... | collective-permute-start | bytes 2027528 | tf_op jit(solution)/shard_map/ppermute | solution.py:558
  66.0 10.6 %copy-start.2 = (bf16[2,1024,128]{2,1,0:T(8,128)(2,1)}, bf16[2,1024,128]{2,1,0:T(8,128)(2,1)S(1)}, u32[]{:S(2)}) copy-start(bf16[2,1024,128]{2,1,0:T(8,128)(2,1)S(1)} %collective-permute-done.4.left_ref) | copy-start | bytes 1572868
  74.8 30.5 %copy-start.6 = (bf16[144,592]{1,0:T(8,128)(2,1)S(1)}, bf16[144,592]{1,0:T(8,128)(2,1)}, u32[]{:S(2)}) copy-start(bf16[144,592]{1,0:T(8,128)(2,1)} %constant.26.clone.one_zy_ref) | copy-start | bytes 511492
  74.8 30.5 %copy-start.15 = (bf16[384,128]{1,0:T(8,128)(2,1)S(1)}, bf16[384,128]{1,0:T(8,128)(2,1)}, u32[]{:S(2)}) copy-start(bf16[384,128]{1,0:T(8,128)(2,1)} %constant.27.clone.two_x_ref) | copy-start | bytes 294916
  74.8 30.5 %copy-start.22 = (bf16[32,144]{1,0:T(8,128)(2,1)S(1)}, bf16[32,144]{1,0:T(8,128)(2,1)}, u32[]{:S(2)}) copy-start(bf16[32,144]{1,0:T(8,128)(2,1)} %constant.28.clone.two_zy_ref) | copy-start | bytes 27652
  79.2 10.8 %collective-permute-start.6 = (bf16[2,32,640]{2,1,0:T(8,128)(2,1)S(1)}, bf16[2,32,640]{2,1,0:T(8,128)(2,1)}, u32[]{:S(2)}, u32[]{:S(2)}) collective-permute-start(bf16[2,32,640]{2,1,0:T(8,128)(2,1)S(1)} %pad_maximum_fusion), channel_id=1, source_target_pairs={{0,2},{1,3},{4,6},{5,7},{8,10},{9,11},{12,14},{13,15},{16,18},{17,... | collective-permute-start | bytes 245768 | tf_op jit(solution)/shard_map/ppermute | solution.py:558
  84.1 9.3 %collective-permute-start.13 = (bf16[1,32,640]{2,1,0:T(8,128)(2,1)}, bf16[1,32,640]{2,1,0:T(8,128)(2,1)}, u32[]{:S(2)}, u32[]{:S(2)}) collective-permute-start(bf16[1,32,640]{2,1,0:T(8,128)(2,1)} %get-tuple-element.55), channel_id=1, source_target_pairs={{0,2},{1,3},{4,6},{5,7},{8,10},{9,11},{12,14},{13,15},{16,18},{17,... | collective-permute-start | bytes 122888 | tf_op jit(solution)/shard_map/ppermute | solution.py:558
  86.0 19.3 %collective-permute-start.12 = (bf16[1,528,640]{2,1,0:T(8,128)(2,1)}, bf16[1,528,640]{2,1,0:T(8,128)(2,1)}, u32[]{:S(2)}, u32[]{:S(2)}) collective-permute-start(bf16[1,528,640]{2,1,0:T(8,128)(2,1)} %get-tuple-element.42.refs_3_), channel_id=1, source_target_pairs={{1,0},{2,1},{3,2},{5,4},{6,5},{7,6},{9,8},{10,9},{11,10},{13,12},{... | collective-permute-start | bytes 2027528 | tf_op jit(solution)/shard_map/ppermute | solution.py:558
  88.1 33.4 %collective-permute-start.10 = (bf16[1,528,640]{2,1,0:T(8,128)(2,1)}, bf16[1,528,640]{2,1,0:T(8,128)(2,1)}, u32[]{:S(2)}, u32[]{:S(2)}) collective-permute-start(bf16[1,528,640]{2,1,0:T(8,128)(2,1)} %get-tuple-element.52), channel_id=1, source_target_pairs={{1,0},{2,1},{3,2},{5,4},{6,5},{7,6},{9,8},{10,9},{11,10},{13,12},{... | collective-permute-start | bytes 2027528 | tf_op jit(solution)/shard_map/ppermute | solution.py:558
  90.0 31.4 %collective-permute-start.9 = (bf16[1,528,640]{2,1,0:T(8,128)(2,1)}, bf16[1,528,640]{2,1,0:T(8,128)(2,1)}, u32[]{:S(2)}, u32[]{:S(2)}) collective-permute-start(bf16[1,528,640]{2,1,0:T(8,128)(2,1)} %get-tuple-element.52), channel_id=1, source_target_pairs={{0,1},{1,2},{2,3},{4,5},{5,6},{6,7},{8,9},{9,10},{10,11},{12,13},{... | collective-permute-start | bytes 2027528 | tf_op jit(solution)/shard_map/ppermute | solution.py:558
  93.4 40.2 %collective-permute-start.7 = (bf16[1,528,640]{2,1,0:T(8,128)(2,1)}, bf16[1,528,640]{2,1,0:T(8,128)(2,1)S(1)}, u32[]{:S(2)}, u32[]{:S(2)}) collective-permute-start(bf16[1,528,640]{2,1,0:T(8,128)(2,1)} %gate.1), channel_id=1, source_target_pairs={{0,1},{1,2},{2,3},{4,5},{5,6},{6,7},{8,9},{9,10},{10,11},{12,13},{... | collective-permute-start | bytes 2027528 | tf_op jit(solution)/shard_map/ppermute | solution.py:558
  97.4 36.2 %collective-permute-start.8 = (bf16[1,528,640]{2,1,0:T(8,128)(2,1)}, bf16[1,528,640]{2,1,0:T(8,128)(2,1)S(1)}, u32[]{:S(2)}, u32[]{:S(2)}) collective-permute-start(bf16[1,528,640]{2,1,0:T(8,128)(2,1)} %gate.1), channel_id=1, source_target_pairs={{1,0},{2,1},{3,2},{5,4},{6,5},{7,6},{9,8},{10,9},{11,10},{13,12},{... | collective-permute-start | bytes 2027528 | tf_op jit(solution)/shard_map/ppermute | solution.py:558
  109.5 12.0 %copy-start.3 = (bf16[2,1024,128]{2,1,0:T(8,128)(2,1)S(1)}, bf16[2,1024,128]{2,1,0:T(8,128)(2,1)}, u32[]{:S(2)}) copy-start(bf16[2,1024,128]{2,1,0:T(8,128)(2,1)} %copy-done.2) | copy-start | bytes 1572868
  109.5 12.0 %copy-start.5 = (bf16[768,384]{1,0:T(8,128)(2,1)S(1)}, bf16[768,384]{1,0:T(8,128)(2,1)}, u32[]{:S(2)}) copy-start(bf16[768,384]{1,0:T(8,128)(2,1)} %constant.25.clone.one_x_ref) | copy-start | bytes 1769476
  109.5 12.0 %copy-start.12 = (f32[1,512,512]{2,1,0:T(8,128)S(1)}, f32[1,512,512]{2,1,0:T(8,128)}, u32[]{:S(2)}) copy-start(f32[1,512,512]{2,1,0:T(8,128)} %copy-done.11) | copy-start | bytes 3145732
  109.5 12.0 %copy-start.26 = (bf16[1,512,128]{2,1,0:T(8,128)(2,1)S(1)}, bf16[1,512,128]{2,1,0:T(8,128)(2,1)}, u32[]{:S(2)}) copy-start(bf16[1,512,128]{2,1,0:T(8,128)(2,1)} %copy-done.25) | copy-start | bytes 393220
  121.5 12.2 %copy-start.8 = (f32[1,512,512]{2,1,0:T(8,128)S(1)}, f32[1,512,512]{2,1,0:T(8,128)}, u32[]{:S(2)}) copy-start(f32[1,512,512]{2,1,0:T(8,128)} %copy-done.7) | copy-start | bytes 3145732
  121.5 12.2 %copy-start.24 = (bf16[1,512,128]{2,1,0:T(8,128)(2,1)S(1)}, bf16[1,512,128]{2,1,0:T(8,128)(2,1)}, u32[]{:S(2)}) copy-start(bf16[1,512,128]{2,1,0:T(8,128)(2,1)} %copy-done.23) | copy-start | bytes 393220
  (16 other events, 14.6 us)

commit v5 on v4

--- a/solution.py
+++ b/solution.py
@@ -35,6 +35,7 @@
 
 
 ANY = pl.BlockSpec(memory_space=pl.ANY)
+VMEM = pl.BlockSpec(memory_space=pltpu.VMEM)
 
 
 def skipping(kernel, at, count):
@@ -154,9 +155,12 @@
 
 
 def join_kernel(
-    sides_ref, own_ref, low_ref, mine_ref, left_ref, right_ref, exact_ref, strip_ref, out_ref, tail_ref
+    at, sides_ref, own_ref, low_ref, mine_ref, left_ref, right_ref, exact_ref, strip_ref, out_ref, tail_ref
 ):
     rows, cols = own_ref.shape[1:]
+    own_ref, low_ref, mine_ref, left_ref, right_ref = (
+        ref.at[at : at + 1] for ref in (own_ref, low_ref, mine_ref, left_ref, right_ref)
+    )
     inside = lanes(rows) < LANE // 2
 
     def parts(ref):
@@ -164,7 +168,7 @@
         return jnp.where(inside, pair, 0.0), jnp.where(inside, pltpu.roll(pair, LANE // 2, 1), 0.0)
 
     own = own_ref[0].astype(F32)
-    low = low_ref[0].astype(F32)
+    low = low_ref[0, :rows].astype(F32)
     total = own + low
     count = seen(own) + seen(low)
     a, b = parts(left_ref)
@@ -197,8 +201,6 @@
 
 def join(sides, own, low, mine, left, right, at):
     _, rows, cols = own.shape
-    block = lambda r, c, k: pl.BlockSpec((1, r, c), lambda i: (k, 0, 0))
-    pair = block(2 * rows, LANE, at)
     extra = 2 * DEPTH
     sizes = (
         (rows, cols, F32),
@@ -207,28 +209,14 @@
         (2 * extra, cols + LANE, BF16),
     )
     return pl.pallas_call(
-        join_kernel,
-        grid=(1,),
-        in_specs=[pl.BlockSpec(memory_space=pltpu.SMEM)]
-        + [block(rows, cols, at), block(rows, cols, at), pair, pair, pair],
-        out_specs=[block(r, c, 0) for r, c, _ in sizes],
+        functools.partial(join_kernel, at),
+        in_specs=[pl.BlockSpec(memory_space=pltpu.SMEM)] + [VMEM] * 5,
+        out_specs=[VMEM] * 4,
         out_shape=[jax.ShapeDtypeStruct((1, r, c), t) for r, c, t in sizes],
-        compiler_params=params(16),
+        compiler_params=params(12),
         cost_estimate=cost(1, 1),
         name="join",
     )(sides, own, low, mine, left, right)
-
-
-def gate(message, after):
-    return pl.pallas_call(
-        lambda *refs: None,
-        in_specs=[ANY] * (1 + len(after)),
-        out_specs=ANY,
-        out_shape=jax.ShapeDtypeStruct(message.shape, message.dtype),
-        input_output_aliases={0: 0},
-        cost_estimate=cost(1, 1),
-        name="gate",
-    )(message, *after)
 
 
 def bands_kernel(kern_ref, across_ref, within_ref):
@@ -320,6 +308,7 @@
 
 
 def deconvolve_kernel(
+    places,
     sides_ref,
     exact_ref,
     above_ref,
@@ -337,6 +326,11 @@
 ):
     if len(others) > 11:
         others = others[3:]
+    at, k = places
+    far_ref = far_ref.at[at : at + 1]
+    left_ref = left_ref.at[k : k + 1]
+    across_ref = across_ref.at[at : at + 1]
+    within_ref = within_ref.at[at : at + 1]
     deconvolve_body(
         sides_ref,
         exact_ref,
@@ -501,13 +495,12 @@
     level_two_ref[0] = two.reshape(level_two_ref.shape[1:])
 
 
-def deconvolve(at, chans, sides, group, places, across, within, matrices, earlier):
+def deconvolve(at, places, sides, group, across, within, matrices, earlier):
+    chans = across.shape[0]
     rows8, cols = group[0].shape[1:]
     rows = rows8 // DEPTH
     wide = cols + 2 * LANE
-    one = lambda a, k: pl.BlockSpec((1,) + a.shape[1:], lambda i: (k, 0, 0))
     mine = lambda s: pl.BlockSpec((1,) + s[1:], lambda i: (at,) + (0,) * (len(s) - 1))
-    same = lambda a: pl.BlockSpec(a.shape, lambda i: (0,) * a.ndim)
     outs = (
         (chans, DEPTH, rows, cols),
         (chans, DEPTH // 2, rows // 2, cols // 2),
@@ -519,13 +512,11 @@
     result_rows = 3 * SMALL * DEPTH
     operands = [sides, *group, across, within, *matrices]
     return pl.pallas_call(
-        deconvolve_kernel,
+        functools.partial(deconvolve_kernel, places),
         grid=(1,),
         in_specs=[pl.BlockSpec(memory_space=pltpu.SMEM)]
-        + [one(a, k) for a, k in zip(group, places)]
-        + [mine(across.shape), mine(within.shape)]
-        + [same(m) for m in matrices]
-        + [pl.BlockSpec(memory_space=pl.ANY) for _ in earlier],
+        + [VMEM] * (len(operands) - 1)
+        + [ANY] * len(earlier),
         out_specs=[mine(s) for s in outs],
         out_shape=shapes,
         input_output_aliases={len(operands) + k: k for k in range(len(earlier))},
@@ -539,8 +530,8 @@
             pltpu.VMEM((ratio_rows, wide), BF16),
             pltpu.VMEM((ratio_rows, wide), BF16),
         ],
-        compiler_params=params(40),
-        cost_estimate=cost(1, 1),
+        compiler_params=params(32),
+        cost_estimate=cost(1e10, 1),
         name="deconvolve",
     )(*operands, *earlier)
 
@@ -573,27 +564,25 @@
     within = within.reshape((chans, 2) + within.shape[1:])
 
     groups = []
+    tails = []
     before = (pieces[1][1],)
     for own, right, low in pieces:
         mine, to_left = edges(own, right, low, before)
         left = shift(mine, "gx", 1)
         right = shift(to_left, "gx", -1)
-        joined = [
-            join(sides, own, low, mine, left, right, k) for k in range(own.shape[0])
-        ]
-        before = (joined[0][2],)
-        far = jnp.concatenate([tail for *_, tail in joined], axis=0)
-        far = shift(far, "gy", 2)
-        for k, (exact, strip, message, _) in enumerate(joined):
-            if k:
-                message = gate(message, (far,))
+        for k in range(own.shape[0]):
+            exact, strip, message, tail = join(sides, own, low, mine, left, right, k)
             above = shift(message, "gy", 1)
             below = shift(message, "gy", -1)
-            groups.append(((exact, above, below, far, left, strip), (0, 0, 0, k, k, 0)))
+            groups.append([exact, above, below, left, strip, k])
+            tails.append(tail)
+        before = (message,)
+    far = shift(jnp.concatenate(tails, axis=0), "gy", 2)
 
     outs = ()
-    for at, (group, places) in enumerate(groups):
-        outs = deconvolve(at, chans, sides, group, places, across, within, matrices, outs)
+    for at, (exact, above, below, left, strip, k) in enumerate(groups):
+        group = (exact, above, below, far, left, strip)
+        outs = deconvolve(at, (at, k), sides, group, across, within, matrices, outs)
     return tuple(outs)
 
 

time: 147 us -> 121 us (0.82); the launches traced: 145 us -> 121 us
  local copies, waits for them, and re-layouts: 16.7 us -> 3.67 us
  Pallas kernels: 56.9 us -> 51.5 us
  starting transfers between devices: 43.9 us -> 40.8 us
  waiting for transfers between devices: 26.2 us -> 23.6 us
    unnamed x68 -> x30, local copies, waits for them, and re-layouts: 16.5 us -> 3.49 us
    pallas_call x7 -> x6, Pallas kernels: 42.7 us -> 39.4 us  [the longest x3 35 us: deconvolve(): pl.pallas_call(functools.partial(deconvolve_kernel, places), grid=(1,), i...]
    ppermute x14 -> x13, starting transfers between devices: 43.9 us -> 40.8 us  [shift(): return lax.ppermute(block, axis, route)]
    ppermute x14 -> x13, waiting for transfers between devices: 26.2 us -> 23.6 us  [shift(): return lax.ppermute(block, axis, route)]
    pallas_call x2, Pallas kernels: 3.66 us -> 1.53 us  [edges(): pl.pallas_call(skipping(edges_kernel, 3, len(after)), grid=(n,), in_specs...]
  transfers between devices with their start and end apart: 14 -> 13, of which waited for: 7 -> 7; matrix products, arithmetic and copies ran while one was open for 0% -> 0% of each run, Pallas kernels for 28% -> 30%
where the time goes in v5:
time: 121 us
  Pallas kernels  51.5 us (43%)
  starting transfers between devices  40.8 us (34%)
  waiting for transfers between devices  23.6 us (20%)
  local copies, waits for them, and re-layouts  3.67 us (3%)
    ppermute x13, starting transfers between devices, shift(): return lax.ppermute(block, axis, route)  40.8 us
    pallas_call x3, Pallas kernels, deconvolve(): pl.pallas_call(functools.partial(deconvolve_kernel, places), grid=(1,), i...  35 us
    ppermute x13, waiting for transfers between devices, shift(): return lax.ppermute(block, axis, route)  23.6 us
    pallas_call x2, Pallas kernels, place(): pl.pallas_call(skipping(place_kernel, 2, len(after)), grid_spec=pltpu.Pre...  8.24 us
    pallas_call x3, Pallas kernels, join(): pl.pallas_call(functools.partial(join_kernel, at), in_specs=[pl.BlockSpec...  4.48 us
    unnamed x30, local copies, waits for them, and re-layouts  3.49 us
  transfers between devices with their start and end apart: 13, of which 7 were waited for; matrix products, arithmetic and copies ran while one was open for 0% of the time, Pallas kernels for 30%

profile of v5, /device:TPU:11, one launch (start us, length us, event | category | flops | bytes accessed | tf_op | source)
XLA Modules:
  0.0 120.9 jit_solution(17100262646633803269)
XLA Ops:
  0.6 1.8 %copy-done.2 = bf16[3,8,96,544]{3,2,1,0:T(8,128)(2,1)S(1)} copy-done((bf16[3,8,96,544]{3,2,1,0:T(8,128)(2,1)S(1)}, bf16[3,8,96,544]{3,2,1,0:T(8,128)(2,1)}, u32[]{:S(2)}) %copy-start.2) | copy-done | bytes 2506776
  3.1 3.2 %place.2 = (bf16[1,512,512]{2,1,0:T(8,128)(2,1)S(1)}, bf16[1,512,128]{2,1,0:T(8,128)(2,1)S(1)}, bf16[1,576,512]{2,1,0:T(8,128)(2,1)}) custom-call(s32[2]{0:T(128)S(1)} %bitcast.10, bf16[3,8,96,544]{3,2,1,0:T(8,128)(2,1)S(1)} %copy-done.2), custom_call_target="tpu_custom_call" | custom-call | flops 2000000000 | bytes 1 | tf_op jit(solution)/shard_map/place/pallas_call | solution.py:99
  6.3 3.2 %collective-permute-start.1 = (bf16[1,576,512]{2,1,0:T(8,128)(2,1)}, bf16[1,576,512]{2,1,0:T(8,128)(2,1)S(1)}, u32[]{:S(2)}, u32[]{:S(2)}) collective-permute-start(bf16[1,576,512]{2,1,0:T(8,128)(2,1)} %get-tuple-element.39), channel_id=1, source_target_pairs={{0,1},{1,2},{2,3},{4,5},{5,6},{6,7},{8,9},{9,10},{10,11},{12,13},{... | collective-permute-start | bytes 1769480 | tf_op jit(solution)/shard_map/ppermute | solution.py:549
  10.0 2.3 %bands.1 = (bf16[6,512,256]{2,1,0:T(8,128)(2,1)S(1)}, bf16[6,272,512]{2,1,0:T(8,128)(2,1)S(1)}) custom-call(f32[6,93]{1,0:T(8,128)S(1)} %reshape.20.refs_0_, bf16[1,512,128]{2,1,0:T(8,128)(2,1)S(1)} %get-tuple-element.33.refs_1_), custom_call_target="tpu_custom_call" | custom-call | flops 2000000000 | bytes 1 | tf_op jit(solution)/shard_map/bands/pallas_call | solution.py:258
  12.3 5.0 %place.3 = (bf16[2,512,512]{2,1,0:T(8,128)(2,1)S(1)}, bf16[2,512,128]{2,1,0:T(8,128)(2,1)S(1)}, bf16[2,576,512]{2,1,0:T(8,128)(2,1)}) custom-call(s32[2]{0:T(128)S(1)} %bitcast.11, bf16[3,8,96,544]{3,2,1,0:T(8,128)(2,1)S(1)} %copy-done.3, bf16[6,272,512]{2,1,0:T(8,128)(2,1)S(1)} %get-tuple-element.34.refs_2_), custom_call_target="tpu_custom_call" | custom-call | flops 4000000000 | bytes 1 | tf_op jit(solution)/shard_map/place/pallas_call | solution.py:99
  17.4 3.2 %collective-permute-start = (bf16[2,576,512]{2,1,0:T(8,128)(2,1)}, bf16[2,576,512]{2,1,0:T(8,128)(2,1)S(1)}, u32[]{:S(2)}, u32[]{:S(2)}) collective-permute-start(bf16[2,576,512]{2,1,0:T(8,128)(2,1)} %get-tuple-element.36), channel_id=1, source_target_pairs={{0,1},{1,2},{2,3},{4,5},{5,6},{6,7},{8,9},{9,10},{10,11},{12,13},{... | collective-permute-start | bytes 3538952 | tf_op jit(solution)/shard_map/ppermute | solution.py:549
  20.6 2.0 %collective-permute-done.1.refs_2_.low_ref = bf16[1,576,512]{2,1,0:T(8,128)(2,1)S(1)} collective-permute-done((bf16[1,576,512]{2,1,0:T(8,128)(2,1)}, bf16[1,576,512]{2,1,0:T(8,128)(2,1)S(1)}, u32[]{:S(2)}, u32[]{:S(2)}) %collective-permute-start.1) | collective-permute-done | bytes 589856 | tf_op jit(solution)/shard_map/ppermute | solution.py:549
  22.6 1.0 edges.2
  23.6 5.7 %collective-permute-start.2 = (bf16[1,1024,128]{2,1,0:T(8,128)(2,1)}, bf16[1,1024,128]{2,1,0:T(8,128)(2,1)}, u32[]{:S(2)}, u32[]{:S(2)}) collective-permute-start(bf16[1,1024,128]{2,1,0:T(8,128)(2,1)} %get-tuple-element.40.mine_ref), channel_id=1, source_target_pairs={{0,4},{4,8},{8,12},{12,16},{16,20},{20,24},{24,28},{1,5},{5,9},{9,... | collective-permute-start | bytes 786440 | tf_op jit(solution)/shard_map/ppermute | solution.py:549
  29.3 1.9 %collective-permute-start.3 = (bf16[1,1024,128]{2,1,0:T(8,128)(2,1)}, bf16[1,1024,128]{2,1,0:T(8,128)(2,1)}, u32[]{:S(2)}, u32[]{:S(2)}) collective-permute-start(bf16[1,1024,128]{2,1,0:T(8,128)(2,1)} %get-tuple-element.41), channel_id=1, source_target_pairs={{4,0},{8,4},{12,8},{16,12},{20,16},{24,20},{28,24},{5,1},{9,5},{13... | collective-permute-start | bytes 786440 | tf_op jit(solution)/shard_map/ppermute | solution.py:549
  31.3 1.6 %collective-permute-done.2.left_ref = bf16[1,1024,128]{2,1,0:T(8,128)(2,1)} collective-permute-done((bf16[1,1024,128]{2,1,0:T(8,128)(2,1)}, bf16[1,1024,128]{2,1,0:T(8,128)(2,1)}, u32[]{:S(2)}, u32[]{:S(2)}) %collective-permute-start.2) | collective-permute-done | bytes 262176 | tf_op jit(solution)/shard_map/ppermute | solution.py:549
  32.9 5.3 %collective-permute-done.3.right_ref = bf16[1,1024,128]{2,1,0:T(8,128)(2,1)} collective-permute-done((bf16[1,1024,128]{2,1,0:T(8,128)(2,1)}, bf16[1,1024,128]{2,1,0:T(8,128)(2,1)}, u32[]{:S(2)}, u32[]{:S(2)}) %collective-permute-start.3) | collective-permute-done | bytes 262176 | tf_op jit(solution)/shard_map/ppermute | solution.py:549
  38.2 1.9 %join.3 = (f32[1,512,512]{2,1,0:T(8,128)S(1)}, bf16[1,512,128]{2,1,0:T(8,128)(2,1)S(1)}, bf16[1,528,640]{2,1,0:T(8,128)(2,1)S(1)}, bf16[1,32,640]{2,1,0:T(8,128)(2,1)S(1)}) custom-call(s32[4]{0:T(128)S(1)} %add_convert_fusion.sides_ref, bf16[1,512,512]{2,1,0:T(8,128)(2,1)S(1)} %get-tuple-element.38.refs_0_.own_ref, ...), custom_call_target="tpu_custom_call" | custom-call | flops 1 | bytes 1 | tf_op jit(solution)/shard_map/join/pallas_call | solution.py:211
  40.1 7.8 %collective-permute-done.refs_2_.low_ref = bf16[2,576,512]{2,1,0:T(8,128)(2,1)S(1)} collective-permute-done((bf16[2,576,512]{2,1,0:T(8,128)(2,1)}, bf16[2,576,512]{2,1,0:T(8,128)(2,1)S(1)}, u32[]{:S(2)}, u32[]{:S(2)}) %collective-permute-start) | collective-permute-done | bytes 1179680 | tf_op jit(solution)/shard_map/ppermute | solution.py:549
  47.9 0.9 copy-done.1
  49.4 4.6 %collective-permute-start.4 = (bf16[2,1024,128]{2,1,0:T(8,128)(2,1)S(1)}, bf16[2,1024,128]{2,1,0:T(8,128)(2,1)S(1)}, u32[]{:S(2)}, u32[]{:S(2)}) collective-permute-start(bf16[2,1024,128]{2,1,0:T(8,128)(2,1)S(1)} %get-tuple-element.43.mine_ref), channel_id=1, source_target_pairs={{0,4},{4,8},{8,12},{12,16},{16,20},{20,24},{24,28},{1,5},{5,9},{9,... | collective-permute-start | bytes 1572872 | tf_op jit(solution)/shard_map/ppermute | solution.py:549
  54.0 1.9 %collective-permute-start.5 = (bf16[2,1024,128]{2,1,0:T(8,128)(2,1)S(1)}, bf16[2,1024,128]{2,1,0:T(8,128)(2,1)S(1)}, u32[]{:S(2)}, u32[]{:S(2)}) collective-permute-start(bf16[2,1024,128]{2,1,0:T(8,128)(2,1)S(1)} %get-tuple-element.44), channel_id=1, source_target_pairs={{4,0},{8,4},{12,8},{16,12},{20,16},{24,20},{28,24},{5,1},{9,5},{13... | collective-permute-start | bytes 1572872 | tf_op jit(solution)/shard_map/ppermute | solution.py:549
  55.9 3.2 %collective-permute-start.11 = (bf16[1,528,640]{2,1,0:T(8,128)(2,1)S(1)}, bf16[1,528,640]{2,1,0:T(8,128)(2,1)S(1)}, u32[]{:S(2)}, u32[]{:S(2)}) collective-permute-start(bf16[1,528,640]{2,1,0:T(8,128)(2,1)S(1)} %get-tuple-element.42.refs_3_), channel_id=1, source_target_pairs={{0,1},{1,2},{2,3},{4,5},{5,6},{6,7},{8,9},{9,10},{10,11},{12,13},{... | collective-permute-start | bytes 2027528 | tf_op jit(solution)/shard_map/ppermute | solution.py:549
  59.1 2.1 %collective-permute-start.12 = (bf16[1,528,640]{2,1,0:T(8,128)(2,1)S(1)}, bf16[1,528,640]{2,1,0:T(8,128)(2,1)S(1)}, u32[]{:S(2)}, u32[]{:S(2)}) collective-permute-start(bf16[1,528,640]{2,1,0:T(8,128)(2,1)S(1)} %get-tuple-element.42.refs_3_), channel_id=1, source_target_pairs={{1,0},{2,1},{3,2},{5,4},{6,5},{7,6},{9,8},{10,9},{11,10},{13,12},{... | collective-permute-start | bytes 2027528 | tf_op jit(solution)/shard_map/ppermute | solution.py:549
  61.2 1.6 %collective-permute-done.4.left_ref = bf16[2,1024,128]{2,1,0:T(8,128)(2,1)S(1)} collective-permute-done((bf16[2,1024,128]{2,1,0:T(8,128)(2,1)S(1)}, bf16[2,1024,128]{2,1,0:T(8,128)(2,1)S(1)}, u32[]{:S(2)}, u32[]{:S(2)}) %collective-permute-start.4) | collective-permute-done | bytes 524320 | tf_op jit(solution)/shard_map/ppermute | solution.py:549
  62.9 4.5 %collective-permute-done.5.right_ref = bf16[2,1024,128]{2,1,0:T(8,128)(2,1)S(1)} collective-permute-done((bf16[2,1024,128]{2,1,0:T(8,128)(2,1)S(1)}, bf16[2,1024,128]{2,1,0:T(8,128)(2,1)S(1)}, u32[]{:S(2)}, u32[]{:S(2)}) %collective-permute-start.5) | collective-permute-done | bytes 524320 | tf_op jit(solution)/shard_map/ppermute | solution.py:549
  67.3 1.3 %join.5 = (f32[1,512,512]{2,1,0:T(8,128)S(1)}, bf16[1,512,128]{2,1,0:T(8,128)(2,1)S(1)}, bf16[1,528,640]{2,1,0:T(8,128)(2,1)S(1)}, bf16[1,32,640]{2,1,0:T(8,128)(2,1)S(1)}) custom-call(s32[4]{0:T(128)S(1)} %add_convert_fusion.sides_ref, bf16[2,512,512]{2,1,0:T(8,128)(2,1)S(1)} %get-tuple-element.35.refs_0_.own_ref, ...), custom_call_target="tpu_custom_call" | custom-call | flops 1 | bytes 1 | tf_op jit(solution)/shard_map/join/pallas_call | solution.py:211
  68.7 1.3 %join.4 = (f32[1,512,512]{2,1,0:T(8,128)S(1)}, bf16[1,512,128]{2,1,0:T(8,128)(2,1)S(1)}, bf16[1,528,640]{2,1,0:T(8,128)(2,1)S(1)}, bf16[1,32,640]{2,1,0:T(8,128)(2,1)S(1)}) custom-call(s32[4]{0:T(128)S(1)} %add_convert_fusion.sides_ref, bf16[2,512,512]{2,1,0:T(8,128)(2,1)S(1)} %get-tuple-element.35.refs_0_.own_ref, ...), custom_call_target="tpu_custom_call" | custom-call | flops 1 | bytes 1 | tf_op jit(solution)/shard_map/join/pallas_call | solution.py:211
  70.0 4.2 %collective-permute-start.8 = (bf16[3,32,640]{2,1,0:T(8,128)(2,1)S(1)}, bf16[3,32,640]{2,1,0:T(8,128)(2,1)S(1)}, u32[]{:S(2)}, u32[]{:S(2)}) collective-permute-start(bf16[3,32,640]{2,1,0:T(8,128)(2,1)S(1)} %pad_maximum_fusion), channel_id=1, source_target_pairs={{0,2},{1,3},{4,6},{5,7},{8,10},{9,11},{12,14},{13,15},{16,18},{17,... | collective-permute-start | bytes 368648 | tf_op jit(solution)/shard_map/ppermute | solution.py:549
  74.3 2.1 %collective-permute-start.10 = (bf16[1,528,640]{2,1,0:T(8,128)(2,1)S(1)}, bf16[1,528,640]{2,1,0:T(8,128)(2,1)S(1)}, u32[]{:S(2)}, u32[]{:S(2)}) collective-permute-start(bf16[1,528,640]{2,1,0:T(8,128)(2,1)S(1)} %get-tuple-element.53), channel_id=1, source_target_pairs={{1,0},{2,1},{3,2},{5,4},{6,5},{7,6},{9,8},{10,9},{11,10},{13,12},{... | collective-permute-start | bytes 2027528 | tf_op jit(solution)/shard_map/ppermute | solution.py:549
  76.3 3.2 %collective-permute-start.9 = (bf16[1,528,640]{2,1,0:T(8,128)(2,1)S(1)}, bf16[1,528,640]{2,1,0:T(8,128)(2,1)S(1)}, u32[]{:S(2)}, u32[]{:S(2)}) collective-permute-start(bf16[1,528,640]{2,1,0:T(8,128)(2,1)S(1)} %get-tuple-element.53), channel_id=1, source_target_pairs={{0,1},{1,2},{2,3},{4,5},{5,6},{6,7},{8,9},{9,10},{10,11},{12,13},{... | collective-permute-start | bytes 2027528 | tf_op jit(solution)/shard_map/ppermute | solution.py:549
  79.6 1.9 %collective-permute-start.6 = (bf16[1,528,640]{2,1,0:T(8,128)(2,1)S(1)}, bf16[1,528,640]{2,1,0:T(8,128)(2,1)S(1)}, u32[]{:S(2)}, u32[]{:S(2)}) collective-permute-start(bf16[1,528,640]{2,1,0:T(8,128)(2,1)S(1)} %get-tuple-element.46), channel_id=1, source_target_pairs={{0,1},{1,2},{2,3},{4,5},{5,6},{6,7},{8,9},{9,10},{10,11},{12,13},{... | collective-permute-start | bytes 2027528 | tf_op jit(solution)/shard_map/ppermute | solution.py:549
  81.5 3.6 %collective-permute-start.7 = (bf16[1,528,640]{2,1,0:T(8,128)(2,1)S(1)}, bf16[1,528,640]{2,1,0:T(8,128)(2,1)S(1)}, u32[]{:S(2)}, u32[]{:S(2)}) collective-permute-start(bf16[1,528,640]{2,1,0:T(8,128)(2,1)S(1)} %get-tuple-element.46), channel_id=1, source_target_pairs={{1,0},{2,1},{3,2},{5,4},{6,5},{7,6},{9,8},{10,9},{11,10},{13,12},{... | collective-permute-start | bytes 2027528 | tf_op jit(solution)/shard_map/ppermute | solution.py:549
  85.2 11.8 %deconvolve.3 = (f32[3,8,64,512]{3,2,1,0:T(8,128)}, f32[3,4,32,256]{3,2,1,0:T(8,128)}, f32[3,2,16,128]{3,2,1,0:T(8,128)}) custom-call(s32[4]{0:T(128)S(1)} %add_convert_fusion.sides_ref, f32[1,512,512]{2,1,0:T(8,128)S(1)} %get-tuple-element.55.exact_ref, bf16[1,528,640]{2,1,0:T(8,128)(2,1)S(1)} %collective-permute-done.11.above_ref, ...), custom_call_target="tpu_custom_call" | custom-call | flops 10000000000 | bytes 1 | tf_op jit(solution)/shard_map/deconvolve/pallas_call | solution.py:514
  97.0 11.7 %deconvolve.4 = (f32[3,8,64,512]{3,2,1,0:T(8,128)}, f32[3,4,32,256]{3,2,1,0:T(8,128)}, f32[3,2,16,128]{3,2,1,0:T(8,128)}) custom-call(s32[4]{0:T(128)S(1)} %add_convert_fusion.sides_ref, f32[1,512,512]{2,1,0:T(8,128)S(1)} %get-tuple-element.52.exact_ref, ...), custom_call_target="tpu_custom_call", output_to_operand_aliasing={{0}: (13, {}), {1}: (14, {}), {2}: (15, {})} | custom-call | flops 10000000000 | bytes 1 | tf_op jit(solution)/shard_map/deconvolve/pallas_call | solution.py:514
  108.7 0.7 collective-permute-done.6.above_ref
  109.4 11.4 %deconvolve.5 = (f32[3,8,64,512]{3,2,1,0:T(8,128)}, f32[3,4,32,256]{3,2,1,0:T(8,128)}, f32[3,2,16,128]{3,2,1,0:T(8,128)}) custom-call(s32[4]{0:T(128)S(1)} %add_convert_fusion.sides_ref, f32[1,512,512]{2,1,0:T(8,128)S(1)} %get-tuple-element.45.exact_ref, ...), custom_call_target="tpu_custom_call", output_to_operand_aliasing={{0}: (13, {}), {1}: (14, {}), {2}: (15, {})} | custom-call | flops 10000000000 | bytes 1 | tf_op jit(solution)/shard_map/deconvolve/pallas_call | solution.py:514
  (44 shorter events, 1.8 us)
Async XLA Ops:
  0.6 1.8 %copy-start.2 = (bf16[3,8,96,544]{3,2,1,0:T(8,128)(2,1)S(1)}, bf16[3,8,96,544]{3,2,1,0:T(8,128)(2,1)}, u32[]{:S(2)}) copy-start(bf16[3,8,96,544]{3,2,1,0:T(8,128)(2,1)} %refs_1_.3) | copy-start | bytes 7520260
  2.5 0.7 copy-start.4
  3.1 6.4 %copy-start.14 = (f32[3,3,31]{2,1,0:T(4,128)S(1)}, f32[3,3,31]{2,1,0:T(4,128)}, u32[]{:S(2)}) copy-start(f32[3,3,31]{2,1,0:T(4,128)} %param.9) | copy-start | bytes 3352
  6.3 16.3 %collective-permute-start.1 = (bf16[1,576,512]{2,1,0:T(8,128)(2,1)}, bf16[1,576,512]{2,1,0:T(8,128)(2,1)S(1)}, u32[]{:S(2)}, u32[]{:S(2)}) collective-permute-start(bf16[1,576,512]{2,1,0:T(8,128)(2,1)} %get-tuple-element.39), channel_id=1, source_target_pairs={{0,1},{1,2},{2,3},{4,5},{5,6},{6,7},{8,9},{9,10},{10,11},{12,13},{... | collective-permute-start | bytes 1769480 | tf_op jit(solution)/shard_map/ppermute | solution.py:549
  10.0 2.3 %copy-start.3 = (bf16[3,8,96,544]{3,2,1,0:T(8,128)(2,1)S(1)}, bf16[3,8,96,544]{3,2,1,0:T(8,128)(2,1)}, u32[]{:S(2)}) copy-start(bf16[3,8,96,544]{3,2,1,0:T(8,128)(2,1)} %refs_1_.3) | copy-start | bytes 7520260
  10.0 2.3 %copy-start.5 = (s32[1,1,2]{2,1,0:T(1,128)S(1)}, s32[1,1,2]{2,1,0:T(1,128)}, u32[]{:S(2)}) copy-start(s32[1,1,2]{2,1,0:T(1,128)} %param.8) | copy-start | bytes 28
  12.3 5.1 %copy-start.6 = (bf16[6,272,512]{2,1,0:T(8,128)(2,1)}, bf16[6,272,512]{2,1,0:T(8,128)(2,1)S(1)}, u32[]{:S(2)}) copy-start(bf16[6,272,512]{2,1,0:T(8,128)(2,1)S(1)} %get-tuple-element.34.refs_2_) | copy-start | bytes 5013508
  12.3 5.1 %copy-start.8 = (bf16[6,512,256]{2,1,0:T(8,128)(2,1)}, bf16[6,512,256]{2,1,0:T(8,128)(2,1)S(1)}, u32[]{:S(2)}) copy-start(bf16[6,512,256]{2,1,0:T(8,128)(2,1)S(1)} %get-tuple-element.51) | copy-start | bytes 4718596
  17.4 6.2 %copy-start = (bf16[2,512,128]{2,1,0:T(8,128)(2,1)}, bf16[2,512,128]{2,1,0:T(8,128)(2,1)S(1)}, u32[]{:S(2)}) copy-start(bf16[2,512,128]{2,1,0:T(8,128)(2,1)S(1)} %get-tuple-element.37.refs_3_.refs_1_) | copy-start | bytes 786436
  17.4 30.5 %collective-permute-start = (bf16[2,576,512]{2,1,0:T(8,128)(2,1)}, bf16[2,576,512]{2,1,0:T(8,128)(2,1)S(1)}, u32[]{:S(2)}, u32[]{:S(2)}) collective-permute-start(bf16[2,576,512]{2,1,0:T(8,128)(2,1)} %get-tuple-element.36), channel_id=1, source_target_pairs={{0,1},{1,2},{2,3},{4,5},{5,6},{6,7},{8,9},{9,10},{10,11},{12,13},{... | collective-permute-start | bytes 3538952 | tf_op jit(solution)/shard_map/ppermute | solution.py:549
  23.6 9.3 %collective-permute-start.2 = (bf16[1,1024,128]{2,1,0:T(8,128)(2,1)}, bf16[1,1024,128]{2,1,0:T(8,128)(2,1)}, u32[]{:S(2)}, u32[]{:S(2)}) collective-permute-start(bf16[1,1024,128]{2,1,0:T(8,128)(2,1)} %get-tuple-element.40.mine_ref), channel_id=1, source_target_pairs={{0,4},{4,8},{8,12},{12,16},{16,20},{20,24},{24,28},{1,5},{5,9},{9,... | collective-permute-start | bytes 786440 | tf_op jit(solution)/shard_map/ppermute | solution.py:549
  29.3 8.9 %collective-permute-start.3 = (bf16[1,1024,128]{2,1,0:T(8,128)(2,1)}, bf16[1,1024,128]{2,1,0:T(8,128)(2,1)}, u32[]{:S(2)}, u32[]{:S(2)}) collective-permute-start(bf16[1,1024,128]{2,1,0:T(8,128)(2,1)} %get-tuple-element.41), channel_id=1, source_target_pairs={{4,0},{8,4},{12,8},{16,12},{20,16},{24,20},{28,24},{5,1},{9,5},{13... | collective-permute-start | bytes 786440 | tf_op jit(solution)/shard_map/ppermute | solution.py:549
  47.9 1.0 copy-start.1
  49.4 13.5 %collective-permute-start.4 = (bf16[2,1024,128]{2,1,0:T(8,128)(2,1)S(1)}, bf16[2,1024,128]{2,1,0:T(8,128)(2,1)S(1)}, u32[]{:S(2)}, u32[]{:S(2)}) collective-permute-start(bf16[2,1024,128]{2,1,0:T(8,128)(2,1)S(1)} %get-tuple-element.43.mine_ref), channel_id=1, source_target_pairs={{0,4},{4,8},{8,12},{12,16},{16,20},{20,24},{24,28},{1,5},{5,9},{9,... | collective-permute-start | bytes 1572872 | tf_op jit(solution)/shard_map/ppermute | solution.py:549
  54.0 13.4 %collective-permute-start.5 = (bf16[2,1024,128]{2,1,0:T(8,128)(2,1)S(1)}, bf16[2,1024,128]{2,1,0:T(8,128)(2,1)S(1)}, u32[]{:S(2)}, u32[]{:S(2)}) collective-permute-start(bf16[2,1024,128]{2,1,0:T(8,128)(2,1)S(1)} %get-tuple-element.44), channel_id=1, source_target_pairs={{4,0},{8,4},{12,8},{16,12},{20,16},{24,20},{28,24},{5,1},{9,5},{13... | collective-permute-start | bytes 1572872 | tf_op jit(solution)/shard_map/ppermute | solution.py:549
  55.9 23.7 %collective-permute-start.11 = (bf16[1,528,640]{2,1,0:T(8,128)(2,1)S(1)}, bf16[1,528,640]{2,1,0:T(8,128)(2,1)S(1)}, u32[]{:S(2)}, u32[]{:S(2)}) collective-permute-start(bf16[1,528,640]{2,1,0:T(8,128)(2,1)S(1)} %get-tuple-element.42.refs_3_), channel_id=1, source_target_pairs={{0,1},{1,2},{2,3},{4,5},{5,6},{6,7},{8,9},{9,10},{10,11},{12,13},{... | collective-permute-start | bytes 2027528 | tf_op jit(solution)/shard_map/ppermute | solution.py:549
  59.1 22.4 %collective-permute-start.12 = (bf16[1,528,640]{2,1,0:T(8,128)(2,1)S(1)}, bf16[1,528,640]{2,1,0:T(8,128)(2,1)S(1)}, u32[]{:S(2)}, u32[]{:S(2)}) collective-permute-start(bf16[1,528,640]{2,1,0:T(8,128)(2,1)S(1)} %get-tuple-element.42.refs_3_), channel_id=1, source_target_pairs={{1,0},{2,1},{3,2},{5,4},{6,5},{7,6},{9,8},{10,9},{11,10},{13,12},{... | collective-permute-start | bytes 2027528 | tf_op jit(solution)/shard_map/ppermute | solution.py:549
  67.3 17.8 %copy-start.12 = (bf16[384,128]{1,0:T(8,128)(2,1)S(1)}, bf16[384,128]{1,0:T(8,128)(2,1)}, u32[]{:S(2)}) copy-start(bf16[384,128]{1,0:T(8,128)(2,1)} %constant.27.clone.two_x_ref) | copy-start | bytes 294916
  68.6 16.5 %copy-start.7 = (bf16[6,272,512]{2,1,0:T(8,128)(2,1)S(1)}, bf16[6,272,512]{2,1,0:T(8,128)(2,1)}, u32[]{:S(2)}) copy-start(bf16[6,272,512]{2,1,0:T(8,128)(2,1)} %copy-done.6) | copy-start | bytes 5013508
  68.6 16.5 %copy-start.9 = (bf16[6,512,256]{2,1,0:T(8,128)(2,1)S(1)}, bf16[6,512,256]{2,1,0:T(8,128)(2,1)}, u32[]{:S(2)}) copy-start(bf16[6,512,256]{2,1,0:T(8,128)(2,1)} %copy-done.8) | copy-start | bytes 4718596
  68.7 16.5 %copy-start.10 = (bf16[768,384]{1,0:T(8,128)(2,1)S(1)}, bf16[768,384]{1,0:T(8,128)(2,1)}, u32[]{:S(2)}) copy-start(bf16[768,384]{1,0:T(8,128)(2,1)} %constant.25.clone.one_x_ref) | copy-start | bytes 1769476
  68.7 16.5 %copy-start.11 = (bf16[144,592]{1,0:T(8,128)(2,1)S(1)}, bf16[144,592]{1,0:T(8,128)(2,1)}, u32[]{:S(2)}) copy-start(bf16[144,592]{1,0:T(8,128)(2,1)} %constant.26.clone.one_zy_ref) | copy-start | bytes 511492
  68.7 16.5 %copy-start.13 = (bf16[32,144]{1,0:T(8,128)(2,1)S(1)}, bf16[32,144]{1,0:T(8,128)(2,1)}, u32[]{:S(2)}) copy-start(bf16[32,144]{1,0:T(8,128)(2,1)} %constant.28.clone.two_zy_ref) | copy-start | bytes 27652
  70.0 15.1 %collective-permute-start.8 = (bf16[3,32,640]{2,1,0:T(8,128)(2,1)S(1)}, bf16[3,32,640]{2,1,0:T(8,128)(2,1)S(1)}, u32[]{:S(2)}, u32[]{:S(2)}) collective-permute-start(bf16[3,32,640]{2,1,0:T(8,128)(2,1)S(1)} %pad_maximum_fusion), channel_id=1, source_target_pairs={{0,2},{1,3},{4,6},{5,7},{8,10},{9,11},{12,14},{13,15},{16,18},{17,... | collective-permute-start | bytes 368648 | tf_op jit(solution)/shard_map/ppermute | solution.py:549
  74.3 22.8 %collective-permute-start.10 = (bf16[1,528,640]{2,1,0:T(8,128)(2,1)S(1)}, bf16[1,528,640]{2,1,0:T(8,128)(2,1)S(1)}, u32[]{:S(2)}, u32[]{:S(2)}) collective-permute-start(bf16[1,528,640]{2,1,0:T(8,128)(2,1)S(1)} %get-tuple-element.53), channel_id=1, source_target_pairs={{1,0},{2,1},{3,2},{5,4},{6,5},{7,6},{9,8},{10,9},{11,10},{13,12},{... | collective-permute-start | bytes 2027528 | tf_op jit(solution)/shard_map/ppermute | solution.py:549
  76.3 20.7 %collective-permute-start.9 = (bf16[1,528,640]{2,1,0:T(8,128)(2,1)S(1)}, bf16[1,528,640]{2,1,0:T(8,128)(2,1)S(1)}, u32[]{:S(2)}, u32[]{:S(2)}) collective-permute-start(bf16[1,528,640]{2,1,0:T(8,128)(2,1)S(1)} %get-tuple-element.53), channel_id=1, source_target_pairs={{0,1},{1,2},{2,3},{4,5},{5,6},{6,7},{8,9},{9,10},{10,11},{12,13},{... | collective-permute-start | bytes 2027528 | tf_op jit(solution)/shard_map/ppermute | solution.py:549
  79.6 29.9 %collective-permute-start.6 = (bf16[1,528,640]{2,1,0:T(8,128)(2,1)S(1)}, bf16[1,528,640]{2,1,0:T(8,128)(2,1)S(1)}, u32[]{:S(2)}, u32[]{:S(2)}) collective-permute-start(bf16[1,528,640]{2,1,0:T(8,128)(2,1)S(1)} %get-tuple-element.46), channel_id=1, source_target_pairs={{0,1},{1,2},{2,3},{4,5},{5,6},{6,7},{8,9},{9,10},{10,11},{12,13},{... | collective-permute-start | bytes 2027528 | tf_op jit(solution)/shard_map/ppermute | solution.py:549
  81.5 27.9 %collective-permute-start.7 = (bf16[1,528,640]{2,1,0:T(8,128)(2,1)S(1)}, bf16[1,528,640]{2,1,0:T(8,128)(2,1)S(1)}, u32[]{:S(2)}, u32[]{:S(2)}) collective-permute-start(bf16[1,528,640]{2,1,0:T(8,128)(2,1)S(1)} %get-tuple-element.46), channel_id=1, source_target_pairs={{1,0},{2,1},{3,2},{5,4},{6,5},{7,6},{9,8},{10,9},{11,10},{13,12},{... | collective-permute-start | bytes 2027528 | tf_op jit(solution)/shard_map/ppermute | solution.py:549

commit v6 on v5

--- a/solution.py
+++ b/solution.py
@@ -131,20 +131,21 @@
     own = own_ref[0, :, cols - LANE :].astype(F32)
     low = low_ref[0, :rows, cols - LANE :].astype(F32)
     to_right_ref[0, rows:] = ((own + low) / (seen(own) + seen(low))).astype(BF16)
-    to_left_ref[0, :rows] = own_ref[0, :, :LANE]
-    to_left_ref[0, rows:] = low_ref[0, :rows, :LANE]
+    own = own_ref[0, :, :LANE].astype(F32)
+    low = pltpu.roll(low_ref[0, :rows, :LANE].astype(F32), LANE // 2, 1)
+    to_left_ref[0] = jnp.where(lanes(rows) < LANE // 2, own, low).astype(BF16)
 
 
 def edges(own, right, low, after):
     n, rows, _ = own.shape
     block = lambda r, c: pl.BlockSpec((1, r, c), lambda i: (i, 0, 0))
-    out = (2 * rows, LANE)
+    outs = ((2 * rows, LANE), (rows, LANE))
     return pl.pallas_call(
         skipping(edges_kernel, 3, len(after)),
         grid=(n,),
         in_specs=[block(*a.shape[1:]) for a in (own, right, low)] + [ANY] * len(after),
-        out_specs=[block(*out)] * 2,
-        out_shape=[jax.ShapeDtypeStruct((n,) + out, BF16)] * 2,
+        out_specs=[block(*out) for out in outs],
+        out_shape=[jax.ShapeDtypeStruct((n,) + out, BF16) for out in outs],
         compiler_params=params(16),
         cost_estimate=cost(4e10 if own.shape[0] == 1 else 1, 1),
         name="edges",
@@ -155,7 +156,7 @@
 
 
 def join_kernel(
-    at, sides_ref, own_ref, low_ref, mine_ref, left_ref, right_ref, exact_ref, strip_ref, out_ref, tail_ref
+    at, sides_ref, own_ref, low_ref, mine_ref, left_ref, right_ref, exact_ref, out_ref, tail_ref
 ):
     rows, cols = own_ref.shape[1:]
     own_ref, low_ref, mine_ref, left_ref, right_ref = (
@@ -180,12 +181,10 @@
     out_ref[0, :rows, LANE:cols] = rest.astype(BF16)
 
     a, b = parts(mine_ref)
-    own = right_ref[0, :rows].astype(F32)
-    low = right_ref[0, rows:].astype(F32)
+    own, low = parts(right_ref)
     count = seen(own) + seen(low) + seen(a) + seen(b)
     strip = (own + low + a + b) / jnp.maximum(count, 1.0)
     strip = jnp.where(sides_ref[3] > 0, strip, 0.0)
-    strip_ref[0] = strip.astype(BF16)
 
     left = left_ref[0, rows:]
     out_ref[0, :rows, cols:] = jnp.where(lanes(rows) < SIDE, strip, left.astype(F32)).astype(BF16)
@@ -204,14 +203,13 @@
     extra = 2 * DEPTH
     sizes = (
         (rows, cols, F32),
-        (rows, LANE, BF16),
         (rows + extra, cols + LANE, BF16),
         (2 * extra, cols + LANE, BF16),
     )
     return pl.pallas_call(
         functools.partial(join_kernel, at),
         in_specs=[pl.BlockSpec(memory_space=pltpu.SMEM)] + [VMEM] * 5,
-        out_specs=[VMEM] * 4,
+        out_specs=[VMEM] * 3,
         out_shape=[jax.ShapeDtypeStruct((1, r, c), t) for r, c, t in sizes],
         compiler_params=params(12),
         cost_estimate=cost(1, 1),
@@ -219,7 +217,7 @@
     )(sides, own, low, mine, left, right)
 
 
-def bands_kernel(kern_ref, across_ref, within_ref):
+def bands_kernel(kern_ref, across_ref, within_ref, corner_ref):
     which = pl.program_id(0)
     wide = 3 * 2 * LANE
     shape = (16, wide)
@@ -233,6 +231,15 @@
     for q in range(across_ref.shape[1] // 16):
         turned = pltpu.roll(base, (wide - 4 * LANE + 16 * q) % wide, 1)
         across_ref[0, 16 * q : 16 * (q + 1), :] = turned[:, : 2 * LANE].astype(BF16)
+
+    at, to = 3 * LANE - LANE - (LANE - SIDE) - 1, LANE - (BEFORE - REACH)
+    row = lax.broadcasted_iota(jnp.int32, (3 * LANE, LANE), 0)
+    lane = lanes(3 * LANE)
+    band = across_ref[0, : 3 * LANE, :LANE].astype(F32)
+    corner_ref[0, : 3 * LANE] = jnp.where((row == at) & (lane == to), 0.0, band).astype(BF16)
+    row = lax.broadcasted_iota(jnp.int32, (LANE, LANE), 0)
+    lone = (row == SIDE - 1) & (lanes(LANE) == to)
+    corner_ref[0, 3 * LANE :] = jnp.where(lone, kern_ref[which, 2 * TAPS], 0.0).astype(BF16)
 
     shape = (16, within_ref.shape[2])
     row = lax.broadcasted_iota(jnp.int32, shape, 0)
@@ -254,7 +261,11 @@
 
 def bands(kern, after):
     count = kern.shape[0]
-    shapes = ((4 * LANE, 2 * LANE), (BIG * DEPTH, (BIG + 2 * REACH) * DEPTH))
+    shapes = (
+        (4 * LANE, 2 * LANE),
+        (BIG * DEPTH, (BIG + 2 * REACH) * DEPTH),
+        (4 * LANE, LANE),
+    )
     return pl.pallas_call(
         skipping(bands_kernel, 1, len(after)),
         grid=(count,),
@@ -272,11 +283,11 @@
     half_x, half_y, half_z = cols // 2, rows // 2, depth // 2
     taps = np.array(GAUSS, np.float32) / 16
     extra_x = (-2, -1, half_x)
-    one_x = np.zeros((cols + 2 * LANE, half_x + LANE), np.float32)
+    one_x = np.zeros((cols + LANE, half_x + LANE), np.float32)
     for lane in range(half_x + len(extra_x)):
         x = lane if lane < half_x else extra_x[lane - half_x]
         for k in range(5):
-            one_x[LANE + 2 * x + k - 2, lane] = taps[k]
+            one_x[(2 * x + k - 2) % (cols + LANE), lane] = taps[k]
     extra_y = (-2, -1, half_y)
     order = [(z, y) for z in range(half_z) for y in range(half_y)]
     order += [(z, y) for y in extra_y for z in range(half_z)]
@@ -308,16 +319,16 @@
 
 
 def deconvolve_kernel(
-    places,
+    at,
     sides_ref,
     exact_ref,
+    message_ref,
     above_ref,
     below_ref,
     far_ref,
-    left_ref,
-    right_ref,
     across_ref,
     within_ref,
+    corner_ref,
     one_x_ref,
     one_zy_ref,
     two_x_ref,
@@ -326,21 +337,20 @@
 ):
     if len(others) > 11:
         others = others[3:]
-    at, k = places
     far_ref = far_ref.at[at : at + 1]
-    left_ref = left_ref.at[k : k + 1]
+    corner_ref = corner_ref.at[at : at + 1]
     across_ref = across_ref.at[at : at + 1]
     within_ref = within_ref.at[at : at + 1]
     deconvolve_body(
         sides_ref,
         exact_ref,
+        message_ref,
         above_ref,
         below_ref,
         far_ref,
-        left_ref,
-        right_ref,
         across_ref,
         within_ref,
+        corner_ref,
         one_x_ref,
         one_zy_ref,
         two_x_ref,
@@ -352,13 +362,13 @@
 def deconvolve_body(
     sides_ref,
     exact_ref,
+    message_ref,
     above_ref,
     below_ref,
     far_ref,
-    left_ref,
-    right_ref,
     across_ref,
     within_ref,
+    corner_ref,
     one_x_ref,
     one_zy_ref,
     two_x_ref,
@@ -376,60 +386,65 @@
     low,
 ):
     rows8, cols = exact_ref.shape[1:]
-    wide = cols + 2 * LANE
+    wide = cols + LANE
     far8 = far_ref.shape[1] // 2
-    own = slice(far8 + rows8, far8 + 2 * rows8)
     frame8 = far8 + 3 * rows8
-    middle = slice(LANE, LANE + cols)
-    after = slice(LANE + cols, wide)
-
-    extra = far8
-    lane = lax.broadcasted_iota(jnp.int32, (extra, LANE), 1)
-    pick = jnp.where(lane == SIDE - 1, 1.0, 0.0).astype(BF16)
+
+    pick = jnp.where(lanes(far8) == SIDE - 1, 1.0, 0.0).astype(BF16)
 
     def unpack(source, count, begin):
         to = slice(begin, begin + count)
-        joined_short[to, middle] = source[0, :count, :cols]
-        sides = source[0, :count, cols:]
-        joined_short[to, after] = sides
+        joined_short[to, :wide] = source[0, :count, :]
         column = lax.dot_general(
             source[0, count:, :cols], pick, (((0,), (0,)), ((), ())), preferred_element_type=F32
-        )[rows8 - count :]
-        lane = lax.broadcasted_iota(jnp.int32, (count, LANE), 1)
-        joined_short[to, :LANE] = jnp.where(lane == SIDE - 1, column, sides.astype(F32)).astype(BF16)
+        )
+        joined_short[to, wide:] = column[rows8 - count :].astype(BF16)
 
     unpack(far_ref, far8, 0)
     unpack(above_ref, rows8, far8)
+    unpack(message_ref, rows8, far8 + rows8)
     unpack(below_ref, rows8, far8 + 2 * rows8)
-    joined_short[own, middle] = exact_ref[0].astype(BF16)
-    joined_short[own, :LANE] = left_ref[0, rows8:]
-    joined_short[own, after] = right_ref[0]
     joined_short[frame8:, :] = jnp.zeros_like(joined_short[frame8:, :])
-    joined[...] = joined_short[...].astype(F32)
-    joined[own, middle] = exact_ref[0]
-
-    blocks = range(wide // (2 * LANE))
-
-    def correlate(source, which, size, start, exact, finish):
+    joined[...] = joined_short[:, :wide].astype(F32)
+    joined[far8 + rows8 : far8 + 2 * rows8, :cols] = exact_ref[0]
+
+    blocks = [slice(k, min(k + 2 * LANE, wide)) for k in range(0, wide, 2 * LANE)]
+
+    def window(ref, here, to, lone):
+        begin, end = to.start - LANE, to.stop + LANE
+        if begin < 0:
+            pieces = [ref[here, begin + wide : wide], ref[here, :end]]
+        elif end > wide:
+            pieces = [ref[here, begin:wide], ref[here, : end - wide]]
+        else:
+            return ref[here, begin:end]
+        if lone and to.stop == wide:
+            pieces.append(ref[here, wide:])
+        return jnp.concatenate(pieces, axis=1)
+
+    def correlate(source, which, size, start, exact, finish, lone=False):
         deep = (size + 2 * REACH) * DEPTH
         size8 = size * DEPTH
         matrix = within_ref[0, which, :size8, :deep]
         here = slice(start, start + size8)
-        for n in blocks:
-            to = slice(2 * LANE * n, 2 * LANE * (n + 1))
+        for to in blocks:
+            if lone and to.stop == wide:
+                to = slice(to.start, wide + LANE)
             out = dot(matrix, source[start : start + deep, to])
             if exact:
                 high[here, to], low[here, to] = split(out)
             else:
                 high[here, to] = out.astype(BF16)
-        for n in blocks:
-            begin = 2 * LANE * n - LANE
-            lo, hi = max(begin, 0), min(begin + 4 * LANE, wide)
-            band = across_ref[0, which, lo - begin : hi - begin, :]
-            out = dot(high[here, lo:hi], band)
+        for to in blocks:
+            width = to.stop - to.start
+            if lone and to.stop == wide:
+                band = corner_ref[0, which]
+            else:
+                band = across_ref[0, which, : width + 2 * LANE, :width]
+            out = dot(window(high, here, to, lone), band)
             if exact:
-                out = out + dot(low[here, lo:hi], band)
-            finish(start, size8, slice(2 * LANE * n, 2 * LANE * (n + 1)), out)
+                out = out + dot(window(low, here, to, False), band)
+            finish(start, size8, to, out)
 
     def ratio_from(shift):
         def finish(start, size8, to, out):
@@ -451,11 +466,11 @@
     def last_estimate(start, size8, to, out):
         begin = start + 2 * REACH * DEPTH
         value = estimate[begin : begin + size8, to] * out
-        for b in range(2):
+        for b in range((to.stop - to.start) // LANE):
             result[to.start // LANE + b, start : start + size8, :] = value[:, b * LANE : (b + 1) * LANE]
 
     for i in range(5):
-        correlate(joined_short, 0, BIG, i * BIG * DEPTH, False, ratio_from(REACH))
+        correlate(joined_short, 0, BIG, i * BIG * DEPTH, False, ratio_from(REACH), True)
     for i in range(4):
         correlate(ratio, 1, BIG, i * BIG * DEPTH, i in (1, 2), first_estimate)
     for i in range(4):
@@ -469,7 +484,7 @@
     for z in range(planes):
         at = pl.ds(6 * planes + z, height, stride=planes)
         for b in range(cols // LANE):
-            restored_ref[0, z, :, b * LANE : (b + 1) * LANE] = result[1 + b, at, :]
+            restored_ref[0, z, :, b * LANE : (b + 1) * LANE] = result[b, at, :]
 
     def twice(left, right):
         big, small = split(right)
@@ -495,11 +510,11 @@
     level_two_ref[0] = two.reshape(level_two_ref.shape[1:])
 
 
-def deconvolve(at, places, sides, group, across, within, matrices, earlier):
-    chans = across.shape[0]
+def deconvolve(at, sides, group, tables, matrices, earlier):
+    chans = tables[0].shape[0]
     rows8, cols = group[0].shape[1:]
     rows = rows8 // DEPTH
-    wide = cols + 2 * LANE
+    wide = cols + LANE
     mine = lambda s: pl.BlockSpec((1,) + s[1:], lambda i: (at,) + (0,) * (len(s) - 1))
     outs = (
         (chans, DEPTH, rows, cols),
@@ -510,9 +525,9 @@
     ratio_rows = 5 * BIG * DEPTH
     estimate_rows = 4 * BIG * DEPTH
     result_rows = 3 * SMALL * DEPTH
-    operands = [sides, *group, across, within, *matrices]
+    operands = [sides, *group, *tables, *matrices]
     return pl.pallas_call(
-        functools.partial(deconvolve_kernel, places),
+        functools.partial(deconvolve_kernel, at),
         grid=(1,),
         in_specs=[pl.BlockSpec(memory_space=pltpu.SMEM)]
         + [VMEM] * (len(operands) - 1)
@@ -522,12 +537,12 @@
         input_output_aliases={len(operands) + k: k for k in range(len(earlier))},
         scratch_shapes=[
             pltpu.VMEM((FRAME * DEPTH, wide), F32),
-            pltpu.VMEM((FRAME * DEPTH, wide), BF16),
+            pltpu.VMEM((FRAME * DEPTH, wide + LANE), BF16),
             pltpu.VMEM((ratio_rows, wide), BF16),
             pltpu.VMEM((estimate_rows, wide), F32),
             pltpu.VMEM((estimate_rows, wide), BF16),
             pltpu.VMEM((wide // LANE, result_rows, LANE), F32),
-            pltpu.VMEM((ratio_rows, wide), BF16),
+            pltpu.VMEM((ratio_rows, wide + LANE), BF16),
             pltpu.VMEM((ratio_rows, wide), BF16),
         ],
         compiler_params=params(32),
@@ -556,12 +571,11 @@
     own, right, low = place(tiles, at_tile, 0, 1, ())
     kern = psf / jnp.sum(psf, axis=-1, keepdims=True)
     both = jnp.stack([kern, kern[:, :, ::-1]], axis=1)
-    across, within = bands(both.reshape(chans * 2, 3 * TAPS), (right,))
+    tables = bands(both.reshape(chans * 2, 3 * TAPS), (right,))
     pieces = [(own, right, shift(low, "gy", 1))]
-    own, right, low = place(tiles, at_tile, 1, chans - 1, (within,))
+    own, right, low = place(tiles, at_tile, 1, chans - 1, (tables[1],))
     pieces.append((own, right, shift(low, "gy", 1)))
-    across = across.reshape((chans, 2) + across.shape[1:])
-    within = within.reshape((chans, 2) + within.shape[1:])
+    tables = [t.reshape((chans, 2) + t.shape[1:]) for t in tables]
 
     groups = []
     tails = []
@@ -571,18 +585,17 @@
         left = shift(mine, "gx", 1)
         right = shift(to_left, "gx", -1)
         for k in range(own.shape[0]):
-            exact, strip, message, tail = join(sides, own, low, mine, left, right, k)
+            exact, message, tail = join(sides, own, low, mine, left, right, k)
             above = shift(message, "gy", 1)
             below = shift(message, "gy", -1)
-            groups.append([exact, above, below, left, strip, k])
+            groups.append([exact, message, above, below])
             tails.append(tail)
         before = (message,)
     far = shift(jnp.concatenate(tails, axis=0), "gy", 2)
 
     outs = ()
-    for at, (exact, above, below, left, strip, k) in enumerate(groups):
-        group = (exact, above, below, far, left, strip)
-        outs = deconvolve(at, (at, k), sides, group, across, within, matrices, outs)
+    for at, group in enumerate(groups):
+        outs = deconvolve(at, sides, [*group, far], tables, matrices, outs)
     return tuple(outs)
 
 

time: 121 us -> 123 us (1.017); the launches traced: 121 us -> 122 us
  Pallas kernels: 51.5 us -> 52.9 us
    pallas_call x3, Pallas kernels: 35 us -> 36.3 us  [deconvolve(): pl.pallas_call(functools.partial(deconvolve_kernel, at), grid=(1,), in_sp...]
    unnamed x30 -> x34, local copies, waits for them, and re-layouts: 3.49 us -> 3.51 us
  transfers between devices with their start and end apart: 13 -> 13, of which waited for: 7 -> 5; matrix products, arithmetic and copies ran while one was open for 0% -> 0% of each run, Pallas kernels for 30% -> 30%
where the time goes in v6:
time: 123 us; the launch traced here: 122 us
  Pallas kernels  52.9 us (43%)
  starting transfers between devices  39.8 us (32%)
  waiting for transfers between devices  23.8 us (19%)
  local copies, waits for them, and re-layouts  3.69 us (3%)
    ppermute x13, starting transfers between devices, shift(): return lax.ppermute(block, axis, route)  39.8 us
    pallas_call x3, Pallas kernels, deconvolve(): pl.pallas_call(functools.partial(deconvolve_kernel, at), grid=(1,), in_sp...  36.3 us
    ppermute x13, waiting for transfers between devices, shift(): return lax.ppermute(block, axis, route)  23.8 us
    pallas_call x2, Pallas kernels, place(): pl.pallas_call(skipping(place_kernel, 2, len(after)), grid_spec=pltpu.Pre...  8.24 us
    pallas_call x3, Pallas kernels, join(): pl.pallas_call(functools.partial(join_kernel, at), in_specs=[pl.BlockSpec...  4.51 us
    unnamed x34, local copies, waits for them, and re-layouts  3.51 us
  transfers between devices with their start and end apart: 13, of which 5 were waited for; matrix products, arithmetic and copies ran while one was open for 0% of the time, Pallas kernels for 30%

profile of v6, /device:TPU:11, one launch (start us, length us, event | category | flops | bytes accessed | tf_op | source)
XLA Modules:
  0.0 121.5 jit_solution(8023830150741103405)
XLA Ops:
  0.6 1.8 %copy-done.2 = bf16[3,8,96,544]{3,2,1,0:T(8,128)(2,1)S(1)} copy-done((bf16[3,8,96,544]{3,2,1,0:T(8,128)(2,1)S(1)}, bf16[3,8,96,544]{3,2,1,0:T(8,128)(2,1)}, u32[]{:S(2)}) %copy-start.2) | copy-done | bytes 2506776
  2.5 0.7 copy-done.4
  3.1 3.2 %place.2 = (bf16[1,512,512]{2,1,0:T(8,128)(2,1)S(1)}, bf16[1,512,128]{2,1,0:T(8,128)(2,1)S(1)}, bf16[1,576,512]{2,1,0:T(8,128)(2,1)}) custom-call(s32[2]{0:T(128)S(1)} %bitcast.11, bf16[3,8,96,544]{3,2,1,0:T(8,128)(2,1)S(1)} %copy-done.2), custom_call_target="tpu_custom_call" | custom-call | flops 2000000000 | bytes 1 | tf_op jit(solution)/shard_map/place/pallas_call | solution.py:99
  6.3 3.2 %collective-permute-start.1 = (bf16[1,576,512]{2,1,0:T(8,128)(2,1)}, bf16[1,576,512]{2,1,0:T(8,128)(2,1)S(1)}, u32[]{:S(2)}, u32[]{:S(2)}) collective-permute-start(bf16[1,576,512]{2,1,0:T(8,128)(2,1)} %get-tuple-element.37), channel_id=1, source_target_pairs={{0,1},{1,2},{2,3},{4,5},{5,6},{6,7},{8,9},{9,10},{10,11},{12,13},{... | collective-permute-start | bytes 1769480 | tf_op jit(solution)/shard_map/ppermute | solution.py:564
  10.0 2.4 %bands.1 = (bf16[6,512,256]{2,1,0:T(8,128)(2,1)S(1)}, bf16[6,272,512]{2,1,0:T(8,128)(2,1)S(1)}, bf16[6,512,128]{2,1,0:T(8,128)(2,1)S(1)}) custom-call(f32[6,93]{1,0:T(8,128)S(1)} %reshape.23.refs_0_, bf16[1,512,128]{2,1,0:T(8,128)(2,1)S(1)} %get-tuple-element.31.refs_1_), custom_call_target="tpu_custom_call" | custom-call | flops 2000000000 | bytes 1 | tf_op jit(solution)/shard_map/bands/pallas_call | solution.py:269
  12.4 5.0 %place.3 = (bf16[2,512,512]{2,1,0:T(8,128)(2,1)S(1)}, bf16[2,512,128]{2,1,0:T(8,128)(2,1)S(1)}, bf16[2,576,512]{2,1,0:T(8,128)(2,1)}) custom-call(s32[2]{0:T(128)S(1)} %bitcast.12, bf16[3,8,96,544]{3,2,1,0:T(8,128)(2,1)S(1)} %copy-done.3, bf16[6,272,512]{2,1,0:T(8,128)(2,1)S(1)} %get-tuple-element.32.refs_2_), custom_call_target="tpu_custom_call" | custom-call | flops 4000000000 | bytes 1 | tf_op jit(solution)/shard_map/place/pallas_call | solution.py:99
  17.5 3.2 %collective-permute-start = (bf16[2,576,512]{2,1,0:T(8,128)(2,1)}, bf16[2,576,512]{2,1,0:T(8,128)(2,1)S(1)}, u32[]{:S(2)}, u32[]{:S(2)}) collective-permute-start(bf16[2,576,512]{2,1,0:T(8,128)(2,1)} %get-tuple-element.34), channel_id=1, source_target_pairs={{0,1},{1,2},{2,3},{4,5},{5,6},{6,7},{8,9},{9,10},{10,11},{12,13},{... | collective-permute-start | bytes 3538952 | tf_op jit(solution)/shard_map/ppermute | solution.py:564
  20.7 1.9 %collective-permute-done.1.refs_2_.low_ref = bf16[1,576,512]{2,1,0:T(8,128)(2,1)S(1)} collective-permute-done((bf16[1,576,512]{2,1,0:T(8,128)(2,1)}, bf16[1,576,512]{2,1,0:T(8,128)(2,1)S(1)}, u32[]{:S(2)}, u32[]{:S(2)}) %collective-permute-start.1) | collective-permute-done | bytes 589856 | tf_op jit(solution)/shard_map/ppermute | solution.py:564
  22.6 0.9 edges.2
  23.6 5.7 %collective-permute-start.2 = (bf16[1,1024,128]{2,1,0:T(8,128)(2,1)}, bf16[1,1024,128]{2,1,0:T(8,128)(2,1)}, u32[]{:S(2)}, u32[]{:S(2)}) collective-permute-start(bf16[1,1024,128]{2,1,0:T(8,128)(2,1)} %get-tuple-element.38.mine_ref), channel_id=1, source_target_pairs={{0,4},{4,8},{8,12},{12,16},{16,20},{20,24},{24,28},{1,5},{5,9},{9,... | collective-permute-start | bytes 786440 | tf_op jit(solution)/shard_map/ppermute | solution.py:564
  29.3 1.9 %collective-permute-start.3 = (bf16[1,512,128]{2,1,0:T(8,128)(2,1)}, bf16[1,512,128]{2,1,0:T(8,128)(2,1)S(1)}, u32[]{:S(2)}, u32[]{:S(2)}) collective-permute-start(bf16[1,512,128]{2,1,0:T(8,128)(2,1)} %get-tuple-element.39), channel_id=1, source_target_pairs={{4,0},{8,4},{12,8},{16,12},{20,16},{24,20},{28,24},{5,1},{9,5},{13... | collective-permute-start | bytes 393224 | tf_op jit(solution)/shard_map/ppermute | solution.py:564
  31.3 5.4 %collective-permute-done.3.right_ref = bf16[1,512,128]{2,1,0:T(8,128)(2,1)S(1)} collective-permute-done((bf16[1,512,128]{2,1,0:T(8,128)(2,1)}, bf16[1,512,128]{2,1,0:T(8,128)(2,1)S(1)}, u32[]{:S(2)}, u32[]{:S(2)}) %collective-permute-start.3) | collective-permute-done | bytes 131104 | tf_op jit(solution)/shard_map/ppermute | solution.py:564
  36.7 1.8 %join.3 = (f32[1,512,512]{2,1,0:T(8,128)S(1)}, bf16[1,528,640]{2,1,0:T(8,128)(2,1)S(1)}, bf16[1,32,640]{2,1,0:T(8,128)(2,1)S(1)}) custom-call(s32[4]{0:T(128)S(1)} %add_convert_fusion.sides_ref, bf16[1,512,512]{2,1,0:T(8,128)(2,1)S(1)} %get-tuple-element.36.refs_0_.own_ref, bf16[1,576,512]{2,1,0:T(8,128)(2,1)S(1)} %collective-permute-done.1.refs_2_.low_ref, ...), custom_call_target="tpu_custom_call" | custom-call | flops 1 | bytes 1 | tf_op jit(solution)/shard_map/join/pallas_call | solution.py:209
  38.5 9.4 %collective-permute-done.refs_2_.low_ref = bf16[2,576,512]{2,1,0:T(8,128)(2,1)S(1)} collective-permute-done((bf16[2,576,512]{2,1,0:T(8,128)(2,1)}, bf16[2,576,512]{2,1,0:T(8,128)(2,1)S(1)}, u32[]{:S(2)}, u32[]{:S(2)}) %collective-permute-start) | collective-permute-done | bytes 1179680 | tf_op jit(solution)/shard_map/ppermute | solution.py:564
  47.9 0.9 copy-done.1
  48.8 0.6 edges.3
  49.4 4.6 %collective-permute-start.4 = (bf16[2,1024,128]{2,1,0:T(8,128)(2,1)S(1)}, bf16[2,1024,128]{2,1,0:T(8,128)(2,1)S(1)}, u32[]{:S(2)}, u32[]{:S(2)}) collective-permute-start(bf16[2,1024,128]{2,1,0:T(8,128)(2,1)S(1)} %get-tuple-element.41.mine_ref), channel_id=1, source_target_pairs={{0,4},{4,8},{8,12},{12,16},{16,20},{20,24},{24,28},{1,5},{5,9},{9,... | collective-permute-start | bytes 1572872 | tf_op jit(solution)/shard_map/ppermute | solution.py:564
  54.0 1.9 %collective-permute-start.12 = (bf16[1,528,640]{2,1,0:T(8,128)(2,1)S(1)}, bf16[1,528,640]{2,1,0:T(8,128)(2,1)S(1)}, u32[]{:S(2)}, u32[]{:S(2)}) collective-permute-start(bf16[1,528,640]{2,1,0:T(8,128)(2,1)S(1)} %get-tuple-element.40.refs_3_.message_ref), channel_id=1, source_target_pairs={{1,0},{2,1},{3,2},{5,4},{6,5},{7,6},{9,8},{10,9},{11,10},{13,12},{... | collective-permute-start | bytes 2027528 | tf_op jit(solution)/shard_map/ppermute | solution.py:564
  55.9 3.4 %collective-permute-start.11 = (bf16[1,528,640]{2,1,0:T(8,128)(2,1)S(1)}, bf16[1,528,640]{2,1,0:T(8,128)(2,1)S(1)}, u32[]{:S(2)}, u32[]{:S(2)}) collective-permute-start(bf16[1,528,640]{2,1,0:T(8,128)(2,1)S(1)} %get-tuple-element.40.refs_3_.message_ref), channel_id=1, source_target_pairs={{0,1},{1,2},{2,3},{4,5},{5,6},{6,7},{8,9},{9,10},{10,11},{12,13},{... | collective-permute-start | bytes 2027528 | tf_op jit(solution)/shard_map/ppermute | solution.py:564
  59.3 2.2 %collective-permute-start.5 = (bf16[2,512,128]{2,1,0:T(8,128)(2,1)S(1)}, bf16[2,512,128]{2,1,0:T(8,128)(2,1)S(1)}, u32[]{:S(2)}, u32[]{:S(2)}) collective-permute-start(bf16[2,512,128]{2,1,0:T(8,128)(2,1)S(1)} %get-tuple-element.42), channel_id=1, source_target_pairs={{4,0},{8,4},{12,8},{16,12},{20,16},{24,20},{28,24},{5,1},{9,5},{13... | collective-permute-start | bytes 786440 | tf_op jit(solution)/shard_map/ppermute | solution.py:564
  61.5 6.7 %collective-permute-done.5.right_ref = bf16[2,512,128]{2,1,0:T(8,128)(2,1)S(1)} collective-permute-done((bf16[2,512,128]{2,1,0:T(8,128)(2,1)S(1)}, bf16[2,512,128]{2,1,0:T(8,128)(2,1)S(1)}, u32[]{:S(2)}, u32[]{:S(2)}) %collective-permute-start.5) | collective-permute-done | bytes 262176 | tf_op jit(solution)/shard_map/ppermute | solution.py:564
  68.2 1.3 %join.5 = (f32[1,512,512]{2,1,0:T(8,128)S(1)}, bf16[1,528,640]{2,1,0:T(8,128)(2,1)S(1)}, bf16[1,32,640]{2,1,0:T(8,128)(2,1)S(1)}) custom-call(s32[4]{0:T(128)S(1)} %add_convert_fusion.sides_ref, bf16[2,512,512]{2,1,0:T(8,128)(2,1)S(1)} %get-tuple-element.33.refs_0_.own_ref, bf16[2,576,512]{2,1,0:T(8,128)(2,1)S(1)} %collective-permute-done.refs_2_.low_ref, ...), custom_call_target="tpu_custom_call" | custom-call | flops 1 | bytes 1 | tf_op jit(solution)/shard_map/join/pallas_call | solution.py:209
  69.5 1.3 %join.4 = (f32[1,512,512]{2,1,0:T(8,128)S(1)}, bf16[1,528,640]{2,1,0:T(8,128)(2,1)S(1)}, bf16[1,32,640]{2,1,0:T(8,128)(2,1)S(1)}) custom-call(s32[4]{0:T(128)S(1)} %add_convert_fusion.sides_ref, bf16[2,512,512]{2,1,0:T(8,128)(2,1)S(1)} %get-tuple-element.33.refs_0_.own_ref, bf16[2,576,512]{2,1,0:T(8,128)(2,1)S(1)} %collective-permute-done.refs_2_.low_ref, ...), custom_call_target="tpu_custom_call" | custom-call | flops 1 | bytes 1 | tf_op jit(solution)/shard_map/join/pallas_call | solution.py:209
  70.9 2.3 %collective-permute-start.8 = (bf16[3,32,640]{2,1,0:T(8,128)(2,1)S(1)}, bf16[3,32,640]{2,1,0:T(8,128)(2,1)S(1)}, u32[]{:S(2)}, u32[]{:S(2)}) collective-permute-start(bf16[3,32,640]{2,1,0:T(8,128)(2,1)S(1)} %pad_maximum_fusion), channel_id=1, source_target_pairs={{0,2},{1,3},{4,6},{5,7},{8,10},{9,11},{12,14},{13,15},{16,18},{17,... | collective-permute-start | bytes 368648 | tf_op jit(solution)/shard_map/ppermute | solution.py:564
  73.3 4.0 %collective-permute-start.10 = (bf16[1,528,640]{2,1,0:T(8,128)(2,1)S(1)}, bf16[1,528,640]{2,1,0:T(8,128)(2,1)S(1)}, u32[]{:S(2)}, u32[]{:S(2)}) collective-permute-start(bf16[1,528,640]{2,1,0:T(8,128)(2,1)S(1)} %get-tuple-element.51.message_ref), channel_id=1, source_target_pairs={{1,0},{2,1},{3,2},{5,4},{6,5},{7,6},{9,8},{10,9},{11,10},{13,12},{... | collective-permute-start | bytes 2027528 | tf_op jit(solution)/shard_map/ppermute | solution.py:564
  77.3 1.9 %collective-permute-start.9 = (bf16[1,528,640]{2,1,0:T(8,128)(2,1)S(1)}, bf16[1,528,640]{2,1,0:T(8,128)(2,1)S(1)}, u32[]{:S(2)}, u32[]{:S(2)}) collective-permute-start(bf16[1,528,640]{2,1,0:T(8,128)(2,1)S(1)} %get-tuple-element.51.message_ref), channel_id=1, source_target_pairs={{0,1},{1,2},{2,3},{4,5},{5,6},{6,7},{8,9},{9,10},{10,11},{12,13},{... | collective-permute-start | bytes 2027528 | tf_op jit(solution)/shard_map/ppermute | solution.py:564
  79.2 3.4 %collective-permute-start.7 = (bf16[1,528,640]{2,1,0:T(8,128)(2,1)S(1)}, bf16[1,528,640]{2,1,0:T(8,128)(2,1)S(1)}, u32[]{:S(2)}, u32[]{:S(2)}) collective-permute-start(bf16[1,528,640]{2,1,0:T(8,128)(2,1)S(1)} %get-tuple-element.44.message_ref), channel_id=1, source_target_pairs={{1,0},{2,1},{3,2},{5,4},{6,5},{7,6},{9,8},{10,9},{11,10},{13,12},{... | collective-permute-start | bytes 2027528 | tf_op jit(solution)/shard_map/ppermute | solution.py:564
  82.6 2.1 %collective-permute-start.6 = (bf16[1,528,640]{2,1,0:T(8,128)(2,1)S(1)}, bf16[1,528,640]{2,1,0:T(8,128)(2,1)S(1)}, u32[]{:S(2)}, u32[]{:S(2)}) collective-permute-start(bf16[1,528,640]{2,1,0:T(8,128)(2,1)S(1)} %get-tuple-element.44.message_ref), channel_id=1, source_target_pairs={{0,1},{1,2},{2,3},{4,5},{5,6},{6,7},{8,9},{9,10},{10,11},{12,13},{... | collective-permute-start | bytes 2027528 | tf_op jit(solution)/shard_map/ppermute | solution.py:564
  84.8 11.8 %deconvolve.3 = (f32[3,8,64,512]{3,2,1,0:T(8,128)}, f32[3,4,32,256]{3,2,1,0:T(8,128)}, f32[3,2,16,128]{3,2,1,0:T(8,128)}) custom-call(s32[4]{0:T(128)S(1)} %add_convert_fusion.sides_ref, f32[1,512,512]{2,1,0:T(8,128)S(1)} %get-tuple-element.52.exact_ref, bf16[1,528,640]{2,1,0:T(8,128)(2,1)S(1)} %get-tuple-element.40.refs_3_.message_ref, ...), custom_call_target="tpu_custom_call" | custom-call | flops 10000000000 | bytes 1 | tf_op jit(solution)/shard_map/deconvolve/pallas_call | solution.py:529
  96.7 12.4 %deconvolve.4 = (f32[3,8,64,512]{3,2,1,0:T(8,128)}, f32[3,4,32,256]{3,2,1,0:T(8,128)}, f32[3,2,16,128]{3,2,1,0:T(8,128)}) custom-call(s32[4]{0:T(128)S(1)} %add_convert_fusion.sides_ref, f32[1,512,512]{2,1,0:T(8,128)S(1)} %get-tuple-element.50.exact_ref, ...), custom_call_target="tpu_custom_call", output_to_operand_aliasing={{0}: (13, {}), {1}: (14, {}), {2}: (15, {})} | custom-call | flops 10000000000 | bytes 1 | tf_op jit(solution)/shard_map/deconvolve/pallas_call | solution.py:529
  109.0 0.4 collective-permute-done.6.above_ref
  109.4 12.1 %deconvolve.5 = (f32[3,8,64,512]{3,2,1,0:T(8,128)}, f32[3,4,32,256]{3,2,1,0:T(8,128)}, f32[3,2,16,128]{3,2,1,0:T(8,128)}) custom-call(s32[4]{0:T(128)S(1)} %add_convert_fusion.sides_ref, f32[1,512,512]{2,1,0:T(8,128)S(1)} %get-tuple-element.43.exact_ref, ...), custom_call_target="tpu_custom_call", output_to_operand_aliasing={{0}: (13, {}), {1}: (14, {}), {2}: (15, {})} | custom-call | flops 10000000000 | bytes 1 | tf_op jit(solution)/shard_map/deconvolve/pallas_call | solution.py:529
  (48 shorter events, 0.6 us)
Async XLA Ops:
  0.6 1.8 %copy-start.2 = (bf16[3,8,96,544]{3,2,1,0:T(8,128)(2,1)S(1)}, bf16[3,8,96,544]{3,2,1,0:T(8,128)(2,1)}, u32[]{:S(2)}) copy-start(bf16[3,8,96,544]{3,2,1,0:T(8,128)(2,1)} %refs_1_.3) | copy-start | bytes 7520260
  2.5 0.7 copy-start.4
  3.1 6.4 %copy-start.16 = (f32[3,3,31]{2,1,0:T(4,128)S(1)}, f32[3,3,31]{2,1,0:T(4,128)}, u32[]{:S(2)}) copy-start(f32[3,3,31]{2,1,0:T(4,128)} %param.9) | copy-start | bytes 3352
  6.3 16.3 %collective-permute-start.1 = (bf16[1,576,512]{2,1,0:T(8,128)(2,1)}, bf16[1,576,512]{2,1,0:T(8,128)(2,1)S(1)}, u32[]{:S(2)}, u32[]{:S(2)}) collective-permute-start(bf16[1,576,512]{2,1,0:T(8,128)(2,1)} %get-tuple-element.37), channel_id=1, source_target_pairs={{0,1},{1,2},{2,3},{4,5},{5,6},{6,7},{8,9},{9,10},{10,11},{12,13},{... | collective-permute-start | bytes 1769480 | tf_op jit(solution)/shard_map/ppermute | solution.py:564
  10.0 2.4 %copy-start.3 = (bf16[3,8,96,544]{3,2,1,0:T(8,128)(2,1)S(1)}, bf16[3,8,96,544]{3,2,1,0:T(8,128)(2,1)}, u32[]{:S(2)}) copy-start(bf16[3,8,96,544]{3,2,1,0:T(8,128)(2,1)} %refs_1_.3) | copy-start | bytes 7520260
  10.0 2.4 %copy-start.5 = (s32[1,1,2]{2,1,0:T(1,128)S(1)}, s32[1,1,2]{2,1,0:T(1,128)}, u32[]{:S(2)}) copy-start(s32[1,1,2]{2,1,0:T(1,128)} %param.8) | copy-start | bytes 28
  12.3 5.1 %copy-start.6 = (bf16[6,272,512]{2,1,0:T(8,128)(2,1)}, bf16[6,272,512]{2,1,0:T(8,128)(2,1)S(1)}, u32[]{:S(2)}) copy-start(bf16[6,272,512]{2,1,0:T(8,128)(2,1)S(1)} %get-tuple-element.32.refs_2_) | copy-start | bytes 5013508
  12.4 5.1 %copy-start.8 = (bf16[6,512,256]{2,1,0:T(8,128)(2,1)}, bf16[6,512,256]{2,1,0:T(8,128)(2,1)S(1)}, u32[]{:S(2)}) copy-start(bf16[6,512,256]{2,1,0:T(8,128)(2,1)S(1)} %get-tuple-element.48) | copy-start | bytes 4718596
  12.4 5.1 %copy-start.10 = (bf16[6,512,128]{2,1,0:T(8,128)(2,1)}, bf16[6,512,128]{2,1,0:T(8,128)(2,1)S(1)}, u32[]{:S(2)}) copy-start(bf16[6,512,128]{2,1,0:T(8,128)(2,1)S(1)} %get-tuple-element.49) | copy-start | bytes 2359300
  17.4 6.1 %copy-start = (bf16[2,512,128]{2,1,0:T(8,128)(2,1)}, bf16[2,512,128]{2,1,0:T(8,128)(2,1)S(1)}, u32[]{:S(2)}) copy-start(bf16[2,512,128]{2,1,0:T(8,128)(2,1)S(1)} %get-tuple-element.35.refs_3_.refs_1_) | copy-start | bytes 786436
  17.5 30.4 %collective-permute-start = (bf16[2,576,512]{2,1,0:T(8,128)(2,1)}, bf16[2,576,512]{2,1,0:T(8,128)(2,1)S(1)}, u32[]{:S(2)}, u32[]{:S(2)}) collective-permute-start(bf16[2,576,512]{2,1,0:T(8,128)(2,1)} %get-tuple-element.34), channel_id=1, source_target_pairs={{0,1},{1,2},{2,3},{4,5},{5,6},{6,7},{8,9},{9,10},{10,11},{12,13},{... | collective-permute-start | bytes 3538952 | tf_op jit(solution)/shard_map/ppermute | solution.py:564
  23.6 13.1 %collective-permute-start.2 = (bf16[1,1024,128]{2,1,0:T(8,128)(2,1)}, bf16[1,1024,128]{2,1,0:T(8,128)(2,1)}, u32[]{:S(2)}, u32[]{:S(2)}) collective-permute-start(bf16[1,1024,128]{2,1,0:T(8,128)(2,1)} %get-tuple-element.38.mine_ref), channel_id=1, source_target_pairs={{0,4},{4,8},{8,12},{12,16},{16,20},{20,24},{24,28},{1,5},{5,9},{9,... | collective-permute-start | bytes 786440 | tf_op jit(solution)/shard_map/ppermute | solution.py:564
  29.3 7.4 %collective-permute-start.3 = (bf16[1,512,128]{2,1,0:T(8,128)(2,1)}, bf16[1,512,128]{2,1,0:T(8,128)(2,1)S(1)}, u32[]{:S(2)}, u32[]{:S(2)}) collective-permute-start(bf16[1,512,128]{2,1,0:T(8,128)(2,1)} %get-tuple-element.39), channel_id=1, source_target_pairs={{4,0},{8,4},{12,8},{16,12},{20,16},{24,20},{28,24},{5,1},{9,5},{13... | collective-permute-start | bytes 393224 | tf_op jit(solution)/shard_map/ppermute | solution.py:564
  47.9 1.0 copy-start.1
  49.4 18.8 %collective-permute-start.4 = (bf16[2,1024,128]{2,1,0:T(8,128)(2,1)S(1)}, bf16[2,1024,128]{2,1,0:T(8,128)(2,1)S(1)}, u32[]{:S(2)}, u32[]{:S(2)}) collective-permute-start(bf16[2,1024,128]{2,1,0:T(8,128)(2,1)S(1)} %get-tuple-element.41.mine_ref), channel_id=1, source_target_pairs={{0,4},{4,8},{8,12},{12,16},{16,20},{20,24},{24,28},{1,5},{5,9},{9,... | collective-permute-start | bytes 1572872 | tf_op jit(solution)/shard_map/ppermute | solution.py:564
  54.0 25.2 %collective-permute-start.12 = (bf16[1,528,640]{2,1,0:T(8,128)(2,1)S(1)}, bf16[1,528,640]{2,1,0:T(8,128)(2,1)S(1)}, u32[]{:S(2)}, u32[]{:S(2)}) collective-permute-start(bf16[1,528,640]{2,1,0:T(8,128)(2,1)S(1)} %get-tuple-element.40.refs_3_.message_ref), channel_id=1, source_target_pairs={{1,0},{2,1},{3,2},{5,4},{6,5},{7,6},{9,8},{10,9},{11,10},{13,12},{... | collective-permute-start | bytes 2027528 | tf_op jit(solution)/shard_map/ppermute | solution.py:564
  55.9 26.7 %collective-permute-start.11 = (bf16[1,528,640]{2,1,0:T(8,128)(2,1)S(1)}, bf16[1,528,640]{2,1,0:T(8,128)(2,1)S(1)}, u32[]{:S(2)}, u32[]{:S(2)}) collective-permute-start(bf16[1,528,640]{2,1,0:T(8,128)(2,1)S(1)} %get-tuple-element.40.refs_3_.message_ref), channel_id=1, source_target_pairs={{0,1},{1,2},{2,3},{4,5},{5,6},{6,7},{8,9},{9,10},{10,11},{12,13},{... | collective-permute-start | bytes 2027528 | tf_op jit(solution)/shard_map/ppermute | solution.py:564
  59.3 25.5 %copy-start.7 = (bf16[6,272,512]{2,1,0:T(8,128)(2,1)S(1)}, bf16[6,272,512]{2,1,0:T(8,128)(2,1)}, u32[]{:S(2)}) copy-start(bf16[6,272,512]{2,1,0:T(8,128)(2,1)} %copy-done.6) | copy-start | bytes 5013508
  59.3 25.5 %copy-start.9 = (bf16[6,512,256]{2,1,0:T(8,128)(2,1)S(1)}, bf16[6,512,256]{2,1,0:T(8,128)(2,1)}, u32[]{:S(2)}) copy-start(bf16[6,512,256]{2,1,0:T(8,128)(2,1)} %copy-done.8) | copy-start | bytes 4718596
  59.3 25.5 %copy-start.11 = (bf16[6,512,128]{2,1,0:T(8,128)(2,1)S(1)}, bf16[6,512,128]{2,1,0:T(8,128)(2,1)}, u32[]{:S(2)}) copy-start(bf16[6,512,128]{2,1,0:T(8,128)(2,1)} %copy-done.10) | copy-start | bytes 2359300
  59.3 25.5 %copy-start.12 = (bf16[640,384]{1,0:T(8,128)(2,1)S(1)}, bf16[640,384]{1,0:T(8,128)(2,1)}, u32[]{:S(2)}) copy-start(bf16[640,384]{1,0:T(8,128)(2,1)} %constant.25.clone.one_x_ref) | copy-start | bytes 1474564
  59.3 25.5 %copy-start.13 = (bf16[144,592]{1,0:T(8,128)(2,1)S(1)}, bf16[144,592]{1,0:T(8,128)(2,1)}, u32[]{:S(2)}) copy-start(bf16[144,592]{1,0:T(8,128)(2,1)} %constant.26.clone.one_zy_ref) | copy-start | bytes 511492
  59.3 25.5 %copy-start.14 = (bf16[384,128]{1,0:T(8,128)(2,1)S(1)}, bf16[384,128]{1,0:T(8,128)(2,1)}, u32[]{:S(2)}) copy-start(bf16[384,128]{1,0:T(8,128)(2,1)} %constant.27.clone.two_x_ref) | copy-start | bytes 294916
  59.3 25.5 %copy-start.15 = (bf16[32,144]{1,0:T(8,128)(2,1)S(1)}, bf16[32,144]{1,0:T(8,128)(2,1)}, u32[]{:S(2)}) copy-start(bf16[32,144]{1,0:T(8,128)(2,1)} %constant.28.clone.two_zy_ref) | copy-start | bytes 27652
  59.3 8.9 %collective-permute-start.5 = (bf16[2,512,128]{2,1,0:T(8,128)(2,1)S(1)}, bf16[2,512,128]{2,1,0:T(8,128)(2,1)S(1)}, u32[]{:S(2)}, u32[]{:S(2)}) collective-permute-start(bf16[2,512,128]{2,1,0:T(8,128)(2,1)S(1)} %get-tuple-element.42), channel_id=1, source_target_pairs={{4,0},{8,4},{12,8},{16,12},{20,16},{24,20},{28,24},{5,1},{9,5},{13... | collective-permute-start | bytes 786440 | tf_op jit(solution)/shard_map/ppermute | solution.py:564
  70.9 13.8 %collective-permute-start.8 = (bf16[3,32,640]{2,1,0:T(8,128)(2,1)S(1)}, bf16[3,32,640]{2,1,0:T(8,128)(2,1)S(1)}, u32[]{:S(2)}, u32[]{:S(2)}) collective-permute-start(bf16[3,32,640]{2,1,0:T(8,128)(2,1)S(1)} %pad_maximum_fusion), channel_id=1, source_target_pairs={{0,2},{1,3},{4,6},{5,7},{8,10},{9,11},{12,14},{13,15},{16,18},{17,... | collective-permute-start | bytes 368648 | tf_op jit(solution)/shard_map/ppermute | solution.py:564
  73.3 23.4 %collective-permute-start.10 = (bf16[1,528,640]{2,1,0:T(8,128)(2,1)S(1)}, bf16[1,528,640]{2,1,0:T(8,128)(2,1)S(1)}, u32[]{:S(2)}, u32[]{:S(2)}) collective-permute-start(bf16[1,528,640]{2,1,0:T(8,128)(2,1)S(1)} %get-tuple-element.51.message_ref), channel_id=1, source_target_pairs={{1,0},{2,1},{3,2},{5,4},{6,5},{7,6},{9,8},{10,9},{11,10},{13,12},{... | collective-permute-start | bytes 2027528 | tf_op jit(solution)/shard_map/ppermute | solution.py:564
  77.3 19.4 %collective-permute-start.9 = (bf16[1,528,640]{2,1,0:T(8,128)(2,1)S(1)}, bf16[1,528,640]{2,1,0:T(8,128)(2,1)S(1)}, u32[]{:S(2)}, u32[]{:S(2)}) collective-permute-start(bf16[1,528,640]{2,1,0:T(8,128)(2,1)S(1)} %get-tuple-element.51.message_ref), channel_id=1, source_target_pairs={{0,1},{1,2},{2,3},{4,5},{5,6},{6,7},{8,9},{9,10},{10,11},{12,13},{... | collective-permute-start | bytes 2027528 | tf_op jit(solution)/shard_map/ppermute | solution.py:564
  79.2 29.8 %collective-permute-start.7 = (bf16[1,528,640]{2,1,0:T(8,128)(2,1)S(1)}, bf16[1,528,640]{2,1,0:T(8,128)(2,1)S(1)}, u32[]{:S(2)}, u32[]{:S(2)}) collective-permute-start(bf16[1,528,640]{2,1,0:T(8,128)(2,1)S(1)} %get-tuple-element.44.message_ref), channel_id=1, source_target_pairs={{1,0},{2,1},{3,2},{5,4},{6,5},{7,6},{9,8},{10,9},{11,10},{13,12},{... | collective-permute-start | bytes 2027528 | tf_op jit(solution)/shard_map/ppermute | solution.py:564
  82.6 26.8 %collective-permute-start.6 = (bf16[1,528,640]{2,1,0:T(8,128)(2,1)S(1)}, bf16[1,528,640]{2,1,0:T(8,128)(2,1)S(1)}, u32[]{:S(2)}, u32[]{:S(2)}) collective-permute-start(bf16[1,528,640]{2,1,0:T(8,128)(2,1)S(1)} %get-tuple-element.44.message_ref), channel_id=1, source_target_pairs={{0,1},{1,2},{2,3},{4,5},{5,6},{6,7},{8,9},{9,10},{10,11},{12,13},{... | collective-permute-start | bytes 2027528 | tf_op jit(solution)/shard_map/ppermute | solution.py:564

commit v7 on v6

--- a/solution.py
+++ b/solution.py
@@ -422,29 +422,38 @@
             pieces.append(ref[here, wide:])
         return jnp.concatenate(pieces, axis=1)
 
-    def correlate(source, which, size, start, exact, finish, lone=False):
+    def correlate(source, which, size, count, exact, finish, lone=False):
         deep = (size + 2 * REACH) * DEPTH
         size8 = size * DEPTH
         matrix = within_ref[0, which, :size8, :deep]
-        here = slice(start, start + size8)
-        for to in blocks:
-            if lone and to.stop == wide:
-                to = slice(to.start, wide + LANE)
-            out = dot(matrix, source[start : start + deep, to])
-            if exact:
-                high[here, to], low[here, to] = split(out)
-            else:
-                high[here, to] = out.astype(BF16)
+        for i in range(count):
+            here = slice(i * size8, (i + 1) * size8)
+            for to in blocks:
+                if lone and to.stop == wide:
+                    to = slice(to.start, wide + LANE)
+                out = dot(matrix, source[here.start : here.start + deep, to])
+                if i in exact:
+                    high[here, to], low[here, to] = split(out)
+                else:
+                    high[here, to] = out.astype(BF16)
+        everything = slice(0, count * size8)
         for to in blocks:
             width = to.stop - to.start
             if lone and to.stop == wide:
                 band = corner_ref[0, which]
             else:
                 band = across_ref[0, which, : width + 2 * LANE, :width]
-            out = dot(window(high, here, to, lone), band)
-            if exact:
-                out = out + dot(window(low, here, to, False), band)
-            finish(start, size8, to, out)
+            left = window(high, everything, to, lone)
+            if not exact:
+                finish(0, everything.stop, to, dot(left, band))
+                continue
+            here = slice(exact[0] * size8, (exact[-1] + 1) * size8)
+            out = dot(jnp.concatenate([left, window(low, here, to, False)], axis=0), band)
+            if here.start:
+                finish(0, here.start, to, out[: here.start])
+            finish(here.start, here.stop - here.start, to, out[here] + out[everything.stop :])
+            if here.stop < everything.stop:
+                finish(here.stop, everything.stop - here.stop, to, out[here.stop : everything.stop])
 
     def ratio_from(shift):
         def finish(start, size8, to, out):
@@ -469,15 +478,11 @@
         for b in range((to.stop - to.start) // LANE):
             result[to.start // LANE + b, start : start + size8, :] = value[:, b * LANE : (b + 1) * LANE]
 
-    for i in range(5):
-        correlate(joined_short, 0, BIG, i * BIG * DEPTH, False, ratio_from(REACH), True)
-    for i in range(4):
-        correlate(ratio, 1, BIG, i * BIG * DEPTH, i in (1, 2), first_estimate)
-    for i in range(4):
-        correlate(estimate_short, 0, SMALL, i * SMALL * DEPTH, False, ratio_from(3 * REACH))
+    correlate(joined_short, 0, BIG, 5, (), ratio_from(REACH), True)
+    correlate(ratio, 1, BIG, 4, (1, 2), first_estimate)
+    correlate(estimate_short, 0, SMALL, 4, (), ratio_from(3 * REACH))
     ratio[4 * SMALL * DEPTH : (4 * SMALL + 4) * DEPTH, :] = jnp.zeros((4 * DEPTH, wide), BF16)
-    for i in range(3):
-        correlate(ratio, 1, SMALL, i * SMALL * DEPTH, True, last_estimate)
+    correlate(ratio, 1, SMALL, 3, (0, 1, 2), last_estimate)
 
     planes = restored_ref.shape[1]
     height = restored_ref.shape[2]

time: 123 us -> 121 us (0.984)
  Pallas kernels: 52.9 us -> 48.7 us
  waiting for transfers between devices: 23.8 us -> 26.6 us
    pallas_call x3, Pallas kernels: 36.3 us -> 32.1 us  [deconvolve(): pl.pallas_call(functools.partial(deconvolve_kernel, at), grid=(1,), in_sp...]
    ppermute x13, waiting for transfers between devices: 23.8 us -> 26.6 us  [shift(): return lax.ppermute(block, axis, route)]
  transfers between devices with their start and end apart: 13 -> 13, of which waited for: 5 -> 6; matrix products, arithmetic and copies ran while one was open for 0% -> 0% of each run, Pallas kernels for 30% -> 28%
where the time goes in v7:
time: 121 us; the launch traced here: 120 us
  Pallas kernels  48.7 us (40%)
  starting transfers between devices  39.8 us (33%)
  waiting for transfers between devices  26.6 us (22%)
  local copies, waits for them, and re-layouts  3.69 us (3%)
    ppermute x13, starting transfers between devices, shift(): return lax.ppermute(block, axis, route)  39.8 us
    pallas_call x3, Pallas kernels, deconvolve(): pl.pallas_call(functools.partial(deconvolve_kernel, at), grid=(1,), in_sp...  32.1 us
    ppermute x13, waiting for transfers between devices, shift(): return lax.ppermute(block, axis, route)  26.6 us
    pallas_call x2, Pallas kernels, place(): pl.pallas_call(skipping(place_kernel, 2, len(after)), grid_spec=pltpu.Pre...  8.24 us
    pallas_call x3, Pallas kernels, join(): pl.pallas_call(functools.partial(join_kernel, at), in_specs=[pl.BlockSpec...  4.51 us
    unnamed x34, local copies, waits for them, and re-layouts  3.51 us
  transfers between devices with their start and end apart: 13, of which 6 were waited for; matrix products, arithmetic and copies ran while one was open for 0% of the time, Pallas kernels for 28%

profile of v7, /device:TPU:11, one launch (start us, length us, event | category | flops | bytes accessed | tf_op | source)
XLA Modules:
  0.0 120.1 jit_solution(3293973632217995252)
XLA Ops:
  0.6 1.8 %copy-done.2 = bf16[3,8,96,544]{3,2,1,0:T(8,128)(2,1)S(1)} copy-done((bf16[3,8,96,544]{3,2,1,0:T(8,128)(2,1)S(1)}, bf16[3,8,96,544]{3,2,1,0:T(8,128)(2,1)}, u32[]{:S(2)}) %copy-start.2) | copy-done | bytes 2506776
  2.5 0.7 copy-done.4
  3.1 3.2 %place.2 = (bf16[1,512,512]{2,1,0:T(8,128)(2,1)S(1)}, bf16[1,512,128]{2,1,0:T(8,128)(2,1)S(1)}, bf16[1,576,512]{2,1,0:T(8,128)(2,1)}) custom-call(s32[2]{0:T(128)S(1)} %bitcast.11, bf16[3,8,96,544]{3,2,1,0:T(8,128)(2,1)S(1)} %copy-done.2), custom_call_target="tpu_custom_call" | custom-call | flops 2000000000 | bytes 1 | tf_op jit(solution)/shard_map/place/pallas_call | solution.py:99
  6.3 3.2 %collective-permute-start.1 = (bf16[1,576,512]{2,1,0:T(8,128)(2,1)}, bf16[1,576,512]{2,1,0:T(8,128)(2,1)S(1)}, u32[]{:S(2)}, u32[]{:S(2)}) collective-permute-start(bf16[1,576,512]{2,1,0:T(8,128)(2,1)} %get-tuple-element.37), channel_id=1, source_target_pairs={{0,1},{1,2},{2,3},{4,5},{5,6},{6,7},{8,9},{9,10},{10,11},{12,13},{... | collective-permute-start | bytes 1769480 | tf_op jit(solution)/shard_map/ppermute | solution.py:569
  10.0 2.4 %bands.1 = (bf16[6,512,256]{2,1,0:T(8,128)(2,1)S(1)}, bf16[6,272,512]{2,1,0:T(8,128)(2,1)S(1)}, bf16[6,512,128]{2,1,0:T(8,128)(2,1)S(1)}) custom-call(f32[6,93]{1,0:T(8,128)S(1)} %reshape.23.refs_0_, bf16[1,512,128]{2,1,0:T(8,128)(2,1)S(1)} %get-tuple-element.31.refs_1_), custom_call_target="tpu_custom_call" | custom-call | flops 2000000000 | bytes 1 | tf_op jit(solution)/shard_map/bands/pallas_call | solution.py:269
  12.4 5.0 %place.3 = (bf16[2,512,512]{2,1,0:T(8,128)(2,1)S(1)}, bf16[2,512,128]{2,1,0:T(8,128)(2,1)S(1)}, bf16[2,576,512]{2,1,0:T(8,128)(2,1)}) custom-call(s32[2]{0:T(128)S(1)} %bitcast.12, bf16[3,8,96,544]{3,2,1,0:T(8,128)(2,1)S(1)} %copy-done.3, bf16[6,272,512]{2,1,0:T(8,128)(2,1)S(1)} %get-tuple-element.32.refs_2_), custom_call_target="tpu_custom_call" | custom-call | flops 4000000000 | bytes 1 | tf_op jit(solution)/shard_map/place/pallas_call | solution.py:99
  17.5 3.2 %collective-permute-start = (bf16[2,576,512]{2,1,0:T(8,128)(2,1)}, bf16[2,576,512]{2,1,0:T(8,128)(2,1)S(1)}, u32[]{:S(2)}, u32[]{:S(2)}) collective-permute-start(bf16[2,576,512]{2,1,0:T(8,128)(2,1)} %get-tuple-element.34), channel_id=1, source_target_pairs={{0,1},{1,2},{2,3},{4,5},{5,6},{6,7},{8,9},{9,10},{10,11},{12,13},{... | collective-permute-start | bytes 3538952 | tf_op jit(solution)/shard_map/ppermute | solution.py:569
  20.7 2.0 %collective-permute-done.1.refs_2_.low_ref = bf16[1,576,512]{2,1,0:T(8,128)(2,1)S(1)} collective-permute-done((bf16[1,576,512]{2,1,0:T(8,128)(2,1)}, bf16[1,576,512]{2,1,0:T(8,128)(2,1)S(1)}, u32[]{:S(2)}, u32[]{:S(2)}) %collective-permute-start.1) | collective-permute-done | bytes 589856 | tf_op jit(solution)/shard_map/ppermute | solution.py:569
  22.6 0.9 edges.2
  23.6 5.7 %collective-permute-start.2 = (bf16[1,1024,128]{2,1,0:T(8,128)(2,1)}, bf16[1,1024,128]{2,1,0:T(8,128)(2,1)}, u32[]{:S(2)}, u32[]{:S(2)}) collective-permute-start(bf16[1,1024,128]{2,1,0:T(8,128)(2,1)} %get-tuple-element.38.mine_ref), channel_id=1, source_target_pairs={{0,4},{4,8},{8,12},{12,16},{16,20},{20,24},{24,28},{1,5},{5,9},{9,... | collective-permute-start | bytes 786440 | tf_op jit(solution)/shard_map/ppermute | solution.py:569
  29.3 1.9 %collective-permute-start.3 = (bf16[1,512,128]{2,1,0:T(8,128)(2,1)}, bf16[1,512,128]{2,1,0:T(8,128)(2,1)S(1)}, u32[]{:S(2)}, u32[]{:S(2)}) collective-permute-start(bf16[1,512,128]{2,1,0:T(8,128)(2,1)} %get-tuple-element.39), channel_id=1, source_target_pairs={{4,0},{8,4},{12,8},{16,12},{20,16},{24,20},{28,24},{5,1},{9,5},{13... | collective-permute-start | bytes 393224 | tf_op jit(solution)/shard_map/ppermute | solution.py:569
  31.3 5.4 %collective-permute-done.3.right_ref = bf16[1,512,128]{2,1,0:T(8,128)(2,1)S(1)} collective-permute-done((bf16[1,512,128]{2,1,0:T(8,128)(2,1)}, bf16[1,512,128]{2,1,0:T(8,128)(2,1)S(1)}, u32[]{:S(2)}, u32[]{:S(2)}) %collective-permute-start.3) | collective-permute-done | bytes 131104 | tf_op jit(solution)/shard_map/ppermute | solution.py:569
  36.7 1.8 %join.3 = (f32[1,512,512]{2,1,0:T(8,128)S(1)}, bf16[1,528,640]{2,1,0:T(8,128)(2,1)S(1)}, bf16[1,32,640]{2,1,0:T(8,128)(2,1)S(1)}) custom-call(s32[4]{0:T(128)S(1)} %add_convert_fusion.sides_ref, bf16[1,512,512]{2,1,0:T(8,128)(2,1)S(1)} %get-tuple-element.36.refs_0_.own_ref, bf16[1,576,512]{2,1,0:T(8,128)(2,1)S(1)} %collective-permute-done.1.refs_2_.low_ref, ...), custom_call_target="tpu_custom_call" | custom-call | flops 1 | bytes 1 | tf_op jit(solution)/shard_map/join/pallas_call | solution.py:209
  38.5 9.4 %collective-permute-done.refs_2_.low_ref = bf16[2,576,512]{2,1,0:T(8,128)(2,1)S(1)} collective-permute-done((bf16[2,576,512]{2,1,0:T(8,128)(2,1)}, bf16[2,576,512]{2,1,0:T(8,128)(2,1)S(1)}, u32[]{:S(2)}, u32[]{:S(2)}) %collective-permute-start) | collective-permute-done | bytes 1179680 | tf_op jit(solution)/shard_map/ppermute | solution.py:569
  47.9 0.9 copy-done.1
  49.4 4.5 %collective-permute-start.4 = (bf16[2,1024,128]{2,1,0:T(8,128)(2,1)S(1)}, bf16[2,1024,128]{2,1,0:T(8,128)(2,1)S(1)}, u32[]{:S(2)}, u32[]{:S(2)}) collective-permute-start(bf16[2,1024,128]{2,1,0:T(8,128)(2,1)S(1)} %get-tuple-element.41.mine_ref), channel_id=1, source_target_pairs={{0,4},{4,8},{8,12},{12,16},{16,20},{20,24},{24,28},{1,5},{5,9},{9,... | collective-permute-start | bytes 1572872 | tf_op jit(solution)/shard_map/ppermute | solution.py:569
  54.0 1.9 %collective-permute-start.12 = (bf16[1,528,640]{2,1,0:T(8,128)(2,1)S(1)}, bf16[1,528,640]{2,1,0:T(8,128)(2,1)S(1)}, u32[]{:S(2)}, u32[]{:S(2)}) collective-permute-start(bf16[1,528,640]{2,1,0:T(8,128)(2,1)S(1)} %get-tuple-element.40.refs_3_.message_ref), channel_id=1, source_target_pairs={{1,0},{2,1},{3,2},{5,4},{6,5},{7,6},{9,8},{10,9},{11,10},{13,12},{... | collective-permute-start | bytes 2027528 | tf_op jit(solution)/shard_map/ppermute | solution.py:569
  55.9 3.4 %collective-permute-start.11 = (bf16[1,528,640]{2,1,0:T(8,128)(2,1)S(1)}, bf16[1,528,640]{2,1,0:T(8,128)(2,1)S(1)}, u32[]{:S(2)}, u32[]{:S(2)}) collective-permute-start(bf16[1,528,640]{2,1,0:T(8,128)(2,1)S(1)} %get-tuple-element.40.refs_3_.message_ref), channel_id=1, source_target_pairs={{0,1},{1,2},{2,3},{4,5},{5,6},{6,7},{8,9},{9,10},{10,11},{12,13},{... | collective-permute-start | bytes 2027528 | tf_op jit(solution)/shard_map/ppermute | solution.py:569
  59.3 2.2 %collective-permute-start.5 = (bf16[2,512,128]{2,1,0:T(8,128)(2,1)S(1)}, bf16[2,512,128]{2,1,0:T(8,128)(2,1)S(1)}, u32[]{:S(2)}, u32[]{:S(2)}) collective-permute-start(bf16[2,512,128]{2,1,0:T(8,128)(2,1)S(1)} %get-tuple-element.42), channel_id=1, source_target_pairs={{4,0},{8,4},{12,8},{16,12},{20,16},{24,20},{28,24},{5,1},{9,5},{13... | collective-permute-start | bytes 786440 | tf_op jit(solution)/shard_map/ppermute | solution.py:569
  61.5 6.7 %collective-permute-done.5.right_ref = bf16[2,512,128]{2,1,0:T(8,128)(2,1)S(1)} collective-permute-done((bf16[2,512,128]{2,1,0:T(8,128)(2,1)S(1)}, bf16[2,512,128]{2,1,0:T(8,128)(2,1)S(1)}, u32[]{:S(2)}, u32[]{:S(2)}) %collective-permute-start.5) | collective-permute-done | bytes 262176 | tf_op jit(solution)/shard_map/ppermute | solution.py:569
  68.2 1.3 %join.5 = (f32[1,512,512]{2,1,0:T(8,128)S(1)}, bf16[1,528,640]{2,1,0:T(8,128)(2,1)S(1)}, bf16[1,32,640]{2,1,0:T(8,128)(2,1)S(1)}) custom-call(s32[4]{0:T(128)S(1)} %add_convert_fusion.sides_ref, bf16[2,512,512]{2,1,0:T(8,128)(2,1)S(1)} %get-tuple-element.33.refs_0_.own_ref, bf16[2,576,512]{2,1,0:T(8,128)(2,1)S(1)} %collective-permute-done.refs_2_.low_ref, ...), custom_call_target="tpu_custom_call" | custom-call | flops 1 | bytes 1 | tf_op jit(solution)/shard_map/join/pallas_call | solution.py:209
  69.5 1.3 %join.4 = (f32[1,512,512]{2,1,0:T(8,128)S(1)}, bf16[1,528,640]{2,1,0:T(8,128)(2,1)S(1)}, bf16[1,32,640]{2,1,0:T(8,128)(2,1)S(1)}) custom-call(s32[4]{0:T(128)S(1)} %add_convert_fusion.sides_ref, bf16[2,512,512]{2,1,0:T(8,128)(2,1)S(1)} %get-tuple-element.33.refs_0_.own_ref, bf16[2,576,512]{2,1,0:T(8,128)(2,1)S(1)} %collective-permute-done.refs_2_.low_ref, ...), custom_call_target="tpu_custom_call" | custom-call | flops 1 | bytes 1 | tf_op jit(solution)/shard_map/join/pallas_call | solution.py:209
  70.9 2.3 %collective-permute-start.8 = (bf16[3,32,640]{2,1,0:T(8,128)(2,1)S(1)}, bf16[3,32,640]{2,1,0:T(8,128)(2,1)S(1)}, u32[]{:S(2)}, u32[]{:S(2)}) collective-permute-start(bf16[3,32,640]{2,1,0:T(8,128)(2,1)S(1)} %pad_maximum_fusion), channel_id=1, source_target_pairs={{0,2},{1,3},{4,6},{5,7},{8,10},{9,11},{12,14},{13,15},{16,18},{17,... | collective-permute-start | bytes 368648 | tf_op jit(solution)/shard_map/ppermute | solution.py:569
  73.3 4.0 %collective-permute-start.10 = (bf16[1,528,640]{2,1,0:T(8,128)(2,1)S(1)}, bf16[1,528,640]{2,1,0:T(8,128)(2,1)S(1)}, u32[]{:S(2)}, u32[]{:S(2)}) collective-permute-start(bf16[1,528,640]{2,1,0:T(8,128)(2,1)S(1)} %get-tuple-element.51.message_ref), channel_id=1, source_target_pairs={{1,0},{2,1},{3,2},{5,4},{6,5},{7,6},{9,8},{10,9},{11,10},{13,12},{... | collective-permute-start | bytes 2027528 | tf_op jit(solution)/shard_map/ppermute | solution.py:569
  77.3 1.9 %collective-permute-start.9 = (bf16[1,528,640]{2,1,0:T(8,128)(2,1)S(1)}, bf16[1,528,640]{2,1,0:T(8,128)(2,1)S(1)}, u32[]{:S(2)}, u32[]{:S(2)}) collective-permute-start(bf16[1,528,640]{2,1,0:T(8,128)(2,1)S(1)} %get-tuple-element.51.message_ref), channel_id=1, source_target_pairs={{0,1},{1,2},{2,3},{4,5},{5,6},{6,7},{8,9},{9,10},{10,11},{12,13},{... | collective-permute-start | bytes 2027528 | tf_op jit(solution)/shard_map/ppermute | solution.py:569
  79.2 3.4 %collective-permute-start.7 = (bf16[1,528,640]{2,1,0:T(8,128)(2,1)S(1)}, bf16[1,528,640]{2,1,0:T(8,128)(2,1)S(1)}, u32[]{:S(2)}, u32[]{:S(2)}) collective-permute-start(bf16[1,528,640]{2,1,0:T(8,128)(2,1)S(1)} %get-tuple-element.44.message_ref), channel_id=1, source_target_pairs={{1,0},{2,1},{3,2},{5,4},{6,5},{7,6},{9,8},{10,9},{11,10},{13,12},{... | collective-permute-start | bytes 2027528 | tf_op jit(solution)/shard_map/ppermute | solution.py:569
  82.6 2.1 %collective-permute-start.6 = (bf16[1,528,640]{2,1,0:T(8,128)(2,1)S(1)}, bf16[1,528,640]{2,1,0:T(8,128)(2,1)S(1)}, u32[]{:S(2)}, u32[]{:S(2)}) collective-permute-start(bf16[1,528,640]{2,1,0:T(8,128)(2,1)S(1)} %get-tuple-element.44.message_ref), channel_id=1, source_target_pairs={{0,1},{1,2},{2,3},{4,5},{5,6},{6,7},{8,9},{9,10},{10,11},{12,13},{... | collective-permute-start | bytes 2027528 | tf_op jit(solution)/shard_map/ppermute | solution.py:569
  84.8 10.4 %deconvolve.3 = (f32[3,8,64,512]{3,2,1,0:T(8,128)}, f32[3,4,32,256]{3,2,1,0:T(8,128)}, f32[3,2,16,128]{3,2,1,0:T(8,128)}) custom-call(s32[4]{0:T(128)S(1)} %add_convert_fusion.sides_ref, f32[1,512,512]{2,1,0:T(8,128)S(1)} %get-tuple-element.52.exact_ref, bf16[1,528,640]{2,1,0:T(8,128)(2,1)S(1)} %get-tuple-element.40.refs_3_.message_ref, ...), custom_call_target="tpu_custom_call" | custom-call | flops 10000000000 | bytes 1 | tf_op jit(solution)/shard_map/deconvolve/pallas_call | solution.py:534
  95.2 1.1 collective-permute-done.9.above_ref
  96.4 11.0 %deconvolve.4 = (f32[3,8,64,512]{3,2,1,0:T(8,128)}, f32[3,4,32,256]{3,2,1,0:T(8,128)}, f32[3,2,16,128]{3,2,1,0:T(8,128)}) custom-call(s32[4]{0:T(128)S(1)} %add_convert_fusion.sides_ref, f32[1,512,512]{2,1,0:T(8,128)S(1)} %get-tuple-element.50.exact_ref, ...), custom_call_target="tpu_custom_call", output_to_operand_aliasing={{0}: (13, {}), {1}: (14, {}), {2}: (15, {})} | custom-call | flops 10000000000 | bytes 1 | tf_op jit(solution)/shard_map/deconvolve/pallas_call | solution.py:534
  107.3 2.1 %collective-permute-done.6.above_ref = bf16[1,528,640]{2,1,0:T(8,128)(2,1)S(1)} collective-permute-done((bf16[1,528,640]{2,1,0:T(8,128)(2,1)S(1)}, bf16[1,528,640]{2,1,0:T(8,128)(2,1)S(1)}, u32[]{:S(2)}, u32[]{:S(2)}) %collective-permute-start.6) | collective-permute-done | bytes 675872 | tf_op jit(solution)/shard_map/ppermute | solution.py:569
  109.4 10.7 %deconvolve.5 = (f32[3,8,64,512]{3,2,1,0:T(8,128)}, f32[3,4,32,256]{3,2,1,0:T(8,128)}, f32[3,2,16,128]{3,2,1,0:T(8,128)}) custom-call(s32[4]{0:T(128)S(1)} %add_convert_fusion.sides_ref, f32[1,512,512]{2,1,0:T(8,128)S(1)} %get-tuple-element.43.exact_ref, ...), custom_call_target="tpu_custom_call", output_to_operand_aliasing={{0}: (13, {}), {1}: (14, {}), {2}: (15, {})} | custom-call | flops 10000000000 | bytes 1 | tf_op jit(solution)/shard_map/deconvolve/pallas_call | solution.py:534
  (48 shorter events, 1.2 us)
Async XLA Ops:
  0.6 1.8 %copy-start.2 = (bf16[3,8,96,544]{3,2,1,0:T(8,128)(2,1)S(1)}, bf16[3,8,96,544]{3,2,1,0:T(8,128)(2,1)}, u32[]{:S(2)}) copy-start(bf16[3,8,96,544]{3,2,1,0:T(8,128)(2,1)} %refs_1_.3) | copy-start | bytes 7520260
  2.5 0.7 copy-start.4
  3.1 6.4 %copy-start.16 = (f32[3,3,31]{2,1,0:T(4,128)S(1)}, f32[3,3,31]{2,1,0:T(4,128)}, u32[]{:S(2)}) copy-start(f32[3,3,31]{2,1,0:T(4,128)} %param.9) | copy-start | bytes 3352
  6.3 16.3 %collective-permute-start.1 = (bf16[1,576,512]{2,1,0:T(8,128)(2,1)}, bf16[1,576,512]{2,1,0:T(8,128)(2,1)S(1)}, u32[]{:S(2)}, u32[]{:S(2)}) collective-permute-start(bf16[1,576,512]{2,1,0:T(8,128)(2,1)} %get-tuple-element.37), channel_id=1, source_target_pairs={{0,1},{1,2},{2,3},{4,5},{5,6},{6,7},{8,9},{9,10},{10,11},{12,13},{... | collective-permute-start | bytes 1769480 | tf_op jit(solution)/shard_map/ppermute | solution.py:569
  10.0 2.4 %copy-start.3 = (bf16[3,8,96,544]{3,2,1,0:T(8,128)(2,1)S(1)}, bf16[3,8,96,544]{3,2,1,0:T(8,128)(2,1)}, u32[]{:S(2)}) copy-start(bf16[3,8,96,544]{3,2,1,0:T(8,128)(2,1)} %refs_1_.3) | copy-start | bytes 7520260
  10.0 2.4 %copy-start.5 = (s32[1,1,2]{2,1,0:T(1,128)S(1)}, s32[1,1,2]{2,1,0:T(1,128)}, u32[]{:S(2)}) copy-start(s32[1,1,2]{2,1,0:T(1,128)} %param.8) | copy-start | bytes 28
  12.3 5.1 %copy-start.6 = (bf16[6,272,512]{2,1,0:T(8,128)(2,1)}, bf16[6,272,512]{2,1,0:T(8,128)(2,1)S(1)}, u32[]{:S(2)}) copy-start(bf16[6,272,512]{2,1,0:T(8,128)(2,1)S(1)} %get-tuple-element.32.refs_2_) | copy-start | bytes 5013508
  12.4 5.1 %copy-start.8 = (bf16[6,512,256]{2,1,0:T(8,128)(2,1)}, bf16[6,512,256]{2,1,0:T(8,128)(2,1)S(1)}, u32[]{:S(2)}) copy-start(bf16[6,512,256]{2,1,0:T(8,128)(2,1)S(1)} %get-tuple-element.48) | copy-start | bytes 4718596
  12.4 5.1 %copy-start.10 = (bf16[6,512,128]{2,1,0:T(8,128)(2,1)}, bf16[6,512,128]{2,1,0:T(8,128)(2,1)S(1)}, u32[]{:S(2)}) copy-start(bf16[6,512,128]{2,1,0:T(8,128)(2,1)S(1)} %get-tuple-element.49) | copy-start | bytes 2359300
  17.4 6.1 %copy-start = (bf16[2,512,128]{2,1,0:T(8,128)(2,1)}, bf16[2,512,128]{2,1,0:T(8,128)(2,1)S(1)}, u32[]{:S(2)}) copy-start(bf16[2,512,128]{2,1,0:T(8,128)(2,1)S(1)} %get-tuple-element.35.refs_3_.refs_1_) | copy-start | bytes 786436
  17.5 30.4 %collective-permute-start = (bf16[2,576,512]{2,1,0:T(8,128)(2,1)}, bf16[2,576,512]{2,1,0:T(8,128)(2,1)S(1)}, u32[]{:S(2)}, u32[]{:S(2)}) collective-permute-start(bf16[2,576,512]{2,1,0:T(8,128)(2,1)} %get-tuple-element.34), channel_id=1, source_target_pairs={{0,1},{1,2},{2,3},{4,5},{5,6},{6,7},{8,9},{9,10},{10,11},{12,13},{... | collective-permute-start | bytes 3538952 | tf_op jit(solution)/shard_map/ppermute | solution.py:569
  23.6 13.1 %collective-permute-start.2 = (bf16[1,1024,128]{2,1,0:T(8,128)(2,1)}, bf16[1,1024,128]{2,1,0:T(8,128)(2,1)}, u32[]{:S(2)}, u32[]{:S(2)}) collective-permute-start(bf16[1,1024,128]{2,1,0:T(8,128)(2,1)} %get-tuple-element.38.mine_ref), channel_id=1, source_target_pairs={{0,4},{4,8},{8,12},{12,16},{16,20},{20,24},{24,28},{1,5},{5,9},{9,... | collective-permute-start | bytes 786440 | tf_op jit(solution)/shard_map/ppermute | solution.py:569
  29.3 7.4 %collective-permute-start.3 = (bf16[1,512,128]{2,1,0:T(8,128)(2,1)}, bf16[1,512,128]{2,1,0:T(8,128)(2,1)S(1)}, u32[]{:S(2)}, u32[]{:S(2)}) collective-permute-start(bf16[1,512,128]{2,1,0:T(8,128)(2,1)} %get-tuple-element.39), channel_id=1, source_target_pairs={{4,0},{8,4},{12,8},{16,12},{20,16},{24,20},{28,24},{5,1},{9,5},{13... | collective-permute-start | bytes 393224 | tf_op jit(solution)/shard_map/ppermute | solution.py:569
  47.9 1.0 copy-start.1
  49.4 18.8 %collective-permute-start.4 = (bf16[2,1024,128]{2,1,0:T(8,128)(2,1)S(1)}, bf16[2,1024,128]{2,1,0:T(8,128)(2,1)S(1)}, u32[]{:S(2)}, u32[]{:S(2)}) collective-permute-start(bf16[2,1024,128]{2,1,0:T(8,128)(2,1)S(1)} %get-tuple-element.41.mine_ref), channel_id=1, source_target_pairs={{0,4},{4,8},{8,12},{12,16},{16,20},{20,24},{24,28},{1,5},{5,9},{9,... | collective-permute-start | bytes 1572872 | tf_op jit(solution)/shard_map/ppermute | solution.py:569
  54.0 25.2 %collective-permute-start.12 = (bf16[1,528,640]{2,1,0:T(8,128)(2,1)S(1)}, bf16[1,528,640]{2,1,0:T(8,128)(2,1)S(1)}, u32[]{:S(2)}, u32[]{:S(2)}) collective-permute-start(bf16[1,528,640]{2,1,0:T(8,128)(2,1)S(1)} %get-tuple-element.40.refs_3_.message_ref), channel_id=1, source_target_pairs={{1,0},{2,1},{3,2},{5,4},{6,5},{7,6},{9,8},{10,9},{11,10},{13,12},{... | collective-permute-start | bytes 2027528 | tf_op jit(solution)/shard_map/ppermute | solution.py:569
  55.9 26.7 %collective-permute-start.11 = (bf16[1,528,640]{2,1,0:T(8,128)(2,1)S(1)}, bf16[1,528,640]{2,1,0:T(8,128)(2,1)S(1)}, u32[]{:S(2)}, u32[]{:S(2)}) collective-permute-start(bf16[1,528,640]{2,1,0:T(8,128)(2,1)S(1)} %get-tuple-element.40.refs_3_.message_ref), channel_id=1, source_target_pairs={{0,1},{1,2},{2,3},{4,5},{5,6},{6,7},{8,9},{9,10},{10,11},{12,13},{... | collective-permute-start | bytes 2027528 | tf_op jit(solution)/shard_map/ppermute | solution.py:569
  59.3 25.5 %copy-start.7 = (bf16[6,272,512]{2,1,0:T(8,128)(2,1)S(1)}, bf16[6,272,512]{2,1,0:T(8,128)(2,1)}, u32[]{:S(2)}) copy-start(bf16[6,272,512]{2,1,0:T(8,128)(2,1)} %copy-done.6) | copy-start | bytes 5013508
  59.3 25.5 %copy-start.9 = (bf16[6,512,256]{2,1,0:T(8,128)(2,1)S(1)}, bf16[6,512,256]{2,1,0:T(8,128)(2,1)}, u32[]{:S(2)}) copy-start(bf16[6,512,256]{2,1,0:T(8,128)(2,1)} %copy-done.8) | copy-start | bytes 4718596
  59.3 25.5 %copy-start.11 = (bf16[6,512,128]{2,1,0:T(8,128)(2,1)S(1)}, bf16[6,512,128]{2,1,0:T(8,128)(2,1)}, u32[]{:S(2)}) copy-start(bf16[6,512,128]{2,1,0:T(8,128)(2,1)} %copy-done.10) | copy-start | bytes 2359300
  59.3 25.5 %copy-start.12 = (bf16[640,384]{1,0:T(8,128)(2,1)S(1)}, bf16[640,384]{1,0:T(8,128)(2,1)}, u32[]{:S(2)}) copy-start(bf16[640,384]{1,0:T(8,128)(2,1)} %constant.25.clone.one_x_ref) | copy-start | bytes 1474564
  59.3 25.5 %copy-start.13 = (bf16[144,592]{1,0:T(8,128)(2,1)S(1)}, bf16[144,592]{1,0:T(8,128)(2,1)}, u32[]{:S(2)}) copy-start(bf16[144,592]{1,0:T(8,128)(2,1)} %constant.26.clone.one_zy_ref) | copy-start | bytes 511492
  59.3 25.5 %copy-start.14 = (bf16[384,128]{1,0:T(8,128)(2,1)S(1)}, bf16[384,128]{1,0:T(8,128)(2,1)}, u32[]{:S(2)}) copy-start(bf16[384,128]{1,0:T(8,128)(2,1)} %constant.27.clone.two_x_ref) | copy-start | bytes 294916
  59.3 25.5 %copy-start.15 = (bf16[32,144]{1,0:T(8,128)(2,1)S(1)}, bf16[32,144]{1,0:T(8,128)(2,1)}, u32[]{:S(2)}) copy-start(bf16[32,144]{1,0:T(8,128)(2,1)} %constant.28.clone.two_zy_ref) | copy-start | bytes 27652
  59.3 8.9 %collective-permute-start.5 = (bf16[2,512,128]{2,1,0:T(8,128)(2,1)S(1)}, bf16[2,512,128]{2,1,0:T(8,128)(2,1)S(1)}, u32[]{:S(2)}, u32[]{:S(2)}) collective-permute-start(bf16[2,512,128]{2,1,0:T(8,128)(2,1)S(1)} %get-tuple-element.42), channel_id=1, source_target_pairs={{4,0},{8,4},{12,8},{16,12},{20,16},{24,20},{28,24},{5,1},{9,5},{13... | collective-permute-start | bytes 786440 | tf_op jit(solution)/shard_map/ppermute | solution.py:569
  70.9 13.8 %collective-permute-start.8 = (bf16[3,32,640]{2,1,0:T(8,128)(2,1)S(1)}, bf16[3,32,640]{2,1,0:T(8,128)(2,1)S(1)}, u32[]{:S(2)}, u32[]{:S(2)}) collective-permute-start(bf16[3,32,640]{2,1,0:T(8,128)(2,1)S(1)} %pad_maximum_fusion), channel_id=1, source_target_pairs={{0,2},{1,3},{4,6},{5,7},{8,10},{9,11},{12,14},{13,15},{16,18},{17,... | collective-permute-start | bytes 368648 | tf_op jit(solution)/shard_map/ppermute | solution.py:569
  73.3 22.0 %collective-permute-start.10 = (bf16[1,528,640]{2,1,0:T(8,128)(2,1)S(1)}, bf16[1,528,640]{2,1,0:T(8,128)(2,1)S(1)}, u32[]{:S(2)}, u32[]{:S(2)}) collective-permute-start(bf16[1,528,640]{2,1,0:T(8,128)(2,1)S(1)} %get-tuple-element.51.message_ref), channel_id=1, source_target_pairs={{1,0},{2,1},{3,2},{5,4},{6,5},{7,6},{9,8},{10,9},{11,10},{13,12},{... | collective-permute-start | bytes 2027528 | tf_op jit(solution)/shard_map/ppermute | solution.py:569
  77.3 19.1 %collective-permute-start.9 = (bf16[1,528,640]{2,1,0:T(8,128)(2,1)S(1)}, bf16[1,528,640]{2,1,0:T(8,128)(2,1)S(1)}, u32[]{:S(2)}, u32[]{:S(2)}) collective-permute-start(bf16[1,528,640]{2,1,0:T(8,128)(2,1)S(1)} %get-tuple-element.51.message_ref), channel_id=1, source_target_pairs={{0,1},{1,2},{2,3},{4,5},{5,6},{6,7},{8,9},{9,10},{10,11},{12,13},{... | collective-permute-start | bytes 2027528 | tf_op jit(solution)/shard_map/ppermute | solution.py:569
  79.2 28.1 %collective-permute-start.7 = (bf16[1,528,640]{2,1,0:T(8,128)(2,1)S(1)}, bf16[1,528,640]{2,1,0:T(8,128)(2,1)S(1)}, u32[]{:S(2)}, u32[]{:S(2)}) collective-permute-start(bf16[1,528,640]{2,1,0:T(8,128)(2,1)S(1)} %get-tuple-element.44.message_ref), channel_id=1, source_target_pairs={{1,0},{2,1},{3,2},{5,4},{6,5},{7,6},{9,8},{10,9},{11,10},{13,12},{... | collective-permute-start | bytes 2027528 | tf_op jit(solution)/shard_map/ppermute | solution.py:569
  82.6 26.8 %collective-permute-start.6 = (bf16[1,528,640]{2,1,0:T(8,128)(2,1)S(1)}, bf16[1,528,640]{2,1,0:T(8,128)(2,1)S(1)}, u32[]{:S(2)}, u32[]{:S(2)}) collective-permute-start(bf16[1,528,640]{2,1,0:T(8,128)(2,1)S(1)} %get-tuple-element.44.message_ref), channel_id=1, source_target_pairs={{0,1},{1,2},{2,3},{4,5},{5,6},{6,7},{8,9},{9,10},{10,11},{12,13},{... | collective-permute-start | bytes 2027528 | tf_op jit(solution)/shard_map/ppermute | solution.py:569

commit v8 on v7

--- a/solution.py
+++ b/solution.py
@@ -54,20 +54,23 @@
     return high, (value - high.astype(F32)).astype(BF16)
 
 
-def place_kernel(off_ref, tile_ref, own_ref, right_ref, low_ref, canvas):
+def place_kernel(begin, off_ref, tiles_ref, own_ref, right_ref, low_ref, canvas, tile_ref, sem):
     depth, tile_y, tile_x = tile_ref.shape[1:]
+    copy = pltpu.make_async_copy(tiles_ref.at[pl.ds(begin + pl.program_id(0), 1)], tile_ref, sem)
+    copy.start()
     parts = canvas.shape[0]
     wide = parts * LANE
     rows = own_ref.shape[1]
     cols = own_ref.shape[2]
-    top = off_ref[0]
-    left = off_ref[1]
+    top = off_ref[0, 0, 0]
+    left = off_ref[0, 0, 1]
     canvas[...] = jnp.zeros_like(canvas)
     shift = (
         lax.broadcasted_iota(jnp.int32, (tile_x, wide), 1)
         == lax.broadcasted_iota(jnp.int32, (tile_x, wide), 0) + left
     )
     shift = jnp.where(shift, 1.0, 0.0).astype(BF16)
+    copy.wait()
     for z in range(depth):
         moved = dot(tile_ref[0, z], shift)
         for b in range(parts):
@@ -91,20 +94,21 @@
     _, depth, tile_y, tile_x = tiles.shape
     rows = (tile_y - MARGIN) * depth
     cols = tile_x - MARGIN
-    block = lambda r, c: pl.BlockSpec((1, r, c), lambda i, off: (i, 0, 0))
+    block = lambda r, c: pl.BlockSpec((1, r, c), lambda i: (i, 0, 0))
     shape = lambda r, c: jax.ShapeDtypeStruct((n, r, c), BF16)
     extra = rows // 2 * LANE // cols
     sizes = ((rows, cols), (rows, LANE), (rows + extra, cols))
-    tile = pl.BlockSpec((1, depth, tile_y, tile_x), lambda i, off: (begin + i, 0, 0, 0))
     return pl.pallas_call(
-        skipping(place_kernel, 2, len(after)),
-        grid_spec=pltpu.PrefetchScalarGridSpec(
-            num_scalar_prefetch=1,
-            grid=(n,),
-            in_specs=[tile] + [ANY] * len(after),
-            out_specs=[block(*s) for s in sizes],
-            scratch_shapes=[pltpu.VMEM((cols // LANE + 1, 2 * rows, LANE), F32)],
-        ),
+        skipping(functools.partial(place_kernel, begin), 2, len(after)),
+        grid=(n,),
+        in_specs=[pl.BlockSpec(memory_space=pltpu.SMEM), pl.BlockSpec(memory_space=pltpu.HBM)]
+        + [ANY] * len(after),
+        out_specs=[block(*s) for s in sizes],
+        scratch_shapes=[
+            pltpu.VMEM((cols // LANE + 1, 2 * rows, LANE), F32),
+            pltpu.VMEM((1, depth, tile_y, tile_x), BF16),
+            pltpu.SemaphoreType.DMA,
+        ],
         out_shape=[shape(*s) for s in sizes],
         compiler_params=params(16),
         cost_estimate=cost(n * 2e9, 1),
@@ -212,7 +216,7 @@
         out_specs=[VMEM] * 3,
         out_shape=[jax.ShapeDtypeStruct((1, r, c), t) for r, c, t in sizes],
         compiler_params=params(12),
-        cost_estimate=cost(1, 1),
+        cost_estimate=cost(5e9 if own.shape[0]>1 else 1, 1),
         name="join",
     )(sides, own, low, mine, left, right)
 
@@ -572,13 +576,12 @@
     sides = sides.astype(jnp.int32)
     matrices = [jnp.asarray(m) for m in pyramid_matrices(rows, cols, depth)]
 
-    at_tile = offsets.reshape(2)
-    own, right, low = place(tiles, at_tile, 0, 1, ())
+    own, right, low = place(tiles, offsets, 0, 1, ())
     kern = psf / jnp.sum(psf, axis=-1, keepdims=True)
     both = jnp.stack([kern, kern[:, :, ::-1]], axis=1)
     tables = bands(both.reshape(chans * 2, 3 * TAPS), (right,))
     pieces = [(own, right, shift(low, "gy", 1))]
-    own, right, low = place(tiles, at_tile, 1, chans - 1, (tables[1],))
+    own, right, low = place(tiles, offsets, 1, chans - 1, (tables[1],))
     pieces.append((own, right, shift(low, "gy", 1)))
     tables = [t.reshape((chans, 2) + t.shape[1:]) for t in tables]
 

time: 121 us -> 123 us (1.017)
  the two profiles are of different devices: /device:TPU:11 before, /device:TPU:20 now
where the time goes in v8:
time: 123 us; the launch traced here: 122 us
  Pallas kernels  50 us (41%)
  starting transfers between devices  38.8 us (32%)
  waiting for transfers between devices  28.2 us (23%)
  local copies, waits for them, and re-layouts  3.69 us (3%)
    ppermute x13, starting transfers between devices, shift(): return lax.ppermute(block, axis, route)  38.8 us
    pallas_call x3, Pallas kernels, deconvolve(): pl.pallas_call(functools.partial(deconvolve_kernel, at), grid=(1,), in_sp...  32.1 us
    ppermute x13, waiting for transfers between devices, shift(): return lax.ppermute(block, axis, route)  28.2 us
    pallas_call x2, Pallas kernels, place(): pl.pallas_call(skipping(functools.partial(place_kernel, begin), 2, len(af...  9.59 us
    pallas_call x3, Pallas kernels, join(): pl.pallas_call(functools.partial(join_kernel, at), in_specs=[pl.BlockSpec...  4.51 us
    unnamed x34, local copies, waits for them, and re-layouts  3.51 us
  transfers between devices with their start and end apart: 13, of which 8 were waited for; matrix products, arithmetic and copies ran while one was open for 0% of the time, Pallas kernels for 29%

profile of v8, /device:TPU:20, one launch (start us, length us, event | category | flops | bytes accessed | tf_op | source)
XLA Modules:
  0.0 122.2 jit_solution(6585127483140764557)
XLA Ops:
  0.6 1.8 %copy-done.2 = bf16[3,8,96,544]{3,2,1,0:T(8,128)(2,1)S(1)} copy-done((bf16[3,8,96,544]{3,2,1,0:T(8,128)(2,1)S(1)}, bf16[3,8,96,544]{3,2,1,0:T(8,128)(2,1)}, u32[]{:S(2)}) %copy-start.2) | copy-done | bytes 2506776
  3.1 3.6 %place.2 = (bf16[1,512,512]{2,1,0:T(8,128)(2,1)S(1)}, bf16[1,512,128]{2,1,0:T(8,128)(2,1)S(1)}, bf16[1,576,512]{2,1,0:T(8,128)(2,1)}) custom-call(s32[1,1,2]{2,1,0:T(1,128)S(1)} %copy-done.4, bf16[3,8,96,544]{3,2,1,0:T(8,128)(2,1)S(1)} %copy-done.2), custom_call_target="tpu_custom_call" | custom-call | flops 2000000000 | bytes 1 | tf_op jit(solution)/shard_map/place/pallas_call | solution.py:101
  6.8 3.5 %collective-permute-start.1 = (bf16[1,576,512]{2,1,0:T(8,128)(2,1)}, bf16[1,576,512]{2,1,0:T(8,128)(2,1)S(1)}, u32[]{:S(2)}, u32[]{:S(2)}) collective-permute-start(bf16[1,576,512]{2,1,0:T(8,128)(2,1)} %get-tuple-element.37), channel_id=1, source_target_pairs={{0,1},{1,2},{2,3},{4,5},{5,6},{6,7},{8,9},{9,10},{10,11},{12,13},{... | collective-permute-start | bytes 1769480 | tf_op jit(solution)/shard_map/ppermute | solution.py:573
  10.7 2.4 %bands.1 = (bf16[6,512,256]{2,1,0:T(8,128)(2,1)S(1)}, bf16[6,272,512]{2,1,0:T(8,128)(2,1)S(1)}, bf16[6,512,128]{2,1,0:T(8,128)(2,1)S(1)}) custom-call(f32[6,93]{1,0:T(8,128)S(1)} %reshape.19.refs_0_, bf16[1,512,128]{2,1,0:T(8,128)(2,1)S(1)} %get-tuple-element.31.refs_1_), custom_call_target="tpu_custom_call" | custom-call | flops 2000000000 | bytes 1 | tf_op jit(solution)/shard_map/bands/pallas_call | solution.py:273
  13.1 6.0 %place.3 = (bf16[2,512,512]{2,1,0:T(8,128)(2,1)S(1)}, bf16[2,512,128]{2,1,0:T(8,128)(2,1)S(1)}, bf16[2,576,512]{2,1,0:T(8,128)(2,1)}) custom-call(s32[1,1,2]{2,1,0:T(1,128)S(1)} %copy-done.5, bf16[3,8,96,544]{3,2,1,0:T(8,128)(2,1)S(1)} %copy-done.3, bf16[6,272,512]{2,1,0:T(8,128)(2,1)S(1)} %get-tuple-element.32.refs_2_), custom_call_target="tpu_custom_call" | custom-call | flops 4000000000 | bytes 1 | tf_op jit(solution)/shard_map/place/pallas_call | solution.py:101
  19.1 1.9 %collective-permute-start = (bf16[2,576,512]{2,1,0:T(8,128)(2,1)}, bf16[2,576,512]{2,1,0:T(8,128)(2,1)S(1)}, u32[]{:S(2)}, u32[]{:S(2)}) collective-permute-start(bf16[2,576,512]{2,1,0:T(8,128)(2,1)} %get-tuple-element.34), channel_id=1, source_target_pairs={{0,1},{1,2},{2,3},{4,5},{5,6},{6,7},{8,9},{9,10},{10,11},{12,13},{... | collective-permute-start | bytes 3538952 | tf_op jit(solution)/shard_map/ppermute | solution.py:573
  21.1 3.3 %collective-permute-done.1.refs_2_.low_ref = bf16[1,576,512]{2,1,0:T(8,128)(2,1)S(1)} collective-permute-done((bf16[1,576,512]{2,1,0:T(8,128)(2,1)}, bf16[1,576,512]{2,1,0:T(8,128)(2,1)S(1)}, u32[]{:S(2)}, u32[]{:S(2)}) %collective-permute-start.1) | collective-permute-done | bytes 589856 | tf_op jit(solution)/shard_map/ppermute | solution.py:573
  24.4 0.9 edges.2
  25.4 1.9 %collective-permute-start.2 = (bf16[1,1024,128]{2,1,0:T(8,128)(2,1)}, bf16[1,1024,128]{2,1,0:T(8,128)(2,1)}, u32[]{:S(2)}, u32[]{:S(2)}) collective-permute-start(bf16[1,1024,128]{2,1,0:T(8,128)(2,1)} %get-tuple-element.38.mine_ref), channel_id=1, source_target_pairs={{0,4},{4,8},{8,12},{12,16},{16,20},{20,24},{24,28},{1,5},{5,9},{9,... | collective-permute-start | bytes 786440 | tf_op jit(solution)/shard_map/ppermute | solution.py:573
  27.3 4.5 %collective-permute-start.3 = (bf16[1,512,128]{2,1,0:T(8,128)(2,1)}, bf16[1,512,128]{2,1,0:T(8,128)(2,1)S(1)}, u32[]{:S(2)}, u32[]{:S(2)}) collective-permute-start(bf16[1,512,128]{2,1,0:T(8,128)(2,1)} %get-tuple-element.39), channel_id=1, source_target_pairs={{4,0},{8,4},{12,8},{16,12},{20,16},{24,20},{28,24},{5,1},{9,5},{13... | collective-permute-start | bytes 393224 | tf_op jit(solution)/shard_map/ppermute | solution.py:573
  31.9 2.7 %collective-permute-done.3.right_ref = bf16[1,512,128]{2,1,0:T(8,128)(2,1)S(1)} collective-permute-done((bf16[1,512,128]{2,1,0:T(8,128)(2,1)}, bf16[1,512,128]{2,1,0:T(8,128)(2,1)S(1)}, u32[]{:S(2)}, u32[]{:S(2)}) %collective-permute-start.3) | collective-permute-done | bytes 131104 | tf_op jit(solution)/shard_map/ppermute | solution.py:573
  34.6 1.8 %join.3 = (f32[1,512,512]{2,1,0:T(8,128)S(1)}, bf16[1,528,640]{2,1,0:T(8,128)(2,1)S(1)}, bf16[1,32,640]{2,1,0:T(8,128)(2,1)S(1)}) custom-call(s32[4]{0:T(128)S(1)} %add_convert_fusion.sides_ref, bf16[1,512,512]{2,1,0:T(8,128)(2,1)S(1)} %get-tuple-element.36.refs_0_.own_ref, bf16[1,576,512]{2,1,0:T(8,128)(2,1)S(1)} %collective-permute-done.1.refs_2_.low_ref, ...), custom_call_target="tpu_custom_call" | custom-call | flops 1 | bytes 1 | tf_op jit(solution)/shard_map/join/pallas_call | solution.py:213
  36.5 12.7 %collective-permute-done.refs_2_.low_ref = bf16[2,576,512]{2,1,0:T(8,128)(2,1)S(1)} collective-permute-done((bf16[2,576,512]{2,1,0:T(8,128)(2,1)}, bf16[2,576,512]{2,1,0:T(8,128)(2,1)S(1)}, u32[]{:S(2)}, u32[]{:S(2)}) %collective-permute-start) | collective-permute-done | bytes 1179680 | tf_op jit(solution)/shard_map/ppermute | solution.py:573
  49.2 0.9 copy-done.1
  50.7 1.9 %collective-permute-start.4 = (bf16[2,1024,128]{2,1,0:T(8,128)(2,1)S(1)}, bf16[2,1024,128]{2,1,0:T(8,128)(2,1)S(1)}, u32[]{:S(2)}, u32[]{:S(2)}) collective-permute-start(bf16[2,1024,128]{2,1,0:T(8,128)(2,1)S(1)} %get-tuple-element.41.mine_ref), channel_id=1, source_target_pairs={{0,4},{4,8},{8,12},{12,16},{16,20},{20,24},{24,28},{1,5},{5,9},{9,... | collective-permute-start | bytes 1572872 | tf_op jit(solution)/shard_map/ppermute | solution.py:573
  52.7 4.5 %collective-permute-start.5 = (bf16[2,512,128]{2,1,0:T(8,128)(2,1)S(1)}, bf16[2,512,128]{2,1,0:T(8,128)(2,1)S(1)}, u32[]{:S(2)}, u32[]{:S(2)}) collective-permute-start(bf16[2,512,128]{2,1,0:T(8,128)(2,1)S(1)} %get-tuple-element.42), channel_id=1, source_target_pairs={{4,0},{8,4},{12,8},{16,12},{20,16},{24,20},{28,24},{5,1},{9,5},{13... | collective-permute-start | bytes 786440 | tf_op jit(solution)/shard_map/ppermute | solution.py:573
  57.2 2.4 %collective-permute-start.12 = (bf16[1,528,640]{2,1,0:T(8,128)(2,1)S(1)}, bf16[1,528,640]{2,1,0:T(8,128)(2,1)S(1)}, u32[]{:S(2)}, u32[]{:S(2)}) collective-permute-start(bf16[1,528,640]{2,1,0:T(8,128)(2,1)S(1)} %get-tuple-element.40.refs_3_.message_ref), channel_id=1, source_target_pairs={{1,0},{2,1},{3,2},{5,4},{6,5},{7,6},{9,8},{10,9},{11,10},{13,12},{... | collective-permute-start | bytes 2027528 | tf_op jit(solution)/shard_map/ppermute | solution.py:573
  59.6 3.5 %collective-permute-start.11 = (bf16[1,528,640]{2,1,0:T(8,128)(2,1)S(1)}, bf16[1,528,640]{2,1,0:T(8,128)(2,1)S(1)}, u32[]{:S(2)}, u32[]{:S(2)}) collective-permute-start(bf16[1,528,640]{2,1,0:T(8,128)(2,1)S(1)} %get-tuple-element.40.refs_3_.message_ref), channel_id=1, source_target_pairs={{0,1},{1,2},{2,3},{4,5},{5,6},{6,7},{8,9},{9,10},{10,11},{12,13},{... | collective-permute-start | bytes 2027528 | tf_op jit(solution)/shard_map/ppermute | solution.py:573
  63.1 1.8 %collective-permute-done.4.left_ref = bf16[2,1024,128]{2,1,0:T(8,128)(2,1)S(1)} collective-permute-done((bf16[2,1024,128]{2,1,0:T(8,128)(2,1)S(1)}, bf16[2,1024,128]{2,1,0:T(8,128)(2,1)S(1)}, u32[]{:S(2)}, u32[]{:S(2)}) %collective-permute-start.4) | collective-permute-done | bytes 524320 | tf_op jit(solution)/shard_map/ppermute | solution.py:573
  64.9 1.3 %join.5 = (f32[1,512,512]{2,1,0:T(8,128)S(1)}, bf16[1,528,640]{2,1,0:T(8,128)(2,1)S(1)}, bf16[1,32,640]{2,1,0:T(8,128)(2,1)S(1)}) custom-call(s32[4]{0:T(128)S(1)} %add_convert_fusion.sides_ref, bf16[2,512,512]{2,1,0:T(8,128)(2,1)S(1)} %get-tuple-element.33.refs_0_.own_ref, bf16[2,576,512]{2,1,0:T(8,128)(2,1)S(1)} %collective-permute-done.refs_2_.low_ref, ...), custom_call_target="tpu_custom_call" | custom-call | flops 5000000000 | bytes 1 | tf_op jit(solution)/shard_map/join/pallas_call | solution.py:213
  66.3 1.3 %join.4 = (f32[1,512,512]{2,1,0:T(8,128)S(1)}, bf16[1,528,640]{2,1,0:T(8,128)(2,1)S(1)}, bf16[1,32,640]{2,1,0:T(8,128)(2,1)S(1)}) custom-call(s32[4]{0:T(128)S(1)} %add_convert_fusion.sides_ref, bf16[2,512,512]{2,1,0:T(8,128)(2,1)S(1)} %get-tuple-element.33.refs_0_.own_ref, bf16[2,576,512]{2,1,0:T(8,128)(2,1)S(1)} %collective-permute-done.refs_2_.low_ref, ...), custom_call_target="tpu_custom_call" | custom-call | flops 5000000000 | bytes 1 | tf_op jit(solution)/shard_map/join/pallas_call | solution.py:213
  67.7 1.4 %collective-permute-start.8 = (bf16[3,32,640]{2,1,0:T(8,128)(2,1)S(1)}, bf16[3,32,640]{2,1,0:T(8,128)(2,1)S(1)}, u32[]{:S(2)}, u32[]{:S(2)}) collective-permute-start(bf16[3,32,640]{2,1,0:T(8,128)(2,1)S(1)} %pad_maximum_fusion), channel_id=1, source_target_pairs={{0,2},{1,3},{4,6},{5,7},{8,10},{9,11},{12,14},{13,15},{16,18},{17,... | collective-permute-start | bytes 368648 | tf_op jit(solution)/shard_map/ppermute | solution.py:573
  69.1 5.6 %collective-permute-start.10 = (bf16[1,528,640]{2,1,0:T(8,128)(2,1)S(1)}, bf16[1,528,640]{2,1,0:T(8,128)(2,1)S(1)}, u32[]{:S(2)}, u32[]{:S(2)}) collective-permute-start(bf16[1,528,640]{2,1,0:T(8,128)(2,1)S(1)} %get-tuple-element.51.message_ref), channel_id=1, source_target_pairs={{1,0},{2,1},{3,2},{5,4},{6,5},{7,6},{9,8},{10,9},{11,10},{13,12},{... | collective-permute-start | bytes 2027528 | tf_op jit(solution)/shard_map/ppermute | solution.py:573
  74.7 1.9 %collective-permute-start.9 = (bf16[1,528,640]{2,1,0:T(8,128)(2,1)S(1)}, bf16[1,528,640]{2,1,0:T(8,128)(2,1)S(1)}, u32[]{:S(2)}, u32[]{:S(2)}) collective-permute-start(bf16[1,528,640]{2,1,0:T(8,128)(2,1)S(1)} %get-tuple-element.51.message_ref), channel_id=1, source_target_pairs={{0,1},{1,2},{2,3},{4,5},{5,6},{6,7},{8,9},{9,10},{10,11},{12,13},{... | collective-permute-start | bytes 2027528 | tf_op jit(solution)/shard_map/ppermute | solution.py:573
  77.2 3.4 %collective-permute-start.7 = (bf16[1,528,640]{2,1,0:T(8,128)(2,1)S(1)}, bf16[1,528,640]{2,1,0:T(8,128)(2,1)S(1)}, u32[]{:S(2)}, u32[]{:S(2)}) collective-permute-start(bf16[1,528,640]{2,1,0:T(8,128)(2,1)S(1)} %get-tuple-element.44.message_ref), channel_id=1, source_target_pairs={{1,0},{2,1},{3,2},{5,4},{6,5},{7,6},{9,8},{10,9},{11,10},{13,12},{... | collective-permute-start | bytes 2027528 | tf_op jit(solution)/shard_map/ppermute | solution.py:573
  80.6 1.6 %collective-permute-done.11.above_ref = bf16[1,528,640]{2,1,0:T(8,128)(2,1)S(1)} collective-permute-done((bf16[1,528,640]{2,1,0:T(8,128)(2,1)S(1)}, bf16[1,528,640]{2,1,0:T(8,128)(2,1)S(1)}, u32[]{:S(2)}, u32[]{:S(2)}) %collective-permute-start.11) | collective-permute-done | bytes 675872 | tf_op jit(solution)/shard_map/ppermute | solution.py:573
  82.2 2.4 %collective-permute-start.6 = (bf16[1,528,640]{2,1,0:T(8,128)(2,1)S(1)}, bf16[1,528,640]{2,1,0:T(8,128)(2,1)S(1)}, u32[]{:S(2)}, u32[]{:S(2)}) collective-permute-start(bf16[1,528,640]{2,1,0:T(8,128)(2,1)S(1)} %get-tuple-element.44.message_ref), channel_id=1, source_target_pairs={{0,1},{1,2},{2,3},{4,5},{5,6},{6,7},{8,9},{9,10},{10,11},{12,13},{... | collective-permute-start | bytes 2027528 | tf_op jit(solution)/shard_map/ppermute | solution.py:573
  84.7 10.4 %deconvolve.3 = (f32[3,8,64,512]{3,2,1,0:T(8,128)}, f32[3,4,32,256]{3,2,1,0:T(8,128)}, f32[3,2,16,128]{3,2,1,0:T(8,128)}) custom-call(s32[4]{0:T(128)S(1)} %add_convert_fusion.sides_ref, f32[1,512,512]{2,1,0:T(8,128)S(1)} %get-tuple-element.52.exact_ref, bf16[1,528,640]{2,1,0:T(8,128)(2,1)S(1)} %get-tuple-element.40.refs_3_.message_ref, ...), custom_call_target="tpu_custom_call" | custom-call | flops 10000000000 | bytes 1 | tf_op jit(solution)/shard_map/deconvolve/pallas_call | solution.py:538
  95.1 4.2 %collective-permute-done.9.above_ref = bf16[1,528,640]{2,1,0:T(8,128)(2,1)S(1)} collective-permute-done((bf16[1,528,640]{2,1,0:T(8,128)(2,1)S(1)}, bf16[1,528,640]{2,1,0:T(8,128)(2,1)S(1)}, u32[]{:S(2)}, u32[]{:S(2)}) %collective-permute-start.9) | collective-permute-done | bytes 675872 | tf_op jit(solution)/shard_map/ppermute | solution.py:573
  99.3 11.0 %deconvolve.4 = (f32[3,8,64,512]{3,2,1,0:T(8,128)}, f32[3,4,32,256]{3,2,1,0:T(8,128)}, f32[3,2,16,128]{3,2,1,0:T(8,128)}) custom-call(s32[4]{0:T(128)S(1)} %add_convert_fusion.sides_ref, f32[1,512,512]{2,1,0:T(8,128)S(1)} %get-tuple-element.50.exact_ref, ...), custom_call_target="tpu_custom_call", output_to_operand_aliasing={{0}: (13, {}), {1}: (14, {}), {2}: (15, {})} | custom-call | flops 10000000000 | bytes 1 | tf_op jit(solution)/shard_map/deconvolve/pallas_call | solution.py:538
  110.3 1.2 collective-permute-done.6.above_ref
  111.5 10.7 %deconvolve.5 = (f32[3,8,64,512]{3,2,1,0:T(8,128)}, f32[3,4,32,256]{3,2,1,0:T(8,128)}, f32[3,2,16,128]{3,2,1,0:T(8,128)}) custom-call(s32[4]{0:T(128)S(1)} %add_convert_fusion.sides_ref, f32[1,512,512]{2,1,0:T(8,128)S(1)} %get-tuple-element.43.exact_ref, ...), custom_call_target="tpu_custom_call", output_to_operand_aliasing={{0}: (13, {}), {1}: (14, {}), {2}: (15, {})} | custom-call | flops 10000000000 | bytes 1 | tf_op jit(solution)/shard_map/deconvolve/pallas_call | solution.py:538
  (48 shorter events, 2.4 us)
Async XLA Ops:
  0.6 1.8 %copy-start.2 = (bf16[3,8,96,544]{3,2,1,0:T(8,128)(2,1)S(1)}, bf16[3,8,96,544]{3,2,1,0:T(8,128)(2,1)}, u32[]{:S(2)}) copy-start(bf16[3,8,96,544]{3,2,1,0:T(8,128)(2,1)} %refs_1_.3) | copy-start | bytes 7520260
  2.5 0.7 copy-start.4
  3.1 7.1 %copy-start.16 = (f32[3,3,31]{2,1,0:T(4,128)S(1)}, f32[3,3,31]{2,1,0:T(4,128)}, u32[]{:S(2)}) copy-start(f32[3,3,31]{2,1,0:T(4,128)} %param.9) | copy-start | bytes 3352
  6.8 17.6 %collective-permute-start.1 = (bf16[1,576,512]{2,1,0:T(8,128)(2,1)}, bf16[1,576,512]{2,1,0:T(8,128)(2,1)S(1)}, u32[]{:S(2)}, u32[]{:S(2)}) collective-permute-start(bf16[1,576,512]{2,1,0:T(8,128)(2,1)} %get-tuple-element.37), channel_id=1, source_target_pairs={{0,1},{1,2},{2,3},{4,5},{5,6},{6,7},{8,9},{9,10},{10,11},{12,13},{... | collective-permute-start | bytes 1769480 | tf_op jit(solution)/shard_map/ppermute | solution.py:573
  10.7 2.4 %copy-start.3 = (bf16[3,8,96,544]{3,2,1,0:T(8,128)(2,1)S(1)}, bf16[3,8,96,544]{3,2,1,0:T(8,128)(2,1)}, u32[]{:S(2)}) copy-start(bf16[3,8,96,544]{3,2,1,0:T(8,128)(2,1)} %refs_1_.3) | copy-start | bytes 7520260
  10.7 2.4 %copy-start.5 = (s32[1,1,2]{2,1,0:T(1,128)S(1)}, s32[1,1,2]{2,1,0:T(1,128)}, u32[]{:S(2)}) copy-start(s32[1,1,2]{2,1,0:T(1,128)} %refs_0_.3) | copy-start | bytes 28
  13.1 6.0 %copy-start.6 = (bf16[6,272,512]{2,1,0:T(8,128)(2,1)}, bf16[6,272,512]{2,1,0:T(8,128)(2,1)S(1)}, u32[]{:S(2)}) copy-start(bf16[6,272,512]{2,1,0:T(8,128)(2,1)S(1)} %get-tuple-element.32.refs_2_) | copy-start | bytes 5013508
  13.1 6.0 %copy-start.8 = (bf16[6,512,256]{2,1,0:T(8,128)(2,1)}, bf16[6,512,256]{2,1,0:T(8,128)(2,1)S(1)}, u32[]{:S(2)}) copy-start(bf16[6,512,256]{2,1,0:T(8,128)(2,1)S(1)} %get-tuple-element.48) | copy-start | bytes 4718596
  13.1 6.0 %copy-start.10 = (bf16[6,512,128]{2,1,0:T(8,128)(2,1)}, bf16[6,512,128]{2,1,0:T(8,128)(2,1)S(1)}, u32[]{:S(2)}) copy-start(bf16[6,512,128]{2,1,0:T(8,128)(2,1)S(1)} %get-tuple-element.49) | copy-start | bytes 2359300
  19.1 6.2 %copy-start = (bf16[2,512,128]{2,1,0:T(8,128)(2,1)}, bf16[2,512,128]{2,1,0:T(8,128)(2,1)S(1)}, u32[]{:S(2)}) copy-start(bf16[2,512,128]{2,1,0:T(8,128)(2,1)S(1)} %get-tuple-element.35.refs_3_.refs_1_) | copy-start | bytes 786436
  19.1 30.1 %collective-permute-start = (bf16[2,576,512]{2,1,0:T(8,128)(2,1)}, bf16[2,576,512]{2,1,0:T(8,128)(2,1)S(1)}, u32[]{:S(2)}, u32[]{:S(2)}) collective-permute-start(bf16[2,576,512]{2,1,0:T(8,128)(2,1)} %get-tuple-element.34), channel_id=1, source_target_pairs={{0,1},{1,2},{2,3},{4,5},{5,6},{6,7},{8,9},{9,10},{10,11},{12,13},{... | collective-permute-start | bytes 3538952 | tf_op jit(solution)/shard_map/ppermute | solution.py:573
  25.4 9.3 %collective-permute-start.2 = (bf16[1,1024,128]{2,1,0:T(8,128)(2,1)}, bf16[1,1024,128]{2,1,0:T(8,128)(2,1)}, u32[]{:S(2)}, u32[]{:S(2)}) collective-permute-start(bf16[1,1024,128]{2,1,0:T(8,128)(2,1)} %get-tuple-element.38.mine_ref), channel_id=1, source_target_pairs={{0,4},{4,8},{8,12},{12,16},{16,20},{20,24},{24,28},{1,5},{5,9},{9,... | collective-permute-start | bytes 786440 | tf_op jit(solution)/shard_map/ppermute | solution.py:573
  27.3 7.4 %collective-permute-start.3 = (bf16[1,512,128]{2,1,0:T(8,128)(2,1)}, bf16[1,512,128]{2,1,0:T(8,128)(2,1)S(1)}, u32[]{:S(2)}, u32[]{:S(2)}) collective-permute-start(bf16[1,512,128]{2,1,0:T(8,128)(2,1)} %get-tuple-element.39), channel_id=1, source_target_pairs={{4,0},{8,4},{12,8},{16,12},{20,16},{24,20},{28,24},{5,1},{9,5},{13... | collective-permute-start | bytes 393224 | tf_op jit(solution)/shard_map/ppermute | solution.py:573
  49.2 1.0 copy-start.1
  50.7 14.2 %collective-permute-start.4 = (bf16[2,1024,128]{2,1,0:T(8,128)(2,1)S(1)}, bf16[2,1024,128]{2,1,0:T(8,128)(2,1)S(1)}, u32[]{:S(2)}, u32[]{:S(2)}) collective-permute-start(bf16[2,1024,128]{2,1,0:T(8,128)(2,1)S(1)} %get-tuple-element.41.mine_ref), channel_id=1, source_target_pairs={{0,4},{4,8},{8,12},{12,16},{16,20},{20,24},{24,28},{1,5},{5,9},{9,... | collective-permute-start | bytes 1572872 | tf_op jit(solution)/shard_map/ppermute | solution.py:573
  52.7 10.4 %collective-permute-start.5 = (bf16[2,512,128]{2,1,0:T(8,128)(2,1)S(1)}, bf16[2,512,128]{2,1,0:T(8,128)(2,1)S(1)}, u32[]{:S(2)}, u32[]{:S(2)}) collective-permute-start(bf16[2,512,128]{2,1,0:T(8,128)(2,1)S(1)} %get-tuple-element.42), channel_id=1, source_target_pairs={{4,0},{8,4},{12,8},{16,12},{20,16},{24,20},{28,24},{5,1},{9,5},{13... | collective-permute-start | bytes 786440 | tf_op jit(solution)/shard_map/ppermute | solution.py:573
  57.2 20.0 %collective-permute-start.12 = (bf16[1,528,640]{2,1,0:T(8,128)(2,1)S(1)}, bf16[1,528,640]{2,1,0:T(8,128)(2,1)S(1)}, u32[]{:S(2)}, u32[]{:S(2)}) collective-permute-start(bf16[1,528,640]{2,1,0:T(8,128)(2,1)S(1)} %get-tuple-element.40.refs_3_.message_ref), channel_id=1, source_target_pairs={{1,0},{2,1},{3,2},{5,4},{6,5},{7,6},{9,8},{10,9},{11,10},{13,12},{... | collective-permute-start | bytes 2027528 | tf_op jit(solution)/shard_map/ppermute | solution.py:573
  59.6 22.6 %collective-permute-start.11 = (bf16[1,528,640]{2,1,0:T(8,128)(2,1)S(1)}, bf16[1,528,640]{2,1,0:T(8,128)(2,1)S(1)}, u32[]{:S(2)}, u32[]{:S(2)}) collective-permute-start(bf16[1,528,640]{2,1,0:T(8,128)(2,1)S(1)} %get-tuple-element.40.refs_3_.message_ref), channel_id=1, source_target_pairs={{0,1},{1,2},{2,3},{4,5},{5,6},{6,7},{8,9},{9,10},{10,11},{12,13},{... | collective-permute-start | bytes 2027528 | tf_op jit(solution)/shard_map/ppermute | solution.py:573
  66.3 18.3 %copy-start.7 = (bf16[6,272,512]{2,1,0:T(8,128)(2,1)S(1)}, bf16[6,272,512]{2,1,0:T(8,128)(2,1)}, u32[]{:S(2)}) copy-start(bf16[6,272,512]{2,1,0:T(8,128)(2,1)} %copy-done.6) | copy-start | bytes 5013508
  66.3 18.3 %copy-start.9 = (bf16[6,512,256]{2,1,0:T(8,128)(2,1)S(1)}, bf16[6,512,256]{2,1,0:T(8,128)(2,1)}, u32[]{:S(2)}) copy-start(bf16[6,512,256]{2,1,0:T(8,128)(2,1)} %copy-done.8) | copy-start | bytes 4718596
  66.3 18.3 %copy-start.11 = (bf16[6,512,128]{2,1,0:T(8,128)(2,1)S(1)}, bf16[6,512,128]{2,1,0:T(8,128)(2,1)}, u32[]{:S(2)}) copy-start(bf16[6,512,128]{2,1,0:T(8,128)(2,1)} %copy-done.10) | copy-start | bytes 2359300
  66.3 18.3 %copy-start.12 = (bf16[640,384]{1,0:T(8,128)(2,1)S(1)}, bf16[640,384]{1,0:T(8,128)(2,1)}, u32[]{:S(2)}) copy-start(bf16[640,384]{1,0:T(8,128)(2,1)} %constant.25.clone.one_x_ref) | copy-start | bytes 1474564
  66.3 18.3 %copy-start.13 = (bf16[144,592]{1,0:T(8,128)(2,1)S(1)}, bf16[144,592]{1,0:T(8,128)(2,1)}, u32[]{:S(2)}) copy-start(bf16[144,592]{1,0:T(8,128)(2,1)} %constant.26.clone.one_zy_ref) | copy-start | bytes 511492
  66.3 18.3 %copy-start.14 = (bf16[384,128]{1,0:T(8,128)(2,1)S(1)}, bf16[384,128]{1,0:T(8,128)(2,1)}, u32[]{:S(2)}) copy-start(bf16[384,128]{1,0:T(8,128)(2,1)} %constant.27.clone.two_x_ref) | copy-start | bytes 294916
  66.3 18.3 %copy-start.15 = (bf16[32,144]{1,0:T(8,128)(2,1)S(1)}, bf16[32,144]{1,0:T(8,128)(2,1)}, u32[]{:S(2)}) copy-start(bf16[32,144]{1,0:T(8,128)(2,1)} %constant.28.clone.two_zy_ref) | copy-start | bytes 27652
  67.7 16.9 %collective-permute-start.8 = (bf16[3,32,640]{2,1,0:T(8,128)(2,1)S(1)}, bf16[3,32,640]{2,1,0:T(8,128)(2,1)S(1)}, u32[]{:S(2)}, u32[]{:S(2)}) collective-permute-start(bf16[3,32,640]{2,1,0:T(8,128)(2,1)S(1)} %pad_maximum_fusion), channel_id=1, source_target_pairs={{0,2},{1,3},{4,6},{5,7},{8,10},{9,11},{12,14},{13,15},{16,18},{17,... | collective-permute-start | bytes 368648 | tf_op jit(solution)/shard_map/ppermute | solution.py:573
  69.1 25.9 %collective-permute-start.10 = (bf16[1,528,640]{2,1,0:T(8,128)(2,1)S(1)}, bf16[1,528,640]{2,1,0:T(8,128)(2,1)S(1)}, u32[]{:S(2)}, u32[]{:S(2)}) collective-permute-start(bf16[1,528,640]{2,1,0:T(8,128)(2,1)S(1)} %get-tuple-element.51.message_ref), channel_id=1, source_target_pairs={{1,0},{2,1},{3,2},{5,4},{6,5},{7,6},{9,8},{10,9},{11,10},{13,12},{... | collective-permute-start | bytes 2027528 | tf_op jit(solution)/shard_map/ppermute | solution.py:573
  74.7 24.6 %collective-permute-start.9 = (bf16[1,528,640]{2,1,0:T(8,128)(2,1)S(1)}, bf16[1,528,640]{2,1,0:T(8,128)(2,1)S(1)}, u32[]{:S(2)}, u32[]{:S(2)}) collective-permute-start(bf16[1,528,640]{2,1,0:T(8,128)(2,1)S(1)} %get-tuple-element.51.message_ref), channel_id=1, source_target_pairs={{0,1},{1,2},{2,3},{4,5},{5,6},{6,7},{8,9},{9,10},{10,11},{12,13},{... | collective-permute-start | bytes 2027528 | tf_op jit(solution)/shard_map/ppermute | solution.py:573
  77.2 33.1 %collective-permute-start.7 = (bf16[1,528,640]{2,1,0:T(8,128)(2,1)S(1)}, bf16[1,528,640]{2,1,0:T(8,128)(2,1)S(1)}, u32[]{:S(2)}, u32[]{:S(2)}) collective-permute-start(bf16[1,528,640]{2,1,0:T(8,128)(2,1)S(1)} %get-tuple-element.44.message_ref), channel_id=1, source_target_pairs={{1,0},{2,1},{3,2},{5,4},{6,5},{7,6},{9,8},{10,9},{11,10},{13,12},{... | collective-permute-start | bytes 2027528 | tf_op jit(solution)/shard_map/ppermute | solution.py:573
  82.2 29.3 %collective-permute-start.6 = (bf16[1,528,640]{2,1,0:T(8,128)(2,1)S(1)}, bf16[1,528,640]{2,1,0:T(8,128)(2,1)S(1)}, u32[]{:S(2)}, u32[]{:S(2)}) collective-permute-start(bf16[1,528,640]{2,1,0:T(8,128)(2,1)S(1)} %get-tuple-element.44.message_ref), channel_id=1, source_target_pairs={{0,1},{1,2},{2,3},{4,5},{5,6},{6,7},{8,9},{9,10},{10,11},{12,13},{... | collective-permute-start | bytes 2027528 | tf_op jit(solution)/shard_map/ppermute | solution.py:573

commit v9 on v7

--- a/solution.py
+++ b/solution.py
@@ -198,7 +198,7 @@
     tail_ref[0] = out_ref[0, rows - 2 * DEPTH :, :]
 
 
-def join(sides, own, low, mine, left, right, at):
+def join(sides, own, low, mine, left, right, at, after):
     _, rows, cols = own.shape
     extra = 2 * DEPTH
     sizes = (
@@ -207,14 +207,14 @@
         (2 * extra, cols + LANE, BF16),
     )
     return pl.pallas_call(
-        functools.partial(join_kernel, at),
-        in_specs=[pl.BlockSpec(memory_space=pltpu.SMEM)] + [VMEM] * 5,
+        skipping(functools.partial(join_kernel, at), 6, len(after)),
+        in_specs=[pl.BlockSpec(memory_space=pltpu.SMEM)] + [VMEM] * 5 + [ANY] * len(after),
         out_specs=[VMEM] * 3,
         out_shape=[jax.ShapeDtypeStruct((1, r, c), t) for r, c, t in sizes],
         compiler_params=params(12),
         cost_estimate=cost(1, 1),
         name="join",
-    )(sides, own, low, mine, left, right)
+    )(sides, own, low, mine, left, right, *after)
 
 
 def bands_kernel(kern_ref, across_ref, within_ref, corner_ref):
@@ -320,6 +320,7 @@
 
 def deconvolve_kernel(
     at,
+    place_far,
     sides_ref,
     exact_ref,
     message_ref,
@@ -337,7 +338,7 @@
 ):
     if len(others) > 11:
         others = others[3:]
-    far_ref = far_ref.at[at : at + 1]
+    far_ref = far_ref.at[place_far : place_far + 1]
     corner_ref = corner_ref.at[at : at + 1]
     across_ref = across_ref.at[at : at + 1]
     within_ref = within_ref.at[at : at + 1]
@@ -515,7 +516,7 @@
     level_two_ref[0] = two.reshape(level_two_ref.shape[1:])
 
 
-def deconvolve(at, sides, group, tables, matrices, earlier):
+def deconvolve(at, place_far, sides, group, tables, matrices, earlier):
     chans = tables[0].shape[0]
     rows8, cols = group[0].shape[1:]
     rows = rows8 // DEPTH
@@ -532,7 +533,7 @@
     result_rows = 3 * SMALL * DEPTH
     operands = [sides, *group, *tables, *matrices]
     return pl.pallas_call(
-        functools.partial(deconvolve_kernel, at),
+        functools.partial(deconvolve_kernel, at, place_far),
         grid=(1,),
         in_specs=[pl.BlockSpec(memory_space=pltpu.SMEM)]
         + [VMEM] * (len(operands) - 1)
@@ -583,24 +584,26 @@
     tables = [t.reshape((chans, 2) + t.shape[1:]) for t in tables]
 
     groups = []
-    tails = []
     before = (pieces[1][1],)
+    earlier = ()
     for own, right, low in pieces:
         mine, to_left = edges(own, right, low, before)
         left = shift(mine, "gx", 1)
         right = shift(to_left, "gx", -1)
-        for k in range(own.shape[0]):
-            exact, message, tail = join(sides, own, low, mine, left, right, k)
+        joined = [
+            join(sides, own, low, mine, left, right, k, earlier) for k in range(own.shape[0])
+        ]
+        far = shift(jnp.concatenate([tail for *_, tail in joined], axis=0), "gy", 2)
+        for k, (exact, message, _) in enumerate(joined):
             above = shift(message, "gy", 1)
             below = shift(message, "gy", -1)
-            groups.append([exact, message, above, below])
-            tails.append(tail)
+            groups.append((k, [exact, message, above, below, far]))
         before = (message,)
-    far = shift(jnp.concatenate(tails, axis=0), "gy", 2)
+        earlier = (above, below)
 
     outs = ()
-    for at, group in enumerate(groups):
-        outs = deconvolve(at, sides, [*group, far], tables, matrices, outs)
+    for at, (k, group) in enumerate(groups):
+        outs = deconvolve(at, k, sides, group, tables, matrices, outs)
     return tuple(outs)
 
 

time: 121 us -> 122 us (level)
  waiting for transfers between devices: 26.6 us -> 20.9 us
  starting transfers between devices: 39.8 us -> 45.3 us
    ppermute x13 -> x14, waiting for transfers between devices: 26.6 us -> 20.9 us  [shift(): return lax.ppermute(block, axis, route)]
    ppermute x13 -> x14, starting transfers between devices: 39.8 us -> 45.3 us  [shift(): return lax.ppermute(block, axis, route)]
  transfers between devices with their start and end apart: 13 -> 14, of which waited for: 6 -> 6; matrix products, arithmetic and copies ran while one was open for 0% -> 0% of each run, Pallas kernels for 28% -> 29%
where the time goes in v9:
time: 122 us; the launch traced here: 120 us
  Pallas kernels  48.8 us (40%)
  starting transfers between devices  45.3 us (37%)
  waiting for transfers between devices  20.9 us (17%)
  local copies, waits for them, and re-layouts  3.69 us (3%)
    ppermute x14, starting transfers between devices, shift(): return lax.ppermute(block, axis, route)  45.3 us
    pallas_call x3, Pallas kernels, deconvolve(): pl.pallas_call(functools.partial(deconvolve_kernel, at, place_far), grid=...  32.2 us
    ppermute x14, waiting for transfers between devices, shift(): return lax.ppermute(block, axis, route)  20.9 us
    pallas_call x2, Pallas kernels, place(): pl.pallas_call(skipping(place_kernel, 2, len(after)), grid_spec=pltpu.Pre...  8.23 us
    pallas_call x3, Pallas kernels, join(): pl.pallas_call(skipping(functools.partial(join_kernel, at), 6, len(after)...  4.52 us
    unnamed x34, local copies, waits for them, and re-layouts  3.51 us
  transfers between devices with their start and end apart: 14, of which 6 were waited for; matrix products, arithmetic and copies ran while one was open for 0% of the time, Pallas kernels for 29%

profile of v9, /device:TPU:11, one launch (start us, length us, event | category | flops | bytes accessed | tf_op | source)
XLA Modules:
  0.0 120.0 jit_solution(11465499055363646057)
XLA Ops:
  0.6 1.8 %copy-done.2 = bf16[3,8,96,544]{3,2,1,0:T(8,128)(2,1)S(1)} copy-done((bf16[3,8,96,544]{3,2,1,0:T(8,128)(2,1)S(1)}, bf16[3,8,96,544]{3,2,1,0:T(8,128)(2,1)}, u32[]{:S(2)}) %copy-start.2) | copy-done | bytes 2506776
  3.1 3.2 %place.2 = (bf16[1,512,512]{2,1,0:T(8,128)(2,1)S(1)}, bf16[1,512,128]{2,1,0:T(8,128)(2,1)S(1)}, bf16[1,576,512]{2,1,0:T(8,128)(2,1)}) custom-call(s32[2]{0:T(128)S(1)} %bitcast.11, bf16[3,8,96,544]{3,2,1,0:T(8,128)(2,1)S(1)} %copy-done.2), custom_call_target="tpu_custom_call" | custom-call | flops 2000000000 | bytes 1 | tf_op jit(solution)/shard_map/place/pallas_call | solution.py:99
  6.3 3.2 %collective-permute-start.1 = (bf16[1,576,512]{2,1,0:T(8,128)(2,1)}, bf16[1,576,512]{2,1,0:T(8,128)(2,1)S(1)}, u32[]{:S(2)}, u32[]{:S(2)}) collective-permute-start(bf16[1,576,512]{2,1,0:T(8,128)(2,1)} %get-tuple-element.37), channel_id=1, source_target_pairs={{0,1},{1,2},{2,3},{4,5},{5,6},{6,7},{8,9},{9,10},{10,11},{12,13},{... | collective-permute-start | bytes 1769480 | tf_op jit(solution)/shard_map/ppermute | solution.py:570
  10.0 2.4 %bands.1 = (bf16[6,512,256]{2,1,0:T(8,128)(2,1)S(1)}, bf16[6,272,512]{2,1,0:T(8,128)(2,1)S(1)}, bf16[6,512,128]{2,1,0:T(8,128)(2,1)S(1)}) custom-call(f32[6,93]{1,0:T(8,128)S(1)} %reshape.23.refs_0_, bf16[1,512,128]{2,1,0:T(8,128)(2,1)S(1)} %get-tuple-element.31.refs_1_), custom_call_target="tpu_custom_call" | custom-call | flops 2000000000 | bytes 1 | tf_op jit(solution)/shard_map/bands/pallas_call | solution.py:269
  12.4 5.0 %place.3 = (bf16[2,512,512]{2,1,0:T(8,128)(2,1)S(1)}, bf16[2,512,128]{2,1,0:T(8,128)(2,1)S(1)}, bf16[2,576,512]{2,1,0:T(8,128)(2,1)}) custom-call(s32[2]{0:T(128)S(1)} %bitcast.12, bf16[3,8,96,544]{3,2,1,0:T(8,128)(2,1)S(1)} %copy-done.3, bf16[6,272,512]{2,1,0:T(8,128)(2,1)S(1)} %get-tuple-element.32.refs_2_), custom_call_target="tpu_custom_call" | custom-call | flops 4000000000 | bytes 1 | tf_op jit(solution)/shard_map/place/pallas_call | solution.py:99
  17.5 3.2 %collective-permute-start = (bf16[2,576,512]{2,1,0:T(8,128)(2,1)}, bf16[2,576,512]{2,1,0:T(8,128)(2,1)S(1)}, u32[]{:S(2)}, u32[]{:S(2)}) collective-permute-start(bf16[2,576,512]{2,1,0:T(8,128)(2,1)} %get-tuple-element.34), channel_id=1, source_target_pairs={{0,1},{1,2},{2,3},{4,5},{5,6},{6,7},{8,9},{9,10},{10,11},{12,13},{... | collective-permute-start | bytes 3538952 | tf_op jit(solution)/shard_map/ppermute | solution.py:570
  20.7 1.9 %collective-permute-done.1.refs_2_ = bf16[1,576,512]{2,1,0:T(8,128)(2,1)S(1)} collective-permute-done((bf16[1,576,512]{2,1,0:T(8,128)(2,1)}, bf16[1,576,512]{2,1,0:T(8,128)(2,1)S(1)}, u32[]{:S(2)}, u32[]{:S(2)}) %collective-permute-start.1) | collective-permute-done | bytes 589856 | tf_op jit(solution)/shard_map/ppermute | solution.py:570
  22.6 1.0 edges.2
  23.6 5.7 %collective-permute-start.2 = (bf16[1,1024,128]{2,1,0:T(8,128)(2,1)}, bf16[1,1024,128]{2,1,0:T(8,128)(2,1)}, u32[]{:S(2)}, u32[]{:S(2)}) collective-permute-start(bf16[1,1024,128]{2,1,0:T(8,128)(2,1)} %get-tuple-element.38.refs_3_), channel_id=1, source_target_pairs={{0,4},{4,8},{8,12},{12,16},{16,20},{20,24},{24,28},{1,5},{5,9},{9,... | collective-permute-start | bytes 786440 | tf_op jit(solution)/shard_map/ppermute | solution.py:570
  29.3 1.9 %collective-permute-start.3 = (bf16[1,512,128]{2,1,0:T(8,128)(2,1)}, bf16[1,512,128]{2,1,0:T(8,128)(2,1)S(1)}, u32[]{:S(2)}, u32[]{:S(2)}) collective-permute-start(bf16[1,512,128]{2,1,0:T(8,128)(2,1)} %get-tuple-element.39), channel_id=1, source_target_pairs={{4,0},{8,4},{12,8},{16,12},{20,16},{24,20},{28,24},{5,1},{9,5},{13... | collective-permute-start | bytes 393224 | tf_op jit(solution)/shard_map/ppermute | solution.py:570
  31.3 5.4 %collective-permute-done.3.refs_5_ = bf16[1,512,128]{2,1,0:T(8,128)(2,1)S(1)} collective-permute-done((bf16[1,512,128]{2,1,0:T(8,128)(2,1)}, bf16[1,512,128]{2,1,0:T(8,128)(2,1)S(1)}, u32[]{:S(2)}, u32[]{:S(2)}) %collective-permute-start.3) | collective-permute-done | bytes 131104 | tf_op jit(solution)/shard_map/ppermute | solution.py:570
  36.7 1.8 %join.3 = (f32[1,512,512]{2,1,0:T(8,128)S(1)}, bf16[1,528,640]{2,1,0:T(8,128)(2,1)S(1)}, bf16[1,32,640]{2,1,0:T(8,128)(2,1)S(1)}) custom-call(s32[4]{0:T(128)S(1)} %add_convert_fusion.refs_0_.sides_ref, bf16[1,512,512]{2,1,0:T(8,128)(2,1)S(1)} %get-tuple-element.36.refs_0_.refs_1_, bf16[1,576,512]{2,1,0:T(8,128)(2,1)S(1)} %collective-permute-done.1.refs_2_, ...), custom_call_target="tpu_custom_call" | custom-call | flops 1 | bytes 1 | tf_op jit(solution)/shard_map/join/pallas_call | solution.py:209
  38.5 1.9 %collective-permute-start.7 = (bf16[1,528,640]{2,1,0:T(8,128)(2,1)S(1)}, bf16[1,528,640]{2,1,0:T(8,128)(2,1)S(1)}, u32[]{:S(2)}, u32[]{:S(2)}) collective-permute-start(bf16[1,528,640]{2,1,0:T(8,128)(2,1)S(1)} %get-tuple-element.40.refs_3_.message_ref), channel_id=1, source_target_pairs={{1,0},{2,1},{3,2},{5,4},{6,5},{7,6},{9,8},{10,9},{11,10},{13,12},{... | collective-permute-start | bytes 2027528 | tf_op jit(solution)/shard_map/ppermute | solution.py:570
  40.4 3.4 %collective-permute-start.6 = (bf16[1,528,640]{2,1,0:T(8,128)(2,1)S(1)}, bf16[1,528,640]{2,1,0:T(8,128)(2,1)S(1)}, u32[]{:S(2)}, u32[]{:S(2)}) collective-permute-start(bf16[1,528,640]{2,1,0:T(8,128)(2,1)S(1)} %get-tuple-element.40.refs_3_.message_ref), channel_id=1, source_target_pairs={{0,1},{1,2},{2,3},{4,5},{5,6},{6,7},{8,9},{9,10},{10,11},{12,13},{... | collective-permute-start | bytes 2027528 | tf_op jit(solution)/shard_map/ppermute | solution.py:570
  43.8 4.1 %collective-permute-done.refs_2_ = bf16[2,576,512]{2,1,0:T(8,128)(2,1)S(1)} collective-permute-done((bf16[2,576,512]{2,1,0:T(8,128)(2,1)}, bf16[2,576,512]{2,1,0:T(8,128)(2,1)S(1)}, u32[]{:S(2)}, u32[]{:S(2)}) %collective-permute-start) | collective-permute-done | bytes 1179680 | tf_op jit(solution)/shard_map/ppermute | solution.py:570
  47.9 0.9 copy-done.1
  49.4 5.7 %collective-permute-start.4 = (bf16[2,1024,128]{2,1,0:T(8,128)(2,1)S(1)}, bf16[2,1024,128]{2,1,0:T(8,128)(2,1)S(1)}, u32[]{:S(2)}, u32[]{:S(2)}) collective-permute-start(bf16[2,1024,128]{2,1,0:T(8,128)(2,1)S(1)} %get-tuple-element.41.refs_3_), channel_id=1, source_target_pairs={{0,4},{4,8},{8,12},{12,16},{16,20},{20,24},{24,28},{1,5},{5,9},{9,... | collective-permute-start | bytes 1572872 | tf_op jit(solution)/shard_map/ppermute | solution.py:570
  55.1 1.9 %collective-permute-start.5 = (bf16[2,512,128]{2,1,0:T(8,128)(2,1)S(1)}, bf16[2,512,128]{2,1,0:T(8,128)(2,1)S(1)}, u32[]{:S(2)}, u32[]{:S(2)}) collective-permute-start(bf16[2,512,128]{2,1,0:T(8,128)(2,1)S(1)} %get-tuple-element.42), channel_id=1, source_target_pairs={{4,0},{8,4},{12,8},{16,12},{20,16},{24,20},{28,24},{5,1},{9,5},{13... | collective-permute-start | bytes 786440 | tf_op jit(solution)/shard_map/ppermute | solution.py:570
  57.0 4.2 %collective-permute-start.13 = (bf16[1,32,640]{2,1,0:T(8,128)(2,1)S(1)}, bf16[1,32,640]{2,1,0:T(8,128)(2,1)S(1)}, u32[]{:S(2)}, u32[]{:S(2)}) collective-permute-start(bf16[1,32,640]{2,1,0:T(8,128)(2,1)S(1)} %get-tuple-element.52), channel_id=1, source_target_pairs={{0,2},{1,3},{4,6},{5,7},{8,10},{9,11},{12,14},{13,15},{16,18},{17,... | collective-permute-start | bytes 122888 | tf_op jit(solution)/shard_map/ppermute | solution.py:570
  61.3 4.4 %collective-permute-done.5.refs_5_ = bf16[2,512,128]{2,1,0:T(8,128)(2,1)S(1)} collective-permute-done((bf16[2,512,128]{2,1,0:T(8,128)(2,1)S(1)}, bf16[2,512,128]{2,1,0:T(8,128)(2,1)S(1)}, u32[]{:S(2)}, u32[]{:S(2)}) %collective-permute-start.5) | collective-permute-done | bytes 262176 | tf_op jit(solution)/shard_map/ppermute | solution.py:570
  65.7 1.3 %join.5 = (f32[1,512,512]{2,1,0:T(8,128)S(1)}, bf16[1,528,640]{2,1,0:T(8,128)(2,1)S(1)}, bf16[1,32,640]{2,1,0:T(8,128)(2,1)S(1)}) custom-call(s32[4]{0:T(128)S(1)} %add_convert_fusion.refs_0_.sides_ref, bf16[2,512,512]{2,1,0:T(8,128)(2,1)S(1)} %get-tuple-element.33.refs_0_.refs_1_, bf16[2,576,512]{2,1,0:T(8,128)(2,1)S(1)} %collective-permute-done.refs_2_, ...), custom_call_target="tpu_custom_call" | custom-call | flops 1 | bytes 1 | tf_op jit(solution)/shard_map/join/pallas_call | solution.py:209
  67.1 2.2 %collective-permute-start.12 = (bf16[1,528,640]{2,1,0:T(8,128)(2,1)S(1)}, bf16[1,528,640]{2,1,0:T(8,128)(2,1)S(1)}, u32[]{:S(2)}, u32[]{:S(2)}) collective-permute-start(bf16[1,528,640]{2,1,0:T(8,128)(2,1)S(1)} %get-tuple-element.50.message_ref), channel_id=1, source_target_pairs={{1,0},{2,1},{3,2},{5,4},{6,5},{7,6},{9,8},{10,9},{11,10},{13,12},{... | collective-permute-start | bytes 2027528 | tf_op jit(solution)/shard_map/ppermute | solution.py:570
  69.3 3.4 %collective-permute-start.11 = (bf16[1,528,640]{2,1,0:T(8,128)(2,1)S(1)}, bf16[1,528,640]{2,1,0:T(8,128)(2,1)S(1)}, u32[]{:S(2)}, u32[]{:S(2)}) collective-permute-start(bf16[1,528,640]{2,1,0:T(8,128)(2,1)S(1)} %get-tuple-element.50.message_ref), channel_id=1, source_target_pairs={{0,1},{1,2},{2,3},{4,5},{5,6},{6,7},{8,9},{9,10},{10,11},{12,13},{... | collective-permute-start | bytes 2027528 | tf_op jit(solution)/shard_map/ppermute | solution.py:570
  72.7 1.3 %join.4 = (f32[1,512,512]{2,1,0:T(8,128)S(1)}, bf16[1,528,640]{2,1,0:T(8,128)(2,1)S(1)}, bf16[1,32,640]{2,1,0:T(8,128)(2,1)S(1)}) custom-call(s32[4]{0:T(128)S(1)} %add_convert_fusion.refs_0_.sides_ref, bf16[2,512,512]{2,1,0:T(8,128)(2,1)S(1)} %get-tuple-element.33.refs_0_.refs_1_, bf16[2,576,512]{2,1,0:T(8,128)(2,1)S(1)} %collective-permute-done.refs_2_, ...), custom_call_target="tpu_custom_call" | custom-call | flops 1 | bytes 1 | tf_op jit(solution)/shard_map/join/pallas_call | solution.py:209
  74.0 2.5 %collective-permute-start.10 = (bf16[2,32,640]{2,1,0:T(8,128)(2,1)S(1)}, bf16[2,32,640]{2,1,0:T(8,128)(2,1)S(1)}, u32[]{:S(2)}, u32[]{:S(2)}) collective-permute-start(bf16[2,32,640]{2,1,0:T(8,128)(2,1)S(1)} %pad_maximum_fusion), channel_id=1, source_target_pairs={{0,2},{1,3},{4,6},{5,7},{8,10},{9,11},{12,14},{13,15},{16,18},{17,... | collective-permute-start | bytes 245768 | tf_op jit(solution)/shard_map/ppermute | solution.py:570
  76.6 10.4 %deconvolve.3 = (f32[3,8,64,512]{3,2,1,0:T(8,128)}, f32[3,4,32,256]{3,2,1,0:T(8,128)}, f32[3,2,16,128]{3,2,1,0:T(8,128)}) custom-call(s32[4]{0:T(128)S(1)} %add_convert_fusion.refs_0_.sides_ref, f32[1,512,512]{2,1,0:T(8,128)S(1)} %get-tuple-element.51.exact_ref, bf16[1,528,640]{2,1,0:T(8,128)(2,1)S(1)} %get-tuple-element.40.refs_3_.message_ref, ...), custom_call_target="tpu_custom_call" | custom-call | flops 10000000000 | bytes 1 | tf_op jit(solution)/shard_map/deconvolve/pallas_call | solution.py:535
  87.1 4.0 %collective-permute-start.9 = (bf16[1,528,640]{2,1,0:T(8,128)(2,1)S(1)}, bf16[1,528,640]{2,1,0:T(8,128)(2,1)S(1)}, u32[]{:S(2)}, u32[]{:S(2)}) collective-permute-start(bf16[1,528,640]{2,1,0:T(8,128)(2,1)S(1)} %get-tuple-element.44.message_ref), channel_id=1, source_target_pairs={{1,0},{2,1},{3,2},{5,4},{6,5},{7,6},{9,8},{10,9},{11,10},{13,12},{... | collective-permute-start | bytes 2027528 | tf_op jit(solution)/shard_map/ppermute | solution.py:570
  91.1 2.1 %collective-permute-start.8 = (bf16[1,528,640]{2,1,0:T(8,128)(2,1)S(1)}, bf16[1,528,640]{2,1,0:T(8,128)(2,1)S(1)}, u32[]{:S(2)}, u32[]{:S(2)}) collective-permute-start(bf16[1,528,640]{2,1,0:T(8,128)(2,1)S(1)} %get-tuple-element.44.message_ref), channel_id=1, source_target_pairs={{0,1},{1,2},{2,3},{4,5},{5,6},{6,7},{8,9},{9,10},{10,11},{12,13},{... | collective-permute-start | bytes 2027528 | tf_op jit(solution)/shard_map/ppermute | solution.py:570
  93.3 10.7 %deconvolve.4 = (f32[3,8,64,512]{3,2,1,0:T(8,128)}, f32[3,4,32,256]{3,2,1,0:T(8,128)}, f32[3,2,16,128]{3,2,1,0:T(8,128)}) custom-call(s32[4]{0:T(128)S(1)} %add_convert_fusion.refs_0_.sides_ref, f32[1,512,512]{2,1,0:T(8,128)S(1)} %get-tuple-element.49.exact_ref, ...), custom_call_target="tpu_custom_call", output_to_operand_aliasing={{0}: (13, {}), {1}: (14, {}), {2}: (15, {})} | custom-call | flops 10000000000 | bytes 1 | tf_op jit(solution)/shard_map/deconvolve/pallas_call | solution.py:535
  104.0 1.6 %collective-permute-done.9.below_ref = bf16[1,528,640]{2,1,0:T(8,128)(2,1)S(1)} collective-permute-done((bf16[1,528,640]{2,1,0:T(8,128)(2,1)S(1)}, bf16[1,528,640]{2,1,0:T(8,128)(2,1)S(1)}, u32[]{:S(2)}, u32[]{:S(2)}) %collective-permute-start.9) | collective-permute-done | bytes 675872 | tf_op jit(solution)/shard_map/ppermute | solution.py:570
  105.6 3.5 %collective-permute-done.8.above_ref = bf16[1,528,640]{2,1,0:T(8,128)(2,1)S(1)} collective-permute-done((bf16[1,528,640]{2,1,0:T(8,128)(2,1)S(1)}, bf16[1,528,640]{2,1,0:T(8,128)(2,1)S(1)}, u32[]{:S(2)}, u32[]{:S(2)}) %collective-permute-start.8) | collective-permute-done | bytes 675872 | tf_op jit(solution)/shard_map/ppermute | solution.py:570
  109.1 11.0 %deconvolve.5 = (f32[3,8,64,512]{3,2,1,0:T(8,128)}, f32[3,4,32,256]{3,2,1,0:T(8,128)}, f32[3,2,16,128]{3,2,1,0:T(8,128)}) custom-call(s32[4]{0:T(128)S(1)} %add_convert_fusion.refs_0_.sides_ref, f32[1,512,512]{2,1,0:T(8,128)S(1)} %get-tuple-element.43.exact_ref, ...), custom_call_target="tpu_custom_call", output_to_operand_aliasing={{0}: (13, {}), {1}: (14, {}), {2}: (15, {})} | custom-call | flops 10000000000 | bytes 1 | tf_op jit(solution)/shard_map/deconvolve/pallas_call | solution.py:535
  (50 shorter events, 1.8 us)
Async XLA Ops:
  0.6 1.8 %copy-start.2 = (bf16[3,8,96,544]{3,2,1,0:T(8,128)(2,1)S(1)}, bf16[3,8,96,544]{3,2,1,0:T(8,128)(2,1)}, u32[]{:S(2)}) copy-start(bf16[3,8,96,544]{3,2,1,0:T(8,128)(2,1)} %refs_1_.3) | copy-start | bytes 7520260
  2.5 0.7 copy-start.4
  3.1 6.4 %copy-start.16 = (f32[3,3,31]{2,1,0:T(4,128)S(1)}, f32[3,3,31]{2,1,0:T(4,128)}, u32[]{:S(2)}) copy-start(f32[3,3,31]{2,1,0:T(4,128)} %param.9) | copy-start | bytes 3352
  6.3 16.3 %collective-permute-start.1 = (bf16[1,576,512]{2,1,0:T(8,128)(2,1)}, bf16[1,576,512]{2,1,0:T(8,128)(2,1)S(1)}, u32[]{:S(2)}, u32[]{:S(2)}) collective-permute-start(bf16[1,576,512]{2,1,0:T(8,128)(2,1)} %get-tuple-element.37), channel_id=1, source_target_pairs={{0,1},{1,2},{2,3},{4,5},{5,6},{6,7},{8,9},{9,10},{10,11},{12,13},{... | collective-permute-start | bytes 1769480 | tf_op jit(solution)/shard_map/ppermute | solution.py:570
  10.0 2.4 %copy-start.3 = (bf16[3,8,96,544]{3,2,1,0:T(8,128)(2,1)S(1)}, bf16[3,8,96,544]{3,2,1,0:T(8,128)(2,1)}, u32[]{:S(2)}) copy-start(bf16[3,8,96,544]{3,2,1,0:T(8,128)(2,1)} %refs_1_.3) | copy-start | bytes 7520260
  10.0 2.4 %copy-start.5 = (s32[1,1,2]{2,1,0:T(1,128)S(1)}, s32[1,1,2]{2,1,0:T(1,128)}, u32[]{:S(2)}) copy-start(s32[1,1,2]{2,1,0:T(1,128)} %param.8) | copy-start | bytes 28
  12.3 5.1 %copy-start.6 = (bf16[6,272,512]{2,1,0:T(8,128)(2,1)}, bf16[6,272,512]{2,1,0:T(8,128)(2,1)S(1)}, u32[]{:S(2)}) copy-start(bf16[6,272,512]{2,1,0:T(8,128)(2,1)S(1)} %get-tuple-element.32.refs_2_) | copy-start | bytes 5013508
  12.4 5.1 %copy-start.8 = (bf16[6,512,256]{2,1,0:T(8,128)(2,1)}, bf16[6,512,256]{2,1,0:T(8,128)(2,1)S(1)}, u32[]{:S(2)}) copy-start(bf16[6,512,256]{2,1,0:T(8,128)(2,1)S(1)} %get-tuple-element.47) | copy-start | bytes 4718596
  12.4 5.1 %copy-start.10 = (bf16[6,512,128]{2,1,0:T(8,128)(2,1)}, bf16[6,512,128]{2,1,0:T(8,128)(2,1)S(1)}, u32[]{:S(2)}) copy-start(bf16[6,512,128]{2,1,0:T(8,128)(2,1)S(1)} %get-tuple-element.48) | copy-start | bytes 2359300
  17.4 6.1 %copy-start = (bf16[2,512,128]{2,1,0:T(8,128)(2,1)}, bf16[2,512,128]{2,1,0:T(8,128)(2,1)S(1)}, u32[]{:S(2)}) copy-start(bf16[2,512,128]{2,1,0:T(8,128)(2,1)S(1)} %get-tuple-element.35.refs_3_.refs_1_) | copy-start | bytes 786436
  17.5 30.4 %collective-permute-start = (bf16[2,576,512]{2,1,0:T(8,128)(2,1)}, bf16[2,576,512]{2,1,0:T(8,128)(2,1)S(1)}, u32[]{:S(2)}, u32[]{:S(2)}) collective-permute-start(bf16[2,576,512]{2,1,0:T(8,128)(2,1)} %get-tuple-element.34), channel_id=1, source_target_pairs={{0,1},{1,2},{2,3},{4,5},{5,6},{6,7},{8,9},{9,10},{10,11},{12,13},{... | collective-permute-start | bytes 3538952 | tf_op jit(solution)/shard_map/ppermute | solution.py:570
  23.6 13.1 %collective-permute-start.2 = (bf16[1,1024,128]{2,1,0:T(8,128)(2,1)}, bf16[1,1024,128]{2,1,0:T(8,128)(2,1)}, u32[]{:S(2)}, u32[]{:S(2)}) collective-permute-start(bf16[1,1024,128]{2,1,0:T(8,128)(2,1)} %get-tuple-element.38.refs_3_), channel_id=1, source_target_pairs={{0,4},{4,8},{8,12},{12,16},{16,20},{20,24},{24,28},{1,5},{5,9},{9,... | collective-permute-start | bytes 786440 | tf_op jit(solution)/shard_map/ppermute | solution.py:570
  29.3 7.4 %collective-permute-start.3 = (bf16[1,512,128]{2,1,0:T(8,128)(2,1)}, bf16[1,512,128]{2,1,0:T(8,128)(2,1)S(1)}, u32[]{:S(2)}, u32[]{:S(2)}) collective-permute-start(bf16[1,512,128]{2,1,0:T(8,128)(2,1)} %get-tuple-element.39), channel_id=1, source_target_pairs={{4,0},{8,4},{12,8},{16,12},{20,16},{24,20},{28,24},{5,1},{9,5},{13... | collective-permute-start | bytes 393224 | tf_op jit(solution)/shard_map/ppermute | solution.py:570
  38.5 27.2 %collective-permute-start.7 = (bf16[1,528,640]{2,1,0:T(8,128)(2,1)S(1)}, bf16[1,528,640]{2,1,0:T(8,128)(2,1)S(1)}, u32[]{:S(2)}, u32[]{:S(2)}) collective-permute-start(bf16[1,528,640]{2,1,0:T(8,128)(2,1)S(1)} %get-tuple-element.40.refs_3_.message_ref), channel_id=1, source_target_pairs={{1,0},{2,1},{3,2},{5,4},{6,5},{7,6},{9,8},{10,9},{11,10},{13,12},{... | collective-permute-start | bytes 2027528 | tf_op jit(solution)/shard_map/ppermute | solution.py:570
  40.4 25.2 %collective-permute-start.6 = (bf16[1,528,640]{2,1,0:T(8,128)(2,1)S(1)}, bf16[1,528,640]{2,1,0:T(8,128)(2,1)S(1)}, u32[]{:S(2)}, u32[]{:S(2)}) collective-permute-start(bf16[1,528,640]{2,1,0:T(8,128)(2,1)S(1)} %get-tuple-element.40.refs_3_.message_ref), channel_id=1, source_target_pairs={{0,1},{1,2},{2,3},{4,5},{5,6},{6,7},{8,9},{9,10},{10,11},{12,13},{... | collective-permute-start | bytes 2027528 | tf_op jit(solution)/shard_map/ppermute | solution.py:570
  47.9 1.0 copy-start.1
  49.4 16.3 %collective-permute-start.4 = (bf16[2,1024,128]{2,1,0:T(8,128)(2,1)S(1)}, bf16[2,1024,128]{2,1,0:T(8,128)(2,1)S(1)}, u32[]{:S(2)}, u32[]{:S(2)}) collective-permute-start(bf16[2,1024,128]{2,1,0:T(8,128)(2,1)S(1)} %get-tuple-element.41.refs_3_), channel_id=1, source_target_pairs={{0,4},{4,8},{8,12},{12,16},{16,20},{20,24},{24,28},{1,5},{5,9},{9,... | collective-permute-start | bytes 1572872 | tf_op jit(solution)/shard_map/ppermute | solution.py:570
  55.1 10.6 %collective-permute-start.5 = (bf16[2,512,128]{2,1,0:T(8,128)(2,1)S(1)}, bf16[2,512,128]{2,1,0:T(8,128)(2,1)S(1)}, u32[]{:S(2)}, u32[]{:S(2)}) collective-permute-start(bf16[2,512,128]{2,1,0:T(8,128)(2,1)S(1)} %get-tuple-element.42), channel_id=1, source_target_pairs={{4,0},{8,4},{12,8},{16,12},{20,16},{24,20},{28,24},{5,1},{9,5},{13... | collective-permute-start | bytes 786440 | tf_op jit(solution)/shard_map/ppermute | solution.py:570
  57.0 19.5 %collective-permute-start.13 = (bf16[1,32,640]{2,1,0:T(8,128)(2,1)S(1)}, bf16[1,32,640]{2,1,0:T(8,128)(2,1)S(1)}, u32[]{:S(2)}, u32[]{:S(2)}) collective-permute-start(bf16[1,32,640]{2,1,0:T(8,128)(2,1)S(1)} %get-tuple-element.52), channel_id=1, source_target_pairs={{0,2},{1,3},{4,6},{5,7},{8,10},{9,11},{12,14},{13,15},{16,18},{17,... | collective-permute-start | bytes 122888 | tf_op jit(solution)/shard_map/ppermute | solution.py:570
  67.0 9.5 %copy-start.7 = (bf16[6,272,512]{2,1,0:T(8,128)(2,1)S(1)}, bf16[6,272,512]{2,1,0:T(8,128)(2,1)}, u32[]{:S(2)}) copy-start(bf16[6,272,512]{2,1,0:T(8,128)(2,1)} %copy-done.6) | copy-start | bytes 5013508
  67.0 9.5 %copy-start.9 = (bf16[6,512,256]{2,1,0:T(8,128)(2,1)S(1)}, bf16[6,512,256]{2,1,0:T(8,128)(2,1)}, u32[]{:S(2)}) copy-start(bf16[6,512,256]{2,1,0:T(8,128)(2,1)} %copy-done.8) | copy-start | bytes 4718596
  67.0 9.5 %copy-start.11 = (bf16[6,512,128]{2,1,0:T(8,128)(2,1)S(1)}, bf16[6,512,128]{2,1,0:T(8,128)(2,1)}, u32[]{:S(2)}) copy-start(bf16[6,512,128]{2,1,0:T(8,128)(2,1)} %copy-done.10) | copy-start | bytes 2359300
  67.1 9.5 %copy-start.12 = (bf16[640,384]{1,0:T(8,128)(2,1)S(1)}, bf16[640,384]{1,0:T(8,128)(2,1)}, u32[]{:S(2)}) copy-start(bf16[640,384]{1,0:T(8,128)(2,1)} %constant.25.clone.one_x_ref) | copy-start | bytes 1474564
  67.1 9.5 %copy-start.13 = (bf16[144,592]{1,0:T(8,128)(2,1)S(1)}, bf16[144,592]{1,0:T(8,128)(2,1)}, u32[]{:S(2)}) copy-start(bf16[144,592]{1,0:T(8,128)(2,1)} %constant.26.clone.one_zy_ref) | copy-start | bytes 511492
  67.1 9.5 %copy-start.14 = (bf16[384,128]{1,0:T(8,128)(2,1)S(1)}, bf16[384,128]{1,0:T(8,128)(2,1)}, u32[]{:S(2)}) copy-start(bf16[384,128]{1,0:T(8,128)(2,1)} %constant.27.clone.two_x_ref) | copy-start | bytes 294916
  67.1 9.5 %copy-start.15 = (bf16[32,144]{1,0:T(8,128)(2,1)S(1)}, bf16[32,144]{1,0:T(8,128)(2,1)}, u32[]{:S(2)}) copy-start(bf16[32,144]{1,0:T(8,128)(2,1)} %constant.28.clone.two_zy_ref) | copy-start | bytes 27652
  67.1 26.1 %collective-permute-start.12 = (bf16[1,528,640]{2,1,0:T(8,128)(2,1)S(1)}, bf16[1,528,640]{2,1,0:T(8,128)(2,1)S(1)}, u32[]{:S(2)}, u32[]{:S(2)}) collective-permute-start(bf16[1,528,640]{2,1,0:T(8,128)(2,1)S(1)} %get-tuple-element.50.message_ref), channel_id=1, source_target_pairs={{1,0},{2,1},{3,2},{5,4},{6,5},{7,6},{9,8},{10,9},{11,10},{13,12},{... | collective-permute-start | bytes 2027528 | tf_op jit(solution)/shard_map/ppermute | solution.py:570
  69.3 24.0 %collective-permute-start.11 = (bf16[1,528,640]{2,1,0:T(8,128)(2,1)S(1)}, bf16[1,528,640]{2,1,0:T(8,128)(2,1)S(1)}, u32[]{:S(2)}, u32[]{:S(2)}) collective-permute-start(bf16[1,528,640]{2,1,0:T(8,128)(2,1)S(1)} %get-tuple-element.50.message_ref), channel_id=1, source_target_pairs={{0,1},{1,2},{2,3},{4,5},{5,6},{6,7},{8,9},{9,10},{10,11},{12,13},{... | collective-permute-start | bytes 2027528 | tf_op jit(solution)/shard_map/ppermute | solution.py:570
  74.0 19.2 %collective-permute-start.10 = (bf16[2,32,640]{2,1,0:T(8,128)(2,1)S(1)}, bf16[2,32,640]{2,1,0:T(8,128)(2,1)S(1)}, u32[]{:S(2)}, u32[]{:S(2)}) collective-permute-start(bf16[2,32,640]{2,1,0:T(8,128)(2,1)S(1)} %pad_maximum_fusion), channel_id=1, source_target_pairs={{0,2},{1,3},{4,6},{5,7},{8,10},{9,11},{12,14},{13,15},{16,18},{17,... | collective-permute-start | bytes 245768 | tf_op jit(solution)/shard_map/ppermute | solution.py:570
  87.1 18.5 %collective-permute-start.9 = (bf16[1,528,640]{2,1,0:T(8,128)(2,1)S(1)}, bf16[1,528,640]{2,1,0:T(8,128)(2,1)S(1)}, u32[]{:S(2)}, u32[]{:S(2)}) collective-permute-start(bf16[1,528,640]{2,1,0:T(8,128)(2,1)S(1)} %get-tuple-element.44.message_ref), channel_id=1, source_target_pairs={{1,0},{2,1},{3,2},{5,4},{6,5},{7,6},{9,8},{10,9},{11,10},{13,12},{... | collective-permute-start | bytes 2027528 | tf_op jit(solution)/shard_map/ppermute | solution.py:570
  91.1 18.0 %collective-permute-start.8 = (bf16[1,528,640]{2,1,0:T(8,128)(2,1)S(1)}, bf16[1,528,640]{2,1,0:T(8,128)(2,1)S(1)}, u32[]{:S(2)}, u32[]{:S(2)}) collective-permute-start(bf16[1,528,640]{2,1,0:T(8,128)(2,1)S(1)} %get-tuple-element.44.message_ref), channel_id=1, source_target_pairs={{0,1},{1,2},{2,3},{4,5},{5,6},{6,7},{8,9},{9,10},{10,11},{12,13},{... | collective-permute-start | bytes 2027528 | tf_op jit(solution)/shard_map/ppermute | solution.py:570
